TPU v7x, 32 devices: a whole 2x2x4 slice. The times are simulated.
32 devices in a mesh: sec: 2 (over core), seq: 4 (over z), tp: 4 (over y, x).
Axes of the slice: x: 2, y: 2, z: 4, core: 2. Of those that a mesh axis runs over, the one named last changes fastest.
Arguments:
- vis_hidden: bfloat16 [768, 8192], P('tp', 'seq'), may hold values from -6 to 6
- proj_weight: bfloat16 [8192, 8192], P('seq', 'tp'), may hold values from -0.0625 to 0.0625
- proj_bias: float32 [8192], P('tp'), may hold values from -3 to 3
- text_embed: bfloat16 [4096, 8192], P('seq', 'tp'), may hold values from -6 to 6
- norm_gain: float32 [8192], P('tp'), may hold values from 0.1 to 1.9
- key_weight: bfloat16 [8192, 1024], P('tp'), may hold values from -0.0625 to 0.0625
- key_cotangent: bfloat16 [4096, 1024], P('seq'), may hold values from -0.119628906 to 0.119628906
- tile_counts: int32 [4], replicated, may hold values from 0 to 2, as said below
- text_counts: int32 [4], replicated, may hold values from 1 to 1024, as said below
- owner_map: int32 [4], replicated, may hold values from 0 to 3, each once
Outputs:
- proj_weight_grad: float32 [8192, 4, 2, 1024], P('seq', 'tp', 'sec')
- proj_bias_grad: float32 [8192], P('tp')
- key_weight_grad: float32 [8192, 1024], P('tp', ('sec', 'seq'))
- key_bias_grad: float32 [1024], replicated
- gain_grad: float32 [8192], P('tp')
Inputs may be any that keep to these rules, and one draw needn't show every extreme that they name: `tile_counts`: tiles of all samples sum to exactly 3; some sample has 2. 256 * tile_counts + text_counts is at most 1024 for every sample; some sample without tiles has 1024 text tokens. `owner_map`: each owner index appears once.
All inputs are finite; a program needn't handle non-finite values.
Results may differ from a plain program's by a relative error of at most 0.02.
Values may be sent and summed in bfloat16 or wider, within the bound.
No kernel may reach another device: no remote copies, remote signals or barrier semaphores. Data moves between devices by JAX's collectives and lax.ppermute only.
A program may use at most 128 MiB of HBM per device.

v0:
```python
import jax
import jax.numpy as jnp
from jax import lax
from jax.sharding import PartitionSpec as P

D = 8192
TILE = 256
MAXT = 2


epsilon = 1e-06


def from_behind(x, axis, by):
    count = lax.axis_size(axis)
    pairs = [(i, i + by) for i in range(count) if 0 <= i + by < count]
    return lax.ppermute(x, axis, pairs)


def on_device(
    vis_hidden,
    proj_weight,
    proj_bias,
    text_embed,
    norm_gain,
    key_weight,
    key_cotangent,
    tile_counts,
    text_counts,
    owner_map,
):
    seq_count = lax.axis_size("seq")
    seq_index = lax.axis_index("seq")
    is_vision = lax.axis_index("sec") == 0
    image_slots = MAXT * TILE
    slot_rows = image_slots // seq_count
    columns = proj_weight.shape[1]
    activated = jax.nn.gelu(vis_hidden.astype(jnp.float32), approximate=False).astype(jnp.bfloat16)
    gathered = lax.all_gather(activated, "tp", axis=0, tiled=True)
    stream_rows = gathered.shape[0]
    own_rows = stream_rows // seq_count
    spread = gathered.reshape(own_rows, seq_count, -1).transpose(1, 0, 2).reshape(stream_rows, -1)
    summed = lax.psum_scatter(
        lax.cond(
            is_vision,
            lambda block_in: jnp.dot(block_in, proj_weight, preferred_element_type=jnp.float32),
            lambda block_in: jnp.zeros((lax.axis_size("seq") * own_rows, columns), jnp.float32),
            spread,
        ).astype(jnp.bfloat16),
        "seq",
        scatter_dimension=0,
        tiled=True,
    ).astype(jnp.float32)
    image_embed = (summed + proj_bias).astype(jnp.bfloat16)
    arrived = from_behind(image_embed, "sec", 1)
    starts = TILE * (jnp.cumsum(tile_counts) - tile_counts)
    owner_ids = jnp.arange(seq_count, dtype=jnp.int32)
    matches = owner_map[:, None] == owner_ids[None, :]
    owner_start = jnp.sum(jnp.where(matches, starts[:, None], 0), 0)
    local_start = owner_start // seq_count
    is_mine = owner_map == seq_index
    image_count = TILE * jnp.sum(jnp.where(is_mine, tile_counts, 0))
    text_count = jnp.sum(jnp.where(is_mine, text_counts, 0))
    padded = jnp.concatenate([arrived, jnp.zeros((slot_rows, columns), jnp.bfloat16)], 0)
    outgoing = jax.vmap(
        lambda begin_row: lax.dynamic_slice_in_dim(padded, begin_row, slot_rows, 0)
    )(local_start)
    incoming = lax.all_to_all(outgoing, "seq", split_axis=0, concat_axis=0, tiled=True)
    image_rows = incoming.transpose(1, 0, 2).reshape(image_slots, columns)
    seq_len = text_embed.shape[0]
    positions = jnp.arange(seq_len, dtype=jnp.int32)
    image_full = jnp.concatenate(
        [image_rows, jnp.zeros((seq_len - image_slots, columns), jnp.bfloat16)], 0
    )
    text_padded = jnp.concatenate([jnp.zeros((image_slots, columns), jnp.bfloat16), text_embed], 0)
    shifted = lax.dynamic_slice_in_dim(text_padded, image_slots - image_count, seq_len, 0)
    seq_input = jnp.where(
        (positions < image_count)[:, None],
        image_full,
        jnp.where(
            (positions < image_count + text_count)[:, None], shifted, jnp.zeros_like(shifted)
        ),
    )
    values = seq_input.astype(jnp.float32)
    squares = lax.psum(jnp.sum(values * values, 1), "tp")
    inv_rms = lax.rsqrt(squares / D + epsilon)
    unit_rows = values * inv_rms[:, None]
    normed = (unit_rows * norm_gain).astype(jnp.bfloat16)
    feature_cols = key_weight.shape[0]
    key_cols = key_weight.shape[1]

    def llm_products():
        weight_part = lax.dot_general(
            normed, key_cotangent, (((0,), (0,)), ((), ())), preferred_element_type=jnp.float32
        )
        back_part = lax.dot_general(
            key_cotangent, key_weight, (((1,), (1,)), ((), ())), preferred_element_type=jnp.float32
        )
        return (weight_part, back_part)

    def llm_resting():
        return (
            jnp.zeros((feature_cols, key_cols), jnp.float32),
            jnp.zeros((seq_len, feature_cols), jnp.float32),
        )

    weight_part, normed_grad = lax.cond(is_vision, llm_resting, llm_products)
    gain_part = jnp.sum(normed_grad * unit_rows, 0)
    bias_part = jnp.where(is_vision, 0.0, jnp.sum(key_cotangent.astype(jnp.float32), 0))
    key_bias_grad, gain_grad = lax.psum((bias_part, gain_part), ("sec", "seq"))
    key_weight_grad = lax.psum_scatter(
        weight_part.astype(jnp.bfloat16), ("sec", "seq"), scatter_dimension=1, tiled=True
    ).astype(jnp.float32)
    scaled = normed_grad[:image_slots] * norm_gain
    image_unit = unit_rows[:image_slots]
    mean_term = lax.psum(jnp.sum(scaled * image_unit, 1), "tp") / D
    input_grad = inv_rms[:image_slots, None] * (scaled - image_unit * mean_term[:, None])
    input_grad = jnp.where(
        (positions[:image_slots] < image_count)[:, None], input_grad, jnp.zeros_like(input_grad)
    ).astype(jnp.bfloat16)
    leaving = input_grad.reshape(slot_rows, seq_count, columns).transpose(1, 0, 2)
    coming = lax.all_to_all(leaving, "seq", split_axis=0, concat_axis=0, tiled=True)

    def place(owner_index, rows_acc):
        begin_row = local_start[owner_index]
        current = lax.dynamic_slice_in_dim(rows_acc, begin_row, slot_rows, 0)
        return lax.dynamic_update_slice_in_dim(
            rows_acc, current + coming[owner_index], begin_row, 0
        )

    placed = lax.fori_loop(
        0, seq_count, place, jnp.zeros((own_rows + slot_rows, columns), jnp.bfloat16)
    )
    embed_grad = placed[:own_rows]
    returned = from_behind(embed_grad, "sec", -1)
    grad_stream = lax.all_gather(returned, "seq", axis=0, tiled=True)

    def vision_product():
        return lax.dot_general(
            spread, grad_stream, (((0,), (0,)), ((), ())), preferred_element_type=jnp.float32
        )

    def vision_resting():
        return jnp.zeros((spread.shape[1], columns), jnp.float32)

    weight_grad = lax.cond(is_vision, vision_product, vision_resting)
    bias_local = jnp.where(is_vision, jnp.sum(returned.astype(jnp.float32), 0), 0.0)
    proj_bias_grad = lax.psum(bias_local, ("sec", "seq"))
    halves = weight_grad.reshape(weight_grad.shape[0], 2, columns // 2)
    moved = from_behind(halves[:, 1].astype(jnp.bfloat16), "sec", 1).astype(jnp.float32)
    proj_weight_grad = jnp.where(is_vision, halves[:, 0], moved).reshape(
        weight_grad.shape[0], 1, 1, columns // 2
    )
    return (proj_weight_grad, proj_bias_grad, key_weight_grad, key_bias_grad, gain_grad)


def solution(mesh):
    placed = (
        P("tp", "seq"),
        P("seq", "tp"),
        P("tp"),
        P("seq", "tp"),
        P("tp"),
        P("tp", None),
        P("seq", None),
        P(),
        P(),
        P(),
    )
    return jax.shard_map(
        on_device,
        mesh=mesh,
        in_specs=placed,
        out_specs=(P("seq", "tp", "sec", None), P("tp"), P("tp", ("sec", "seq")), P(), P("tp")),
        check_vma=False,
    )
```

profile of v0, /device:TPU:0, one launch (start us, length us, event | category | flops | bytes accessed | tf_op | source)
XLA Modules:
  0.0 541.2 jit_solution(8664389931102094383)
XLA Ops:
  7.2 5.2 fusion.7
  12.4 46.8 %all-gather.3.cloned.1.call-done = bf16[768,2048]{1,0:T(8,128)(2,1)} async-done(((bf16[192,2048]{1,0:T(8,128)(2,1)}), bf16[768,2048]{1,0:T(8,128)(2,1)}) %all-gather.3.cloned.1.call-update) | async-done | bytes 3145744 | tf_op jit(solution)/shard_map/all_gather | solution.py:39
  59.2 4.0 reshape.129
  63.2 3.4 copy.28
  66.6 10.0 %conditional.3 = (bf16[768,2048]{1,0:T(8,128)(2,1)S(1)}) conditional(s32[]{:T(128)} %convert_element_type.48, () %tuple.43, (bf16[768,2048]{1,0:T(8,128)(2,1)}, bf16[2048,2048]{1,0:T(8,128)(2,1)}) %tuple.98), branch_computations={%region_3.0_spmd, %region_4.5_spmd} | conditional | flops 6442450944 | bytes 14680072 | solution.py:44
  66.6 10.0 %fusion.41 = bf16[768,2048]{1,0:T(8,128)(2,1)S(1)} fusion(bf16[768,2048]{1,0:T(8,128)(2,1)} %get-tuple-element.93, bf16[2048,2048]{1,0:T(8,128)(2,1)} %get-tuple-element.117), kind=kOutput, calls=%fused_computation.81 | convolution fusion | flops 6442450944 | bytes 14680064 | tf_op jit(solution)/shard_map/cond/branch_1_fun/dot_general | solution.py:46
  76.7 1.6 copy-done.3
  78.3 60.4 %reduce-scatter.5.cloned.1.call-done = bf16[192,2048]{1,0:T(8,128)(2,1)} async-done(((bf16[768,2048]{1,0:T(8,128)(2,1)}), bf16[192,2048]{1,0:T(8,128)(2,1)}) %reduce-scatter.5.cloned.1.call-update) | async-done | bytes 786448 | tf_op jit(solution)/shard_map/reduce_scatter | solution.py:43
  138.7 1.3 add_convert_fusion
  140.0 1.6 collective-permute-start
  141.9 0.6 fusion.38
  142.6 0.9 collective-permute-done
  143.7 8.8 %while.15 = (s32[]{:T(128)}, bf16[320,2048]{1,0:T(8,128)(2,1)S(1)}, s32[4,2]{0,1:T(2,128)S(1)}, bf16[4,128,2048]{2,1,0:T(8,128)(2,1)}, s32[]{:T(128)}) while((s32[]{:T(128)}, bf16[320,2048]{1,0:T(8,128)(2,1)S(1)}, s32[4,2]{0,1:T(2,128)S(1)}, bf16[4,128,2048]{2,1,0:T(8,128)(2,1)}, s32[]{:T(128)}) %tuple.78), condition=%wide.while_cond, body=%wide.while_body.sunk | while | flops 2 | bytes 1049189 | solution.py:66
  144.3 1.6 bitcast_dynamic-update-slice_fusion.2
  146.5 1.6 bitcast_dynamic-update-slice_fusion.2
  148.7 1.6 bitcast_dynamic-update-slice_fusion.2
  150.9 1.6 bitcast_dynamic-update-slice_fusion.2
  152.5 3.9 all-to-all-start
  157.7 47.4 %all-to-all-done = bf16[4,128,2048]{2,1,0:T(8,128)(2,1)S(1)} async-done(((bf16[4,128,2048]{2,1,0:T(8,128)(2,1)}), bf16[4,128,2048]{2,1,0:T(8,128)(2,1)S(1)}, u32[]{:S(2)}, u32[]{:S(2)}) %all-to-all-start) | async-done | bytes 2097184 | tf_op jit(solution)/shard_map/all_to_all | solution.py:68
  205.1 2.9 copy.29
  208.1 2.5 reshape.133
  210.6 6.0 %fusion = (f32[1024]{0:T(1024)S(1)}, bf16[1024,2048]{1,0:T(8,128)(2,1)}) fusion(s32[]{:T(128)S(6)} %select_n.94, bf16[1024,2048]{1,0:T(8,128)(2,1)} %param.21, pred[1024]{0:T(1024)(128)(4,1)S(1)} %get-tuple-element.173, bf16[512,2048]{1,0:T(8,128)(2,1)S(1)} %reshape.133, pred[1024]{0:T(1024)(128)(4,1)S(1)} %get-tuple-element.174), kind=kLoop, calls=%fused_computation.5 | loop fusion | flops 10484736 | bytes 10491908 | tf_op jit(solution)/shard_map/reduce_sum | solution.py:85
  216.6 9.8 %psum.35 = f32[1024]{0:T(1024)S(1)} all-reduce(f32[1024]{0:T(1024)S(1)} %get-tuple-element.168), channel_id=1, replica_groups=mesh['sec'=2,'seq'=4,'tp'=4] {'tp'}, use_global_device_ids=true, to_apply=%region_8.9 | all-reduce | flops 1024 | bytes 8192 | tf_op jit(solution)/shard_map/psum | solution.py:85
  226.4 3.3 multiply_convert_fusion
  229.8 0.7 copy-done.16
  230.5 1.6 conditional.4
  231.0 1.0 broadcast.105
  232.1 3.4 copy-done.1
  235.5 2.0 copy-done.4
  237.4 5.8 %multiply_reduce_fusion = (f32[2048]{0:T(1024)S(1)}, f32[1024,2048]{1,0:T(8,128)S(1)}) fusion(f32[1024,2048]{1,0:T(8,128)} %copy-done.1, f32[1024]{0:T(1024)S(1)} %add_rsqrt_fusion, bf16[1024,2048]{1,0:T(8,128)(2,1)} %get-tuple-element.169), kind=kLoop, calls=%fused_computation.10 | loop fusion | flops 8386560 | bytes 20983808 | tf_op jit(solution)/shard_map/reduce_sum | solution.py:108
  243.2 3.2 copy-done
  247.0 8.0 %psum.36 = f32[512]{0:T(512)S(1)} all-reduce(f32[512]{0:T(512)S(1)} %multiply_reduce_fusion.1), channel_id=1, replica_groups=mesh['sec'=2,'seq'=4,'tp'=4] {'tp'}, use_global_device_ids=true, to_apply=%region_12.13 | all-reduce | flops 512 | bytes 4096 | tf_op jit(solution)/shard_map/psum | solution.py:116
  255.0 4.9 select_convert_fusion
  259.9 2.7 reshape.134
  262.7 2.5 copy.30
  265.1 4.5 all-to-all-start.1
  269.9 48.3 %all-to-all-done.1 = bf16[4,128,2048]{2,1,0:T(8,128)(2,1)} async-done(((bf16[4,128,2048]{2,1,0:T(8,128)(2,1)}), bf16[4,128,2048]{2,1,0:T(8,128)(2,1)}, u32[]{:S(2)}, u32[]{:S(2)}) %all-to-all-start.1) | async-done | bytes 2097184 | tf_op jit(solution)/shard_map/all_to_all | solution.py:122
  318.3 26.0 %while.14 = (s32[]{:T(128)}, bf16[320,2048]{1,0:T(8,128)(2,1)S(1)}, s32[4]{0:T(128)S(1)}, bf16[4,128,2048]{2,1,0:T(8,128)(2,1)}, s32[]{:T(128)}, /*index=5*/s32[]{:T(128)}, s32[]{:T(128)}) while((s32[]{:T(128)}, bf16[320,2048]{1,0:T(8,128)(2,1)S(1)}, s32[4]{0:T(128)S(1)}, bf16[4,128,2048]{2,1,0:T(8,128)(2,1)}, s32[]{:T(128)}, ...), condition=%wide.region_14.15_spmd, body=%wide.region_13.14_spmd.sunk | while | flops 1048581 | bytes 2621583 | solution.py:131
  320.9 1.2 bitcast_add_fusion.2
  322.1 2.5 dynamic_update_slice.8
  324.6 0.6 dynamic_slice.38
  327.2 1.2 bitcast_add_fusion.2
  328.4 2.9 dynamic_update_slice.8
  331.3 0.6 dynamic_slice.38
  333.9 1.2 bitcast_add_fusion.2
  335.1 2.5 dynamic_update_slice.8
  340.2 1.2 bitcast_add_fusion.2
  341.4 2.9 dynamic_update_slice.8
  344.4 1.3 collective-permute-start.1
  345.7 2.9 collective-permute-done.1
  348.6 0.9 copy-done.6
  349.5 6.6 %copy.33 = bf16[2048,1024]{0,1:T(8,128)(2,1)} copy(bf16[2048,1024]{1,0:T(8,128)(2,1)} %copy-done.4) | data formatting | bytes 8388608
  356.2 54.9 %all-gather.5.cloned.1.call-done = bf16[768,2048]{1,0:T(8,128)(2,1)} async-done(((bf16[192,2048]{1,0:T(8,128)(2,1)}), bf16[768,2048]{1,0:T(8,128)(2,1)}) %all-gather.5.cloned.1.call-update) | async-done | bytes 3145744 | tf_op jit(solution)/shard_map/all_gather | solution.py:136
  411.1 12.1 %conditional.5 = (f32[2048,2048]{1,0:T(8,128)}) conditional(s32[]{:T(128)} %convert_element_type.48, () %tuple.42, (bf16[768,2048]{1,0:T(8,128)(2,1)S(1)}, bf16[768,2048]{1,0:T(8,128)(2,1)}) %tuple.99), branch_computations={%region_15.16_spmd, %region_16.17_spmd} | conditional | flops 6442450944 | bytes 23068680 | solution.py:146
  411.1 12.1 %fusion.44 = f32[2048,2048]{1,0:T(8,128)} fusion(bf16[768,2048]{1,0:T(8,128)(2,1)S(1)} %get-tuple-element.103, bf16[768,2048]{1,0:T(8,128)(2,1)} %get-tuple-element.104), kind=kOutput, calls=%fused_computation.84 | convolution fusion | flops 6442450944 | bytes 23068672 | tf_op jit(solution)/shard_map/cond/branch_1_fun/dot_general | solution.py:139
  423.2 17.7 %copy.31 = f32[2048,2048]{0,1:T(8,128)} copy(f32[2048,2048]{1,0:T(8,128)} %get-tuple-element.266) | data formatting | bytes 33554432 | tf_op jit(solution)/shard_map/cond | solution.py:146
  440.8 6.2 %fusion.5 = bf16[2048,1024]{0,1:T(8,128)(2,1)} fusion(f32[2048,2,1024]{0,2,1:T(8,128)} %bitcast.55), kind=kLoop, calls=%fused_computation.15 | loop fusion | bytes 8388608 | tf_op jit(solution)/shard_map/convert_element_type | solution.py:150
  447.1 3.4 collective-permute-start.2
  451.0 30.6 %all-reduce.4 = (f32[2048]{0:T(1024)}, f32[1024]{0:T(1024)}, f32[2048]{0:T(1024)}) all-reduce(f32[2048]{0:T(1024)S(1)} %broadcast_select_fusion, f32[1024]{0:T(1024)S(1)} %broadcast_select_fusion.1, f32[2048]{0:T(1024)S(1)} %get-tuple-element.170), channel_id=1, replica_groups=mesh['sec'=2,'seq'=4,'tp'=4] {'sec','seq'}, use_global_device_ids=true, to_apply=%region_18.19 | all-reduce | flops 5120 | bytes 40960 | tf_op jit(solution)/shard_map/psum | solution.py:148
  481.7 20.2 %reduce-scatter.7.cloned.1.call-done = bf16[128,2048]{1,0:T(8,128)(2,1)} async-done(((bf16[1024,2048]{1,0:T(8,128)(2,1)}), bf16[128,2048]{1,0:T(8,128)(2,1)}) %reduce-scatter.7.cloned.1.call-update) | async-done | bytes 524304
  501.9 1.3 copy.34
  503.2 1.0 convert_element_type.61
  504.2 9.9 %fusion.2 = f32[2048,1,1,1024]{0,3,2,1:T(8,128)} fusion(f32[2048,2,1024]{0,2,1:T(8,128)} %bitcast.56, bf16[2048,1024]{0,1:T(8,128)(2,1)} %collective-permute-done.2, pred[]{:T(512)S(6)} %eq.22), kind=kLoop, calls=%fused_computation.9 | loop fusion | flops 4194304 | bytes 20971520 | tf_op jit(solution)/shard_map/reshape | solution.py:151
  514.2 20.5 %copy.32 = f32[2048,1,1,1024]{3,2,1,0:T(1,128)} copy(f32[2048,1,1,1024]{0,3,2,1:T(8,128)} %fusion.2) | data formatting | bytes 16777216
  (69 shorter events, 6.4 us)
Async XLA Ops:
  7.2 52.1 %all-gather.3.cloned.1.call-start = ((), (), s32[]{:S(2)}) async-start(), calls=%async_computation.4 | async-start | bytes 3932160 | tf_op jit(solution)/shard_map/all_gather | solution.py:39
  12.4 126.3 %reduce-scatter.5.cloned.1.call-start = ((), (), s32[]{:S(2)}) async-start(), calls=%async_computation.5 | async-start | bytes 3932160 | tf_op jit(solution)/shard_map/reduce_scatter | solution.py:43
  76.6 1.7 copy-start.3
  76.6 62.1 %copy-start.12 = (f32[2048]{0:T(1024)S(1)}, f32[2048]{0:T(1024)}, u32[]{:S(2)}) copy-start(f32[2048]{0:T(1024)} %param.20) | copy-start | bytes 24580
  76.7 65.0 %copy-start.14 = (s32[4]{0:T(128)S(1)}, s32[4]{0:T(128)}, u32[]{:S(2)}) copy-start(s32[4]{0:T(128)} %param.25) | copy-start | bytes 52
  76.7 65.2 %copy-start.13 = (s32[4]{0:T(128)S(1)}, s32[4]{0:T(128)}, u32[]{:S(2)}) copy-start(s32[4]{0:T(128)} %param.26) | copy-start | bytes 52
  76.7 65.2 %copy-start.15 = (s32[4]{0:T(128)S(1)}, s32[4]{0:T(128)}, u32[]{:S(2)}) copy-start(s32[4]{0:T(128)} %param.27) | copy-start | bytes 52
  140.0 3.5 collective-permute-start
  152.5 52.7 %all-to-all-start = ((bf16[4,128,2048]{2,1,0:T(8,128)(2,1)}), bf16[4,128,2048]{2,1,0:T(8,128)(2,1)S(1)}, u32[]{:S(2)}, u32[]{:S(2)}) async-start(bf16[4,128,2048]{2,1,0:T(8,128)(2,1)} %get-tuple-element.127), calls=%async_computation.1 | async-start | bytes 4194304 | tf_op jit(solution)/shard_map/all_to_all | solution.py:68
  210.6 15.8 %copy-start.10 = (f32[2048]{0:T(1024)S(1)}, f32[2048]{0:T(1024)}, u32[]{:S(2)}) copy-start(f32[2048]{0:T(1024)} %param.22) | copy-start | bytes 24580
  226.4 11.1 %copy-start.11 = (f32[1024]{0:T(1024)}, f32[1024]{0:T(1024)S(1)}, u32[]{:S(2)}) copy-start(f32[1024]{0:T(1024)S(1)} %add_rsqrt_fusion) | copy-start | bytes 12292
  226.4 3.4 copy-start.8
  226.4 4.1 copy-start.16
  232.1 3.4 copy-start.1
  235.5 2.0 copy-start.4
  237.4 9.0 %copy-start.2 = (f32[1024,2048]{1,0:T(8,128)S(1)}, f32[1024,2048]{1,0:T(8,128)}, u32[]{:S(2)}) copy-start(f32[1024,2048]{1,0:T(8,128)} %copy-done.1) | copy-start | bytes 25165828
  243.2 3.2 copy-start
  246.5 8.5 %slice-start = ((f32[1024]{0:T(1024)}), f32[512]{0:T(512)S(1)}, s32[]{:S(2)}) async-start(f32[1024]{0:T(1024)} %copy-done.11), calls=%async_computation.8 | async-start | bytes 4096 | tf_op jit(solution)/shard_map/slice | solution.py:117
  265.1 53.1 %all-to-all-start.1 = ((bf16[4,128,2048]{2,1,0:T(8,128)(2,1)}), bf16[4,128,2048]{2,1,0:T(8,128)(2,1)}, u32[]{:S(2)}, u32[]{:S(2)}) async-start(bf16[4,128,2048]{2,1,0:T(8,128)(2,1)} %copy.30), calls=%async_computation.2 | async-start | bytes 4194304 | tf_op jit(solution)/shard_map/all_to_all | solution.py:122
  269.6 141.5 %all-gather.5.cloned.1.call-start = ((), (), s32[]{:S(2)}) async-start(), calls=%async_computation.6 | async-start | bytes 3932160 | tf_op jit(solution)/shard_map/all_gather | solution.py:136
  344.4 4.2 collective-permute-start.1
  348.6 0.9 copy-start.6
  349.5 152.4 %reduce-scatter.7.cloned.1.call-start = ((), (), s32[]{:S(2)}) async-start(), calls=%async_computation.7 | async-start | bytes 4718592
  356.1 54.9 %copy-start.5 = (bf16[192,4,2048]{2,0,1:T(8,128)(2,1)S(1)}, bf16[192,4,2048]{2,0,1:T(8,128)(2,1)}, u32[]{:S(2)}) copy-start(bf16[192,4,2048]{2,0,1:T(8,128)(2,1)} %copy.28) | copy-start | bytes 9437188
  440.8 9.6 %copy-start.9 = (bf16[1024,1024]{1,0:T(8,128)(2,1)S(1)}, bf16[1024,1024]{1,0:T(8,128)(2,1)}, u32[]{:S(2)}) copy-start(bf16[1024,1024]{1,0:T(8,128)(2,1)} %param.24) | copy-start | bytes 6291460
  447.1 3.8 copy-start.7
  447.1 57.2 %collective-permute-start.2 = (bf16[2048,1024]{0,1:T(8,128)(2,1)}, bf16[2048,1024]{0,1:T(8,128)(2,1)}, u32[]{:S(2)}, u32[]{:S(2)}) collective-permute-start(bf16[2048,1024]{0,1:T(8,128)(2,1)} %fusion.5), channel_id=1, source_target_pairs={{0,16},{1,17},{2,18},{3,19},{4,20},{5,21},{6,22},{7,23},{8,24},{9,... | collective-permute-start | bytes 12582920 | tf_op jit(solution)/shard_map/ppermute | solution.py:17
Sparse Core Ops, SparseCore 0:
  12.5 46.6 all-gather.2
  78.4 60.2 reduce-scatter.4
  349.6 61.4 all-gather.4
  413.2 88.6 reduce-scatter.6
where the time goes:
time: 544 us; the launch traced here: 541 us
  waiting for transfers between devices  282 us (52%)
  local copies, waits for them, and re-layouts  106 us (19%)
  blocking collectives  48.4 us (9%)
  other arithmetic  44.4 us (8%)
  matrix products  22.1 us (4%)
  between operations  15.4 us (3%)
  starting transfers between devices  15.1 us (3%)
  loops' own time  7.91 us (1%)
    reduce_scatter x1, waiting for transfers between devices, on_device(): lax.psum_scatter(lax.cond(is_vision, lambda block_in: jnp.dot(block_in, p...  60.4 us
    all_gather x1, waiting for transfers between devices, on_device(): grad_stream = lax.all_gather(returned, 'seq', axis=0, tiled=True)  54.9 us
    all_to_all x1, waiting for transfers between devices, on_device(): lax.all_to_all(leaving, 'seq', split_axis=0, concat_axis=0, tiled=True)  48.3 us
    all_to_all x1, waiting for transfers between devices, on_device(): lax.all_to_all(outgoing, 'seq', split_axis=0, concat_axis=0, tiled=True)  47.4 us
    all_gather x1, waiting for transfers between devices, on_device(): gathered = lax.all_gather(activated, 'tp', axis=0, tiled=True)  46.8 us
    unnamed x37, local copies, waits for them, and re-layouts  40.2 us
    psum x1, blocking collectives, on_device(): proj_bias_grad = lax.psum(bias_local, ('sec', 'seq'))  30.6 us
    unnamed x5, waiting for transfers between devices  20.3 us
  transfers between devices with their start and end apart: 9, of which 8 were waited for; matrix products, arithmetic and copies ran while one was open for 9% of the time, Pallas kernels for 0%

commit v1 on v0

v1 whole, which is shorter than its diff:
```python
import jax
import jax.numpy as jnp
from jax import lax
from jax.experimental import pallas as pl
from jax.experimental.pallas import tpu as pltpu
from jax.sharding import PartitionSpec as P

D = 8192
TILE = 256
MAXT = 2
LANES = 128
EPSILON = 1e-06


def swap(x, axis, mask):
    count = lax.axis_size(axis)
    return lax.ppermute(x, axis, [(i, i ^ mask) for i in range(count)])


def butterfly(x, axes):
    for axis in axes:
        mask = 1
        while mask < lax.axis_size(axis):
            x = x + swap(x, axis, mask)
            mask *= 2
    return x


def in_order(pieces, index):
    pieces = list(pieces)
    mask = 1
    while mask < len(pieces):
        odd = (index & mask) != 0
        pieces = [jnp.where(odd, pieces[m ^ mask], pieces[m]) for m in range(len(pieces))]
        mask *= 2
    return pieces


def weight_kernel(act_ref, grad_ref, out_ref):
    width = grad_ref.shape[1]
    rows = act_ref.shape[1]
    groups = width // LANES
    product = lax.dot_general(
        act_ref[...], grad_ref[...], (((0,), (0,)), ((), ())), preferred_element_type=jnp.float32
    )
    for c in range(groups):
        out_ref[pl.ds(c, rows, stride=groups), :] = product[:, c * LANES : (c + 1) * LANES]


def weight_product(act, grad):
    rows, features = act.shape
    width = grad.shape[1]
    groups = width // LANES
    step = 256
    return pl.pallas_call(
        weight_kernel,
        grid=(features // step,),
        in_specs=[
            pl.BlockSpec((rows, step), lambda i: (0, i)),
            pl.BlockSpec((rows, width), lambda i: (0, 0)),
        ],
        out_specs=pl.BlockSpec((step * groups, LANES), lambda i: (i, 0)),
        out_shape=jax.ShapeDtypeStruct((features * groups, LANES), jnp.float32),
        compiler_params=pltpu.CompilerParams(vmem_limit_bytes=32 * 1024 * 1024),
        cost_estimate=pl.CostEstimate(
            flops=2 * rows * features * width,
            bytes_accessed=4 * features * width + 2 * rows * (features + width),
            transcendentals=0,
        ),
    )(act, grad)


def on_device(
    vis_hidden,
    proj_weight,
    proj_bias,
    text_embed,
    norm_gain,
    key_weight,
    key_cotangent,
    tile_counts,
    text_counts,
    owner_map,
):
    f32, bf16 = jnp.float32, jnp.bfloat16
    n_sec, n_seq, n_tp = (lax.axis_size(a) for a in ("sec", "seq", "tp"))
    core, z, t = (lax.axis_index(a) for a in ("sec", "seq", "tp"))
    block_rows, features = vis_hidden.shape
    columns = proj_weight.shape[1]
    stream = block_rows * n_tp
    own = stream // n_seq
    half = own // n_sec
    groups = block_rows // own
    keys = key_weight.shape[1]
    seq_len = text_embed.shape[0]
    tiles = stream // TILE

    grouped = vis_hidden.reshape(groups, n_sec, half, features)
    mine = lax.dynamic_index_in_dim(grouped, core, 1, keepdims=False)
    act = jax.nn.gelu(mine.astype(f32), approximate=False).astype(bf16)
    act = act.reshape(groups * half, features)
    pieces = [act] + [swap(act, "tp", m) for m in range(1, n_tp)]
    act_half = jnp.concatenate(in_order(pieces, t), 0)
    partial = jnp.dot(act_half, proj_weight, preferred_element_type=f32).astype(bf16)
    summed = lax.psum_scatter(partial, "seq", scatter_dimension=0, tiled=True).astype(f32)
    image_mine = (summed + proj_bias).astype(bf16)
    image = jnp.concatenate(in_order([image_mine, swap(image_mine, "sec", 1)], core), 0)

    act_other = swap(act_half, "sec", 1)
    act_full = jnp.stack(
        in_order([a.reshape(n_seq, half, features) for a in (act_half, act_other)], core), 1
    ).reshape(stream, features)

    starts = jnp.cumsum(tile_counts) - tile_counts
    tile_ids = jnp.arange(tiles, dtype=jnp.int32)[:, None]
    held = (tile_ids >= starts[None]) & (tile_ids < (starts + tile_counts)[None])
    tile_owner = jnp.sum(jnp.where(held, owner_map[None], 0), 1)
    tile_place = jnp.sum(jnp.where(held, tile_ids - starts[None], 0), 1)
    share = keys // (n_sec * n_tp)
    from_col = (core * n_tp + t) * share
    front = lax.dynamic_slice_in_dim(key_cotangent[: MAXT * TILE], from_col, share, 1)
    front = front.reshape(MAXT, TILE, share)
    given = jnp.zeros((tiles, TILE, share), bf16)
    for place in range(MAXT):
        chosen = (tile_owner == z) & (tile_place == place)
        given = jnp.where(chosen[:, None, None], front[place][None], given)
    taken = lax.psum_scatter(
        given.reshape(stream, share), "seq", scatter_dimension=0, tiled=True
    )
    taken = lax.all_gather(taken, ("sec", "tp"), axis=0, tiled=False)
    image_cot = taken.transpose(1, 0, 2).reshape(own, keys)

    is_mine = owner_map == z
    image_count = TILE * jnp.sum(jnp.where(is_mine, tile_counts, 0))
    text_count = jnp.sum(jnp.where(is_mine, text_counts, 0))
    text_values = text_embed.astype(f32)
    text_sq = butterfly(jnp.sum(text_values * text_values, 1), ("tp",))
    text_inv = lax.rsqrt(text_sq / D + EPSILON)
    text_scale = jnp.where(jnp.arange(seq_len) < text_count, text_inv, 0.0)
    key_half = keys // n_sec
    cot_half = lax.dynamic_slice_in_dim(key_cotangent, core * key_half, key_half, 1)
    cot_padded = jnp.concatenate([cot_half, jnp.zeros((MAXT * TILE, key_half), bf16)], 0)
    cot_text = lax.dynamic_slice_in_dim(cot_padded, image_count, seq_len, 0)
    cot_text = (cot_text.astype(f32) * text_scale[:, None]).astype(bf16)

    values = image.astype(f32)
    scaled = lax.dot_general(
        image_cot, key_weight, (((1,), (1,)), ((), ())), preferred_element_type=f32
    ) * norm_gain
    sums = butterfly(jnp.stack([jnp.sum(values * values, 1), jnp.sum(scaled * values, 1)]), ("tp",))
    inv = lax.rsqrt(sums[0] / D + EPSILON)
    mean = inv * sums[1] / D
    embed_grad = (inv[:, None] * (scaled - values * (inv * mean)[:, None])).astype(bf16)
    col_half = columns // n_sec
    grad_half = lax.dynamic_slice_in_dim(embed_grad, core * col_half, col_half, 1)
    grad_all = lax.all_gather(grad_half, "seq", axis=0, tiled=True)

    cot_image = lax.dynamic_slice_in_dim(image_cot, core * key_half, key_half, 1)
    cot_image = (cot_image.astype(f32) * inv[:, None]).astype(bf16)
    rows_first = (((0,), (0,)), ((), ()))
    moment = lax.dot_general(
        text_embed, cot_text, rows_first, preferred_element_type=f32
    ) + lax.dot_general(image, cot_image, rows_first, preferred_element_type=f32)
    weight_half = lax.dynamic_slice_in_dim(key_weight, core * key_half, key_half, 1)
    gain_part = jnp.sum(moment * weight_half.astype(f32), 1)
    shares = (moment * norm_gain[:, None]).astype(bf16)
    shares = shares.reshape(columns, n_seq, key_half // n_seq).transpose(1, 0, 2)
    key_weight_grad = lax.psum_scatter(shares, "seq", scatter_dimension=0, tiled=False)
    key_weight_grad = key_weight_grad.astype(f32)

    key_bias_part = jnp.sum(key_cotangent.astype(f32), 0)
    bias_part = jnp.sum(embed_grad.astype(f32), 0)
    once = jnp.concatenate([key_bias_part, bias_part])
    small = butterfly(jnp.concatenate([gain_part, jnp.where(core == 0, once, 0.0)]), ("sec", "seq"))
    gain_grad = small[:columns]
    key_bias_grad = small[columns : columns + keys]
    proj_bias_grad = small[columns + keys :]

    proj_weight_grad = weight_product(act_full, grad_all).reshape(features, 1, 1, col_half)
    return (proj_weight_grad, proj_bias_grad, key_weight_grad, key_bias_grad, gain_grad)


def solution(mesh):
    placed = (
        P("tp", "seq"),
        P("seq", "tp"),
        P("tp"),
        P("seq", "tp"),
        P("tp"),
        P("tp", None),
        P("seq", None),
        P(),
        P(),
        P(),
    )
    return jax.shard_map(
        on_device,
        mesh=mesh,
        in_specs=placed,
        out_specs=(P("seq", "tp", "sec", None), P("tp"), P("tp", ("sec", "seq")), P(), P("tp")),
        check_vma=False,
    )
```

time: 544 us -> 230 us (0.42)
  waiting for transfers between devices: 282 us -> 112 us
  local copies, waits for them, and re-layouts: 106 us -> 17.1 us
  blocking collectives: 48.4 us -> 24.5 us
  other arithmetic: 44.4 us -> 21.5 us
  loops' own time: 7.91 us -> 0 us
  Pallas kernels: 0 us -> 7.37 us
    all_gather x2 -> x1, waiting for transfers between devices: 102 us -> 0.01 us  [on_device(): grad_all = lax.all_gather(grad_half, 'seq', axis=0, tiled=True)]
    all_to_all x2 -> x0, waiting for transfers between devices: 95.7 us -> none  [the longest x1 48.3 us: on_device(): lax.all_to_all(leaving, 'seq', split_axis=0, concat_axis=0, tiled=True)]
    psum x3 -> x0, blocking collectives: 48.4 us -> none  [the longest x1 30.6 us: on_device(): proj_bias_grad = lax.psum(bias_local, ('sec', 'seq'))]
    unnamed x37 -> x33, local copies, waits for them, and re-layouts: 40.2 us -> 6.48 us
    ppermute x3 -> x12, waiting for transfers between devices: 3.77 us -> 29.6 us  [swap(): return lax.ppermute(x, axis, [(i, i ^ mask) for i in range(count)])]
    all_gather x0 -> x1, blocking collectives: none -> 24.5 us  [on_device(): taken = lax.all_gather(taken, ('sec', 'tp'), axis=0, tiled=False)]
    reduce_scatter x1 -> x3, waiting for transfers between devices: 60.4 us -> 81.9 us  [the longest x1 33.5 us: on_device(): lax.psum_scatter(partial, 'seq', scatter_dimension=0, tiled=True)]
    unnamed x5 -> x4, waiting for transfers between devices: 20.3 us -> 0.07 us
  transfers between devices with their start and end apart: 9 -> 16, of which waited for: 8 -> 11; matrix products, arithmetic and copies ran while one was open for 9% -> 14% of each run, Pallas kernels for 0% -> 3%
where the time goes in v1:
time: 230 us; the launch traced here: 229 us
  waiting for transfers between devices  112 us (49%)
  blocking collectives  24.5 us (11%)
  other arithmetic  21.5 us (9%)
  matrix products  20.6 us (9%)
  local copies, waits for them, and re-layouts  17.1 us (7%)
  between operations  14.7 us (6%)
  starting transfers between devices  11.8 us (5%)
  Pallas kernels  7.37 us (3%)
    reduce_scatter x1, waiting for transfers between devices, on_device(): lax.psum_scatter(partial, 'seq', scatter_dimension=0, tiled=True)  33.5 us
    ppermute x12, waiting for transfers between devices, swap(): return lax.ppermute(x, axis, [(i, i ^ mask) for i in range(count)])  29.6 us
    reduce_scatter x1, waiting for transfers between devices, on_device(): lax.psum_scatter(shares, 'seq', scatter_dimension=0, tiled=False)  28.4 us
    all_gather x1, blocking collectives, on_device(): taken = lax.all_gather(taken, ('sec', 'tp'), axis=0, tiled=False)  24.5 us
    reduce_scatter x1, waiting for transfers between devices, on_device(): lax.psum_scatter(given.reshape(stream, share), 'seq', scatter_dimension=0...  20 us
    ppermute x12, starting transfers between devices, swap(): return lax.ppermute(x, axis, [(i, i ^ mask) for i in range(count)])  11.4 us
    dot_general x1, matrix products, on_device(): jnp.dot(act_half, proj_weight, preferred_element_type=f32).astype(bf16)  9.07 us
    pallas_call x1, Pallas kernels, weight_product(): pl.pallas_call(weight_kernel, grid=(features // step,), in_specs=[pl.Bloc...  7.37 us
  transfers between devices with their start and end apart: 16, of which 11 were waited for; matrix products, arithmetic and copies ran while one was open for 14% of the time, Pallas kernels for 3%

profile of v1, /device:TPU:0, one launch (start us, length us, event | category | flops | bytes accessed | tf_op | source)
XLA Modules:
  0.0 229.2 jit_solution(12802686631012742362)
XLA Ops:
  7.2 0.0 reduce-scatter.4.cloned.1.call-start
  7.2 2.7 %fusion.9 = bf16[96,2048]{1,0:T(8,128)(2,1)S(1)} fusion(bf16[1,2,96,2048]{3,2,1,0:T(8,128)(2,1)} %bitcast.145, s32[]{:T(128)S(6)} %select_n.137), kind=kLoop, calls=%fused_computation.29 | loop fusion | flops 12976128 | bytes 786436 | tf_op jit(solution)/shard_map/convert_element_type | solution.py:100
  9.9 3.0 %collective-permute-start.2 = (bf16[96,2048]{1,0:T(8,128)(2,1)S(1)}, bf16[96,2048]{1,0:T(8,128)(2,1)S(1)}, u32[]{:S(2)}, u32[]{:S(2)}) collective-permute-start(bf16[96,2048]{1,0:T(8,128)(2,1)S(1)} %fusion.9), channel_id=1, source_target_pairs={{0,1},{1,0},{2,3},{3,2},{4,5},{5,4},{6,7},{7,6},{8,9},{9,8},{10,11... | collective-permute-start | bytes 1179656 | tf_op jit(solution)/shard_map/ppermute | solution.py:17
  12.9 1.5 collective-permute-start.1
  14.4 0.0 collective-permute-start
  14.5 8.4 %collective-permute-done.2 = bf16[96,2048]{1,0:T(8,128)(2,1)S(1)} collective-permute-done((bf16[96,2048]{1,0:T(8,128)(2,1)S(1)}, bf16[96,2048]{1,0:T(8,128)(2,1)S(1)}, u32[]{:S(2)}, u32[]{:S(2)}) %collective-permute-start.2) | collective-permute-done | bytes 393248 | tf_op jit(solution)/shard_map/ppermute | solution.py:17
  22.9 9.1 %collective-permute-done.1 = bf16[96,2048]{1,0:T(8,128)(2,1)S(1)} collective-permute-done((bf16[96,2048]{1,0:T(8,128)(2,1)S(1)}, bf16[96,2048]{1,0:T(8,128)(2,1)S(1)}, u32[]{:S(2)}, u32[]{:S(2)}) %collective-permute-start.1) | collective-permute-done | bytes 393248 | tf_op jit(solution)/shard_map/ppermute | solution.py:17
  31.9 3.0 %broadcast_select_fusion.11 = (bf16[96,2048]{1,0:T(8,128)(2,1)S(1)}, bf16[96,2048]{1,0:T(8,128)(2,1)S(1)}, bf16[96,2048]{1,0:T(8,128)(2,1)S(1)}, bf16[96,2048]{1,0:T(8,128)(2,1)S(1)}) fusion(pred[]{:T(512)S(6)} %ne.11, bf16[96,2048]{1,0:T(8,128)(2,1)S(1)} %collective-permute-done, bf16[96,2048]{1,0:T(8,128)(2,1)S(1)} %collective-permute-done.1, pred[]{:T(512)S(6)} %ne.12, ...), kind=kLoop, calls=%fused_computation.74 | loop fusion | flops 14548992 | bytes 3145734 | tf_op jit(solution)/shard_map/jit(_where)/select_n | solution.py:34
  35.0 0.7 copy-done.3
  35.7 0.1 copy-done.5
  35.8 0.1 copy-done.7
  36.0 9.1 %convolution_convert_fusion = bf16[384,2048]{1,0:T(8,128)(2,1)} fusion(bf16[2048,2048]{1,0:T(8,128)(2,1)} %param.11, bf16[96,2048]{1,0:T(8,128)(2,1)S(1)} %get-tuple-element.40, bf16[96,2048]{1,0:T(8,128)(2,1)S(1)} %get-tuple-element.39, bf16[96,2048]{1,0:T(8,128)(2,1)S(1)} %get-tuple-element.38, bf16[96,2048]{1,0:T(8,128)(2,1)S(1)} %get-tuple-element.37), kind=kOutput, calls=%fused_computation.6 | convolution fusion | flops 3228303360 | bytes 11534336 | tf_op jit(solution)/shard_map/dot_general | solution.py:104
  45.1 0.0 reduce-scatter.4.cloned.1.call-update
  45.1 0.0 reduce-scatter.6.cloned.1.call-start
  45.2 0.2 reduce-window.8
  45.4 0.6 fusion.49
  46.0 0.1 select_reduce_fusion.1
  46.1 0.1 broadcast_in_dim.85
  46.2 0.1 broadcast_in_dim.90
  46.4 1.0 fusion.40
  47.4 0.0 all-gather.3.cloned.1.call-start
  47.4 33.5 %reduce-scatter.4.cloned.1.call-done = bf16[96,2048]{1,0:T(8,128)(2,1)} async-done(((bf16[384,2048]{1,0:T(8,128)(2,1)}), bf16[96,2048]{1,0:T(8,128)(2,1)}) %reduce-scatter.4.cloned.1.call-update) | async-done | bytes 393232 | tf_op jit(solution)/shard_map/reduce_scatter | solution.py:105
  80.9 1.1 add_convert_fusion
  82.0 0.1 collective-permute-start.4
  82.0 20.0 %reduce-scatter.6.cloned.1.call-done = bf16[192,128]{1,0:T(8,128)(2,1)} async-done(((bf16[768,128]{1,0:T(8,128)(2,1)}), bf16[192,128]{1,0:T(8,128)(2,1)}) %reduce-scatter.6.cloned.1.call-update) | async-done | bytes 49168 | tf_op jit(solution)/shard_map/reduce_scatter | solution.py:127
  102.1 24.5 %all-gather = bf16[1536,128]{1,0:T(8,128)(2,1)S(1)} all-gather(bf16[192,128]{1,0:T(8,128)(2,1)} %reduce-scatter.6.cloned.1.call-done), channel_id=2, replica_groups=mesh['sec'=2,'seq'=4,'tp'=4] {'sec','tp'}, dimensions={0}, use_global_device_ids=true | all-gather | bytes 442368 | tf_op jit(solution)/shard_map/all_gather | solution.py:130
  126.5 1.3 broadcast_select_fusion.3
  127.9 3.9 %fusion = (f32[192]{0:T(256)S(1)}, f32[192]{0:T(256)S(1)}, f32[192,2048]{1,0:T(8,128)S(1)}) fusion(bf16[96,2048]{1,0:T(8,128)(2,1)S(1)} %get-tuple-element.44, bf16[96,2048]{1,0:T(8,128)(2,1)S(1)} %get-tuple-element.43, f32[2048]{0:T(1024)S(1)} %copy-done.12, bf16[2048,1024]{1,0:T(8,128)(2,1)} %param.15, bf16[8,24,8,128]{3,2,1,0:T(8,128)(2,1)S(1)} %bitcast.142), kind=kOutput, calls=%fused_computation.12 | convolution fusion | flops 808844928 | bytes 6956544 | tf_op jit(solution)/shard_map/dot_general | solution.py:147
  131.8 2.0 collective-permute-start.5
  133.7 1.7 collective-permute-done.5
  135.4 1.5 collective-permute-start.6
  136.9 2.2 collective-permute-done.6
  139.1 0.4 convert_reduce_fusion.1
  139.5 0.8 constant_dynamic-slice_fusion.2
  140.3 0.2 reduce-scatter.8.cloned.1.call-start
  140.5 3.1 %multiply_reduce_fusion = f32[1024]{0:T(1024)S(1)} fusion(bf16[1024,2048]{1,0:T(8,128)(2,1)} %param.13), kind=kLoop, calls=%fused_computation | loop fusion | flops 6290432 | bytes 4198400 | tf_op jit(solution)/shard_map/reduce_sum | solution.py:137
  143.6 2.0 collective-permute-start.7
  145.6 3.3 %constant_dynamic-slice_fusion = bf16[2048,512]{1,0:T(8,128)(2,1)} fusion(bf16[2048,1024]{1,0:T(8,128)(2,1)} %param.15, s32[]{:T(128)S(6)} %select_n.159), kind=kLoop, calls=%fused_computation.91 | loop fusion | bytes 4194308 | tf_op jit(solution)/shard_map/dynamic_slice | solution.py:164
  148.9 0.5 collective-permute-start.8
  149.4 1.1 constant_dynamic-slice_fusion.1
  151.1 2.9 %copy.29 = bf16[2048,512]{0,1:T(8,128)(2,1)S(1)} copy(bf16[2048,512]{1,0:T(8,128)(2,1)} %constant_dynamic-slice_fusion) | data formatting | bytes 4194304
  154.1 0.7 rsqrt_select_fusion
  154.8 5.2 %fusion.5 = f32[512,2048]{1,0:T(8,128)S(1)} fusion(bf16[1024,2048]{1,0:T(8,128)(2,1)} %param.13, s32[]{:T(128)S(6)} %select_n.161, bf16[1024,512]{1,0:T(8,128)(2,1)} %constant_dynamic-slice_fusion.1, f32[1024]{0:T(1024)S(1)} %rsqrt_select_fusion), kind=kOutput, calls=%fused_computation.23 | convolution fusion | flops 2149056512 | bytes 9441284 | tf_op jit(solution)/shard_map/dot_general | solution.py:161
  160.0 0.1 copy.35
  160.1 2.5 %multiply_convert_fusion = (bf16[2048,512]{0,1:T(8,128)(2,1)}, f32[2048]{0:T(1024)S(1)}) fusion(f32[2048]{0:T(1024)S(1)} %copy-done.12, bf16[2048,512]{0,1:T(8,128)(2,1)S(1)} %copy.29, f32[192]{0:T(256)S(1)} %bitcast.149, bf16[192,1024]{1,0:T(8,128)(2,1)S(1)} %bitcast.144, s32[]{:T(128)S(6)} %select_n.159, bf16[96,2048]{1,0:T(8,128)(2,1)S(1)} %get-tuple-element.44, ...), kind=kOutput, calls=%fused_computation.2 | convolution fusion | flops 410810368 | bytes 9389060 | tf_op jit(solution)/shard_map/dot_general | solution.py:163
  162.6 3.9 %copy.27 = bf16[2048,4,128]{2,0,1:T(8,128)(2,1)} copy(bf16[2048,4,128]{0,2,1:T(8,128)(2,1)} %bitcast.137) | data formatting | bytes 4194304 | tf_op jit(solution)/shard_map/reshape | solution.py:167
  166.6 1.0 copy-done.4
  167.5 0.1 copy-done.6
  167.7 2.4 %pad_maximum_fusion.1 = bf16[384,2048]{1,0:T(8,128)(2,1)} fusion(bf16[96,2048]{1,0:T(8,128)(2,1)} %copy-done.7, bf16[96,2048]{1,0:T(8,128)(2,1)S(1)} %copy-done.6, bf16[96,2048]{1,0:T(8,128)(2,1)S(1)} %copy-done.4, bf16[96,2048]{1,0:T(8,128)(2,1)S(1)} %get-tuple-element.37), kind=kLoop, calls=%fused_computation.17 | loop fusion | flops 6291456 | bytes 3145728 | tf_op jit(solution)/shard_map/concatenate | solution.py:103
  170.1 0.4 convert_reduce_fusion
  170.5 0.6 collective-permute-start.9
  171.0 2.5 %collective-permute-done.9 = f32[5120]{0:T(1024)S(1)} collective-permute-done((f32[5120]{0:T(1024)S(1)}, f32[5120]{0:T(1024)S(1)}, u32[]{:S(2)}, u32[]{:S(2)}) %collective-permute-start.9) | collective-permute-done | bytes 20512 | tf_op jit(solution)/shard_map/ppermute | solution.py:17
  173.5 0.3 collective-permute-done.3
  173.8 2.2 broadcast_select_fusion.1
  176.0 1.3 collective-permute-done.10
  177.3 0.3 collective-permute-start.11
  177.6 0.3 pad_maximum_fusion
  177.9 4.2 %collective-permute-done.11 = f32[5120]{0:T(1024)S(1)} collective-permute-done((f32[5120]{0:T(1024)S(1)}, f32[5120]{0:T(1024)S(1)}, u32[]{:S(2)}, u32[]{:S(2)}) %collective-permute-start.11) | collective-permute-done | bytes 20512 | tf_op jit(solution)/shard_map/ppermute | solution.py:17
  182.2 0.6 slice.37
  182.8 0.6 fusion.55
  183.4 1.4 copy-done
  184.8 7.4 %shard_map.137 = f32[16384,128]{1,0:T(8,128)} custom-call(bf16[768,2048]{1,0:T(8,128)(2,1)S(1)} %bitcast.136, bf16[768,1024]{1,0:T(8,128)(2,1)S(1)} %copy-done), custom_call_target="tpu_custom_call" | custom-call | flops 3221225472 | bytes 13107200 | tf_op jit(solution)/shard_map/pallas_call | solution.py:55
  192.2 28.4 %reduce-scatter.8.cloned.1.call-done = bf16[1,2048,128]{2,1,0:T(8,128)(2,1)} async-done(((bf16[4,2048,128]{2,1,0:T(8,128)(2,1)}), bf16[1,2048,128]{2,1,0:T(8,128)(2,1)}) %reduce-scatter.8.cloned.1.call-update) | async-done | bytes 524304 | tf_op jit(solution)/shard_map/reduce_scatter | solution.py:168
  220.5 2.1 bitcast_convert_fusion
  (53 shorter events, 0.3 us)
Async XLA Ops:
  7.2 73.7 %reduce-scatter.4.cloned.1.call-start = ((), (), s32[]{:S(2)}) async-start(), calls=%async_computation.3 | async-start | bytes 1966080 | tf_op jit(solution)/shard_map/reduce_scatter | solution.py:105
  9.9 12.9 %collective-permute-start.2 = (bf16[96,2048]{1,0:T(8,128)(2,1)S(1)}, bf16[96,2048]{1,0:T(8,128)(2,1)S(1)}, u32[]{:S(2)}, u32[]{:S(2)}) collective-permute-start(bf16[96,2048]{1,0:T(8,128)(2,1)S(1)} %fusion.9), channel_id=1, source_target_pairs={{0,1},{1,0},{2,3},{3,2},{4,5},{5,4},{6,7},{7,6},{8,9},{9,8},{10,11... | collective-permute-start | bytes 1179656 | tf_op jit(solution)/shard_map/ppermute | solution.py:17
  12.9 19.0 %collective-permute-start.1 = (bf16[96,2048]{1,0:T(8,128)(2,1)S(1)}, bf16[96,2048]{1,0:T(8,128)(2,1)S(1)}, u32[]{:S(2)}, u32[]{:S(2)}) collective-permute-start(bf16[96,2048]{1,0:T(8,128)(2,1)S(1)} %fusion.9), channel_id=1, source_target_pairs={{0,2},{1,3},{2,0},{3,1},{4,6},{5,7},{6,4},{7,5},{8,10},{9,11},{10,... | collective-permute-start | bytes 1179656 | tf_op jit(solution)/shard_map/ppermute | solution.py:17
  14.4 17.5 %collective-permute-start = (bf16[96,2048]{1,0:T(8,128)(2,1)S(1)}, bf16[96,2048]{1,0:T(8,128)(2,1)S(1)}, u32[]{:S(2)}, u32[]{:S(2)}) collective-permute-start(bf16[96,2048]{1,0:T(8,128)(2,1)S(1)} %fusion.9), channel_id=1, source_target_pairs={{0,3},{1,2},{2,1},{3,0},{4,7},{5,6},{6,5},{7,4},{8,11},{9,10},{10,... | collective-permute-start | bytes 1179656 | tf_op jit(solution)/shard_map/ppermute | solution.py:17
  35.0 0.7 copy-start.3
  35.0 0.9 copy-start.5
  35.0 1.0 copy-start.7
  36.0 9.2 %copy-start.14 = (s32[4]{0:T(128)S(1)}, s32[4]{0:T(128)}, u32[]{:S(2)}) copy-start(s32[4]{0:T(128)} %param.17) | copy-start | bytes 52
  36.0 9.4 %copy-start.13 = (s32[4]{0:T(128)S(1)}, s32[4]{0:T(128)}, u32[]{:S(2)}) copy-start(s32[4]{0:T(128)} %param.19) | copy-start | bytes 52
  36.0 9.4 %copy-start.15 = (s32[4]{0:T(128)S(1)}, s32[4]{0:T(128)}, u32[]{:S(2)}) copy-start(s32[4]{0:T(128)} %param.18) | copy-start | bytes 52
  45.1 1.3 slice-start
  45.1 35.8 %copy-start.11 = (f32[2048]{0:T(1024)S(1)}, f32[2048]{0:T(1024)}, u32[]{:S(2)}) copy-start(f32[2048]{0:T(1024)} %param.12) | copy-start | bytes 24580
  45.1 57.0 %reduce-scatter.6.cloned.1.call-start = ((), (), s32[]{:S(2)}) async-start(), calls=%async_computation.4 | async-start | bytes 245760 | tf_op jit(solution)/shard_map/reduce_scatter | solution.py:127
  46.3 81.5 %copy-start.12 = (f32[2048]{0:T(1024)S(1)}, f32[2048]{0:T(1024)}, u32[]{:S(2)}) copy-start(f32[2048]{0:T(1024)} %param.14) | copy-start | bytes 24580
  47.4 136.0 %all-gather.3.cloned.1.call-start = ((), (), s32[]{:S(2)}) async-start(), calls=%async_computation.5 | async-start | bytes 1966080 | tf_op jit(solution)/shard_map/all_gather | solution.py:156
  82.0 44.6 %collective-permute-start.4 = (bf16[96,2048]{1,0:T(8,128)(2,1)S(1)}, bf16[96,2048]{1,0:T(8,128)(2,1)S(1)}, u32[]{:S(2)}, u32[]{:S(2)}) collective-permute-start(bf16[96,2048]{1,0:T(8,128)(2,1)S(1)} %add_convert_fusion), channel_id=1, source_target_pairs={{0,16},{16,0},{1,17},{17,1},{2,18},{18,2},{3,19},{19,3},{4,20},{20... | collective-permute-start | bytes 1179656 | tf_op jit(solution)/shard_map/ppermute | solution.py:17
  126.5 5.2 %copy-start.9 = (bf16[1536,128]{1,0:T(8,128)(2,1)}, bf16[1536,128]{1,0:T(8,128)(2,1)S(1)}, u32[]{:S(2)}) copy-start(bf16[1536,128]{1,0:T(8,128)(2,1)S(1)} %all-gather) | copy-start | bytes 1179652
  131.8 3.7 %collective-permute-start.5 = (f32[2,192]{1,0:T(2,128)S(1)}, f32[2,192]{1,0:T(2,128)S(1)}, u32[]{:S(2)}, u32[]{:S(2)}) collective-permute-start(f32[2,192]{1,0:T(2,128)S(1)} %pad_maximum_fusion.4), channel_id=1, source_target_pairs={{0,1},{1,0},{2,3},{3,2},{4,5},{5,4},{6,7},{7,6},{8,9},{9,8},{10,11... | collective-permute-start | bytes 4616 | tf_op jit(solution)/shard_map/ppermute | solution.py:17
  135.4 3.7 %collective-permute-start.6 = (f32[2,192]{1,0:T(2,128)S(1)}, f32[2,192]{1,0:T(2,128)S(1)}, u32[]{:S(2)}, u32[]{:S(2)}) collective-permute-start(f32[2,192]{1,0:T(2,128)S(1)} %fusion.51), channel_id=1, source_target_pairs={{0,2},{1,3},{2,0},{3,1},{4,6},{5,7},{6,4},{7,5},{8,10},{9,11},{10,... | collective-permute-start | bytes 4616 | tf_op jit(solution)/shard_map/ppermute | solution.py:17
  140.3 80.2 %reduce-scatter.8.cloned.1.call-start = ((), (), s32[]{:S(2)}) async-start(), calls=%async_computation.6 | async-start | bytes 2621440 | tf_op jit(solution)/shard_map/reduce_scatter | solution.py:168
  143.6 5.3 %collective-permute-start.7 = (f32[1024]{0:T(1024)S(1)}, f32[1024]{0:T(1024)S(1)}, u32[]{:S(2)}, u32[]{:S(2)}) collective-permute-start(f32[1024]{0:T(1024)S(1)} %multiply_reduce_fusion), channel_id=1, source_target_pairs={{0,1},{1,0},{2,3},{3,2},{4,5},{5,4},{6,7},{7,6},{8,9},{9,8},{10,11... | collective-permute-start | bytes 12296 | tf_op jit(solution)/shard_map/ppermute | solution.py:17
  145.6 3.8 %copy-start.1 = (bf16[1024,1024]{1,0:T(8,128)(2,1)S(1)}, bf16[1024,1024]{1,0:T(8,128)(2,1)}, u32[]{:S(2)}) copy-start(bf16[1024,1024]{1,0:T(8,128)(2,1)} %param.16) | copy-start | bytes 6291460
  148.9 5.2 %collective-permute-start.8 = (f32[1024]{0:T(1024)S(1)}, f32[1024]{0:T(1024)S(1)}, u32[]{:S(2)}, u32[]{:S(2)}) collective-permute-start(f32[1024]{0:T(1024)S(1)} %add.94), channel_id=1, source_target_pairs={{0,2},{1,3},{2,0},{3,1},{4,6},{5,7},{6,4},{7,5},{8,10},{9,11},{10,... | collective-permute-start | bytes 12296 | tf_op jit(solution)/shard_map/ppermute | solution.py:17
  154.8 5.2 %copy-start.10 = (bf16[1536,128]{1,0:T(8,128)(2,1)S(1)}, bf16[1536,128]{1,0:T(8,128)(2,1)}, u32[]{:S(2)}) copy-start(bf16[1536,128]{1,0:T(8,128)(2,1)} %copy-done.9) | copy-start | bytes 1179652
  166.5 1.0 copy-start.4
  166.5 1.1 copy-start.6
  167.7 2.4 %copy-start.2 = (bf16[1024,1024]{1,0:T(8,128)(2,1)S(1)}, bf16[1024,1024]{1,0:T(8,128)(2,1)}, u32[]{:S(2)}) copy-start(bf16[1024,1024]{1,0:T(8,128)(2,1)} %param.16) | copy-start | bytes 6291460
  170.1 3.8 %collective-permute-start.3 = (bf16[384,2048]{1,0:T(8,128)(2,1)}, bf16[384,2048]{1,0:T(8,128)(2,1)}, u32[]{:S(2)}, u32[]{:S(2)}) collective-permute-start(bf16[384,2048]{1,0:T(8,128)(2,1)} %pad_maximum_fusion.1), channel_id=1, source_target_pairs={{0,16},{16,0},{1,17},{17,1},{2,18},{18,2},{3,19},{19,3},{4,20},{20... | collective-permute-start | bytes 4718600 | tf_op jit(solution)/shard_map/ppermute | solution.py:17
  170.1 3.7 %copy-start.8 = (bf16[96,2048]{1,0:T(8,128)(2,1)S(1)}, bf16[96,2048]{1,0:T(8,128)(2,1)}, u32[]{:S(2)}) copy-start(bf16[96,2048]{1,0:T(8,128)(2,1)} %copy-done.7) | copy-start | bytes 1179652
  170.5 3.0 %collective-permute-start.9 = (f32[5120]{0:T(1024)S(1)}, f32[5120]{0:T(1024)S(1)}, u32[]{:S(2)}, u32[]{:S(2)}) collective-permute-start(f32[5120]{0:T(1024)S(1)} %pad_maximum_fusion.3), channel_id=1, source_target_pairs={{0,16},{16,0},{1,17},{17,1},{2,18},{18,2},{3,19},{19,3},{4,20},{20... | collective-permute-start | bytes 61448 | tf_op jit(solution)/shard_map/ppermute | solution.py:17
  173.5 3.8 %collective-permute-start.10 = (f32[5120]{0:T(1024)S(1)}, f32[5120]{0:T(1024)S(1)}, u32[]{:S(2)}, u32[]{:S(2)}) collective-permute-start(f32[5120]{0:T(1024)S(1)} %fusion.52), channel_id=1, source_target_pairs={{0,4},{4,0},{8,12},{12,8},{1,5},{5,1},{9,13},{13,9},{2,6},{6,2},{1... | collective-permute-start | bytes 61448 | tf_op jit(solution)/shard_map/ppermute | solution.py:17
  177.3 4.9 %collective-permute-start.11 = (f32[5120]{0:T(1024)S(1)}, f32[5120]{0:T(1024)S(1)}, u32[]{:S(2)}, u32[]{:S(2)}) collective-permute-start(f32[5120]{0:T(1024)S(1)} %add.100), channel_id=1, source_target_pairs={{0,8},{4,12},{8,0},{12,4},{1,9},{5,13},{9,1},{13,5},{2,10},{6,14},... | collective-permute-start | bytes 61448 | tf_op jit(solution)/shard_map/ppermute | solution.py:17
  183.4 1.4 copy-start
Sparse Core Ops, SparseCore 0:
  45.2 35.6 reduce-scatter.3
  83.7 18.3 reduce-scatter.5
  140.4 34.7 all-gather.2
  177.5 42.9 reduce-scatter.7

commit v2 on v1

v2 whole, which is shorter than its diff:
```python
import jax
import jax.numpy as jnp
from jax import lax
from jax.experimental import pallas as pl
from jax.experimental.pallas import tpu as pltpu
from jax.sharding import PartitionSpec as P

D = 8192
TILE = 256
MAXT = 2
LANES = 128
EPSILON = 1e-06


def swap(x, axis, mask):
    count = lax.axis_size(axis)
    return lax.ppermute(x, axis, [(i, i ^ mask) for i in range(count)])


def total(x, axis):
    pieces = [x] + [swap(x, axis, m) for m in range(1, lax.axis_size(axis))]
    while len(pieces) > 1:
        pieces = [pieces[i] + pieces[i + 1] for i in range(0, len(pieces), 2)]
    return pieces[0]


def butterfly(x, axes):
    for axis in axes:
        mask = 1
        while mask < lax.axis_size(axis):
            x = x + swap(x, axis, mask)
            mask *= 2
    return x


def in_order(pieces, index):
    pieces = list(pieces)
    mask = 1
    while mask < len(pieces):
        odd = (index & mask) != 0
        pieces = [jnp.where(odd, pieces[m ^ mask], pieces[m]) for m in range(len(pieces))]
        mask *= 2
    return pieces


def reduce_to_owner(parts, axis):
    index = lax.axis_index(axis)
    count = parts.shape[0]
    while count > 1:
        pairs = parts.reshape(count // 2, 2, *parts.shape[1:])
        mask = lax.axis_size(axis) // count
        bit = (index // mask) % 2
        sent = lax.dynamic_index_in_dim(pairs, 1 - bit, 1, keepdims=False)
        kept = lax.dynamic_index_in_dim(pairs, bit, 1, keepdims=False)
        came = swap(sent.astype(jnp.bfloat16), axis, mask)
        parts = kept.astype(jnp.float32) + came.astype(jnp.float32)
        count //= 2
    return parts[0]


def along_line(x, axis):
    count = lax.axis_size(axis)
    up, down = [], []
    right = left = x
    for i in range(1, count):
        right = lax.ppermute(right, axis, [(j, j + 1) for j in range(i - 1, count - 1)])
        left = lax.ppermute(left, axis, [(j, j - 1) for j in range(1, count - i + 1)])
        up.append(right)
        down.append(left)
    return up, down


def weight_kernel(*refs):
    act_ref, own_ref, out_ref, grad_ref = refs[0], refs[1], refs[-2], refs[-1]
    others = refs[2:-2]
    count = len(others) // 2
    rows, width = own_ref.shape

    @pl.when(pl.program_id(0) == 0)
    def _():
        grad_ref[:rows, :] = own_ref[...]
        for i in range(count):
            grad_ref[(i + 1) * rows : (i + 2) * rows, :] = (
                others[i][...] + others[count + count - 1 - i][...]
            )

    step = act_ref.shape[1]
    groups = width // LANES
    product = lax.dot_general(
        act_ref[...], grad_ref[...], (((0,), (0,)), ((), ())), preferred_element_type=jnp.float32
    )
    for c in range(groups):
        out_ref[pl.ds(c, step, stride=groups), :] = product[:, c * LANES : (c + 1) * LANES]


def weight_product(act, own, others):
    rows, features = act.shape
    width = own.shape[1]
    groups = width // LANES
    step = 256
    piece = pl.BlockSpec(own.shape, lambda i: (0, 0))
    return pl.pallas_call(
        weight_kernel,
        grid=(features // step,),
        in_specs=[pl.BlockSpec((rows, step), lambda i: (0, i))] + [piece] * (1 + len(others)),
        out_specs=pl.BlockSpec((step * groups, LANES), lambda i: (i, 0)),
        out_shape=jax.ShapeDtypeStruct((features * groups, LANES), jnp.float32),
        scratch_shapes=[pltpu.VMEM((rows, width), jnp.bfloat16)],
        compiler_params=pltpu.CompilerParams(vmem_limit_bytes=40 * 1024 * 1024),
        cost_estimate=pl.CostEstimate(
            flops=2 * rows * features * width,
            bytes_accessed=4 * features * width + 2 * rows * (features + width),
            transcendentals=0,
        ),
    )(act, own, *others)


def on_device(
    vis_hidden,
    proj_weight,
    proj_bias,
    text_embed,
    norm_gain,
    key_weight,
    key_cotangent,
    tile_counts,
    text_counts,
    owner_map,
):
    f32, bf16 = jnp.float32, jnp.bfloat16
    n_sec, n_seq, n_tp = (lax.axis_size(a) for a in ("sec", "seq", "tp"))
    core, z, t = (lax.axis_index(a) for a in ("sec", "seq", "tp"))
    block_rows, features = vis_hidden.shape
    columns = proj_weight.shape[1]
    stream = block_rows * n_tp
    own = stream // n_seq
    part_rows = block_rows // n_sec
    sub = part_rows // n_seq
    keys = key_weight.shape[1]
    seq_len = text_embed.shape[0]
    tiles = stream // TILE

    mine = lax.dynamic_slice_in_dim(vis_hidden, core * part_rows, part_rows, 0)
    act = jax.nn.gelu(mine.astype(f32), approximate=False).astype(bf16)
    pieces = [act] + [swap(act, "tp", m) for m in range(1, n_tp)]
    pieces = [p.reshape(n_seq, sub, features) for p in pieces]

    starts = jnp.cumsum(tile_counts) - tile_counts
    tile_ids = jnp.arange(tiles, dtype=jnp.int32)[:, None]
    held = (tile_ids >= starts[None]) & (tile_ids < (starts + tile_counts)[None])
    tile_owner = jnp.sum(jnp.where(held, owner_map[None], 0), 1)
    tile_place = jnp.sum(jnp.where(held, tile_ids - starts[None], 0), 1)
    share = keys // n_tp
    front = lax.dynamic_slice_in_dim(key_cotangent[: MAXT * TILE], t * share, share, 1)
    front = front.reshape(MAXT, TILE, share)
    given = jnp.zeros((tiles, TILE, share), bf16)
    for place in range(MAXT):
        chosen = (tile_owner == z) & (tile_place == place)
        given = jnp.where(chosen[:, None, None], front[place][None], given)
    given = given.reshape(n_tp, n_sec, n_seq, sub, share).transpose(2, 1, 0, 3, 4)
    taken = lax.psum_scatter(
        given.reshape(stream, share), "seq", scatter_dimension=0, tiled=True
    )
    taken = [taken] + [swap(taken, "tp", m) for m in range(1, n_tp)]
    image_cot = jnp.concatenate(in_order(taken, t), 1)
    scaled = lax.dot_general(
        image_cot, key_weight, (((1,), (1,)), ((), ())), preferred_element_type=f32
    ) * norm_gain

    images = []
    for first in range(0, n_tp, 2):
        chunk = jnp.stack(pieces[first : first + 2], 1).reshape(2 * part_rows, features)
        partial = jnp.dot(chunk, proj_weight, preferred_element_type=f32).astype(bf16)
        summed = reduce_to_owner(partial.reshape(n_seq, 2 * sub, columns), "seq")
        images += list((summed + proj_bias).astype(bf16).reshape(2, sub, columns))
    image_mine = jnp.concatenate(in_order(images, t), 0)
    image = jnp.concatenate(in_order([image_mine, swap(image_mine, "sec", 1)], core), 0)

    act_half = jnp.stack(in_order(pieces, t), 1)
    act_pair = in_order([act_half, swap(act_half, "sec", 1)], core)
    act_full = jnp.stack(act_pair, 1).reshape(n_seq, own, features)

    is_mine = owner_map == z
    image_count = TILE * jnp.sum(jnp.where(is_mine, tile_counts, 0))
    text_count = jnp.sum(jnp.where(is_mine, text_counts, 0))
    text_values = text_embed.astype(f32)
    text_sq = total(jnp.sum(text_values * text_values, 1), "tp")
    text_inv = lax.rsqrt(text_sq / D + EPSILON)
    text_scale = jnp.where(jnp.arange(seq_len) < text_count, text_inv, 0.0)
    key_half = keys // n_sec
    cot_half = lax.dynamic_slice_in_dim(key_cotangent, core * key_half, key_half, 1)
    cot_padded = jnp.concatenate([cot_half, jnp.zeros((MAXT * TILE, key_half), bf16)], 0)
    cot_text = lax.dynamic_slice_in_dim(cot_padded, image_count, seq_len, 0)
    cot_text = (cot_text.astype(f32) * text_scale[:, None]).astype(bf16)
    rows_first = (((0,), (0,)), ((), ()))
    text_moment = lax.dot_general(text_embed, cot_text, rows_first, preferred_element_type=f32)

    values = image.astype(f32)
    sums = total(jnp.stack([jnp.sum(values * values, 1), jnp.sum(scaled * values, 1)]), "tp")
    inv = lax.rsqrt(sums[0] / D + EPSILON)
    mean = inv * sums[1] / D
    embed_grad = (inv[:, None] * (scaled - values * (inv * mean)[:, None])).astype(bf16)
    col_half = columns // n_sec
    grad_half = lax.dynamic_slice_in_dim(embed_grad, core * col_half, col_half, 1)

    cot_image = lax.dynamic_slice_in_dim(image_cot, core * key_half, key_half, 1)
    cot_image = (cot_image.astype(f32) * inv[:, None]).astype(bf16)
    moment = text_moment + lax.dot_general(
        image, cot_image, rows_first, preferred_element_type=f32
    )
    weight_half = lax.dynamic_slice_in_dim(key_weight, core * key_half, key_half, 1)
    gain_part = jnp.sum(moment * weight_half.astype(f32), 1)
    shares = (moment * norm_gain[:, None]).astype(bf16)
    shares = shares.reshape(columns, n_seq, key_half // n_seq).transpose(1, 0, 2)
    key_weight_grad = lax.psum_scatter(shares, "seq", scatter_dimension=0, tiled=False)
    key_weight_grad = key_weight_grad.astype(f32)

    key_bias_part = jnp.sum(key_cotangent.astype(f32), 0)
    bias_part = jnp.sum(embed_grad.astype(f32), 0)
    once = jnp.concatenate([key_bias_part, bias_part])
    small = butterfly(jnp.concatenate([gain_part, jnp.where(core == 0, once, 0.0)]), ("sec", "seq"))
    gain_grad = small[:columns]
    key_bias_grad = small[columns : columns + keys]
    proj_bias_grad = small[columns + keys :]

    if n_seq <= 4:
        up, down = along_line(grad_half, "seq")
        around = jnp.concatenate([act_full[::-1], act_full[::-1]], 0)
        act_used = lax.dynamic_slice_in_dim(around, n_seq - 1 - z, n_seq, 0)
        product = weight_product(act_used.reshape(stream, features), grad_half, up + down)
    else:
        grads = lax.all_gather(grad_half, "seq", axis=0, tiled=True)
        product = weight_product(act_full.reshape(stream, features), grads, [])
    proj_weight_grad = product.reshape(features, 1, 1, col_half)
    return (proj_weight_grad, proj_bias_grad, key_weight_grad, key_bias_grad, gain_grad)


def solution(mesh):
    placed = (
        P("tp", "seq"),
        P("seq", "tp"),
        P("tp"),
        P("seq", "tp"),
        P("tp"),
        P("tp", None),
        P("seq", None),
        P(),
        P(),
        P(),
    )
    return jax.shard_map(
        on_device,
        mesh=mesh,
        in_specs=placed,
        out_specs=(P("seq", "tp", "sec", None), P("tp"), P("tp", ("sec", "seq")), P(), P("tp")),
        check_vma=False,
    )
```

time: 230 us -> 186 us (0.81)
  waiting for transfers between devices: 112 us -> 65.8 us
  blocking collectives: 24.5 us -> 0 us
  starting transfers between devices: 11.8 us -> 32 us
  local copies, waits for them, and re-layouts: 17.1 us -> 23.1 us
  matrix products: 20.6 us -> 17.3 us
  other arithmetic: 21.5 us -> 24.3 us
    reduce_scatter x1 -> x0, waiting for transfers between devices: 33.5 us -> none  [on_device(): lax.psum_scatter(partial, 'seq', scatter_dimension=0, tiled=True)]
    reduce_scatter x1, waiting for transfers between devices: 28.4 us -> 0.01 us  [on_device(): lax.psum_scatter(shares, 'seq', scatter_dimension=0, tiled=False)]
    ppermute x12 -> x21, waiting for transfers between devices: 29.6 us -> 55 us  [swap(): return lax.ppermute(x, axis, [(i, i ^ mask) for i in range(count)])]
    all_gather x1 -> x0, blocking collectives: 24.5 us -> none  [on_device(): taken = lax.all_gather(taken, ('sec', 'tp'), axis=0, tiled=False)]
    reduce_scatter x1, waiting for transfers between devices: 20 us -> 0.02 us  [on_device(): lax.psum_scatter(given.reshape(stream, share), 'seq', scatter_dimension=0...]
    ppermute x12 -> x21, starting transfers between devices: 11.4 us -> 24.9 us  [swap(): return lax.ppermute(x, axis, [(i, i ^ mask) for i in range(count)])]
    ppermute x0 -> x6, waiting for transfers between devices: none -> 10.7 us  [the longest x3 10.7 us: along_line(): lax.ppermute(left, axis, [(j, j - 1) for j in range(1, count - i + 1)])]
    another operation x2 -> x6, other arithmetic: 0.47 us -> 7.87 us  [the longest x2 3.95 us: on_device(): act_full = jnp.stack(act_pair, 1).reshape(n_seq, own, features)]
  transfers between devices with their start and end apart: 16 -> 29, of which waited for: 11 -> 10; matrix products, arithmetic and copies ran while one was open for 14% -> 25% of each run, Pallas kernels for 3% -> 4%
where the time goes in v2:
time: 186 us
  waiting for transfers between devices  65.8 us (35%)
  starting transfers between devices  32 us (17%)
  other arithmetic  24.3 us (13%)
  local copies, waits for them, and re-layouts  23.1 us (12%)
  matrix products  17.3 us (9%)
  between operations  15.4 us (8%)
  Pallas kernels  7.63 us (4%)
    ppermute x21, waiting for transfers between devices, swap(): return lax.ppermute(x, axis, [(i, i ^ mask) for i in range(count)])  55 us
    ppermute x21, starting transfers between devices, swap(): return lax.ppermute(x, axis, [(i, i ^ mask) for i in range(count)])  24.9 us
    ppermute x3, waiting for transfers between devices, along_line(): lax.ppermute(left, axis, [(j, j - 1) for j in range(1, count - i + 1)])  10.7 us
    pallas_call x1, Pallas kernels, weight_product(): pl.pallas_call(weight_kernel, grid=(features // step,), in_specs=[pl.Bloc...  7.63 us
    dot_general x2, matrix products, on_device(): jnp.dot(chunk, proj_weight, preferred_element_type=f32).astype(bf16)  7.28 us
    unnamed x37, local copies, waits for them, and re-layouts  7.27 us
    dot_general x1, matrix products, on_device(): lax.dot_general(text_embed, cot_text, rows_first, preferred_element_type=...  4.82 us
    another operation x2, other arithmetic, on_device(): act_full = jnp.stack(act_pair, 1).reshape(n_seq, own, features)  3.95 us
  transfers between devices with their start and end apart: 29, of which 10 were waited for; matrix products, arithmetic and copies ran while one was open for 25% of the time, Pallas kernels for 4%

profile of v2, /device:TPU:0, one launch (start us, length us, event | category | flops | bytes accessed | tf_op | source)
XLA Modules:
  0.0 185.5 jit_solution(16859156918203549990)
XLA Ops:
  7.2 2.7 %fusion.9 = bf16[96,2048]{1,0:T(8,128)(2,1)S(1)} fusion(bf16[192,2048]{1,0:T(8,128)(2,1)} %param.10, s32[]{:T(128)S(6)} %select_n.309), kind=kLoop, calls=%fused_computation.32 | loop fusion | flops 12976128 | bytes 786436 | tf_op jit(solution)/shard_map/convert_element_type | solution.py:144
  10.0 4.0 %collective-permute-start = (bf16[96,2048]{1,0:T(8,128)(2,1)S(1)}, bf16[96,2048]{1,0:T(8,128)(2,1)}, u32[]{:S(2)}, u32[]{:S(2)}) collective-permute-start(bf16[96,2048]{1,0:T(8,128)(2,1)S(1)} %fusion.9), channel_id=1, source_target_pairs={{0,3},{1,2},{2,1},{3,0},{4,7},{5,6},{6,5},{7,4},{8,11},{9,10},{10,... | collective-permute-start | bytes 1179656 | tf_op jit(solution)/shard_map/ppermute | solution.py:17
  13.9 0.5 collective-permute-start.1
  14.6 3.1 %multiply_reduce_fusion = f32[1024]{0:T(1024)S(1)} fusion(bf16[1024,2048]{1,0:T(8,128)(2,1)} %param.13), kind=kLoop, calls=%fused_computation | loop fusion | flops 6290432 | bytes 4198400 | tf_op jit(solution)/shard_map/reduce_sum | solution.py:187
  17.7 2.0 %collective-permute-start.21 = (f32[1024]{0:T(1024)S(1)}, f32[1024]{0:T(1024)S(1)}, u32[]{:S(2)}, u32[]{:S(2)}) collective-permute-start(f32[1024]{0:T(1024)S(1)} %multiply_reduce_fusion), channel_id=1, source_target_pairs={{0,1},{1,0},{2,3},{3,2},{4,5},{5,4},{6,7},{7,6},{8,9},{9,8},{10,11... | collective-permute-start | bytes 12296 | tf_op jit(solution)/shard_map/ppermute | solution.py:17
  19.6 1.5 collective-permute-start.22
  21.3 0.6 fusion.49
  22.6 0.3 select_bitcast_fusion.2
  22.9 0.8 copy.34
  24.6 3.0 %constant_dynamic-slice_fusion = bf16[2048,512]{1,0:T(8,128)(2,1)} fusion(bf16[2048,1024]{1,0:T(8,128)(2,1)} %param.15, s32[]{:T(128)S(6)} %select_n.357), kind=kLoop, calls=%fused_computation.110 | loop fusion | bytes 4194308 | tf_op jit(solution)/shard_map/dynamic_slice | solution.py:211
  27.7 2.9 %copy.40 = bf16[2048,512]{0,1:T(8,128)(2,1)S(1)} copy(bf16[2048,512]{1,0:T(8,128)(2,1)} %constant_dynamic-slice_fusion) | data formatting | bytes 4194304
  30.6 2.3 %constant_dynamic-slice_fusion.1 = bf16[1024,512]{1,0:T(8,128)(2,1)} fusion(bf16[1024,1024]{1,0:T(8,128)(2,1)} %param.16, s32[]{:T(128)S(6)} %select_n.357), kind=kLoop, calls=%fused_computation.113 | loop fusion | bytes 2097156 | tf_op jit(solution)/shard_map/dynamic_slice | solution.py:191
  33.0 1.3 pad_maximum_fusion.2
  34.4 5.4 %convolution_convert_fusion.1 = bf16[192,2048]{1,0:T(8,128)(2,1)S(1)} fusion(bf16[192,2048]{1,0:T(8,128)(2,1)S(1)} %bitcast.74, bf16[2048,2048]{1,0:T(8,128)(2,1)} %param.11), kind=kOutput, calls=%fused_computation.11 | convolution fusion | flops 1611005952 | bytes 9961472 | tf_op jit(solution)/shard_map/dot_general | solution.py:173
  39.8 2.0 %collective-permute-start.4 = (bf16[2,48,2048]{2,1,0:T(8,128)(2,1)S(1)}, bf16[2,48,2048]{2,1,0:T(8,128)(2,1)S(1)}, u32[]{:S(2)}, u32[]{:S(2)}) collective-permute-start(bf16[2,48,2048]{2,1,0:T(8,128)(2,1)S(1)} %dynamic-slice_bitcast_fusion.1), channel_id=1, source_target_pairs={{0,4},{4,0},{8,12},{12,8},{1,5},{5,1},{9,13},{13,9},{2,6},{6,2},{1... | collective-permute-start | bytes 1179656 | tf_op jit(solution)/shard_map/ppermute | solution.py:17
  41.8 1.1 pad_maximum_fusion.3
  42.9 1.9 %convolution_convert_fusion = bf16[192,2048]{1,0:T(8,128)(2,1)S(1)} fusion(bf16[192,2048]{1,0:T(8,128)(2,1)S(1)} %bitcast.75, bf16[2048,2048]{1,0:T(8,128)(2,1)S(1)} %bitcast.91), kind=kOutput, calls=%fused_computation.10 | convolution fusion | flops 1611005952 | bytes 9961472 | tf_op jit(solution)/shard_map/dot_general | solution.py:173
  45.0 6.9 %collective-permute-done.4 = bf16[2,48,2048]{2,1,0:T(8,128)(2,1)S(1)} collective-permute-done((bf16[2,48,2048]{2,1,0:T(8,128)(2,1)S(1)}, bf16[2,48,2048]{2,1,0:T(8,128)(2,1)S(1)}, u32[]{:S(2)}, u32[]{:S(2)}) %collective-permute-start.4) | collective-permute-done | bytes 393248 | tf_op jit(solution)/shard_map/ppermute | solution.py:17
  52.1 4.2 %collective-permute-start.5 = (bf16[1,48,2048]{2,1,0:T(8,128)(2,1)S(1)}, bf16[1,48,2048]{2,1,0:T(8,128)(2,1)S(1)}, u32[]{:S(2)}, u32[]{:S(2)}) collective-permute-start(bf16[1,48,2048]{2,1,0:T(8,128)(2,1)S(1)} %dynamic-slice_convert_fusion.1), channel_id=1, source_target_pairs={{0,8},{4,12},{8,0},{12,4},{1,9},{5,13},{9,1},{13,5},{2,10},{6,14},... | collective-permute-start | bytes 589832 | tf_op jit(solution)/shard_map/ppermute | solution.py:17
  56.3 6.5 %collective-permute-done.6 = bf16[2,48,2048]{2,1,0:T(8,128)(2,1)S(1)} collective-permute-done((bf16[2,48,2048]{2,1,0:T(8,128)(2,1)S(1)}, bf16[2,48,2048]{2,1,0:T(8,128)(2,1)S(1)}, u32[]{:S(2)}, u32[]{:S(2)}) %collective-permute-start.6) | collective-permute-done | bytes 393248 | tf_op jit(solution)/shard_map/ppermute | solution.py:17
  62.9 0.9 copy-done.6
  63.9 0.7 rsqrt_select_fusion
  64.6 1.6 collective-permute-start.10
  66.2 1.3 collective-permute-start.11
  67.5 0.7 collective-permute-start.9
  68.2 4.7 %collective-permute-done.7 = bf16[1,48,2048]{2,1,0:T(8,128)(2,1)} collective-permute-done((bf16[1,48,2048]{2,1,0:T(8,128)(2,1)S(1)}, bf16[1,48,2048]{2,1,0:T(8,128)(2,1)}, u32[]{:S(2)}, u32[]{:S(2)}) %collective-permute-start.7) | collective-permute-done | bytes 196640 | tf_op jit(solution)/shard_map/ppermute | solution.py:17
  72.9 1.2 fusion.39
  74.3 4.8 %fusion.6 = f32[512,2048]{1,0:T(8,128)S(1)} fusion(bf16[1024,2048]{1,0:T(8,128)(2,1)} %param.13, s32[]{:T(128)S(6)} %select_n.359, bf16[1024,512]{1,0:T(8,128)(2,1)S(1)} %copy-done.8, f32[1024]{0:T(1024)S(1)} %rsqrt_select_fusion), kind=kOutput, calls=%fused_computation.27 | convolution fusion | flops 2149056512 | bytes 9441284 | tf_op jit(solution)/shard_map/dot_general | solution.py:196
  79.4 0.4 copy-done.12
  79.8 2.8 %fusion.1 = (f32[192]{0:T(256)S(1)}, f32[192]{0:T(256)S(1)}, f32[192,2048]{1,0:T(8,128)}) fusion(bf16[96,2048]{1,0:T(8,128)(2,1)S(1)} %get-tuple-element.44, bf16[96,2048]{1,0:T(8,128)(2,1)S(1)} %get-tuple-element.43, f32[2048]{0:T(1024)S(1)} %copy-done.12, bf16[2048,1024]{1,0:T(8,128)(2,1)S(1)} %copy-done.9, bf16[192,256]{1,0:T(8,128)(2,1)S(1)} %get-tuple-element.52, ...), kind=kOutput, calls=%fused_computation.16 | convolution fusion | flops 810417792 | bytes 6956544 | tf_op jit(solution)/shard_map/dot_general | solution.py:166
  82.6 1.8 collective-permute-start.12
  84.4 1.3 collective-permute-start.13
  85.7 0.4 collective-permute-start.14
  86.2 1.8 collective-permute-done.13
  88.0 2.2 %collective-permute-done.14 = f32[2,192]{1,0:T(2,128)S(1)} collective-permute-done((f32[2,192]{1,0:T(2,128)S(1)}, f32[2,192]{1,0:T(2,128)S(1)}, u32[]{:S(2)}, u32[]{:S(2)}) %collective-permute-start.14) | collective-permute-done | bytes 1568 | tf_op jit(solution)/shard_map/ppermute | solution.py:17
  90.2 2.4 %multiply_convert_fusion = (bf16[2048,512]{0,1:T(8,128)(2,1)}, f32[2048]{0:T(1024)S(1)}) fusion(f32[2048]{0:T(1024)S(1)} %copy-done.12, bf16[2048,512]{0,1:T(8,128)(2,1)S(1)} %copy.40, f32[192]{0:T(256)S(1)} %bitcast.80, bf16[192,1024]{1,0:T(8,128)(2,1)S(1)} %pad_maximum_fusion.6, s32[]{:T(128)S(6)} %select_n.357, ...), kind=kOutput, calls=%fused_computation.4 | convolution fusion | flops 410810368 | bytes 9389060 | tf_op jit(solution)/shard_map/dot_general | solution.py:208
  92.7 3.9 %copy.36 = bf16[2048,4,128]{2,0,1:T(8,128)(2,1)} copy(bf16[2048,4,128]{0,2,1:T(8,128)(2,1)} %bitcast.67) | data formatting | bytes 4194304 | tf_op jit(solution)/shard_map/reshape | solution.py:214
  96.7 1.0 copy-done.5
  97.6 1.4 broadcast_select_fusion.9
  99.0 0.7 copy-done.1
  99.8 1.3 pad_maximum_fusion.1
  101.3 0.4 convert_reduce_fusion
  101.7 1.1 copy-done.7
  102.8 0.4 convert_reduce_fusion.1
  103.2 0.3 collective-permute-start.24
  103.6 1.7 collective-permute-start.15
  105.2 1.3 collective-permute-start.18
  106.6 2.7 %collective-permute-start.25 = (f32[5120]{0:T(1024)S(1)}, f32[5120]{0:T(1024)S(1)}, u32[]{:S(2)}, u32[]{:S(2)}) collective-permute-start(f32[5120]{0:T(1024)S(1)} %fusion.51), channel_id=1, source_target_pairs={{0,4},{4,0},{8,12},{12,8},{1,5},{5,1},{9,13},{13,9},{2,6},{6,2},{1... | collective-permute-start | bytes 61448 | tf_op jit(solution)/shard_map/ppermute | solution.py:17
  109.3 27.3 %collective-permute-done.25 = f32[5120]{0:T(1024)S(1)} collective-permute-done((f32[5120]{0:T(1024)S(1)}, f32[5120]{0:T(1024)S(1)}, u32[]{:S(2)}, u32[]{:S(2)}) %collective-permute-start.25) | collective-permute-done | bytes 20512 | tf_op jit(solution)/shard_map/ppermute | solution.py:17
  136.6 5.5 %collective-permute-done.26 = f32[5120]{0:T(1024)S(1)} collective-permute-done((f32[5120]{0:T(1024)S(1)}, f32[5120]{0:T(1024)S(1)}, u32[]{:S(2)}, u32[]{:S(2)}) %collective-permute-start.26) | collective-permute-done | bytes 20512 | tf_op jit(solution)/shard_map/ppermute | solution.py:17
  142.2 0.6 slice.41
  142.8 0.6 fusion.53
  143.4 0.7 collective-permute-start.16
  144.1 1.3 collective-permute-start.19
  145.4 2.0 %select_bitcast_fusion.1 = (bf16[4,1,4,24,2048]{4,3,2,1,0:T(8,128)(2,1)S(1)}, bf16[4,1,4,24,2048]{4,3,2,1,0:T(8,128)(2,1)S(1)}) fusion(bf16[4,4,24,2048]{3,2,1,0:T(8,128)(2,1)} %collective-permute-done.3, pred[]{:T(512)S(6)} %ne.40, bf16[4,1,24,2048]{3,2,1,0:T(8,128)(2,1)} %copy-done.3, bf16[4,1,24,2048]{3,2,1,0:T(8,128)(2,1)} %copy-done.2, ...), kind=kLoop, calls=%fused_computation.25 | loop fusion | flops 3932160 | bytes 6291457 | tf_op jit(solution)/shard_map/stack | solution.py:181
  147.4 0.7 collective-permute-start.17
  148.1 8.9 %collective-permute-done.19.refs_6_ = bf16[192,1024]{1,0:T(8,128)(2,1)S(1)} collective-permute-done((bf16[192,1024]{1,0:T(8,128)(2,1)S(1)}, bf16[192,1024]{1,0:T(8,128)(2,1)S(1)}, u32[]{:S(2)}, u32[]{:S(2)}) %collective-permute-start.19) | collective-permute-done | bytes 393248 | tf_op jit(solution)/shard_map/ppermute | solution.py:67
  157.0 1.3 collective-permute-start.20
  158.2 1.9 %pad_maximum_fusion = bf16[4,2,4,24,2048]{4,3,2,1,0:T(8,128)(2,1)} fusion(bf16[4,1,4,24,2048]{4,3,2,1,0:T(8,128)(2,1)S(1)} %get-tuple-element.36, bf16[4,1,4,24,2048]{4,3,2,1,0:T(8,128)(2,1)S(1)} %get-tuple-element.35), kind=kLoop, calls=%fused_computation.8 | loop fusion | flops 1572864 | bytes 6291456 | tf_op jit(solution)/shard_map/stack | solution.py:181
  160.2 3.9 %rev.4 = bf16[4,192,2048]{2,1,0:T(8,128)(2,1)} reverse(bf16[4,192,2048]{2,1,0:T(8,128)(2,1)} %bitcast.65), dimensions={0} | reverse | bytes 6291456 | tf_op jit(solution)/shard_map/rev | solution.py:228
  164.1 3.0 %fusion = bf16[4,192,2048]{2,1,0:T(8,128)(2,1)S(1)} fusion(s32[]{:T(128)S(6)} %select_n.320, bf16[4,192,2048]{2,1,0:T(8,128)(2,1)} %rev.4), kind=kLoop, calls=%fused_computation.7 | loop fusion | flops 1572864 | bytes 6291460 | tf_op jit(solution)/shard_map/concatenate | solution.py:228
  167.2 1.8 collective-permute-done.20.refs_7_
  169.0 7.6 %shard_map.137 = f32[16384,128]{1,0:T(8,128)} custom-call(bf16[768,2048]{1,0:T(8,128)(2,1)S(1)} %bitcast.64, bf16[192,1024]{1,0:T(8,128)(2,1)S(1)} %constant_dynamic-slice_fusion.2.refs_1_, bf16[192,1024]{1,0:T(8,128)(2,1)S(1)} %collective-permute-done.15.refs_2_, bf16[192,1024]{1,0:T(8,128)(2,1)S(1)} %collective-permute-done.16.refs_3_, ...), custom_call_target="tpu_custom_call" | custom-call | flops 3221225472 | bytes 13107200 | tf_op jit(solution)/shard_map/pallas_call | solution.py:102
  176.6 2.1 %bitcast_convert_fusion = f32[2048,128]{1,0:T(8,128)} fusion(bf16[1,2048,128]{2,1,0:T(8,128)(2,1)} %reduce-scatter.5.cloned.1.call-done), kind=kLoop, calls=%fused_computation.67 | loop fusion | flops 262144 | bytes 1572864 | tf_op jit(solution)/shard_map/convert_element_type | solution.py:216
  (96 shorter events, 2.7 us)
Async XLA Ops:
  7.2 57.4 %reduce-scatter.3.cloned.1.call-start = ((), (), s32[]{:S(2)}) async-start(), calls=%async_computation.2 | async-start | bytes 491520 | tf_op jit(solution)/shard_map/reduce_scatter | solution.py:161
  9.9 31.9 %copy-start.4 = (bf16[96,2048]{1,0:T(8,128)(2,1)}, bf16[96,2048]{1,0:T(8,128)(2,1)S(1)}, u32[]{:S(2)}) copy-start(bf16[96,2048]{1,0:T(8,128)(2,1)S(1)} %fusion.9) | copy-start | bytes 1179652
  9.9 11.2 %copy-start.14 = (s32[4]{0:T(128)S(1)}, s32[4]{0:T(128)}, u32[]{:S(2)}) copy-start(s32[4]{0:T(128)} %param.17) | copy-start | bytes 52
  9.9 11.4 %copy-start.13 = (s32[4]{0:T(128)S(1)}, s32[4]{0:T(128)}, u32[]{:S(2)}) copy-start(s32[4]{0:T(128)} %param.19) | copy-start | bytes 52
  10.0 11.4 %copy-start.15 = (s32[4]{0:T(128)S(1)}, s32[4]{0:T(128)}, u32[]{:S(2)}) copy-start(s32[4]{0:T(128)} %param.18) | copy-start | bytes 52
  10.0 23.0 %collective-permute-start = (bf16[96,2048]{1,0:T(8,128)(2,1)S(1)}, bf16[96,2048]{1,0:T(8,128)(2,1)}, u32[]{:S(2)}, u32[]{:S(2)}) collective-permute-start(bf16[96,2048]{1,0:T(8,128)(2,1)S(1)} %fusion.9), channel_id=1, source_target_pairs={{0,3},{1,2},{2,1},{3,0},{4,7},{5,6},{6,5},{7,4},{8,11},{9,10},{10,... | collective-permute-start | bytes 1179656 | tf_op jit(solution)/shard_map/ppermute | solution.py:17
  13.9 19.1 %collective-permute-start.1 = (bf16[96,2048]{1,0:T(8,128)(2,1)S(1)}, bf16[96,2048]{1,0:T(8,128)(2,1)}, u32[]{:S(2)}, u32[]{:S(2)}) collective-permute-start(bf16[96,2048]{1,0:T(8,128)(2,1)S(1)} %fusion.9), channel_id=1, source_target_pairs={{0,2},{1,3},{2,0},{3,1},{4,6},{5,7},{6,4},{7,5},{8,10},{9,11},{10,... | collective-permute-start | bytes 1179656 | tf_op jit(solution)/shard_map/ppermute | solution.py:17
  14.4 27.4 %collective-permute-start.2 = (bf16[96,2048]{1,0:T(8,128)(2,1)S(1)}, bf16[96,2048]{1,0:T(8,128)(2,1)}, u32[]{:S(2)}, u32[]{:S(2)}) collective-permute-start(bf16[96,2048]{1,0:T(8,128)(2,1)S(1)} %fusion.9), channel_id=1, source_target_pairs={{0,1},{1,0},{2,3},{3,2},{4,5},{5,4},{6,7},{7,6},{8,9},{9,8},{10,11... | collective-permute-start | bytes 1179656 | tf_op jit(solution)/shard_map/ppermute | solution.py:17
  17.6 4.8 %slice-start = ((bf16[1024,1024]{1,0:T(8,128)(2,1)}), bf16[512,1024]{1,0:T(8,128)(2,1)S(1)}, s32[]{:S(2)}) async-start(bf16[1024,1024]{1,0:T(8,128)(2,1)} %param.16), calls=%async_computation.4 | async-start | bytes 2097152 | tf_op jit(solution)/shard_map/slice | solution.py:154
  17.7 46.2 %collective-permute-start.21 = (f32[1024]{0:T(1024)S(1)}, f32[1024]{0:T(1024)S(1)}, u32[]{:S(2)}, u32[]{:S(2)}) collective-permute-start(f32[1024]{0:T(1024)S(1)} %multiply_reduce_fusion), channel_id=1, source_target_pairs={{0,1},{1,0},{2,3},{3,2},{4,5},{5,4},{6,7},{7,6},{8,9},{9,8},{10,11... | collective-permute-start | bytes 12296 | tf_op jit(solution)/shard_map/ppermute | solution.py:17
  19.6 44.3 %collective-permute-start.22 = (f32[1024]{0:T(1024)S(1)}, f32[1024]{0:T(1024)S(1)}, u32[]{:S(2)}, u32[]{:S(2)}) collective-permute-start(f32[1024]{0:T(1024)S(1)} %multiply_reduce_fusion), channel_id=1, source_target_pairs={{0,2},{1,3},{2,0},{3,1},{4,6},{5,7},{6,4},{7,5},{8,10},{9,11},{10,... | collective-permute-start | bytes 12296 | tf_op jit(solution)/shard_map/ppermute | solution.py:17
  23.7 152.9 %reduce-scatter.5.cloned.1.call-start = ((), (), s32[]{:S(2)}) async-start(), calls=%async_computation.3 | async-start | bytes 2621440 | tf_op jit(solution)/shard_map/reduce_scatter | solution.py:215
  32.9 31.0 %collective-permute-start.23 = (f32[1024]{0:T(1024)S(1)}, f32[1024]{0:T(1024)S(1)}, u32[]{:S(2)}, u32[]{:S(2)}) collective-permute-start(f32[1024]{0:T(1024)S(1)} %multiply_reduce_fusion), channel_id=1, source_target_pairs={{0,3},{1,2},{2,1},{3,0},{4,7},{5,6},{6,5},{7,4},{8,11},{9,10},{10,... | collective-permute-start | bytes 12296 | tf_op jit(solution)/shard_map/ppermute | solution.py:17
  33.0 9.9 %slice-start.1 = ((s8[8388608]{0:T(1024)(128)(4,1)}), s8[4194304]{0:T(1024)(128)(4,1)S(1)}, s32[]{:S(2)}) async-start(s8[8388608]{0:T(1024)(128)(4,1)} %bitcast.90), calls=%async_computation.5 | async-start | bytes 8388608
  34.4 8.6 %slice-start.2 = ((s8[8388608]{0:T(1024)(128)(4,1)}), s8[4194304]{0:T(1024)(128)(4,1)S(1)}, s32[]{:S(2)}) async-start(s8[8388608]{0:T(1024)(128)(4,1)} %bitcast.90), calls=%async_computation.6 | async-start | bytes 8388608
  39.8 12.1 %collective-permute-start.4 = (bf16[2,48,2048]{2,1,0:T(8,128)(2,1)S(1)}, bf16[2,48,2048]{2,1,0:T(8,128)(2,1)S(1)}, u32[]{:S(2)}, u32[]{:S(2)}) collective-permute-start(bf16[2,48,2048]{2,1,0:T(8,128)(2,1)S(1)} %dynamic-slice_bitcast_fusion.1), channel_id=1, source_target_pairs={{0,4},{4,0},{8,12},{12,8},{1,5},{5,1},{9,13},{13,9},{2,6},{6,2},{1... | collective-permute-start | bytes 1179656 | tf_op jit(solution)/shard_map/ppermute | solution.py:17
  44.9 28.0 %copy-start.11 = (f32[2048]{0:T(1024)S(1)}, f32[2048]{0:T(1024)}, u32[]{:S(2)}) copy-start(f32[2048]{0:T(1024)} %param.12) | copy-start | bytes 24580
  44.9 17.9 %collective-permute-start.6 = (bf16[2,48,2048]{2,1,0:T(8,128)(2,1)S(1)}, bf16[2,48,2048]{2,1,0:T(8,128)(2,1)S(1)}, u32[]{:S(2)}, u32[]{:S(2)}) collective-permute-start(bf16[2,48,2048]{2,1,0:T(8,128)(2,1)S(1)} %dynamic-slice_bitcast_fusion), channel_id=1, source_target_pairs={{0,4},{4,0},{8,12},{12,8},{1,5},{5,1},{9,13},{13,9},{2,6},{6,2},{1... | collective-permute-start | bytes 1179656 | tf_op jit(solution)/shard_map/ppermute | solution.py:17
  52.1 16.1 %collective-permute-start.5 = (bf16[1,48,2048]{2,1,0:T(8,128)(2,1)S(1)}, bf16[1,48,2048]{2,1,0:T(8,128)(2,1)S(1)}, u32[]{:S(2)}, u32[]{:S(2)}) collective-permute-start(bf16[1,48,2048]{2,1,0:T(8,128)(2,1)S(1)} %dynamic-slice_convert_fusion.1), channel_id=1, source_target_pairs={{0,8},{4,12},{8,0},{12,4},{1,9},{5,13},{9,1},{13,5},{2,10},{6,14},... | collective-permute-start | bytes 589832 | tf_op jit(solution)/shard_map/ppermute | solution.py:17
  62.9 0.9 copy-start.6
  63.8 9.1 %collective-permute-start.7 = (bf16[1,48,2048]{2,1,0:T(8,128)(2,1)S(1)}, bf16[1,48,2048]{2,1,0:T(8,128)(2,1)}, u32[]{:S(2)}, u32[]{:S(2)}) collective-permute-start(bf16[1,48,2048]{2,1,0:T(8,128)(2,1)S(1)} %dynamic-slice_convert_fusion), channel_id=1, source_target_pairs={{0,8},{4,12},{8,0},{12,4},{1,9},{5,13},{9,1},{13,5},{2,10},{6,14},... | collective-permute-start | bytes 589832 | tf_op jit(solution)/shard_map/ppermute | solution.py:17
  64.6 9.7 %copy-start.8 = (bf16[1024,512]{1,0:T(8,128)(2,1)S(1)}, bf16[1024,512]{1,0:T(8,128)(2,1)}, u32[]{:S(2)}) copy-start(bf16[1024,512]{1,0:T(8,128)(2,1)} %constant_dynamic-slice_fusion.1) | copy-start | bytes 3145732
  64.6 14.5 %collective-permute-start.10 = (bf16[192,256]{1,0:T(8,128)(2,1)}, bf16[192,256]{1,0:T(8,128)(2,1)S(1)}, u32[]{:S(2)}, u32[]{:S(2)}) collective-permute-start(bf16[192,256]{1,0:T(8,128)(2,1)} %reduce-scatter.3.cloned.1.call-done), channel_id=1, source_target_pairs={{0,2},{1,3},{2,0},{3,1},{4,6},{5,7},{6,4},{7,5},{8,10},{9,11},{10,... | collective-permute-start | bytes 294920 | tf_op jit(solution)/shard_map/ppermute | solution.py:17
  66.2 13.0 %collective-permute-start.11 = (bf16[192,256]{1,0:T(8,128)(2,1)}, bf16[192,256]{1,0:T(8,128)(2,1)S(1)}, u32[]{:S(2)}, u32[]{:S(2)}) collective-permute-start(bf16[192,256]{1,0:T(8,128)(2,1)} %reduce-scatter.3.cloned.1.call-done), channel_id=1, source_target_pairs={{0,1},{1,0},{2,3},{3,2},{4,5},{5,4},{6,7},{7,6},{8,9},{9,8},{10,11... | collective-permute-start | bytes 294920 | tf_op jit(solution)/shard_map/ppermute | solution.py:17
  67.5 11.7 %collective-permute-start.9 = (bf16[192,256]{1,0:T(8,128)(2,1)}, bf16[192,256]{1,0:T(8,128)(2,1)S(1)}, u32[]{:S(2)}, u32[]{:S(2)}) collective-permute-start(bf16[192,256]{1,0:T(8,128)(2,1)} %reduce-scatter.3.cloned.1.call-done), channel_id=1, source_target_pairs={{0,3},{1,2},{2,1},{3,0},{4,7},{5,6},{6,5},{7,4},{8,11},{9,10},{10,... | collective-permute-start | bytes 294920 | tf_op jit(solution)/shard_map/ppermute | solution.py:17
  74.2 5.0 %copy-start.10 = (bf16[192,256]{1,0:T(8,128)(2,1)S(1)}, bf16[192,256]{1,0:T(8,128)(2,1)}, u32[]{:S(2)}) copy-start(bf16[192,256]{1,0:T(8,128)(2,1)} %reduce-scatter.3.cloned.1.call-done) | copy-start | bytes 294916
  74.2 5.0 %collective-permute-start.8 = (bf16[96,2048]{1,0:T(8,128)(2,1)S(1)}, bf16[96,2048]{1,0:T(8,128)(2,1)S(1)}, u32[]{:S(2)}, u32[]{:S(2)}) collective-permute-start(bf16[96,2048]{1,0:T(8,128)(2,1)S(1)} %pad_maximum_fusion.5), channel_id=1, source_target_pairs={{0,16},{16,0},{1,17},{17,1},{2,18},{18,2},{3,19},{19,3},{4,20},{20... | collective-permute-start | bytes 1179656 | tf_op jit(solution)/shard_map/ppermute | solution.py:17
  74.3 5.1 %copy-start.9 = (bf16[2048,1024]{1,0:T(8,128)(2,1)S(1)}, bf16[2048,1024]{1,0:T(8,128)(2,1)}, u32[]{:S(2)}) copy-start(bf16[2048,1024]{1,0:T(8,128)(2,1)} %param.15) | copy-start | bytes 12582916
  79.1 0.7 copy-start.12
  82.6 3.6 %collective-permute-start.12 = (f32[2,192]{1,0:T(2,128)S(1)}, f32[2,192]{1,0:T(2,128)S(1)}, u32[]{:S(2)}, u32[]{:S(2)}) collective-permute-start(f32[2,192]{1,0:T(2,128)S(1)} %pad_maximum_fusion.8), channel_id=1, source_target_pairs={{0,1},{1,0},{2,3},{3,2},{4,5},{5,4},{6,7},{7,6},{8,9},{9,8},{10,11... | collective-permute-start | bytes 4616 | tf_op jit(solution)/shard_map/ppermute | solution.py:17
  84.4 3.6 %collective-permute-start.13 = (f32[2,192]{1,0:T(2,128)S(1)}, f32[2,192]{1,0:T(2,128)S(1)}, u32[]{:S(2)}, u32[]{:S(2)}) collective-permute-start(f32[2,192]{1,0:T(2,128)S(1)} %pad_maximum_fusion.8), channel_id=1, source_target_pairs={{0,2},{1,3},{2,0},{3,1},{4,6},{5,7},{6,4},{7,5},{8,10},{9,11},{10,... | collective-permute-start | bytes 4616 | tf_op jit(solution)/shard_map/ppermute | solution.py:17
  85.7 4.5 %collective-permute-start.14 = (f32[2,192]{1,0:T(2,128)S(1)}, f32[2,192]{1,0:T(2,128)S(1)}, u32[]{:S(2)}, u32[]{:S(2)}) collective-permute-start(f32[2,192]{1,0:T(2,128)S(1)} %pad_maximum_fusion.8), channel_id=1, source_target_pairs={{0,3},{1,2},{2,1},{3,0},{4,7},{5,6},{6,5},{7,4},{8,11},{9,10},{10,... | collective-permute-start | bytes 4616 | tf_op jit(solution)/shard_map/ppermute | solution.py:17
  96.6 1.0 copy-start.5
  99.0 0.8 copy-start.1
  99.0 2.1 %copy-start.2 = (bf16[4,1,24,2048]{3,2,1,0:T(8,128)(2,1)}, bf16[4,1,24,2048]{3,2,1,0:T(8,128)(2,1)S(1)}, u32[]{:S(2)}) copy-start(bf16[4,1,24,2048]{3,2,1,0:T(8,128)(2,1)S(1)} %get-tuple-element.39) | copy-start | bytes 1179652
  99.0 2.1 %copy-start.3 = (bf16[4,1,24,2048]{3,2,1,0:T(8,128)(2,1)}, bf16[4,1,24,2048]{3,2,1,0:T(8,128)(2,1)S(1)}, u32[]{:S(2)}) copy-start(bf16[4,1,24,2048]{3,2,1,0:T(8,128)(2,1)S(1)} %get-tuple-element.40) | copy-start | bytes 1179652
  99.0 2.3 %copy-start = (bf16[1024,1024]{1,0:T(8,128)(2,1)S(1)}, bf16[1024,1024]{1,0:T(8,128)(2,1)}, u32[]{:S(2)}) copy-start(bf16[1024,1024]{1,0:T(8,128)(2,1)} %param.16) | copy-start | bytes 6291460
  101.1 44.3 %collective-permute-start.3 = (bf16[4,4,24,2048]{3,2,1,0:T(8,128)(2,1)}, bf16[4,4,24,2048]{3,2,1,0:T(8,128)(2,1)}, u32[]{:S(2)}, u32[]{:S(2)}) collective-permute-start(bf16[4,4,24,2048]{3,2,1,0:T(8,128)(2,1)} %pad_maximum_fusion.1), channel_id=1, source_target_pairs={{0,16},{16,0},{1,17},{17,1},{2,18},{18,2},{3,19},{19,3},{4,20},{20... | collective-permute-start | bytes 4718600 | tf_op jit(solution)/shard_map/ppermute | solution.py:17
  101.3 1.4 copy-start.7
  103.2 3.4 %collective-permute-start.24 = (f32[5120]{0:T(1024)S(1)}, f32[5120]{0:T(1024)S(1)}, u32[]{:S(2)}, u32[]{:S(2)}) collective-permute-start(f32[5120]{0:T(1024)S(1)} %pad_maximum_fusion.7), channel_id=1, source_target_pairs={{0,16},{16,0},{1,17},{17,1},{2,18},{18,2},{3,19},{19,3},{4,20},{20... | collective-permute-start | bytes 61448 | tf_op jit(solution)/shard_map/ppermute | solution.py:17
  103.6 39.8 %collective-permute-start.15 = (bf16[192,1024]{1,0:T(8,128)(2,1)S(1)}, bf16[192,1024]{1,0:T(8,128)(2,1)S(1)}, u32[]{:S(2)}, u32[]{:S(2)}) collective-permute-start(bf16[192,1024]{1,0:T(8,128)(2,1)S(1)} %constant_dynamic-slice_fusion.2.refs_1_), channel_id=1, source_target_pairs={{0,4},{4,8},{8,12},{1,5},{5,9},{9,13},{2,6},{6,10},{10,14},{3,7},{... | collective-permute-start | bytes 1179656 | tf_op jit(solution)/shard_map/ppermute | solution.py:66
  105.2 38.8 %collective-permute-start.18 = (bf16[192,1024]{1,0:T(8,128)(2,1)S(1)}, bf16[192,1024]{1,0:T(8,128)(2,1)S(1)}, u32[]{:S(2)}, u32[]{:S(2)}) collective-permute-start(bf16[192,1024]{1,0:T(8,128)(2,1)S(1)} %constant_dynamic-slice_fusion.2.refs_1_), channel_id=1, source_target_pairs={{4,0},{8,4},{12,8},{5,1},{9,5},{13,9},{6,2},{10,6},{14,10},{7,3},{... | collective-permute-start | bytes 1179656 | tf_op jit(solution)/shard_map/ppermute | solution.py:67
  106.6 30.0 %collective-permute-start.25 = (f32[5120]{0:T(1024)S(1)}, f32[5120]{0:T(1024)S(1)}, u32[]{:S(2)}, u32[]{:S(2)}) collective-permute-start(f32[5120]{0:T(1024)S(1)} %fusion.51), channel_id=1, source_target_pairs={{0,4},{4,0},{8,12},{12,8},{1,5},{5,1},{9,13},{13,9},{2,6},{6,2},{1... | collective-permute-start | bytes 61448 | tf_op jit(solution)/shard_map/ppermute | solution.py:17
  136.6 5.5 %collective-permute-start.26 = (f32[5120]{0:T(1024)S(1)}, f32[5120]{0:T(1024)S(1)}, u32[]{:S(2)}, u32[]{:S(2)}) collective-permute-start(f32[5120]{0:T(1024)S(1)} %add.166), channel_id=1, source_target_pairs={{0,8},{4,12},{8,0},{12,4},{1,9},{5,13},{9,1},{13,5},{2,10},{6,14},... | collective-permute-start | bytes 61448 | tf_op jit(solution)/shard_map/ppermute | solution.py:17
  143.4 4.0 %collective-permute-start.16 = (bf16[192,1024]{1,0:T(8,128)(2,1)S(1)}, bf16[192,1024]{1,0:T(8,128)(2,1)S(1)}, u32[]{:S(2)}, u32[]{:S(2)}) collective-permute-start(bf16[192,1024]{1,0:T(8,128)(2,1)S(1)} %collective-permute-done.15.refs_2_), channel_id=1, source_target_pairs={{4,8},{8,12},{5,9},{9,13},{6,10},{10,14},{7,11},{11,15},{20,24},{2... | collective-permute-start | bytes 1179656 | tf_op jit(solution)/shard_map/ppermute | solution.py:66
  144.1 12.9 %collective-permute-start.19 = (bf16[192,1024]{1,0:T(8,128)(2,1)S(1)}, bf16[192,1024]{1,0:T(8,128)(2,1)S(1)}, u32[]{:S(2)}, u32[]{:S(2)}) collective-permute-start(bf16[192,1024]{1,0:T(8,128)(2,1)S(1)} %collective-permute-done.18.refs_5_), channel_id=1, source_target_pairs={{4,0},{8,4},{5,1},{9,5},{6,2},{10,6},{7,3},{11,7},{20,16},{24,20},... | collective-permute-start | bytes 1179656 | tf_op jit(solution)/shard_map/ppermute | solution.py:67
  147.4 19.8 %collective-permute-start.17 = (bf16[192,1024]{1,0:T(8,128)(2,1)S(1)}, bf16[192,1024]{1,0:T(8,128)(2,1)S(1)}, u32[]{:S(2)}, u32[]{:S(2)}) collective-permute-start(bf16[192,1024]{1,0:T(8,128)(2,1)S(1)} %collective-permute-done.16.refs_3_), channel_id=1, source_target_pairs={{8,12},{9,13},{10,14},{11,15},{24,28},{25,29},{26,30},{27,31}} | collective-permute-start | bytes 1179656 | tf_op jit(solution)/shard_map/ppermute | solution.py:66
  157.0 12.0 %collective-permute-start.20 = (bf16[192,1024]{1,0:T(8,128)(2,1)S(1)}, bf16[192,1024]{1,0:T(8,128)(2,1)S(1)}, u32[]{:S(2)}, u32[]{:S(2)}) collective-permute-start(bf16[192,1024]{1,0:T(8,128)(2,1)S(1)} %collective-permute-done.19.refs_6_), channel_id=1, source_target_pairs={{4,0},{5,1},{6,2},{7,3},{20,16},{21,17},{22,18},{23,19}} | collective-permute-start | bytes 1179656 | tf_op jit(solution)/shard_map/ppermute | solution.py:67
Sparse Core Ops, SparseCore 0:
  23.8 19.9 reduce-scatter.2
  96.8 51.4 reduce-scatter.4

commit v3 on v2

v3 whole, which is shorter than its diff:
```python
import jax
import jax.numpy as jnp
from jax import lax
from jax.experimental import pallas as pl
from jax.experimental.pallas import tpu as pltpu
from jax.sharding import PartitionSpec as P

D = 8192
TILE = 256
MAXT = 2
LANES = 128
EPSILON = 1e-06


def swap(x, axis, mask):
    count = lax.axis_size(axis)
    return lax.ppermute(x, axis, [(i, i ^ mask) for i in range(count)])


def total(x, axis):
    pieces = [x] + [swap(x, axis, m) for m in range(1, lax.axis_size(axis))]
    while len(pieces) > 1:
        pieces = [pieces[i] + pieces[i + 1] for i in range(0, len(pieces), 2)]
    return pieces[0]


def butterfly(x, axes):
    for axis in axes:
        mask = 1
        while mask < lax.axis_size(axis):
            x = x + swap(x, axis, mask)
            mask *= 2
    return x


def in_order(pieces, index):
    pieces = list(pieces)
    mask = 1
    while mask < len(pieces):
        odd = (index & mask) != 0
        pieces = [jnp.where(odd, pieces[m ^ mask], pieces[m]) for m in range(len(pieces))]
        mask *= 2
    return pieces


def reduce_to_owner(parts, axis):
    index = lax.axis_index(axis)
    count = parts.shape[0]
    while count > 1:
        pairs = parts.reshape(count // 2, 2, *parts.shape[1:])
        mask = lax.axis_size(axis) // count
        bit = (index // mask) % 2
        sent = lax.dynamic_index_in_dim(pairs, 1 - bit, 1, keepdims=False)
        kept = lax.dynamic_index_in_dim(pairs, bit, 1, keepdims=False)
        came = swap(sent.astype(jnp.bfloat16), axis, mask)
        parts = kept.astype(jnp.float32) + came.astype(jnp.float32)
        count //= 2
    return parts[0]


def along_line(x, axis):
    count = lax.axis_size(axis)
    up, down = [], []
    right = left = x
    for i in range(1, count):
        right = lax.ppermute(right, axis, [(j, j + 1) for j in range(i - 1, count - 1)])
        left = lax.ppermute(left, axis, [(j, j - 1) for j in range(1, count - i + 1)])
        up.append(right)
        down.append(left)
    return up, down


def columns_of(row, count):
    parts = []
    for i in range(count // LANES):
        part = row[:, i * LANES : (i + 1) * LANES]
        parts.append(jnp.broadcast_to(part, (LANES, LANES)).T)
    return jnp.concatenate(parts, 0)


def row_of(folded):
    count = folded.shape[0]
    parts = [
        jnp.sum(folded[i * LANES : (i + 1) * LANES, :].T, 0, keepdims=True)
        for i in range(count // LANES)
    ]
    return jnp.concatenate(parts, 1)


def fold(values):
    width = values.shape[1]
    out = values[:, :LANES]
    for i in range(1, width // LANES):
        out = out + values[:, i * LANES : (i + 1) * LANES]
    return out


def text_kernel(text_ref, cot_ref, weight_ref, moment_ref, gain_ref):
    moment = lax.dot_general(
        text_ref[...], cot_ref[...], (((0,), (0,)), ((), ())), preferred_element_type=jnp.float32
    )
    for i in range(moment_ref.shape[0]):
        moment_ref[i] = moment[:, i * LANES : (i + 1) * LANES].astype(jnp.bfloat16)
    gain_ref[...] = row_of(fold(moment * weight_ref[...].astype(jnp.float32)))


def text_product(text, cot, weight):
    seq_len, columns = text.shape
    width = cot.shape[1]
    groups = width // LANES
    step = 256
    return pl.pallas_call(
        text_kernel,
        grid=(columns // step,),
        in_specs=[
            pl.BlockSpec((seq_len, step), lambda i: (0, i)),
            pl.BlockSpec((seq_len, width), lambda i: (0, 0)),
            pl.BlockSpec((step, width), lambda i: (i, 0)),
        ],
        out_specs=[
            pl.BlockSpec((groups, step, LANES), lambda i: (0, i, 0)),
            pl.BlockSpec((1, step), lambda i: (0, i)),
        ],
        out_shape=[
            jax.ShapeDtypeStruct((groups, columns, LANES), jnp.bfloat16),
            jax.ShapeDtypeStruct((1, columns), jnp.float32),
        ],
        compiler_params=pltpu.CompilerParams(vmem_limit_bytes=32 * 1024 * 1024),
        cost_estimate=pl.CostEstimate(
            flops=2 * seq_len * columns * width,
            bytes_accessed=2 * (seq_len * (columns + width) + 2 * columns * width),
            transcendentals=0,
        ),
    )(text, cot, weight)


def sums_kernel(*refs):
    order_ref, grad_ref, gain_ref, own_ref = refs[:4]
    rows_ref, sums_ref = refs[-2:]
    others = refs[4:-2]
    count = len(others) // 2
    rows = own_ref.shape[0]
    z = order_ref[0]
    for i in range(count + 1):
        at = lax.rem(z + count + 1 - i, count + 1) * rows
        if i == 0:
            piece = own_ref[...]
        else:
            piece = others[i - 1][...] + others[2 * count - i][...]
        rows_ref[pl.ds(pl.multiple_of(at, rows), rows), :] = piece
    values = rows_ref[...].astype(jnp.float32)
    sums_ref[0:1, :] = row_of(fold(values * values))
    sums_ref[1:2, :] = row_of(fold(values * grad_ref[...] * gain_ref[...]))


def row_sums(z, grad, gain, own, others):
    stream, width = grad.shape
    whole = pl.BlockSpec(memory_space=pltpu.VMEM)
    return pl.pallas_call(
        sums_kernel,
        in_specs=[pl.BlockSpec(memory_space=pltpu.SMEM)] + [whole] * (3 + len(others)),
        out_specs=[whole, whole],
        out_shape=[
            jax.ShapeDtypeStruct((stream, width), jnp.bfloat16),
            jax.ShapeDtypeStruct((2, stream), jnp.float32),
        ],
        compiler_params=pltpu.CompilerParams(vmem_limit_bytes=56 * 1024 * 1024),
        cost_estimate=pl.CostEstimate(
            flops=8 * stream * width, bytes_accessed=10 * stream * width, transcendentals=0
        ),
    )(z, grad, gain, own, *others)


def image_kernel(*refs):
    grad_ref, gain_ref, rows_ref, cot_ref = refs[:4]
    embed_ref, here_ref, there_ref, small_ref = refs[-4:]
    parts = [r[...] for r in refs[4:-4]]
    while len(parts) > 1:
        parts = [parts[i] + parts[i + 1] for i in range(0, len(parts), 2)]
    stream, width = rows_ref.shape
    inv_row = lax.rsqrt(parts[0][0:1, :] / D + EPSILON)
    mean_row = inv_row * inv_row * inv_row * parts[0][1:2, :] / D
    inv = columns_of(inv_row, stream)
    mean = columns_of(mean_row, stream)
    for i in range(width // LANES):
        at = slice(i * LANES, (i + 1) * LANES)
        values = rows_ref[:, at].astype(jnp.float32)
        scaled = grad_ref[:, at] * inv
        embed = (scaled * gain_ref[:, at] - values * mean).astype(jnp.bfloat16)
        embed_ref[:, at] = embed
        small_ref[0:1, at] = jnp.sum(scaled * values, 0, keepdims=True)
        small_ref[1:2, at] = jnp.sum(embed.astype(jnp.float32), 0, keepdims=True)
    lanes = cot_ref.shape[1]
    wide = [inv] * (lanes // LANES) if lanes >= LANES else [inv[:, :lanes]]
    cot = (cot_ref[...].astype(jnp.float32) * jnp.concatenate(wide, 1)).astype(jnp.bfloat16)
    moment = lax.dot_general(
        rows_ref[...], cot, (((0,), (0,)), ((), ())), preferred_element_type=jnp.float32
    )
    share = here_ref.shape[1]
    here_ref[...] = moment[:, :share]
    there_ref[...] = moment[:, share:].astype(jnp.bfloat16)


def image_grads(grad, gain, rows, cot, sums):
    stream, width = grad.shape
    share = cot.shape[1] // 2
    whole = pl.BlockSpec(memory_space=pltpu.VMEM)
    return pl.pallas_call(
        image_kernel,
        in_specs=[whole] * (4 + len(sums)),
        out_specs=[whole] * 4,
        out_shape=[
            jax.ShapeDtypeStruct((stream, width), jnp.bfloat16),
            jax.ShapeDtypeStruct((width, share), jnp.float32),
            jax.ShapeDtypeStruct((width, share), jnp.bfloat16),
            jax.ShapeDtypeStruct((2, width), jnp.float32),
        ],
        compiler_params=pltpu.CompilerParams(vmem_limit_bytes=56 * 1024 * 1024),
        cost_estimate=pl.CostEstimate(
            flops=4 * stream * width * share, bytes_accessed=8 * stream * width, transcendentals=0
        ),
    )(grad, gain, rows, cot, *sums)


def weight_kernel(act_ref, grad_ref, out_ref):
    step = act_ref.shape[1]
    groups = grad_ref.shape[1] // LANES
    product = lax.dot_general(
        act_ref[...], grad_ref[...], (((0,), (0,)), ((), ())), preferred_element_type=jnp.float32
    )
    for c in range(groups):
        out_ref[pl.ds(c, step, stride=groups), :] = product[:, c * LANES : (c + 1) * LANES]


def weight_product(act, grad):
    rows, features = act.shape
    width = grad.shape[1]
    groups = width // LANES
    step = 256
    return pl.pallas_call(
        weight_kernel,
        grid=(features // step,),
        in_specs=[
            pl.BlockSpec((rows, step), lambda i: (0, i)),
            pl.BlockSpec((rows, width), lambda i: (0, 0)),
        ],
        out_specs=pl.BlockSpec((step * groups, LANES), lambda i: (i, 0)),
        out_shape=jax.ShapeDtypeStruct((features * groups, LANES), jnp.float32),
        compiler_params=pltpu.CompilerParams(vmem_limit_bytes=32 * 1024 * 1024),
        cost_estimate=pl.CostEstimate(
            flops=2 * rows * features * width,
            bytes_accessed=4 * features * width + 2 * rows * (features + width),
            transcendentals=0,
        ),
    )(act, grad)


def on_device(
    vis_hidden,
    proj_weight,
    proj_bias,
    text_embed,
    norm_gain,
    key_weight,
    key_cotangent,
    tile_counts,
    text_counts,
    owner_map,
):
    f32, bf16 = jnp.float32, jnp.bfloat16
    n_sec, n_seq, n_tp = (lax.axis_size(a) for a in ("sec", "seq", "tp"))
    core, z, t = (lax.axis_index(a) for a in ("sec", "seq", "tp"))
    block_rows, features = vis_hidden.shape
    columns = proj_weight.shape[1]
    col_half = columns // n_sec
    stream = block_rows * n_tp
    own = stream // n_seq
    part_rows = block_rows // n_sec
    sub = part_rows // n_seq
    keys = key_weight.shape[1]
    key_half = keys // n_sec
    seq_len = text_embed.shape[0]
    tiles = stream // TILE

    text_values = text_embed.astype(f32)
    text_sq = total(jnp.sum(text_values * text_values, 1), "tp")

    mine = lax.dynamic_slice_in_dim(vis_hidden, core * part_rows, part_rows, 0)
    act = jax.nn.gelu(mine.astype(f32), approximate=False).astype(bf16)
    pieces = [act] + [swap(act, "tp", m) for m in range(1, n_tp)]
    pieces = [p.reshape(n_seq, sub, features) for p in pieces]

    is_mine = owner_map == z
    image_count = TILE * jnp.sum(jnp.where(is_mine, tile_counts, 0))
    text_count = jnp.sum(jnp.where(is_mine, text_counts, 0))
    text_inv = lax.rsqrt(text_sq / D + EPSILON)
    text_scale = jnp.where(jnp.arange(seq_len) < text_count, text_inv, 0.0)
    cot_half = lax.dynamic_slice_in_dim(key_cotangent, core * key_half, key_half, 1)
    cot_padded = jnp.concatenate([cot_half, jnp.zeros((MAXT * TILE, key_half), bf16)], 0)
    cot_text = lax.dynamic_slice_in_dim(cot_padded, image_count, seq_len, 0)
    cot_text = (cot_text.astype(f32) * text_scale[:, None]).astype(bf16)
    weight_half = lax.dynamic_slice_in_dim(key_weight, core * key_half, key_half, 1)
    moment, gain_text = text_product(text_embed, cot_text, weight_half)
    if n_seq != moment.shape[0]:
        share = key_half // n_seq
        moment = moment.reshape(-1, columns, LANES // share, share).transpose(0, 2, 1, 3)
        moment = moment.reshape(n_seq, columns, share)
    moment = lax.psum_scatter(moment, "seq", scatter_dimension=0, tiled=False)

    starts = jnp.cumsum(tile_counts) - tile_counts
    tile_ids = jnp.arange(tiles, dtype=jnp.int32)[:, None]
    held = (tile_ids >= starts[None]) & (tile_ids < (starts + tile_counts)[None])
    tile_owner = jnp.sum(jnp.where(held, owner_map[None], 0), 1)
    tile_place = jnp.sum(jnp.where(held, tile_ids - starts[None], 0), 1)
    share = key_half // n_tp
    from_col = (core * n_tp + t) * share
    front = lax.dynamic_slice_in_dim(key_cotangent[: MAXT * TILE], from_col, share, 1)
    front = front.reshape(MAXT, TILE, share)
    given = jnp.zeros((tiles, TILE, share), bf16)
    for place in range(MAXT):
        chosen = (tile_owner == z) & (tile_place == place)
        given = jnp.where(chosen[:, None, None], front[place][None], given)
    given = given.reshape(n_tp, n_sec, n_seq, sub, share).transpose(2, 1, 0, 3, 4)
    taken = butterfly(given.reshape(stream, share), ("seq",))
    taken = [taken] + [swap(taken, "tp", m) for m in range(1, n_tp)]
    half_cot = jnp.concatenate(in_order(taken, t), 1)
    other_cot = swap(half_cot, "sec", 1)
    image_cot = jnp.concatenate(in_order([half_cot, other_cot], core), 1)
    weight_rows = lax.dynamic_slice_in_dim(key_weight, core * col_half, col_half, 0)
    normed_grad = lax.dot_general(
        image_cot, weight_rows, (((1,), (1,)), ((), ())), preferred_element_type=f32
    )
    key_share = key_half // n_seq
    cot_own = jnp.concatenate(
        [lax.dynamic_slice_in_dim(c, z * key_share, key_share, 1) for c in (half_cot, other_cot)], 1
    )

    images = []
    for first in range(0, n_tp, 2):
        chunk = jnp.stack(pieces[first : first + 2], 1).reshape(2 * part_rows, features)
        partial = jnp.dot(chunk, proj_weight, preferred_element_type=f32).astype(bf16)
        summed = reduce_to_owner(partial.reshape(n_seq, 2 * sub, columns), "seq")
        images += list((summed + proj_bias).astype(bf16).reshape(2, sub, columns))
    image_mine = jnp.concatenate(in_order(images, t), 0)
    low, high = image_mine[:, :col_half], image_mine[:, col_half:]
    first_core = core == 0
    came = swap(jnp.where(first_core, high, low), "sec", 1)
    image = jnp.concatenate(in_order([jnp.where(first_core, low, high), came], core), 0)

    act_half = jnp.stack(in_order(pieces, t), 1)
    act_pair = in_order([act_half, swap(act_half, "sec", 1)], core)
    act_full = jnp.stack(act_pair, 1).reshape(stream, features)

    gain_half = lax.dynamic_slice_in_dim(norm_gain, core * col_half, col_half, 0)[None]
    if n_seq <= 4:
        up, down = along_line(image, "seq")
        rows, sums = row_sums(z[None], normed_grad, gain_half, image, up + down)
    else:
        gathered = lax.all_gather(image, "seq", axis=0, tiled=True)
        rows, sums = row_sums(jnp.zeros((1,), jnp.int32), normed_grad, gain_half, gathered, [])
    sums = sums + swap(sums, "sec", 1)
    sums = [sums] + [swap(sums, "tp", m) for m in range(1, n_tp)]
    embed_grad, here, there, small = image_grads(normed_grad, gain_half, rows, cot_own, sums)
    there = swap(there, "sec", 1)
    small_other = swap(small, "sec", 1)
    product = weight_product(act_full, embed_grad)
    proj_weight_grad = product.reshape(features, 1, 1, col_half)

    both = in_order([here, there.astype(f32)], core)
    key_weight_grad = (moment.astype(f32) + jnp.concatenate(both, 0)) * norm_gain[:, None]
    gain_image, proj_bias_grad = jnp.concatenate(in_order([small, small_other], core), 1)

    key_bias_part = jnp.sum(key_cotangent.astype(f32), 0)
    early = jnp.concatenate([gain_text[0], jnp.where(core == 0, key_bias_part, 0.0)])
    early = butterfly(early, ("sec", "seq"))
    gain_grad = early[:columns] + gain_image
    key_bias_grad = early[columns:]
    return (proj_weight_grad, proj_bias_grad, key_weight_grad, key_bias_grad, gain_grad)


def solution(mesh):
    placed = (
        P("tp", "seq"),
        P("seq", "tp"),
        P("tp"),
        P("seq", "tp"),
        P("tp"),
        P("tp", None),
        P("seq", None),
        P(),
        P(),
        P(),
    )
    return jax.shard_map(
        on_device,
        mesh=mesh,
        in_specs=placed,
        out_specs=(P("seq", "tp", "sec", None), P("tp"), P("tp", ("sec", "seq")), P(), P("tp")),
        check_vma=False,
    )
```

time: 186 us -> 200 us (1.075)
  Pallas kernels: 7.63 us -> 23.2 us
  waiting for transfers between devices: 65.8 us -> 76.6 us
  local copies, waits for them, and re-layouts: 23.1 us -> 13.5 us
  matrix products: 17.3 us -> 10.8 us
  starting transfers between devices: 32 us -> 35.9 us
    pallas_call x0 -> x3, Pallas kernels: none -> 15.8 us  [the longest x1 6.01 us: text_product(): pl.pallas_call(text_kernel, grid=(columns // step,), in_specs=[pl.BlockSp...]
    ppermute x21 -> x27, waiting for transfers between devices: 55 us -> 67.3 us  [swap(): return lax.ppermute(x, axis, [(i, i ^ mask) for i in range(count)])]
    dot_general x3 -> x1, matrix products: 10 us -> 3.49 us  [on_device(): lax.dot_general(image_cot, weight_rows, (((1,), (1,)), ((), ())), preferr...]
    reshape x1 -> x0, local copies, waits for them, and re-layouts: 3.94 us -> none  [on_device(): shares.reshape(columns, n_seq, key_half // n_seq).transpose(1, 0, 2)]
    rev x1 -> x0, local copies, waits for them, and re-layouts: 3.94 us -> none  [on_device(): around = jnp.concatenate([act_full[::-1], act_full[::-1]], 0)]
    ppermute x3, starting transfers between devices: 3.03 us -> 6.87 us  [along_line(): lax.ppermute(right, axis, [(j, j + 1) for j in range(i - 1, count - 1)])]
    dynamic_slice x1 -> x3, local copies, waits for them, and re-layouts: 0.03 us -> 2.49 us  [the longest x2 1.9 us: on_device(): lax.dynamic_slice_in_dim(c, z * key_share, key_share, 1)]
    mul x1, other arithmetic: 0.01 us -> 2.35 us  [on_device(): (moment.astype(f32) + jnp.concatenate(both, 0)) * norm_gain[:, None]]
  transfers between devices with their start and end apart: 29 -> 34, of which waited for: 10 -> 12; matrix products, arithmetic and copies ran while one was open for 25% -> 18% of each run, Pallas kernels for 4% -> 12%
where the time goes in v3:
time: 200 us; the launch traced here: 199 us
  waiting for transfers between devices  76.6 us (38%)
  starting transfers between devices  35.9 us (18%)
  other arithmetic  23.7 us (12%)
  Pallas kernels  23.2 us (12%)
  between operations  15.3 us (8%)
  local copies, waits for them, and re-layouts  13.5 us (7%)
  matrix products  10.8 us (5%)
    ppermute x27, waiting for transfers between devices, swap(): return lax.ppermute(x, axis, [(i, i ^ mask) for i in range(count)])  67.3 us
    ppermute x27, starting transfers between devices, swap(): return lax.ppermute(x, axis, [(i, i ^ mask) for i in range(count)])  25.1 us
    ppermute x3, waiting for transfers between devices, along_line(): lax.ppermute(left, axis, [(j, j - 1) for j in range(1, count - i + 1)])  9.25 us
    pallas_call x1, Pallas kernels, weight_product(): pl.pallas_call(weight_kernel, grid=(features // step,), in_specs=[pl.Bloc...  7.38 us
    dot_general x2, matrix products, on_device(): jnp.dot(chunk, proj_weight, preferred_element_type=f32).astype(bf16)  7.29 us
    ppermute x3, starting transfers between devices, along_line(): lax.ppermute(right, axis, [(j, j + 1) for j in range(i - 1, count - 1)])  6.87 us
    pallas_call x1, Pallas kernels, text_product(): pl.pallas_call(text_kernel, grid=(columns // step,), in_specs=[pl.BlockSp...  6.01 us
    unnamed x54, local copies, waits for them, and re-layouts  5.79 us
  transfers between devices with their start and end apart: 34, of which 12 were waited for; matrix products, arithmetic and copies ran while one was open for 18% of the time, Pallas kernels for 12%

profile of v3, /device:TPU:0, one launch (start us, length us, event | category | flops | bytes accessed | tf_op | source)
XLA Modules:
  0.0 198.9 jit_solution(4382568528274713937)
XLA Ops:
  7.2 3.2 %multiply_reduce_fusion = f32[1024]{0:T(1024)S(1)} fusion(bf16[1024,2048]{1,0:T(8,128)(2,1)} %text_ref.1), kind=kLoop, calls=%fused_computation | loop fusion | flops 6290432 | bytes 4198400 | tf_op jit(solution)/shard_map/reduce_sum | solution.py:286
  10.5 4.0 %collective-permute-start.28 = (f32[1024]{0:T(1024)S(1)}, f32[1024]{0:T(1024)S(1)}, u32[]{:S(2)}, u32[]{:S(2)}) collective-permute-start(f32[1024]{0:T(1024)S(1)} %multiply_reduce_fusion), channel_id=1, source_target_pairs={{0,3},{1,2},{2,1},{3,0},{4,7},{5,6},{6,5},{7,4},{8,11},{9,10},{10,... | collective-permute-start | bytes 12296 | tf_op jit(solution)/shard_map/ppermute | solution.py:17
  15.1 1.7 fusion.7
  16.8 2.0 collective-permute-start.2
  18.7 1.5 collective-permute-start.1
  20.6 0.6 copy-done.23
  21.4 0.6 fusion.43
  22.6 1.9 constant_dynamic-slice_fusion.weight_ref
  24.6 1.0 select_bitcast_fusion.2
  26.4 1.6 copy.31
  28.1 2.0 collective-permute-start.4
  30.1 1.3 rsqrt_select_fusion
  31.8 2.2 %collective-permute-done.4 = bf16[768,128]{1,0:T(8,128)(2,1)S(1)} collective-permute-done((bf16[768,128]{1,0:T(8,128)(2,1)}, bf16[768,128]{1,0:T(8,128)(2,1)S(1)}, u32[]{:S(2)}, u32[]{:S(2)}) %collective-permute-start.4) | collective-permute-done | bytes 196640 | tf_op jit(solution)/shard_map/ppermute | solution.py:17
  34.0 3.4 %collective-permute-start.5 = (bf16[768,128]{1,0:T(8,128)(2,1)S(1)}, bf16[768,128]{1,0:T(8,128)(2,1)S(1)}, u32[]{:S(2)}, u32[]{:S(2)}) collective-permute-start(bf16[768,128]{1,0:T(8,128)(2,1)S(1)} %bitcast_add_fusion.2), channel_id=1, source_target_pairs={{0,8},{4,12},{8,0},{12,4},{1,9},{5,13},{9,1},{13,5},{2,10},{6,14},... | collective-permute-start | bytes 589832 | tf_op jit(solution)/shard_map/ppermute | solution.py:17
  37.4 2.2 %copy-done = bf16[1024,2048]{1,0:T(8,128)(2,1)S(1)} copy-done((bf16[1024,2048]{1,0:T(8,128)(2,1)S(1)}, bf16[1024,2048]{1,0:T(8,128)(2,1)}, u32[]{:S(2)}) %copy-start) | copy-done | bytes 4194328
  39.6 6.0 %shard_map.140 = (bf16[4,2048,128]{2,1,0:T(8,128)(2,1)}, f32[1,2048]{1,0:T(1,128)S(1)}) custom-call(bf16[1024,2048]{1,0:T(8,128)(2,1)S(1)} %copy-done, bf16[1024,512]{1,0:T(8,128)(2,1)S(1)} %multiply_convert_fusion.cot_ref, bf16[2048,512]{1,0:T(8,128)(2,1)S(1)} %constant_dynamic-slice_fusion.weight_ref), custom_call_target="tpu_custom_call" | custom-call | flops 2147483648 | bytes 9437184 | tf_op jit(solution)/shard_map/pallas_call | solution.py:112
  45.7 1.6 collective-permute-start.8
  47.3 1.2 collective-permute-start.7
  48.5 0.8 collective-permute-start.6
  49.3 1.2 pad_maximum_fusion.3
  50.5 5.4 %convolution_convert_fusion.1 = bf16[192,2048]{1,0:T(8,128)(2,1)S(1)} fusion(bf16[192,2048]{1,0:T(8,128)(2,1)S(1)} %bitcast.63, bf16[2048,2048]{1,0:T(8,128)(2,1)} %param.11), kind=kOutput, calls=%fused_computation.4 | convolution fusion | flops 1611005952 | bytes 9961472 | tf_op jit(solution)/shard_map/dot_general | solution.py:341
  55.9 1.5 collective-permute-start.10
  57.5 1.1 pad_maximum_fusion.4
  58.6 1.9 convolution_convert_fusion
  60.5 0.6 collective-permute-start.12
  61.2 1.4 broadcast_select_fusion.9
  62.5 21.1 %collective-permute-done.10 = bf16[2,48,2048]{2,1,0:T(8,128)(2,1)S(1)} collective-permute-done((bf16[2,48,2048]{2,1,0:T(8,128)(2,1)S(1)}, bf16[2,48,2048]{2,1,0:T(8,128)(2,1)S(1)}, u32[]{:S(2)}, u32[]{:S(2)}) %collective-permute-start.10) | collective-permute-done | bytes 393248 | tf_op jit(solution)/shard_map/ppermute | solution.py:17
  83.8 22.2 %collective-permute-done.12 = bf16[2,48,2048]{2,1,0:T(8,128)(2,1)S(1)} collective-permute-done((bf16[2,48,2048]{2,1,0:T(8,128)(2,1)S(1)}, bf16[2,48,2048]{2,1,0:T(8,128)(2,1)S(1)}, u32[]{:S(2)}, u32[]{:S(2)}) %collective-permute-start.12) | collective-permute-done | bytes 393248 | tf_op jit(solution)/shard_map/ppermute | solution.py:17
  106.2 0.6 collective-permute-start.13
  106.8 1.3 pad_maximum_fusion.1
  108.2 8.2 %collective-permute-done.13 = bf16[1,48,2048]{2,1,0:T(8,128)(2,1)S(1)} collective-permute-done((bf16[1,48,2048]{2,1,0:T(8,128)(2,1)S(1)}, bf16[1,48,2048]{2,1,0:T(8,128)(2,1)S(1)}, u32[]{:S(2)}, u32[]{:S(2)}) %collective-permute-start.13) | collective-permute-done | bytes 196640 | tf_op jit(solution)/shard_map/ppermute | solution.py:17
  116.8 1.0 pad_maximum_fusion.2
  118.3 1.3 collective-permute-start.18
  119.6 5.3 %collective-permute-start.15 = (bf16[192,1024]{1,0:T(8,128)(2,1)S(1)}, bf16[192,1024]{1,0:T(8,128)(2,1)}, u32[]{:S(2)}, u32[]{:S(2)}) collective-permute-start(bf16[192,1024]{1,0:T(8,128)(2,1)S(1)} %pad_maximum_fusion.6.refs_3_), channel_id=1, source_target_pairs={{0,4},{4,8},{8,12},{1,5},{5,9},{9,13},{2,6},{6,10},{10,14},{3,7},{... | collective-permute-start | bytes 1179656 | tf_op jit(solution)/shard_map/ppermute | solution.py:66
  125.0 1.2 collective-permute-done.30
  126.2 6.6 %collective-permute-done.31 = f32[3072]{0:T(1024)S(1)} collective-permute-done((f32[3072]{0:T(1024)S(1)}, f32[3072]{0:T(1024)S(1)}, u32[]{:S(2)}, u32[]{:S(2)}) %collective-permute-start.31) | collective-permute-done | bytes 12320 | tf_op jit(solution)/shard_map/ppermute | solution.py:17
  132.7 0.5 collective-permute-start.32
  133.3 0.6 dynamic_slice.48
  133.9 3.5 %collective-permute-done.32 = f32[3072]{0:T(1024)S(1)} collective-permute-done((f32[3072]{0:T(1024)S(1)}, f32[3072]{0:T(1024)S(1)}, u32[]{:S(2)}, u32[]{:S(2)}) %collective-permute-start.32) | collective-permute-done | bytes 12320 | tf_op jit(solution)/shard_map/ppermute | solution.py:17
  137.4 0.6 slice.36
  138.0 1.3 collective-permute-start.19
  139.3 0.9 collective-permute-start.16
  140.2 0.9 constant_dynamic-slice_fusion.3
  141.1 1.7 broadcast_select_fusion.1
  142.9 6.5 %collective-permute-done.19.refs_8_ = bf16[192,1024]{1,0:T(8,128)(2,1)S(1)} collective-permute-done((bf16[192,1024]{1,0:T(8,128)(2,1)S(1)}, bf16[192,1024]{1,0:T(8,128)(2,1)S(1)}, u32[]{:S(2)}, u32[]{:S(2)}) %collective-permute-start.19) | collective-permute-done | bytes 393248 | tf_op jit(solution)/shard_map/ppermute | solution.py:67
  149.4 1.3 collective-permute-start.20
  150.7 0.7 collective-permute-start.17
  151.4 0.9 constant_dynamic-slice_fusion.2
  152.4 0.8 pad_maximum_fusion.7.refs_3_
  153.2 3.5 %fusion.refs_1_.refs_0_ = f32[768,1024]{1,0:T(8,128)} fusion(bf16[2048,1024]{1,0:T(8,128)(2,1)S(1)} %copy-done.5, s32[]{:T(128)S(6)} %select_n.385, bf16[768,512]{1,0:T(8,128)(2,1)S(1)} %get-tuple-element.43, bf16[768,512]{1,0:T(8,128)(2,1)S(1)} %get-tuple-element.42), kind=kOutput, calls=%fused_computation.6 | convolution fusion | flops 1613758464 | bytes 6815748 | tf_op jit(solution)/shard_map/dot_general | solution.py:330
  156.7 2.7 %collective-permute-done.20.refs_9_ = bf16[192,1024]{1,0:T(8,128)(2,1)S(1)} collective-permute-done((bf16[192,1024]{1,0:T(8,128)(2,1)S(1)}, bf16[192,1024]{1,0:T(8,128)(2,1)S(1)}, u32[]{:S(2)}, u32[]{:S(2)}) %collective-permute-start.20) | collective-permute-done | bytes 393248 | tf_op jit(solution)/shard_map/ppermute | solution.py:67
  159.4 0.7 copy-done.11
  160.3 4.1 %shard_map.137 = (bf16[768,1024]{1,0:T(8,128)(2,1)}, f32[2,768]{1,0:T(2,128)}) custom-call(s32[1]{0:T(128)} %bitcast.14.refs_0_, f32[768,1024]{1,0:T(8,128)} %fusion.refs_1_.refs_0_, f32[1,1024]{1,0:T(1,128)} %bitcast.72, bf16[192,1024]{1,0:T(8,128)(2,1)} %copy-done.4, bf16[192,1024]{1,0:T(8,128)(2,1)} %collective-permute-done.15.refs_4_, ...), custom_call_target="tpu_custom_call" | custom-call | flops 6291456 | bytes 7864320 | tf_op jit(solution)/shard_map/pallas_call | solution.py:159
  164.5 1.7 select_bitcast_fusion.1
  166.2 2.5 %collective-permute-start.24 = (f32[2,768]{1,0:T(2,128)S(1)}, f32[2,768]{1,0:T(2,128)S(1)}, u32[]{:S(2)}, u32[]{:S(2)}) collective-permute-start(f32[2,768]{1,0:T(2,128)S(1)} %add.145.refs_4_), channel_id=1, source_target_pairs={{0,3},{1,2},{2,1},{3,0},{4,7},{5,6},{6,5},{7,4},{8,11},{9,10},{10,... | collective-permute-start | bytes 18440 | tf_op jit(solution)/shard_map/ppermute | solution.py:17
  169.2 0.6 collective-permute-start.22
  170.8 1.5 collective-permute-done.23.refs_6_
  173.4 5.7 %shard_map.138 = (bf16[768,1024]{1,0:T(8,128)(2,1)}, f32[1024,128]{1,0:T(8,128)}, bf16[1024,128]{1,0:T(8,128)(2,1)}, f32[2,1024]{1,0:T(2,128)}) custom-call(f32[768,1024]{1,0:T(8,128)} %fusion.refs_1_.refs_0_, f32[1,1024]{1,0:T(1,128)} %bitcast.73, bf16[768,1024]{1,0:T(8,128)(2,1)} %get-tuple-element.13.refs_2_, bf16[768,256]{1,0:T(8,128)(2,1)} %pad_maximum_fusion.7.refs_3_, ...), custom_call_target="tpu_custom_call" | custom-call | flops 402653184 | bytes 6291456 | tf_op jit(solution)/shard_map/pallas_call | solution.py:208
  179.1 0.5 collective-permute-start.29
  179.6 1.4 copy-done.1
  181.0 7.4 %shard_map.139 = f32[16384,128]{1,0:T(8,128)} custom-call(bf16[768,2048]{1,0:T(8,128)(2,1)S(1)} %bitcast.57, bf16[768,1024]{1,0:T(8,128)(2,1)S(1)} %copy-done.1), custom_call_target="tpu_custom_call" | custom-call | flops 3221225472 | bytes 13107200 | tf_op jit(solution)/shard_map/pallas_call | solution.py:240
  188.4 0.6 pad_maximum_fusion.9
  189.0 0.6 slice_add_fusion
  189.7 2.4 %fusion.5 = f32[2048,128]{1,0:T(8,128)} fusion(f32[1024,128]{1,0:T(8,128)S(1)} %get-tuple-element.51, f32[1024,128]{1,0:T(8,128)S(1)} %get-tuple-element.50, bf16[1,2048,128]{2,1,0:T(8,128)(2,1)} %reduce-scatter.2.cloned.1.call-done, f32[2048]{0:T(1024)S(1)} %copy-done.15), kind=kLoop, calls=%fused_computation.17 | loop fusion | flops 1048576 | bytes 2629632 | tf_op jit(solution)/shard_map/mul | solution.py:370
  (129 shorter events, 6.8 us)
Async XLA Ops:
  7.2 7.9 %copy-start.13 = (bf16[192,2048]{1,0:T(8,128)(2,1)S(1)}, bf16[192,2048]{1,0:T(8,128)(2,1)}, u32[]{:S(2)}) copy-start(bf16[192,2048]{1,0:T(8,128)(2,1)} %param.10) | copy-start | bytes 2359300
  7.2 13.1 %copy-start.2 = (bf16[1024,1024]{1,0:T(8,128)(2,1)S(1)}, bf16[1024,1024]{1,0:T(8,128)(2,1)}, u32[]{:S(2)}) copy-start(bf16[1024,1024]{1,0:T(8,128)(2,1)} %param.16) | copy-start | bytes 6291460
  7.2 182.5 %reduce-scatter.2.cloned.1.call-start = ((), (), s32[]{:S(2)}) async-start(), calls=%async_computation.1 | async-start | bytes 2621440 | tf_op jit(solution)/shard_map/reduce_scatter | solution.py:308
  10.5 17.6 %collective-permute-start.28 = (f32[1024]{0:T(1024)S(1)}, f32[1024]{0:T(1024)S(1)}, u32[]{:S(2)}, u32[]{:S(2)}) collective-permute-start(f32[1024]{0:T(1024)S(1)} %multiply_reduce_fusion), channel_id=1, source_target_pairs={{0,3},{1,2},{2,1},{3,0},{4,7},{5,6},{6,5},{7,4},{8,11},{9,10},{10,... | collective-permute-start | bytes 12296 | tf_op jit(solution)/shard_map/ppermute | solution.py:17
  14.4 13.7 %collective-permute-start.27 = (f32[1024]{0:T(1024)S(1)}, f32[1024]{0:T(1024)S(1)}, u32[]{:S(2)}, u32[]{:S(2)}) collective-permute-start(f32[1024]{0:T(1024)S(1)} %multiply_reduce_fusion), channel_id=1, source_target_pairs={{0,2},{1,3},{2,0},{3,1},{4,6},{5,7},{6,4},{7,5},{8,10},{9,11},{10,... | collective-permute-start | bytes 12296 | tf_op jit(solution)/shard_map/ppermute | solution.py:17
  14.9 15.2 %collective-permute-start.26 = (f32[1024]{0:T(1024)S(1)}, f32[1024]{0:T(1024)}, u32[]{:S(2)}, u32[]{:S(2)}) collective-permute-start(f32[1024]{0:T(1024)S(1)} %multiply_reduce_fusion), channel_id=1, source_target_pairs={{0,1},{1,0},{2,3},{3,2},{4,5},{5,4},{6,7},{7,6},{8,9},{9,8},{10,11... | collective-permute-start | bytes 12296 | tf_op jit(solution)/shard_map/ppermute | solution.py:17
  16.8 40.7 %collective-permute-start.2 = (bf16[96,2048]{1,0:T(8,128)(2,1)S(1)}, bf16[96,2048]{1,0:T(8,128)(2,1)}, u32[]{:S(2)}, u32[]{:S(2)}) collective-permute-start(bf16[96,2048]{1,0:T(8,128)(2,1)S(1)} %fusion.7), channel_id=1, source_target_pairs={{0,1},{1,0},{2,3},{3,2},{4,5},{5,4},{6,7},{7,6},{8,9},{9,8},{10,11... | collective-permute-start | bytes 1179656 | tf_op jit(solution)/shard_map/ppermute | solution.py:17
  18.7 29.7 %collective-permute-start.1 = (bf16[96,2048]{1,0:T(8,128)(2,1)S(1)}, bf16[96,2048]{1,0:T(8,128)(2,1)}, u32[]{:S(2)}, u32[]{:S(2)}) collective-permute-start(bf16[96,2048]{1,0:T(8,128)(2,1)S(1)} %fusion.7), channel_id=1, source_target_pairs={{0,2},{1,3},{2,0},{3,1},{4,6},{5,7},{6,4},{7,5},{8,10},{9,11},{10,... | collective-permute-start | bytes 1179656 | tf_op jit(solution)/shard_map/ppermute | solution.py:17
  20.6 0.7 copy-start.23
  20.6 0.8 copy-start.22
  20.6 0.8 copy-start.24
  22.6 1.9 slice-start
  22.6 3.0 %copy-start.3 = (bf16[1024,1024]{1,0:T(8,128)(2,1)S(1)}, bf16[1024,1024]{1,0:T(8,128)(2,1)}, u32[]{:S(2)}) copy-start(bf16[1024,1024]{1,0:T(8,128)(2,1)} %param.16) | copy-start | bytes 6291460
  28.0 6.0 %copy-start.6 = (bf16[4,2,4,24,128]{4,3,2,1,0:T(8,128)(2,1)S(1)}, bf16[4,2,4,24,128]{4,3,2,1,0:T(8,128)(2,1)}, u32[]{:S(2)}) copy-start(bf16[4,2,4,24,128]{4,3,2,1,0:T(8,128)(2,1)} %copy.31) | copy-start | bytes 589828
  28.0 21.3 %collective-permute-start = (bf16[96,2048]{1,0:T(8,128)(2,1)S(1)}, bf16[96,2048]{1,0:T(8,128)(2,1)}, u32[]{:S(2)}, u32[]{:S(2)}) collective-permute-start(bf16[96,2048]{1,0:T(8,128)(2,1)S(1)} %fusion.7), channel_id=1, source_target_pairs={{0,3},{1,2},{2,1},{3,0},{4,7},{5,6},{6,5},{7,4},{8,11},{9,10},{10,... | collective-permute-start | bytes 1179656 | tf_op jit(solution)/shard_map/ppermute | solution.py:17
  28.1 5.9 %collective-permute-start.4 = (bf16[768,128]{1,0:T(8,128)(2,1)}, bf16[768,128]{1,0:T(8,128)(2,1)S(1)}, u32[]{:S(2)}, u32[]{:S(2)}) collective-permute-start(bf16[768,128]{1,0:T(8,128)(2,1)} %bitcast.65), channel_id=1, source_target_pairs={{0,4},{4,0},{8,12},{12,8},{1,5},{5,1},{9,13},{13,9},{2,6},{6,2},{1... | collective-permute-start | bytes 589832 | tf_op jit(solution)/shard_map/ppermute | solution.py:17
  34.0 11.6 %collective-permute-start.5 = (bf16[768,128]{1,0:T(8,128)(2,1)S(1)}, bf16[768,128]{1,0:T(8,128)(2,1)S(1)}, u32[]{:S(2)}, u32[]{:S(2)}) collective-permute-start(bf16[768,128]{1,0:T(8,128)(2,1)S(1)} %bitcast_add_fusion.2), channel_id=1, source_target_pairs={{0,8},{4,12},{8,0},{12,4},{1,9},{5,13},{9,1},{13,5},{2,10},{6,14},... | collective-permute-start | bytes 589832 | tf_op jit(solution)/shard_map/ppermute | solution.py:17
  37.4 2.2 %copy-start = (bf16[1024,2048]{1,0:T(8,128)(2,1)S(1)}, bf16[1024,2048]{1,0:T(8,128)(2,1)}, u32[]{:S(2)}) copy-start(bf16[1024,2048]{1,0:T(8,128)(2,1)} %text_ref.1) | copy-start | bytes 12582916
  45.7 70.9 %collective-permute-start.8 = (bf16[768,128]{1,0:T(8,128)(2,1)S(1)}, bf16[768,128]{1,0:T(8,128)(2,1)S(1)}, u32[]{:S(2)}, u32[]{:S(2)}) collective-permute-start(bf16[768,128]{1,0:T(8,128)(2,1)S(1)} %add.129), channel_id=1, source_target_pairs={{0,1},{1,0},{2,3},{3,2},{4,5},{5,4},{6,7},{7,6},{8,9},{9,8},{10,11... | collective-permute-start | bytes 589832 | tf_op jit(solution)/shard_map/ppermute | solution.py:17
  47.3 69.4 %collective-permute-start.7 = (bf16[768,128]{1,0:T(8,128)(2,1)S(1)}, bf16[768,128]{1,0:T(8,128)(2,1)S(1)}, u32[]{:S(2)}, u32[]{:S(2)}) collective-permute-start(bf16[768,128]{1,0:T(8,128)(2,1)S(1)} %add.129), channel_id=1, source_target_pairs={{0,2},{1,3},{2,0},{3,1},{4,6},{5,7},{6,4},{7,5},{8,10},{9,11},{10,... | collective-permute-start | bytes 589832 | tf_op jit(solution)/shard_map/ppermute | solution.py:17
  48.5 68.2 %collective-permute-start.6 = (bf16[768,128]{1,0:T(8,128)(2,1)S(1)}, bf16[768,128]{1,0:T(8,128)(2,1)S(1)}, u32[]{:S(2)}, u32[]{:S(2)}) collective-permute-start(bf16[768,128]{1,0:T(8,128)(2,1)S(1)} %add.129), channel_id=1, source_target_pairs={{0,3},{1,2},{2,1},{3,0},{4,7},{5,6},{6,5},{7,4},{8,11},{9,10},{10,... | collective-permute-start | bytes 589832 | tf_op jit(solution)/shard_map/ppermute | solution.py:17
  50.5 8.1 %slice-start.1 = ((s8[8388608]{0:T(1024)(128)(4,1)}), s8[4194304]{0:T(1024)(128)(4,1)S(1)}, s32[]{:S(2)}) async-start(s8[8388608]{0:T(1024)(128)(4,1)} %bitcast.78), calls=%async_computation.3 | async-start | bytes 8388608
  50.5 8.1 %slice-start.2 = ((s8[8388608]{0:T(1024)(128)(4,1)}), s8[4194304]{0:T(1024)(128)(4,1)S(1)}, s32[]{:S(2)}) async-start(s8[8388608]{0:T(1024)(128)(4,1)} %bitcast.78), calls=%async_computation.4 | async-start | bytes 8388608
  55.9 27.7 %collective-permute-start.10 = (bf16[2,48,2048]{2,1,0:T(8,128)(2,1)S(1)}, bf16[2,48,2048]{2,1,0:T(8,128)(2,1)S(1)}, u32[]{:S(2)}, u32[]{:S(2)}) collective-permute-start(bf16[2,48,2048]{2,1,0:T(8,128)(2,1)S(1)} %dynamic-slice_bitcast_fusion.1), channel_id=1, source_target_pairs={{0,4},{4,0},{8,12},{12,8},{1,5},{5,1},{9,13},{13,9},{2,6},{6,2},{1... | collective-permute-start | bytes 1179656 | tf_op jit(solution)/shard_map/ppermute | solution.py:17
  60.5 45.5 %collective-permute-start.12 = (bf16[2,48,2048]{2,1,0:T(8,128)(2,1)S(1)}, bf16[2,48,2048]{2,1,0:T(8,128)(2,1)S(1)}, u32[]{:S(2)}, u32[]{:S(2)}) collective-permute-start(bf16[2,48,2048]{2,1,0:T(8,128)(2,1)S(1)} %dynamic-slice_bitcast_fusion), channel_id=1, source_target_pairs={{0,4},{4,0},{8,12},{12,8},{1,5},{5,1},{9,13},{13,9},{2,6},{6,2},{1... | collective-permute-start | bytes 1179656 | tf_op jit(solution)/shard_map/ppermute | solution.py:17
  83.8 24.4 %collective-permute-start.11 = (bf16[1,48,2048]{2,1,0:T(8,128)(2,1)S(1)}, bf16[1,48,2048]{2,1,0:T(8,128)(2,1)S(1)}, u32[]{:S(2)}, u32[]{:S(2)}) collective-permute-start(bf16[1,48,2048]{2,1,0:T(8,128)(2,1)S(1)} %dynamic-slice_convert_fusion.1), channel_id=1, source_target_pairs={{0,8},{4,12},{8,0},{12,4},{1,9},{5,13},{9,1},{13,5},{2,10},{6,14},... | collective-permute-start | bytes 589832 | tf_op jit(solution)/shard_map/ppermute | solution.py:17
  106.2 10.2 %collective-permute-start.13 = (bf16[1,48,2048]{2,1,0:T(8,128)(2,1)S(1)}, bf16[1,48,2048]{2,1,0:T(8,128)(2,1)S(1)}, u32[]{:S(2)}, u32[]{:S(2)}) collective-permute-start(bf16[1,48,2048]{2,1,0:T(8,128)(2,1)S(1)} %dynamic-slice_convert_fusion), channel_id=1, source_target_pairs={{0,8},{4,12},{8,0},{12,4},{1,9},{5,13},{9,1},{13,5},{2,10},{6,14},... | collective-permute-start | bytes 589832 | tf_op jit(solution)/shard_map/ppermute | solution.py:17
  106.8 9.5 %copy-start.16 = (f32[2048]{0:T(1024)S(1)}, f32[2048]{0:T(1024)}, u32[]{:S(2)}) copy-start(f32[2048]{0:T(1024)} %param.12) | copy-start | bytes 24580
  108.2 56.3 %collective-permute-start.3 = (bf16[4,4,24,2048]{3,2,1,0:T(8,128)(2,1)}, bf16[4,4,24,2048]{3,2,1,0:T(8,128)(2,1)}, u32[]{:S(2)}, u32[]{:S(2)}) collective-permute-start(bf16[4,4,24,2048]{3,2,1,0:T(8,128)(2,1)} %pad_maximum_fusion.1), channel_id=1, source_target_pairs={{0,16},{16,0},{1,17},{17,1},{2,18},{18,2},{3,19},{19,3},{4,20},{20... | collective-permute-start | bytes 4718600 | tf_op jit(solution)/shard_map/ppermute | solution.py:17
  116.6 1.7 collective-permute-start.14
  116.8 16.5 %copy-start.15 = (f32[2048]{0:T(1024)S(1)}, f32[2048]{0:T(1024)}, u32[]{:S(2)}) copy-start(f32[2048]{0:T(1024)} %param.14) | copy-start | bytes 24580
  117.8 23.4 %collective-permute-start.9 = (bf16[768,512]{1,0:T(8,128)(2,1)}, bf16[768,512]{1,0:T(8,128)(2,1)}, u32[]{:S(2)}, u32[]{:S(2)}) collective-permute-start(bf16[768,512]{1,0:T(8,128)(2,1)} %pad_maximum_fusion.2), channel_id=1, source_target_pairs={{0,16},{16,0},{1,17},{17,1},{2,18},{18,2},{3,19},{19,3},{4,20},{20... | collective-permute-start | bytes 2359304 | tf_op jit(solution)/shard_map/ppermute | solution.py:17
  118.3 24.6 %copy-start.4 = (bf16[192,1024]{1,0:T(8,128)(2,1)}, bf16[192,1024]{1,0:T(8,128)(2,1)S(1)}, u32[]{:S(2)}) copy-start(bf16[192,1024]{1,0:T(8,128)(2,1)S(1)} %pad_maximum_fusion.6.refs_3_) | copy-start | bytes 1179652
  118.3 19.6 %collective-permute-start.18 = (bf16[192,1024]{1,0:T(8,128)(2,1)S(1)}, bf16[192,1024]{1,0:T(8,128)(2,1)S(1)}, u32[]{:S(2)}, u32[]{:S(2)}) collective-permute-start(bf16[192,1024]{1,0:T(8,128)(2,1)S(1)} %pad_maximum_fusion.6.refs_3_), channel_id=1, source_target_pairs={{4,0},{8,4},{12,8},{5,1},{9,5},{13,9},{6,2},{10,6},{14,10},{7,3},{... | collective-permute-start | bytes 1179656 | tf_op jit(solution)/shard_map/ppermute | solution.py:67
  119.6 19.6 %collective-permute-start.15 = (bf16[192,1024]{1,0:T(8,128)(2,1)S(1)}, bf16[192,1024]{1,0:T(8,128)(2,1)}, u32[]{:S(2)}, u32[]{:S(2)}) collective-permute-start(bf16[192,1024]{1,0:T(8,128)(2,1)S(1)} %pad_maximum_fusion.6.refs_3_), channel_id=1, source_target_pairs={{0,4},{4,8},{8,12},{1,5},{5,9},{9,13},{2,6},{6,10},{10,14},{3,7},{... | collective-permute-start | bytes 1179656 | tf_op jit(solution)/shard_map/ppermute | solution.py:66
  125.0 1.2 collective-permute-start.30
  126.2 6.6 %collective-permute-start.31 = (f32[3072]{0:T(1024)S(1)}, f32[3072]{0:T(1024)S(1)}, u32[]{:S(2)}, u32[]{:S(2)}) collective-permute-start(f32[3072]{0:T(1024)S(1)} %fusion.45), channel_id=1, source_target_pairs={{0,4},{4,0},{8,12},{12,8},{1,5},{5,1},{9,13},{13,9},{2,6},{6,2},{1... | collective-permute-start | bytes 36872 | tf_op jit(solution)/shard_map/ppermute | solution.py:17
  132.7 4.6 %collective-permute-start.32 = (f32[3072]{0:T(1024)S(1)}, f32[3072]{0:T(1024)S(1)}, u32[]{:S(2)}, u32[]{:S(2)}) collective-permute-start(f32[3072]{0:T(1024)S(1)} %add.155), channel_id=1, source_target_pairs={{0,8},{4,12},{8,0},{12,4},{1,9},{5,13},{9,1},{13,5},{2,10},{6,14},... | collective-permute-start | bytes 36872 | tf_op jit(solution)/shard_map/ppermute | solution.py:17
  138.0 4.9 %copy-start.8 = (bf16[192,1024]{1,0:T(8,128)(2,1)}, bf16[192,1024]{1,0:T(8,128)(2,1)S(1)}, u32[]{:S(2)}) copy-start(bf16[192,1024]{1,0:T(8,128)(2,1)S(1)} %collective-permute-done.18.refs_7_) | copy-start | bytes 1179652
  138.0 11.4 %collective-permute-start.19 = (bf16[192,1024]{1,0:T(8,128)(2,1)S(1)}, bf16[192,1024]{1,0:T(8,128)(2,1)S(1)}, u32[]{:S(2)}, u32[]{:S(2)}) collective-permute-start(bf16[192,1024]{1,0:T(8,128)(2,1)S(1)} %collective-permute-done.18.refs_7_), channel_id=1, source_target_pairs={{4,0},{8,4},{5,1},{9,5},{6,2},{10,6},{7,3},{11,7},{20,16},{24,20},... | collective-permute-start | bytes 1179656 | tf_op jit(solution)/shard_map/ppermute | solution.py:67
  139.3 11.4 %collective-permute-start.16 = (bf16[192,1024]{1,0:T(8,128)(2,1)}, bf16[192,1024]{1,0:T(8,128)(2,1)S(1)}, u32[]{:S(2)}, u32[]{:S(2)}) collective-permute-start(bf16[192,1024]{1,0:T(8,128)(2,1)} %collective-permute-done.15.refs_4_), channel_id=1, source_target_pairs={{4,8},{8,12},{5,9},{9,13},{6,10},{10,14},{7,11},{11,15},{20,24},{2... | collective-permute-start | bytes 1179656 | tf_op jit(solution)/shard_map/ppermute | solution.py:66
  141.1 12.1 %copy-start.5 = (bf16[2048,1024]{1,0:T(8,128)(2,1)S(1)}, bf16[2048,1024]{1,0:T(8,128)(2,1)}, u32[]{:S(2)}) copy-start(bf16[2048,1024]{1,0:T(8,128)(2,1)} %param.15) | copy-start | bytes 12582916
  149.4 7.3 %copy-start.9 = (bf16[192,1024]{1,0:T(8,128)(2,1)}, bf16[192,1024]{1,0:T(8,128)(2,1)S(1)}, u32[]{:S(2)}) copy-start(bf16[192,1024]{1,0:T(8,128)(2,1)S(1)} %collective-permute-done.19.refs_8_) | copy-start | bytes 1179652
  149.4 10.0 %collective-permute-start.20 = (bf16[192,1024]{1,0:T(8,128)(2,1)S(1)}, bf16[192,1024]{1,0:T(8,128)(2,1)S(1)}, u32[]{:S(2)}, u32[]{:S(2)}) collective-permute-start(bf16[192,1024]{1,0:T(8,128)(2,1)S(1)} %collective-permute-done.19.refs_8_), channel_id=1, source_target_pairs={{4,0},{5,1},{6,2},{7,3},{20,16},{21,17},{22,18},{23,19}} | collective-permute-start | bytes 1179656 | tf_op jit(solution)/shard_map/ppermute | solution.py:67
  150.7 6.0 %copy-start.10 = (bf16[192,1024]{1,0:T(8,128)(2,1)}, bf16[192,1024]{1,0:T(8,128)(2,1)S(1)}, u32[]{:S(2)}) copy-start(bf16[192,1024]{1,0:T(8,128)(2,1)S(1)} %collective-permute-done.16.refs_5_) | copy-start | bytes 1179652
  150.7 8.7 %collective-permute-start.17 = (bf16[192,1024]{1,0:T(8,128)(2,1)S(1)}, bf16[192,1024]{1,0:T(8,128)(2,1)S(1)}, u32[]{:S(2)}, u32[]{:S(2)}) collective-permute-start(bf16[192,1024]{1,0:T(8,128)(2,1)S(1)} %collective-permute-done.16.refs_5_), channel_id=1, source_target_pairs={{8,12},{9,13},{10,14},{11,15},{24,28},{25,29},{26,30},{27,31}} | collective-permute-start | bytes 1179656 | tf_op jit(solution)/shard_map/ppermute | solution.py:66
  159.4 0.8 copy-start.11
  159.4 0.9 copy-start.12
  164.4 1.7 copy-start.21
  164.4 1.7 collective-permute-start.21
  166.2 3.9 %copy-start.14 = (f32[2,768]{1,0:T(2,128)}, f32[2,768]{1,0:T(2,128)S(1)}, u32[]{:S(2)}) copy-start(f32[2,768]{1,0:T(2,128)S(1)} %add.145.refs_4_) | copy-start | bytes 18436
  166.2 4.6 %collective-permute-start.24 = (f32[2,768]{1,0:T(2,128)S(1)}, f32[2,768]{1,0:T(2,128)S(1)}, u32[]{:S(2)}, u32[]{:S(2)}) collective-permute-start(f32[2,768]{1,0:T(2,128)S(1)} %add.145.refs_4_), channel_id=1, source_target_pairs={{0,3},{1,2},{2,1},{3,0},{4,7},{5,6},{6,5},{7,4},{8,11},{9,10},{10,... | collective-permute-start | bytes 18440 | tf_op jit(solution)/shard_map/ppermute | solution.py:17
  168.7 3.6 %collective-permute-start.23 = (f32[2,768]{1,0:T(2,128)S(1)}, f32[2,768]{1,0:T(2,128)S(1)}, u32[]{:S(2)}, u32[]{:S(2)}) collective-permute-start(f32[2,768]{1,0:T(2,128)S(1)} %add.145.refs_4_), channel_id=1, source_target_pairs={{0,2},{1,3},{2,0},{3,1},{4,6},{5,7},{6,4},{7,5},{8,10},{9,11},{10,... | collective-permute-start | bytes 18440 | tf_op jit(solution)/shard_map/ppermute | solution.py:17
  169.2 3.6 %collective-permute-start.22 = (f32[2,768]{1,0:T(2,128)S(1)}, f32[2,768]{1,0:T(2,128)S(1)}, u32[]{:S(2)}, u32[]{:S(2)}) collective-permute-start(f32[2,768]{1,0:T(2,128)S(1)} %add.145.refs_4_), channel_id=1, source_target_pairs={{0,1},{1,0},{2,3},{3,2},{4,5},{5,4},{6,7},{7,6},{8,9},{9,8},{10,11... | collective-permute-start | bytes 18440 | tf_op jit(solution)/shard_map/ppermute | solution.py:17
  170.8 2.0 %copy-start.18 = (f32[2,768]{1,0:T(2,128)}, f32[2,768]{1,0:T(2,128)S(1)}, u32[]{:S(2)}) copy-start(f32[2,768]{1,0:T(2,128)S(1)} %collective-permute-done.24.refs_7_) | copy-start | bytes 18436
  172.3 0.6 copy-start.19
  172.8 0.6 copy-start.20
  179.1 9.3 %collective-permute-start.25 = (f32[2,1024]{1,0:T(2,128)}, f32[2,1024]{1,0:T(2,128)S(1)}, u32[]{:S(2)}, u32[]{:S(2)}) collective-permute-start(f32[2,1024]{1,0:T(2,128)} %get-tuple-element.16), channel_id=1, source_target_pairs={{0,16},{16,0},{1,17},{17,1},{2,18},{18,2},{3,19},{19,3},{4,20},{20... | collective-permute-start | bytes 24584 | tf_op jit(solution)/shard_map/ppermute | solution.py:17
  179.1 10.5 %collective-permute-start.29 = (bf16[1024,128]{1,0:T(8,128)(2,1)}, bf16[1024,128]{1,0:T(8,128)(2,1)S(1)}, u32[]{:S(2)}, u32[]{:S(2)}) collective-permute-start(bf16[1024,128]{1,0:T(8,128)(2,1)} %get-tuple-element.18), channel_id=1, source_target_pairs={{0,16},{16,0},{1,17},{17,1},{2,18},{18,2},{3,19},{19,3},{4,20},{20... | collective-permute-start | bytes 786440 | tf_op jit(solution)/shard_map/ppermute | solution.py:17
  179.6 1.4 copy-start.1
  181.0 7.4 %copy-start.17 = (f32[2,1024]{1,0:T(2,128)S(1)}, f32[2,1024]{1,0:T(2,128)}, u32[]{:S(2)}) copy-start(f32[2,1024]{1,0:T(2,128)} %get-tuple-element.16) | copy-start | bytes 24580
  181.0 8.6 %copy-start.7 = (f32[1024,128]{1,0:T(8,128)S(1)}, f32[1024,128]{1,0:T(8,128)}, u32[]{:S(2)}) copy-start(f32[1024,128]{1,0:T(8,128)} %get-tuple-element.19) | copy-start | bytes 1572868
Sparse Core Ops, SparseCore 0:
  45.8 63.4 reduce-scatter.1

commit v4 on v3

--- a/solution.py
+++ b/solution.py
@@ -134,54 +134,53 @@
     )(text, cot, weight)
 
 
-def sums_kernel(*refs):
-    order_ref, grad_ref, gain_ref, own_ref = refs[:4]
-    rows_ref, sums_ref = refs[-2:]
-    others = refs[4:-2]
+def sums_kernel(rows_ref, grad_ref, gain_ref, sums_ref):
+    values = rows_ref[...].astype(jnp.float32)
+    more = sums_ref.shape[1] - values.shape[0]
+    for i, terms in enumerate((values * values, values * grad_ref[...] * gain_ref[...])):
+        folded = jnp.concatenate([fold(terms), jnp.zeros((more, LANES), jnp.float32)], 0)
+        sums_ref[i : i + 1, :] = row_of(folded)
+
+
+def row_sums(rows, grad, gain):
+    count, width = rows.shape
+    padded = -(-count // LANES) * LANES
+    whole = pl.BlockSpec(memory_space=pltpu.VMEM)
+    return pl.pallas_call(
+        sums_kernel,
+        in_specs=[whole] * 3,
+        out_specs=whole,
+        out_shape=jax.ShapeDtypeStruct((2, padded), jnp.float32),
+        compiler_params=pltpu.CompilerParams(vmem_limit_bytes=16 * 1024 * 1024),
+        cost_estimate=pl.CostEstimate(
+            flops=8 * count * width, bytes_accessed=6 * count * width, transcendentals=0
+        ),
+    )(rows, grad, gain)
+
+
+def image_kernel(*refs):
+    order_ref, grad_ref, gain_ref, cot_ref, sums_ref, own_ref = refs[:6]
+    embed_ref, here_ref, there_ref, small_ref, rows_ref = refs[-5:]
+    others = refs[6:-5]
     count = len(others) // 2
     rows = own_ref.shape[0]
-    z = order_ref[0]
+    stream, width = embed_ref.shape
     for i in range(count + 1):
-        at = lax.rem(z + count + 1 - i, count + 1) * rows
+        at = lax.rem(order_ref[0] + count + 1 - i, count + 1) * rows
         if i == 0:
             piece = own_ref[...]
         else:
             piece = others[i - 1][...] + others[2 * count - i][...]
         rows_ref[pl.ds(pl.multiple_of(at, rows), rows), :] = piece
-    values = rows_ref[...].astype(jnp.float32)
-    sums_ref[0:1, :] = row_of(fold(values * values))
-    sums_ref[1:2, :] = row_of(fold(values * grad_ref[...] * gain_ref[...]))
-
-
-def row_sums(z, grad, gain, own, others):
-    stream, width = grad.shape
-    whole = pl.BlockSpec(memory_space=pltpu.VMEM)
-    return pl.pallas_call(
-        sums_kernel,
-        in_specs=[pl.BlockSpec(memory_space=pltpu.SMEM)] + [whole] * (3 + len(others)),
-        out_specs=[whole, whole],
-        out_shape=[
-            jax.ShapeDtypeStruct((stream, width), jnp.bfloat16),
-            jax.ShapeDtypeStruct((2, stream), jnp.float32),
-        ],
-        compiler_params=pltpu.CompilerParams(vmem_limit_bytes=56 * 1024 * 1024),
-        cost_estimate=pl.CostEstimate(
-            flops=8 * stream * width, bytes_accessed=10 * stream * width, transcendentals=0
-        ),
-    )(z, grad, gain, own, *others)
-
-
-def image_kernel(*refs):
-    grad_ref, gain_ref, rows_ref, cot_ref = refs[:4]
-    embed_ref, here_ref, there_ref, small_ref = refs[-4:]
-    parts = [r[...] for r in refs[4:-4]]
-    while len(parts) > 1:
-        parts = [parts[i] + parts[i + 1] for i in range(0, len(parts), 2)]
-    stream, width = rows_ref.shape
-    inv_row = lax.rsqrt(parts[0][0:1, :] / D + EPSILON)
-    mean_row = inv_row * inv_row * inv_row * parts[0][1:2, :] / D
-    inv = columns_of(inv_row, stream)
-    mean = columns_of(mean_row, stream)
+    groups = sums_ref.shape[0]
+    inv, mean = [], []
+    for i in range(groups):
+        inv_row = lax.rsqrt(sums_ref[i, 0:1, :] / D + EPSILON)
+        mean_row = inv_row * inv_row * inv_row * sums_ref[i, 1:2, :] / D
+        inv.append(columns_of(inv_row, inv_row.shape[1])[: stream // groups])
+        mean.append(columns_of(mean_row, mean_row.shape[1])[: stream // groups])
+    inv = jnp.concatenate(inv, 0)
+    mean = jnp.concatenate(mean, 0)
     for i in range(width // LANES):
         at = slice(i * LANES, (i + 1) * LANES)
         values = rows_ref[:, at].astype(jnp.float32)
@@ -201,13 +200,13 @@
     there_ref[...] = moment[:, share:].astype(jnp.bfloat16)
 
 
-def image_grads(grad, gain, rows, cot, sums):
+def image_grads(z, grad, gain, cot, sums, own, others):
     stream, width = grad.shape
     share = cot.shape[1] // 2
     whole = pl.BlockSpec(memory_space=pltpu.VMEM)
     return pl.pallas_call(
         image_kernel,
-        in_specs=[whole] * (4 + len(sums)),
+        in_specs=[pl.BlockSpec(memory_space=pltpu.SMEM)] + [whole] * (5 + len(others)),
         out_specs=[whole] * 4,
         out_shape=[
             jax.ShapeDtypeStruct((stream, width), jnp.bfloat16),
@@ -215,11 +214,12 @@
             jax.ShapeDtypeStruct((width, share), jnp.bfloat16),
             jax.ShapeDtypeStruct((2, width), jnp.float32),
         ],
+        scratch_shapes=[pltpu.VMEM((stream, width), jnp.bfloat16)],
         compiler_params=pltpu.CompilerParams(vmem_limit_bytes=56 * 1024 * 1024),
         cost_estimate=pl.CostEstimate(
             flops=4 * stream * width * share, bytes_accessed=8 * stream * width, transcendentals=0
         ),
-    )(grad, gain, rows, cot, *sums)
+    )(z, grad, gain, cot, sums, own, *others)
 
 
 def weight_kernel(act_ref, grad_ref, out_ref):
@@ -282,14 +282,27 @@
     seq_len = text_embed.shape[0]
     tiles = stream // TILE
 
-    text_values = text_embed.astype(f32)
-    text_sq = total(jnp.sum(text_values * text_values, 1), "tp")
-
     mine = lax.dynamic_slice_in_dim(vis_hidden, core * part_rows, part_rows, 0)
     act = jax.nn.gelu(mine.astype(f32), approximate=False).astype(bf16)
     pieces = [act] + [swap(act, "tp", m) for m in range(1, n_tp)]
     pieces = [p.reshape(n_seq, sub, features) for p in pieces]
 
+    images = []
+    for first, last in ((0, 1), (1, 2), (2, n_tp)):
+        blocks = last - first
+        chunk = jnp.stack(pieces[first:last], 1).reshape(blocks * part_rows, features)
+        partial = jnp.dot(chunk, proj_weight, preferred_element_type=f32).astype(bf16)
+        summed = reduce_to_owner(partial.reshape(n_seq, blocks * sub, columns), "seq")
+        images += list((summed + proj_bias).astype(bf16).reshape(blocks, sub, columns))
+    image_mine = jnp.concatenate(in_order(images, t), 0)
+    low, high = image_mine[:, :col_half], image_mine[:, col_half:]
+    first_core = core == 0
+    came = swap(jnp.where(first_core, high, low), "sec", 1)
+    image = jnp.concatenate(in_order([jnp.where(first_core, low, high), came], core), 0)
+
+    act, text_embed, key_cotangent = lax.optimization_barrier((act, text_embed, key_cotangent))
+    text_values = text_embed.astype(f32)
+    text_sq = total(jnp.sum(text_values * text_values, 1), "tp")
     is_mine = owner_map == z
     image_count = TILE * jnp.sum(jnp.where(is_mine, tile_counts, 0))
     text_count = jnp.sum(jnp.where(is_mine, text_counts, 0))
@@ -305,6 +318,7 @@
         share = key_half // n_seq
         moment = moment.reshape(-1, columns, LANES // share, share).transpose(0, 2, 1, 3)
         moment = moment.reshape(n_seq, columns, share)
+    moment, image_mine = lax.optimization_barrier((moment, image_mine))
     moment = lax.psum_scatter(moment, "seq", scatter_dimension=0, tiled=False)
 
     starts = jnp.cumsum(tile_counts) - tile_counts
@@ -335,32 +349,29 @@
         [lax.dynamic_slice_in_dim(c, z * key_share, key_share, 1) for c in (half_cot, other_cot)], 1
     )
 
-    images = []
-    for first in range(0, n_tp, 2):
-        chunk = jnp.stack(pieces[first : first + 2], 1).reshape(2 * part_rows, features)
-        partial = jnp.dot(chunk, proj_weight, preferred_element_type=f32).astype(bf16)
-        summed = reduce_to_owner(partial.reshape(n_seq, 2 * sub, columns), "seq")
-        images += list((summed + proj_bias).astype(bf16).reshape(2, sub, columns))
-    image_mine = jnp.concatenate(in_order(images, t), 0)
-    low, high = image_mine[:, :col_half], image_mine[:, col_half:]
-    first_core = core == 0
-    came = swap(jnp.where(first_core, high, low), "sec", 1)
-    image = jnp.concatenate(in_order([jnp.where(first_core, low, high), came], core), 0)
-
     act_half = jnp.stack(in_order(pieces, t), 1)
     act_pair = in_order([act_half, swap(act_half, "sec", 1)], core)
     act_full = jnp.stack(act_pair, 1).reshape(stream, features)
 
+    own_cot = lax.dynamic_slice_in_dim(image_cot, (z * n_sec + core) * (own // n_sec), own // n_sec, 0)
+    own_grad = lax.dot_general(
+        own_cot, key_weight, (((1,), (1,)), ((), ())), preferred_element_type=f32
+    )
+    sums = total(row_sums(image_mine, own_grad, norm_gain[None]), "tp")
     gain_half = lax.dynamic_slice_in_dim(norm_gain, core * col_half, col_half, 0)[None]
     if n_seq <= 4:
         up, down = along_line(image, "seq")
-        rows, sums = row_sums(z[None], normed_grad, gain_half, image, up + down)
+        sums = jnp.stack(in_order([sums] + [swap(sums, "seq", m) for m in range(1, n_seq)], z), 0)
+        others = up + down
     else:
-        gathered = lax.all_gather(image, "seq", axis=0, tiled=True)
-        rows, sums = row_sums(jnp.zeros((1,), jnp.int32), normed_grad, gain_half, gathered, [])
-    sums = sums + swap(sums, "sec", 1)
-    sums = [sums] + [swap(sums, "tp", m) for m in range(1, n_tp)]
-    embed_grad, here, there, small = image_grads(normed_grad, gain_half, rows, cot_own, sums)
+        image = lax.all_gather(image, "seq", axis=0, tiled=True)
+        sums = lax.all_gather(sums, "seq", axis=0, tiled=False)
+        others = []
+    sums = jnp.stack(in_order([sums, swap(sums, "sec", 1)], core), 1)
+    sums = sums.reshape(n_seq * n_sec, *sums.shape[2:])
+    embed_grad, here, there, small = image_grads(
+        z[None], normed_grad, gain_half, cot_own, sums, image, others
+    )
     there = swap(there, "sec", 1)
     small_other = swap(small, "sec", 1)
     product = weight_product(act_full, embed_grad)
@@ -372,7 +383,8 @@
 
     key_bias_part = jnp.sum(key_cotangent.astype(f32), 0)
     early = jnp.concatenate([gain_text[0], jnp.where(core == 0, key_bias_part, 0.0)])
-    early = butterfly(early, ("sec", "seq"))
+    early = total(early, "seq") if n_seq <= 4 else butterfly(early, ("seq",))
+    early = total(early, "sec")
     gain_grad = early[:columns] + gain_image
     key_bias_grad = early[columns:]
     return (proj_weight_grad, proj_bias_grad, key_weight_grad, key_bias_grad, gain_grad)

time: 200 us -> 217 us (1.085)
  starting transfers between devices: 35.9 us -> 47.2 us
  matrix products: 10.8 us -> 20.1 us
  other arithmetic: 23.7 us -> 28.4 us
  waiting for transfers between devices: 76.6 us -> 72.2 us
  Pallas kernels: 23.2 us -> 19.7 us
    ppermute x27 -> x33, starting transfers between devices: 25.1 us -> 40.4 us  [swap(): return lax.ppermute(x, axis, [(i, i ^ mask) for i in range(count)])]
    ppermute x27 -> x33, waiting for transfers between devices: 67.3 us -> 52.3 us  [swap(): return lax.ppermute(x, axis, [(i, i ^ mask) for i in range(count)])]
    ppermute x3, waiting for transfers between devices: 9.25 us -> 19.9 us  [along_line(): lax.ppermute(left, axis, [(j, j - 1) for j in range(1, count - i + 1)])]
    dot_general x2 -> x3, matrix products: 7.29 us -> 12.5 us  [on_device(): jnp.dot(chunk, proj_weight, preferred_element_type=f32).astype(bf16)]
    ppermute x3, starting transfers between devices: 6.87 us -> 2.67 us  [along_line(): lax.ppermute(right, axis, [(j, j + 1) for j in range(i - 1, count - 1)])]
    dot_general x0 -> x1, matrix products: none -> 4.15 us  [on_device(): lax.dot_general(own_cot, key_weight, (((1,), (1,)), ((), ())), preferred_...]
    pallas_call x2, Pallas kernels: 9.78 us -> 6.37 us  [the longest x1 6.12 us: image_grads(): pl.pallas_call(image_kernel, in_specs=[pl.BlockSpec(memory_space=pltpu.SM...]
    select_n x7 -> x9, other arithmetic: 3.35 us -> 5.89 us  [in_order(): jnp.where(odd, pieces[m ^ mask], pieces[m])]
  transfers between devices with their start and end apart: 34 -> 40, of which waited for: 12 -> 13; matrix products, arithmetic and copies ran while one was open for 18% -> 22% of each run, Pallas kernels for 12% -> 9%
where the time goes in v4:
time: 217 us; the launch traced here: 216 us
  waiting for transfers between devices  72.2 us (33%)
  starting transfers between devices  47.2 us (22%)
  other arithmetic  28.4 us (13%)
  matrix products  20.1 us (9%)
  Pallas kernels  19.7 us (9%)
  between operations  15.5 us (7%)
  local copies, waits for them, and re-layouts  13 us (6%)
    ppermute x33, waiting for transfers between devices, swap(): return lax.ppermute(x, axis, [(i, i ^ mask) for i in range(count)])  52.3 us
    ppermute x33, starting transfers between devices, swap(): return lax.ppermute(x, axis, [(i, i ^ mask) for i in range(count)])  40.4 us
    ppermute x3, waiting for transfers between devices, along_line(): lax.ppermute(left, axis, [(j, j - 1) for j in range(1, count - i + 1)])  19.9 us
    dot_general x3, matrix products, on_device(): jnp.dot(chunk, proj_weight, preferred_element_type=f32).astype(bf16)  12.5 us
    pallas_call x1, Pallas kernels, weight_product(): pl.pallas_call(weight_kernel, grid=(features // step,), in_specs=[pl.Bloc...  7.39 us
    pallas_call x1, Pallas kernels, image_grads(): pl.pallas_call(image_kernel, in_specs=[pl.BlockSpec(memory_space=pltpu.SM...  6.12 us
    pallas_call x1, Pallas kernels, text_product(): pl.pallas_call(text_kernel, grid=(columns // step,), in_specs=[pl.BlockSp...  5.97 us
    select_n x9, other arithmetic, in_order(): jnp.where(odd, pieces[m ^ mask], pieces[m])  5.89 us
  transfers between devices with their start and end apart: 40, of which 13 were waited for; matrix products, arithmetic and copies ran while one was open for 22% of the time, Pallas kernels for 9%

profile of v4, /device:TPU:0, one launch (start us, length us, event | category | flops | bytes accessed | tf_op | source)
XLA Modules:
  0.0 216.2 jit_solution(11644745707135245232)
XLA Ops:
  7.2 2.7 %fusion.4 = bf16[96,2048]{1,0:T(8,128)(2,1)S(1)} fusion(bf16[192,2048]{1,0:T(8,128)(2,1)} %param.10, s32[]{:T(128)S(6)} %select_n.429), kind=kLoop, calls=%fused_computation.22 | loop fusion | flops 12976128 | bytes 786436 | tf_op jit(solution)/shard_map/convert_element_type | solution.py:286
  9.9 3.2 %multiply_reduce_fusion = f32[1024]{0:T(1024)S(1)} fusion(bf16[1024,2048]{1,0:T(8,128)(2,1)} %text_ref), kind=kLoop, calls=%fused_computation | loop fusion | flops 6290432 | bytes 4198400 | tf_op jit(solution)/shard_map/reduce_sum | solution.py:305
  13.1 3.0 %collective-permute-start.10 = (f32[1024]{0:T(1024)S(1)}, f32[1024]{0:T(1024)}, u32[]{:S(2)}, u32[]{:S(2)}) collective-permute-start(f32[1024]{0:T(1024)S(1)} %multiply_reduce_fusion), channel_id=1, source_target_pairs={{0,1},{1,0},{2,3},{3,2},{4,5},{5,4},{6,7},{7,6},{8,9},{9,8},{10,11... | collective-permute-start | bytes 12296 | tf_op jit(solution)/shard_map/ppermute | solution.py:17
  16.2 1.5 collective-permute-start.11
  17.7 2.9 %collective-permute-start = (bf16[96,2048]{1,0:T(8,128)(2,1)S(1)}, bf16[96,2048]{1,0:T(8,128)(2,1)}, u32[]{:S(2)}, u32[]{:S(2)}) collective-permute-start(bf16[96,2048]{1,0:T(8,128)(2,1)S(1)} %fusion.4), channel_id=1, source_target_pairs={{0,3},{1,2},{2,1},{3,0},{4,7},{5,6},{6,5},{7,4},{8,11},{9,10},{10,... | collective-permute-start | bytes 1179656 | tf_op jit(solution)/shard_map/ppermute | solution.py:17
  21.5 0.6 copy-done.25
  22.1 0.7 reduce-window.8
  22.8 1.1 constant_dynamic-slice_fusion.1
  23.9 1.7 constant_dynamic-slice_fusion.weight_ref
  25.7 5.7 %convolution_convert_fusion.1 = bf16[96,2048]{1,0:T(8,128)(2,1)} fusion(bf16[96,2048]{1,0:T(8,128)(2,1)S(1)} %fusion.4, bf16[2048,2048]{1,0:T(8,128)(2,1)} %param.11), kind=kOutput, calls=%fused_computation.4 | convolution fusion | flops 805502976 | bytes 9175040 | tf_op jit(solution)/shard_map/dot_general | solution.py:294
  31.9 1.3 fusion.45
  33.4 0.7 constant_dynamic-slice_fusion.4
  35.2 1.3 rsqrt_select_fusion
  36.5 1.5 multiply_convert_fusion.cot_ref
  38.0 2.2 %copy-done = bf16[1024,2048]{1,0:T(8,128)(2,1)S(1)} copy-done((bf16[1024,2048]{1,0:T(8,128)(2,1)S(1)}, bf16[1024,2048]{1,0:T(8,128)(2,1)}, u32[]{:S(2)}) %copy-start) | copy-done | bytes 4194328
  40.2 6.0 %shard_map.137 = (bf16[4,2048,128]{2,1,0:T(8,128)(2,1)}, f32[1,2048]{1,0:T(1,128)S(1)}) custom-call(bf16[1024,2048]{1,0:T(8,128)(2,1)S(1)} %copy-done, bf16[1024,512]{1,0:T(8,128)(2,1)S(1)} %multiply_convert_fusion.cot_ref, bf16[2048,512]{1,0:T(8,128)(2,1)S(1)} %constant_dynamic-slice_fusion.weight_ref), custom_call_target="tpu_custom_call" | custom-call | flops 2147483648 | bytes 9437184 | tf_op jit(solution)/shard_map/pallas_call | solution.py:112
  46.2 1.5 collective-permute-start.35
  47.8 2.7 %collective-permute-start.36 = (f32[3072]{0:T(1024)S(1)}, f32[3072]{0:T(1024)S(1)}, u32[]{:S(2)}, u32[]{:S(2)}) collective-permute-start(f32[3072]{0:T(1024)S(1)} %pad_maximum_fusion.9), channel_id=1, source_target_pairs={{0,8},{4,12},{8,0},{12,4},{1,9},{5,13},{9,1},{13,5},{2,10},{6,14},... | collective-permute-start | bytes 36872 | tf_op jit(solution)/shard_map/ppermute | solution.py:17
  51.4 1.1 collective-permute-done.36
  52.9 3.2 %collective-permute-done.37 = f32[3072]{0:T(1024)S(1)} collective-permute-done((f32[3072]{0:T(1024)S(1)}, f32[3072]{0:T(1024)S(1)}, u32[]{:S(2)}, u32[]{:S(2)}) %collective-permute-start.37) | collective-permute-done | bytes 12320 | tf_op jit(solution)/shard_map/ppermute | solution.py:17
  58.3 3.8 %collective-permute-start.5 = (bf16[768,128]{1,0:T(8,128)(2,1)S(1)}, bf16[768,128]{1,0:T(8,128)(2,1)S(1)}, u32[]{:S(2)}, u32[]{:S(2)}) collective-permute-start(bf16[768,128]{1,0:T(8,128)(2,1)S(1)} %bitcast_add_fusion.3), channel_id=1, source_target_pairs={{0,8},{4,12},{8,0},{12,4},{1,9},{5,13},{9,1},{13,5},{2,10},{6,14},... | collective-permute-start | bytes 589832 | tf_op jit(solution)/shard_map/ppermute | solution.py:17
  62.0 5.2 %collective-permute-done.17 = bf16[2,24,2048]{2,1,0:T(8,128)(2,1)S(1)} collective-permute-done((bf16[2,24,2048]{2,1,0:T(8,128)(2,1)S(1)}, bf16[2,24,2048]{2,1,0:T(8,128)(2,1)S(1)}, u32[]{:S(2)}, u32[]{:S(2)}) %collective-permute-start.17) | collective-permute-done | bytes 196640 | tf_op jit(solution)/shard_map/ppermute | solution.py:17
  67.4 5.9 %collective-permute-done.5 = bf16[768,128]{1,0:T(8,128)(2,1)S(1)} collective-permute-done((bf16[768,128]{1,0:T(8,128)(2,1)S(1)}, bf16[768,128]{1,0:T(8,128)(2,1)S(1)}, u32[]{:S(2)}, u32[]{:S(2)}) %collective-permute-start.5) | collective-permute-done | bytes 196640 | tf_op jit(solution)/shard_map/ppermute | solution.py:17
  73.3 1.6 collective-permute-start.6
  75.4 1.5 collective-permute-start.8
  76.9 1.3 pad_maximum_fusion.5
  78.2 5.3 %convolution_convert_fusion = bf16[192,2048]{1,0:T(8,128)(2,1)S(1)} fusion(bf16[192,2048]{1,0:T(8,128)(2,1)S(1)} %bitcast.100, bf16[2048,2048]{1,0:T(8,128)(2,1)} %param.11), kind=kOutput, calls=%fused_computation.3 | convolution fusion | flops 1611005952 | bytes 9961472 | tf_op jit(solution)/shard_map/dot_general | solution.py:294
  83.6 1.5 convolution_convert_fusion.2
  85.2 1.8 broadcast_select_fusion.3
  87.0 1.2 broadcast_select_fusion.9
  88.3 4.2 %collective-permute-done.15 = bf16[2,24,2048]{2,1,0:T(8,128)(2,1)S(1)} collective-permute-done((bf16[2,24,2048]{2,1,0:T(8,128)(2,1)S(1)}, bf16[2,24,2048]{2,1,0:T(8,128)(2,1)S(1)}, u32[]{:S(2)}, u32[]{:S(2)}) %collective-permute-start.15) | collective-permute-done | bytes 196640 | tf_op jit(solution)/shard_map/ppermute | solution.py:17
  93.1 10.0 %collective-permute-done.13 = bf16[2,48,2048]{2,1,0:T(8,128)(2,1)S(1)} collective-permute-done((bf16[2,48,2048]{2,1,0:T(8,128)(2,1)S(1)}, bf16[2,48,2048]{2,1,0:T(8,128)(2,1)S(1)}, u32[]{:S(2)}, u32[]{:S(2)}) %collective-permute-start.13) | collective-permute-done | bytes 393248 | tf_op jit(solution)/shard_map/ppermute | solution.py:17
  103.1 0.8 collective-permute-start.16
  104.1 2.2 %collective-permute-start.14 = (bf16[1,48,2048]{2,1,0:T(8,128)(2,1)S(1)}, bf16[1,48,2048]{2,1,0:T(8,128)(2,1)S(1)}, u32[]{:S(2)}, u32[]{:S(2)}) collective-permute-start(bf16[1,48,2048]{2,1,0:T(8,128)(2,1)S(1)} %dynamic-slice_convert_fusion), channel_id=1, source_target_pairs={{0,8},{4,12},{8,0},{12,4},{1,9},{5,13},{9,1},{13,5},{2,10},{6,14},... | collective-permute-start | bytes 589832 | tf_op jit(solution)/shard_map/ppermute | solution.py:17
  106.5 7.4 %collective-permute-done.14 = bf16[1,48,2048]{2,1,0:T(8,128)(2,1)S(1)} collective-permute-done((bf16[1,48,2048]{2,1,0:T(8,128)(2,1)S(1)}, bf16[1,48,2048]{2,1,0:T(8,128)(2,1)S(1)}, u32[]{:S(2)}, u32[]{:S(2)}) %collective-permute-start.14) | collective-permute-done | bytes 196640 | tf_op jit(solution)/shard_map/ppermute | solution.py:17
  114.1 0.7 broadcast_select_fusion.11
  114.8 1.4 pad_maximum_fusion.3
  116.7 0.7 constant_dynamic-slice_fusion.3
  117.4 1.0 broadcast_select_fusion.13
  118.4 1.6 broadcast_select_fusion.1
  120.0 4.2 %fusion.36.grad_ref = f32[96,2048]{1,0:T(8,128)S(1)} fusion(bf16[2048,1024]{1,0:T(8,128)(2,1)} %param.15, s32[]{:T(128)S(6)} %select_n.488, bf16[768,512]{1,0:T(8,128)(2,1)S(1)} %get-tuple-element.49, bf16[768,512]{1,0:T(8,128)(2,1)S(1)} %get-tuple-element.50), kind=kOutput, calls=%fused_computation.77 | convolution fusion | flops 403046400 | bytes 6553604 | tf_op jit(solution)/shard_map/dot_general | solution.py:357
  124.8 1.5 collective-permute-start.20
  126.3 1.7 collective-permute-start.21
  128.0 1.3 collective-permute-start.27
  129.4 1.5 collective-permute-start.30
  130.9 4.0 %collective-permute-start.22 = (f32[2,128]{1,0:T(2,128)S(1)}, f32[2,128]{1,0:T(2,128)S(1)}, u32[]{:S(2)}, u32[]{:S(2)}) collective-permute-start(f32[2,128]{1,0:T(2,128)S(1)} %add_add_fusion.1), channel_id=1, source_target_pairs={{0,12},{4,8},{8,4},{12,0},{1,13},{5,9},{9,5},{13,1},{2,14},{6,10},... | collective-permute-start | bytes 3080 | tf_op jit(solution)/shard_map/ppermute | solution.py:17
  135.0 3.5 %fusion.refs_1_ = f32[768,1024]{1,0:T(8,128)} fusion(bf16[2048,1024]{1,0:T(8,128)(2,1)S(1)} %copy-done.3, s32[]{:T(128)S(6)} %select_n.461, bf16[768,512]{1,0:T(8,128)(2,1)S(1)} %get-tuple-element.50, bf16[768,512]{1,0:T(8,128)(2,1)S(1)} %get-tuple-element.49), kind=kOutput, calls=%fused_computation.7 | convolution fusion | flops 1613758464 | bytes 6815748 | tf_op jit(solution)/shard_map/dot_general | solution.py:344
  138.6 13.7 %collective-permute-done.22 = f32[2,128]{1,0:T(2,128)S(1)} collective-permute-done((f32[2,128]{1,0:T(2,128)S(1)}, f32[2,128]{1,0:T(2,128)S(1)}, u32[]{:S(2)}, u32[]{:S(2)}) %collective-permute-start.22) | collective-permute-done | bytes 1056 | tf_op jit(solution)/shard_map/ppermute | solution.py:17
  152.3 7.5 %collective-permute-start.24 = (f32[2,128]{1,0:T(2,128)S(1)}, f32[2,128]{1,0:T(2,128)S(1)}, u32[]{:S(2)}, u32[]{:S(2)}) collective-permute-start(f32[2,128]{1,0:T(2,128)S(1)} %add_add_fusion.1), channel_id=1, source_target_pairs={{0,4},{4,0},{8,12},{12,8},{1,5},{5,1},{9,13},{13,9},{2,6},{6,2},{1... | collective-permute-start | bytes 3080 | tf_op jit(solution)/shard_map/ppermute | solution.py:17
  159.8 0.9 constant_dynamic-slice_fusion.2
  160.7 0.8 collective-permute-done.24
  161.6 0.7 collective-permute-start.28
  162.4 1.3 collective-permute-start.31
  163.7 0.8 pad_maximum_fusion.6.refs_3_
  165.1 0.7 collective-permute-start.29
  165.8 10.9 %collective-permute-done.31.refs_10_ = bf16[192,1024]{1,0:T(8,128)(2,1)S(1)} collective-permute-done((bf16[192,1024]{1,0:T(8,128)(2,1)S(1)}, bf16[192,1024]{1,0:T(8,128)(2,1)S(1)}, u32[]{:S(2)}, u32[]{:S(2)}) %collective-permute-start.31) | collective-permute-done | bytes 393248 | tf_op jit(solution)/shard_map/ppermute | solution.py:67
  176.7 1.3 collective-permute-start.32
  178.0 1.7 select_bitcast_fusion.1
  180.5 9.0 %collective-permute-done.32.refs_11_ = bf16[192,1024]{1,0:T(8,128)(2,1)S(1)} collective-permute-done((bf16[192,1024]{1,0:T(8,128)(2,1)S(1)}, bf16[192,1024]{1,0:T(8,128)(2,1)S(1)}, u32[]{:S(2)}, u32[]{:S(2)}) %collective-permute-start.32) | collective-permute-done | bytes 393248 | tf_op jit(solution)/shard_map/ppermute | solution.py:67
  189.5 0.7 copy-done.15
  190.2 6.1 %shard_map.139 = (bf16[768,1024]{1,0:T(8,128)(2,1)}, f32[1024,128]{1,0:T(8,128)}, bf16[1024,128]{1,0:T(8,128)(2,1)}, f32[2,1024]{1,0:T(2,128)}) custom-call(s32[1]{0:T(128)} %bitcast.7.refs_0_, f32[768,1024]{1,0:T(8,128)} %fusion.refs_1_, f32[1,1024]{1,0:T(1,128)} %bitcast.108, bf16[768,256]{1,0:T(8,128)(2,1)} %pad_maximum_fusion.6.refs_3_, ...), custom_call_target="tpu_custom_call" | custom-call | flops 402653184 | bytes 6291456 | tf_op jit(solution)/shard_map/pallas_call | solution.py:207
  196.8 1.4 copy-done.1
  198.2 7.4 %shard_map.140 = f32[16384,128]{1,0:T(8,128)} custom-call(bf16[768,2048]{1,0:T(8,128)(2,1)S(1)} %bitcast.87, bf16[768,1024]{1,0:T(8,128)(2,1)S(1)} %copy-done.1), custom_call_target="tpu_custom_call" | custom-call | flops 3221225472 | bytes 13107200 | tf_op jit(solution)/shard_map/pallas_call | solution.py:240
  207.0 2.4 %fusion.2 = f32[2048,128]{1,0:T(8,128)} fusion(f32[1024,128]{1,0:T(8,128)S(1)} %get-tuple-element.58, f32[1024,128]{1,0:T(8,128)S(1)} %get-tuple-element.57, bf16[1,2048,128]{2,1,0:T(8,128)(2,1)} %reduce-scatter.2.cloned.1.call-done, f32[2048]{0:T(1024)S(1)} %copy-done.2), kind=kLoop, calls=%fused_computation.18 | loop fusion | flops 1048576 | bytes 2629632 | tf_op jit(solution)/shard_map/mul | solution.py:381
  (153 shorter events, 11.9 us)
Async XLA Ops:
  7.2 199.8 %reduce-scatter.2.cloned.1.call-start = ((), (), s32[]{:S(2)}) async-start(), calls=%async_computation.1 | async-start | bytes 2621440 | tf_op jit(solution)/shard_map/reduce_scatter | solution.py:322
  9.9 11.2 %copy-start.4 = (bf16[1024,1024]{1,0:T(8,128)(2,1)S(1)}, bf16[1024,1024]{1,0:T(8,128)(2,1)}, u32[]{:S(2)}) copy-start(bf16[1024,1024]{1,0:T(8,128)(2,1)} %param.16) | copy-start | bytes 6291460
  13.1 22.0 %collective-permute-start.10 = (f32[1024]{0:T(1024)S(1)}, f32[1024]{0:T(1024)}, u32[]{:S(2)}, u32[]{:S(2)}) collective-permute-start(f32[1024]{0:T(1024)S(1)} %multiply_reduce_fusion), channel_id=1, source_target_pairs={{0,1},{1,0},{2,3},{3,2},{4,5},{5,4},{6,7},{7,6},{8,9},{9,8},{10,11... | collective-permute-start | bytes 12296 | tf_op jit(solution)/shard_map/ppermute | solution.py:17
  16.2 19.0 %collective-permute-start.11 = (f32[1024]{0:T(1024)S(1)}, f32[1024]{0:T(1024)}, u32[]{:S(2)}, u32[]{:S(2)}) collective-permute-start(f32[1024]{0:T(1024)S(1)} %multiply_reduce_fusion), channel_id=1, source_target_pairs={{0,2},{1,3},{2,0},{3,1},{4,6},{5,7},{6,4},{7,5},{8,10},{9,11},{10,... | collective-permute-start | bytes 12296 | tf_op jit(solution)/shard_map/ppermute | solution.py:17
  17.7 17.5 %collective-permute-start.12 = (f32[1024]{0:T(1024)S(1)}, f32[1024]{0:T(1024)}, u32[]{:S(2)}, u32[]{:S(2)}) collective-permute-start(f32[1024]{0:T(1024)S(1)} %multiply_reduce_fusion), channel_id=1, source_target_pairs={{0,3},{1,2},{2,1},{3,0},{4,7},{5,6},{6,5},{7,4},{8,11},{9,10},{10,... | collective-permute-start | bytes 12296 | tf_op jit(solution)/shard_map/ppermute | solution.py:17
  17.7 57.2 %collective-permute-start = (bf16[96,2048]{1,0:T(8,128)(2,1)S(1)}, bf16[96,2048]{1,0:T(8,128)(2,1)}, u32[]{:S(2)}, u32[]{:S(2)}) collective-permute-start(bf16[96,2048]{1,0:T(8,128)(2,1)S(1)} %fusion.4), channel_id=1, source_target_pairs={{0,3},{1,2},{2,1},{3,0},{4,7},{5,6},{6,5},{7,4},{8,11},{9,10},{10,... | collective-permute-start | bytes 1179656 | tf_op jit(solution)/shard_map/ppermute | solution.py:17
  20.6 54.8 %collective-permute-start.1 = (bf16[96,2048]{1,0:T(8,128)(2,1)S(1)}, bf16[96,2048]{1,0:T(8,128)(2,1)}, u32[]{:S(2)}, u32[]{:S(2)}) collective-permute-start(bf16[96,2048]{1,0:T(8,128)(2,1)S(1)} %fusion.4), channel_id=1, source_target_pairs={{0,2},{1,3},{2,0},{3,1},{4,6},{5,7},{6,4},{7,5},{8,10},{9,11},{10,... | collective-permute-start | bytes 1179656 | tf_op jit(solution)/shard_map/ppermute | solution.py:17
  25.6 6.3 %copy-start.23 = (s32[4]{0:T(128)S(1)}, s32[4]{0:T(128)}, u32[]{:S(2)}) copy-start(s32[4]{0:T(128)} %param.19) | copy-start | bytes 52
  25.6 6.3 %copy-start.24 = (s32[4,1]{0,1:T(1,128)S(1)}, s32[4,1]{0,1:T(1,128)}, u32[]{:S(2)}) copy-start(s32[4,1]{0,1:T(1,128)} %reduce-window.8) | copy-start | bytes 52
  25.6 7.8 %slice-start.2 = ((bf16[1024,1024]{1,0:T(8,128)(2,1)}), bf16[512,1024]{1,0:T(8,128)(2,1)S(1)}, s32[]{:S(2)}) async-start(bf16[1024,1024]{1,0:T(8,128)(2,1)} %param.16), calls=%async_computation.4 | async-start | bytes 2097152 | tf_op jit(solution)/shard_map/slice | solution.py:331
  38.0 2.2 %copy-start = (bf16[1024,2048]{1,0:T(8,128)(2,1)S(1)}, bf16[1024,2048]{1,0:T(8,128)(2,1)}, u32[]{:S(2)}) copy-start(bf16[1024,2048]{1,0:T(8,128)(2,1)} %text_ref) | copy-start | bytes 12582916
  40.2 6.0 %copy-start.20 = (f32[1024]{0:T(1024)S(1)}, f32[1024]{0:T(1024)}, u32[]{:S(2)}) copy-start(f32[1024]{0:T(1024)} %broadcast_select_fusion.32) | copy-start | bytes 12292
  40.2 10.4 %copy-start.17 = (bf16[256,128]{1,0:T(8,128)(2,1)S(1)}, bf16[256,128]{1,0:T(8,128)(2,1)}, u32[]{:S(2)}) copy-start(bf16[256,128]{1,0:T(8,128)(2,1)} %get-tuple-element.56) | copy-start | bytes 196612
  40.2 10.5 %copy-start.16 = (bf16[256,128]{1,0:T(8,128)(2,1)S(1)}, bf16[256,128]{1,0:T(8,128)(2,1)}, u32[]{:S(2)}) copy-start(bf16[256,128]{1,0:T(8,128)(2,1)} %get-tuple-element.55) | copy-start | bytes 196612
  46.2 9.9 %copy-start.6 = (bf16[96,2048]{1,0:T(8,128)(2,1)S(1)}, bf16[96,2048]{1,0:T(8,128)(2,1)}, u32[]{:S(2)}) copy-start(bf16[96,2048]{1,0:T(8,128)(2,1)} %convolution_convert_fusion.1) | copy-start | bytes 1179652
  46.2 10.1 %copy-start.2 = (f32[2048]{0:T(1024)S(1)}, f32[2048]{0:T(1024)}, u32[]{:S(2)}) copy-start(f32[2048]{0:T(1024)} %param.14) | copy-start | bytes 24580
  46.2 4.8 %collective-permute-start.35 = (f32[3072]{0:T(1024)S(1)}, f32[3072]{0:T(1024)S(1)}, u32[]{:S(2)}, u32[]{:S(2)}) collective-permute-start(f32[3072]{0:T(1024)S(1)} %pad_maximum_fusion.9), channel_id=1, source_target_pairs={{0,4},{4,0},{8,12},{12,8},{1,5},{5,1},{9,13},{13,9},{2,6},{6,2},{1... | collective-permute-start | bytes 36872 | tf_op jit(solution)/shard_map/ppermute | solution.py:17
  47.8 4.8 %collective-permute-start.36 = (f32[3072]{0:T(1024)S(1)}, f32[3072]{0:T(1024)S(1)}, u32[]{:S(2)}, u32[]{:S(2)}) collective-permute-start(f32[3072]{0:T(1024)S(1)} %pad_maximum_fusion.9), channel_id=1, source_target_pairs={{0,8},{4,12},{8,0},{12,4},{1,9},{5,13},{9,1},{13,5},{2,10},{6,14},... | collective-permute-start | bytes 36872 | tf_op jit(solution)/shard_map/ppermute | solution.py:17
  50.4 5.7 %collective-permute-start.37 = (f32[3072]{0:T(1024)S(1)}, f32[3072]{0:T(1024)S(1)}, u32[]{:S(2)}, u32[]{:S(2)}) collective-permute-start(f32[3072]{0:T(1024)S(1)} %pad_maximum_fusion.9), channel_id=1, source_target_pairs={{0,12},{4,8},{8,4},{12,0},{1,13},{5,9},{9,5},{13,1},{2,14},{6,10},... | collective-permute-start | bytes 36872 | tf_op jit(solution)/shard_map/ppermute | solution.py:17
  51.1 32.5 %collective-permute-start.2 = (bf16[96,2048]{1,0:T(8,128)(2,1)S(1)}, bf16[96,2048]{1,0:T(8,128)(2,1)S(1)}, u32[]{:S(2)}, u32[]{:S(2)}) collective-permute-start(bf16[96,2048]{1,0:T(8,128)(2,1)S(1)} %fusion.4), channel_id=1, source_target_pairs={{0,1},{1,0},{2,3},{3,2},{4,5},{5,4},{6,7},{7,6},{8,9},{9,8},{10,11... | collective-permute-start | bytes 1179656 | tf_op jit(solution)/shard_map/ppermute | solution.py:17
  52.6 5.7 %collective-permute-start.4 = (bf16[768,128]{1,0:T(8,128)(2,1)S(1)}, bf16[768,128]{1,0:T(8,128)(2,1)S(1)}, u32[]{:S(2)}, u32[]{:S(2)}) collective-permute-start(bf16[768,128]{1,0:T(8,128)(2,1)S(1)} %bitcast.101), channel_id=1, source_target_pairs={{0,4},{4,0},{8,12},{12,8},{1,5},{5,1},{9,13},{13,9},{2,6},{6,2},{1... | collective-permute-start | bytes 589832 | tf_op jit(solution)/shard_map/ppermute | solution.py:17
  56.1 1.2 collective-permute-start.38
  57.3 9.9 %collective-permute-start.17 = (bf16[2,24,2048]{2,1,0:T(8,128)(2,1)S(1)}, bf16[2,24,2048]{2,1,0:T(8,128)(2,1)S(1)}, u32[]{:S(2)}, u32[]{:S(2)}) collective-permute-start(bf16[2,24,2048]{2,1,0:T(8,128)(2,1)S(1)} %dynamic-slice_bitcast_fusion.1), channel_id=1, source_target_pairs={{0,4},{4,0},{8,12},{12,8},{1,5},{5,1},{9,13},{13,9},{2,6},{6,2},{1... | collective-permute-start | bytes 589832 | tf_op jit(solution)/shard_map/ppermute | solution.py:17
  58.3 15.0 %collective-permute-start.5 = (bf16[768,128]{1,0:T(8,128)(2,1)S(1)}, bf16[768,128]{1,0:T(8,128)(2,1)S(1)}, u32[]{:S(2)}, u32[]{:S(2)}) collective-permute-start(bf16[768,128]{1,0:T(8,128)(2,1)S(1)} %bitcast_add_fusion.3), channel_id=1, source_target_pairs={{0,8},{4,12},{8,0},{12,4},{1,9},{5,13},{9,1},{13,5},{2,10},{6,14},... | collective-permute-start | bytes 589832 | tf_op jit(solution)/shard_map/ppermute | solution.py:17
  67.3 46.7 %collective-permute-start.18 = (bf16[1,24,2048]{2,1,0:T(8,128)(2,1)S(1)}, bf16[1,24,2048]{2,1,0:T(8,128)(2,1)S(1)}, u32[]{:S(2)}, u32[]{:S(2)}) collective-permute-start(bf16[1,24,2048]{2,1,0:T(8,128)(2,1)S(1)} %dynamic-slice_convert_fusion.1), channel_id=1, source_target_pairs={{0,8},{4,12},{8,0},{12,4},{1,9},{5,13},{9,1},{13,5},{2,10},{6,14},... | collective-permute-start | bytes 294920 | tf_op jit(solution)/shard_map/ppermute | solution.py:17
  73.3 30.8 %collective-permute-start.6 = (bf16[768,128]{1,0:T(8,128)(2,1)S(1)}, bf16[768,128]{1,0:T(8,128)(2,1)S(1)}, u32[]{:S(2)}, u32[]{:S(2)}) collective-permute-start(bf16[768,128]{1,0:T(8,128)(2,1)S(1)} %add.166), channel_id=1, source_target_pairs={{0,3},{1,2},{2,1},{3,0},{4,7},{5,6},{6,5},{7,4},{8,11},{9,10},{10,... | collective-permute-start | bytes 589832 | tf_op jit(solution)/shard_map/ppermute | solution.py:17
  74.9 31.4 %collective-permute-start.7 = (bf16[768,128]{1,0:T(8,128)(2,1)S(1)}, bf16[768,128]{1,0:T(8,128)(2,1)S(1)}, u32[]{:S(2)}, u32[]{:S(2)}) collective-permute-start(bf16[768,128]{1,0:T(8,128)(2,1)S(1)} %add.166), channel_id=1, source_target_pairs={{0,2},{1,3},{2,0},{3,1},{4,6},{5,7},{6,4},{7,5},{8,10},{9,11},{10,... | collective-permute-start | bytes 589832 | tf_op jit(solution)/shard_map/ppermute | solution.py:17
  75.4 30.8 %collective-permute-start.8 = (bf16[768,128]{1,0:T(8,128)(2,1)S(1)}, bf16[768,128]{1,0:T(8,128)(2,1)S(1)}, u32[]{:S(2)}, u32[]{:S(2)}) collective-permute-start(bf16[768,128]{1,0:T(8,128)(2,1)S(1)} %add.166), channel_id=1, source_target_pairs={{0,1},{1,0},{2,3},{3,2},{4,5},{5,4},{6,7},{7,6},{8,9},{9,8},{10,11... | collective-permute-start | bytes 589832 | tf_op jit(solution)/shard_map/ppermute | solution.py:17
  76.9 6.7 %slice-start = ((s8[8388608]{0:T(1024)(128)(4,1)}), s8[4194304]{0:T(1024)(128)(4,1)S(1)}, s32[]{:S(2)}) async-start(s8[8388608]{0:T(1024)(128)(4,1)} %bitcast.91), calls=%async_computation.2 | async-start | bytes 8388608
  78.2 5.4 %slice-start.1 = ((s8[8388608]{0:T(1024)(128)(4,1)}), s8[4194304]{0:T(1024)(128)(4,1)S(1)}, s32[]{:S(2)}) async-start(s8[8388608]{0:T(1024)(128)(4,1)} %bitcast.91), calls=%async_computation.3 | async-start | bytes 8388608
  85.1 7.4 %collective-permute-start.15 = (bf16[2,24,2048]{2,1,0:T(8,128)(2,1)S(1)}, bf16[2,24,2048]{2,1,0:T(8,128)(2,1)S(1)}, u32[]{:S(2)}, u32[]{:S(2)}) collective-permute-start(bf16[2,24,2048]{2,1,0:T(8,128)(2,1)S(1)} %dynamic-slice_bitcast_fusion.2), channel_id=1, source_target_pairs={{0,4},{4,0},{8,12},{12,8},{1,5},{5,1},{9,13},{13,9},{2,6},{6,2},{1... | collective-permute-start | bytes 589832 | tf_op jit(solution)/shard_map/ppermute | solution.py:17
  92.6 10.5 %collective-permute-start.13 = (bf16[2,48,2048]{2,1,0:T(8,128)(2,1)S(1)}, bf16[2,48,2048]{2,1,0:T(8,128)(2,1)S(1)}, u32[]{:S(2)}, u32[]{:S(2)}) collective-permute-start(bf16[2,48,2048]{2,1,0:T(8,128)(2,1)S(1)} %dynamic-slice_bitcast_fusion), channel_id=1, source_target_pairs={{0,4},{4,0},{8,12},{12,8},{1,5},{5,1},{9,13},{13,9},{2,6},{6,2},{1... | collective-permute-start | bytes 1179656 | tf_op jit(solution)/shard_map/ppermute | solution.py:17
  103.1 10.9 %collective-permute-start.16 = (bf16[1,24,2048]{2,1,0:T(8,128)(2,1)S(1)}, bf16[1,24,2048]{2,1,0:T(8,128)(2,1)S(1)}, u32[]{:S(2)}, u32[]{:S(2)}) collective-permute-start(bf16[1,24,2048]{2,1,0:T(8,128)(2,1)S(1)} %dynamic-slice_convert_fusion.2), channel_id=1, source_target_pairs={{0,8},{4,12},{8,0},{12,4},{1,9},{5,13},{9,1},{13,5},{2,10},{6,14},... | collective-permute-start | bytes 294920 | tf_op jit(solution)/shard_map/ppermute | solution.py:17
  104.0 9.8 %copy-start.21 = (f32[2048]{0:T(1024)S(1)}, f32[2048]{0:T(1024)}, u32[]{:S(2)}) copy-start(f32[2048]{0:T(1024)} %param.12) | copy-start | bytes 24580
  104.1 9.8 %collective-permute-start.14 = (bf16[1,48,2048]{2,1,0:T(8,128)(2,1)S(1)}, bf16[1,48,2048]{2,1,0:T(8,128)(2,1)S(1)}, u32[]{:S(2)}, u32[]{:S(2)}) collective-permute-start(bf16[1,48,2048]{2,1,0:T(8,128)(2,1)S(1)} %dynamic-slice_convert_fusion), channel_id=1, source_target_pairs={{0,8},{4,12},{8,0},{12,4},{1,9},{5,13},{9,1},{13,5},{2,10},{6,14},... | collective-permute-start | bytes 589832 | tf_op jit(solution)/shard_map/ppermute | solution.py:17
  106.4 12.0 %collective-permute-start.9 = (bf16[768,512]{1,0:T(8,128)(2,1)S(1)}, bf16[768,512]{1,0:T(8,128)(2,1)}, u32[]{:S(2)}, u32[]{:S(2)}) collective-permute-start(bf16[768,512]{1,0:T(8,128)(2,1)S(1)} %pad_maximum_fusion.4), channel_id=1, source_target_pairs={{0,16},{16,0},{1,17},{17,1},{2,18},{18,2},{3,19},{19,3},{4,20},{20... | collective-permute-start | bytes 2359304 | tf_op jit(solution)/shard_map/ppermute | solution.py:17
  114.8 2.6 %collective-permute-start.26 = (bf16[96,1024]{1,0:T(8,128)(2,1)}, bf16[96,1024]{1,0:T(8,128)(2,1)}, u32[]{:S(2)}, u32[]{:S(2)}) collective-permute-start(bf16[96,1024]{1,0:T(8,128)(2,1)} %broadcast_select_fusion.11), channel_id=1, source_target_pairs={{0,16},{16,0},{1,17},{17,1},{2,18},{18,2},{3,19},{19,3},{4,20},{20... | collective-permute-start | bytes 589832 | tf_op jit(solution)/shard_map/ppermute | solution.py:17
  116.2 61.8 %collective-permute-start.3 = (bf16[4,4,24,2048]{3,2,1,0:T(8,128)(2,1)}, bf16[4,4,24,2048]{3,2,1,0:T(8,128)(2,1)}, u32[]{:S(2)}, u32[]{:S(2)}) collective-permute-start(bf16[4,4,24,2048]{3,2,1,0:T(8,128)(2,1)} %pad_maximum_fusion.3), channel_id=1, source_target_pairs={{0,16},{16,0},{1,17},{17,1},{2,18},{18,2},{3,19},{19,3},{4,20},{20... | collective-permute-start | bytes 4718600 | tf_op jit(solution)/shard_map/ppermute | solution.py:17
  120.0 14.9 %copy-start.3 = (bf16[2048,1024]{1,0:T(8,128)(2,1)S(1)}, bf16[2048,1024]{1,0:T(8,128)(2,1)}, u32[]{:S(2)}) copy-start(bf16[2048,1024]{1,0:T(8,128)(2,1)} %param.15) | copy-start | bytes 12582916
  124.4 4.9 %collective-permute-start.19 = (f32[2,128]{1,0:T(2,128)S(1)}, f32[2,128]{1,0:T(2,128)S(1)}, u32[]{:S(2)}, u32[]{:S(2)}) collective-permute-start(f32[2,128]{1,0:T(2,128)S(1)} %shard_map.138), channel_id=1, source_target_pairs={{0,1},{1,0},{2,3},{3,2},{4,5},{5,4},{6,7},{7,6},{8,9},{9,8},{10,11... | collective-permute-start | bytes 3080 | tf_op jit(solution)/shard_map/ppermute | solution.py:17
  124.8 6.1 %collective-permute-start.20 = (f32[2,128]{1,0:T(2,128)S(1)}, f32[2,128]{1,0:T(2,128)S(1)}, u32[]{:S(2)}, u32[]{:S(2)}) collective-permute-start(f32[2,128]{1,0:T(2,128)S(1)} %shard_map.138), channel_id=1, source_target_pairs={{0,2},{1,3},{2,0},{3,1},{4,6},{5,7},{6,4},{7,5},{8,10},{9,11},{10,... | collective-permute-start | bytes 3080 | tf_op jit(solution)/shard_map/ppermute | solution.py:17
  126.3 4.6 %collective-permute-start.21 = (f32[2,128]{1,0:T(2,128)S(1)}, f32[2,128]{1,0:T(2,128)S(1)}, u32[]{:S(2)}, u32[]{:S(2)}) collective-permute-start(f32[2,128]{1,0:T(2,128)S(1)} %shard_map.138), channel_id=1, source_target_pairs={{0,3},{1,2},{2,1},{3,0},{4,7},{5,6},{6,5},{7,4},{8,11},{9,10},{10,... | collective-permute-start | bytes 3080 | tf_op jit(solution)/shard_map/ppermute | solution.py:17
  128.0 10.4 %copy-start.5 = (bf16[192,1024]{1,0:T(8,128)(2,1)}, bf16[192,1024]{1,0:T(8,128)(2,1)S(1)}, u32[]{:S(2)}) copy-start(bf16[192,1024]{1,0:T(8,128)(2,1)S(1)} %pad_maximum_fusion.8.refs_5_) | copy-start | bytes 1179652
  128.0 33.6 %collective-permute-start.27 = (bf16[192,1024]{1,0:T(8,128)(2,1)S(1)}, bf16[192,1024]{1,0:T(8,128)(2,1)S(1)}, u32[]{:S(2)}, u32[]{:S(2)}) collective-permute-start(bf16[192,1024]{1,0:T(8,128)(2,1)S(1)} %pad_maximum_fusion.8.refs_5_), channel_id=1, source_target_pairs={{0,4},{4,8},{8,12},{1,5},{5,9},{9,13},{2,6},{6,10},{10,14},{3,7},{... | collective-permute-start | bytes 1179656 | tf_op jit(solution)/shard_map/ppermute | solution.py:66
  129.4 33.0 %collective-permute-start.30 = (bf16[192,1024]{1,0:T(8,128)(2,1)S(1)}, bf16[192,1024]{1,0:T(8,128)(2,1)S(1)}, u32[]{:S(2)}, u32[]{:S(2)}) collective-permute-start(bf16[192,1024]{1,0:T(8,128)(2,1)S(1)} %pad_maximum_fusion.8.refs_5_), channel_id=1, source_target_pairs={{4,0},{8,4},{12,8},{5,1},{9,5},{13,9},{6,2},{10,6},{14,10},{7,3},{... | collective-permute-start | bytes 1179656 | tf_op jit(solution)/shard_map/ppermute | solution.py:67
  130.9 32.7 %copy-start.7 = (bf16[768,128]{1,0:T(8,128)(2,1)S(1)}, bf16[768,128]{1,0:T(8,128)(2,1)}, u32[]{:S(2)}) copy-start(bf16[768,128]{1,0:T(8,128)(2,1)} %constant_dynamic-slice_fusion.3) | copy-start | bytes 589828
  130.9 21.3 %collective-permute-start.22 = (f32[2,128]{1,0:T(2,128)S(1)}, f32[2,128]{1,0:T(2,128)S(1)}, u32[]{:S(2)}, u32[]{:S(2)}) collective-permute-start(f32[2,128]{1,0:T(2,128)S(1)} %add_add_fusion.1), channel_id=1, source_target_pairs={{0,12},{4,8},{8,4},{12,0},{1,13},{5,9},{9,5},{13,1},{2,14},{6,10},... | collective-permute-start | bytes 3080 | tf_op jit(solution)/shard_map/ppermute | solution.py:17
  138.4 22.3 %collective-permute-start.23 = (f32[2,128]{1,0:T(2,128)S(1)}, f32[2,128]{1,0:T(2,128)S(1)}, u32[]{:S(2)}, u32[]{:S(2)}) collective-permute-start(f32[2,128]{1,0:T(2,128)S(1)} %add_add_fusion.1), channel_id=1, source_target_pairs={{0,8},{4,12},{8,0},{12,4},{1,9},{5,13},{9,1},{13,5},{2,10},{6,14},... | collective-permute-start | bytes 3080 | tf_op jit(solution)/shard_map/ppermute | solution.py:17
  152.3 9.2 %collective-permute-start.24 = (f32[2,128]{1,0:T(2,128)S(1)}, f32[2,128]{1,0:T(2,128)S(1)}, u32[]{:S(2)}, u32[]{:S(2)}) collective-permute-start(f32[2,128]{1,0:T(2,128)S(1)} %add_add_fusion.1), channel_id=1, source_target_pairs={{0,4},{4,0},{8,12},{12,8},{1,5},{5,1},{9,13},{13,9},{2,6},{6,2},{1... | collective-permute-start | bytes 3080 | tf_op jit(solution)/shard_map/ppermute | solution.py:17
  161.5 2.9 %collective-permute-start.25 = (f32[4,2,128]{2,1,0:T(2,128)S(1)}, f32[4,2,128]{2,1,0:T(2,128)S(1)}, u32[]{:S(2)}, u32[]{:S(2)}) collective-permute-start(f32[4,2,128]{2,1,0:T(2,128)S(1)} %pad_maximum_fusion.12), channel_id=1, source_target_pairs={{0,16},{16,0},{1,17},{17,1},{2,18},{18,2},{3,19},{19,3},{4,20},{20... | collective-permute-start | bytes 12296 | tf_op jit(solution)/shard_map/ppermute | solution.py:17
  161.6 18.1 %copy-start.10 = (bf16[192,1024]{1,0:T(8,128)(2,1)}, bf16[192,1024]{1,0:T(8,128)(2,1)S(1)}, u32[]{:S(2)}) copy-start(bf16[192,1024]{1,0:T(8,128)(2,1)S(1)} %collective-permute-done.27.refs_6_) | copy-start | bytes 1179652
  161.6 3.4 %collective-permute-start.28 = (bf16[192,1024]{1,0:T(8,128)(2,1)S(1)}, bf16[192,1024]{1,0:T(8,128)(2,1)S(1)}, u32[]{:S(2)}, u32[]{:S(2)}) collective-permute-start(bf16[192,1024]{1,0:T(8,128)(2,1)S(1)} %collective-permute-done.27.refs_6_), channel_id=1, source_target_pairs={{4,8},{8,12},{5,9},{9,13},{6,10},{10,14},{7,11},{11,15},{20,24},{2... | collective-permute-start | bytes 1179656 | tf_op jit(solution)/shard_map/ppermute | solution.py:66
  162.3 17.4 %copy-start.11 = (bf16[192,1024]{1,0:T(8,128)(2,1)}, bf16[192,1024]{1,0:T(8,128)(2,1)S(1)}, u32[]{:S(2)}) copy-start(bf16[192,1024]{1,0:T(8,128)(2,1)S(1)} %collective-permute-done.30.refs_9_) | copy-start | bytes 1179652
  162.4 14.3 %collective-permute-start.31 = (bf16[192,1024]{1,0:T(8,128)(2,1)S(1)}, bf16[192,1024]{1,0:T(8,128)(2,1)S(1)}, u32[]{:S(2)}, u32[]{:S(2)}) collective-permute-start(bf16[192,1024]{1,0:T(8,128)(2,1)S(1)} %collective-permute-done.30.refs_9_), channel_id=1, source_target_pairs={{4,0},{8,4},{5,1},{9,5},{6,2},{10,6},{7,3},{11,7},{20,16},{24,20},... | collective-permute-start | bytes 1179656 | tf_op jit(solution)/shard_map/ppermute | solution.py:67
  165.1 14.6 %copy-start.12 = (bf16[192,1024]{1,0:T(8,128)(2,1)}, bf16[192,1024]{1,0:T(8,128)(2,1)S(1)}, u32[]{:S(2)}) copy-start(bf16[192,1024]{1,0:T(8,128)(2,1)S(1)} %collective-permute-done.28.refs_7_) | copy-start | bytes 1179652
  165.1 15.4 %collective-permute-start.29 = (bf16[192,1024]{1,0:T(8,128)(2,1)S(1)}, bf16[192,1024]{1,0:T(8,128)(2,1)S(1)}, u32[]{:S(2)}, u32[]{:S(2)}) collective-permute-start(bf16[192,1024]{1,0:T(8,128)(2,1)S(1)} %collective-permute-done.28.refs_7_), channel_id=1, source_target_pairs={{8,12},{9,13},{10,14},{11,15},{24,28},{25,29},{26,30},{27,31}} | collective-permute-start | bytes 1179656 | tf_op jit(solution)/shard_map/ppermute | solution.py:66
  176.7 3.1 %copy-start.13 = (bf16[192,1024]{1,0:T(8,128)(2,1)}, bf16[192,1024]{1,0:T(8,128)(2,1)S(1)}, u32[]{:S(2)}) copy-start(bf16[192,1024]{1,0:T(8,128)(2,1)S(1)} %collective-permute-done.31.refs_10_) | copy-start | bytes 1179652
  176.7 12.8 %collective-permute-start.32 = (bf16[192,1024]{1,0:T(8,128)(2,1)S(1)}, bf16[192,1024]{1,0:T(8,128)(2,1)S(1)}, u32[]{:S(2)}, u32[]{:S(2)}) collective-permute-start(bf16[192,1024]{1,0:T(8,128)(2,1)S(1)} %collective-permute-done.31.refs_10_), channel_id=1, source_target_pairs={{4,0},{5,1},{6,2},{7,3},{20,16},{21,17},{22,18},{23,19}} | collective-permute-start | bytes 1179656 | tf_op jit(solution)/shard_map/ppermute | solution.py:67
  180.5 9.0 %copy-start.14 = (bf16[192,1024]{1,0:T(8,128)(2,1)}, bf16[192,1024]{1,0:T(8,128)(2,1)S(1)}, u32[]{:S(2)}) copy-start(bf16[192,1024]{1,0:T(8,128)(2,1)S(1)} %collective-permute-done.29.refs_8_) | copy-start | bytes 1179652
  196.3 9.3 %collective-permute-start.33 = (f32[2,1024]{1,0:T(2,128)}, f32[2,1024]{1,0:T(2,128)S(1)}, u32[]{:S(2)}, u32[]{:S(2)}) collective-permute-start(f32[2,1024]{1,0:T(2,128)} %get-tuple-element.20), channel_id=1, source_target_pairs={{0,16},{16,0},{1,17},{17,1},{2,18},{18,2},{3,19},{19,3},{4,20},{20... | collective-permute-start | bytes 24584 | tf_op jit(solution)/shard_map/ppermute | solution.py:17
  196.3 10.6 %collective-permute-start.34 = (bf16[1024,128]{1,0:T(8,128)(2,1)}, bf16[1024,128]{1,0:T(8,128)(2,1)S(1)}, u32[]{:S(2)}, u32[]{:S(2)}) collective-permute-start(bf16[1024,128]{1,0:T(8,128)(2,1)} %get-tuple-element.22), channel_id=1, source_target_pairs={{0,16},{16,0},{1,17},{17,1},{2,18},{18,2},{3,19},{19,3},{4,20},{20... | collective-permute-start | bytes 786440 | tf_op jit(solution)/shard_map/ppermute | solution.py:17
  198.2 7.4 %copy-start.22 = (f32[2,1024]{1,0:T(2,128)S(1)}, f32[2,1024]{1,0:T(2,128)}, u32[]{:S(2)}) copy-start(f32[2,1024]{1,0:T(2,128)} %get-tuple-element.20) | copy-start | bytes 24580
  198.2 8.0 %copy-start.19 = (f32[3072]{0:T(1024)S(1)}, f32[3072]{0:T(1024)}, u32[]{:S(2)}) copy-start(f32[3072]{0:T(1024)} %copy-done.18) | copy-start | bytes 36868
  198.2 8.6 %copy-start.9 = (f32[1024,128]{1,0:T(8,128)S(1)}, f32[1024,128]{1,0:T(8,128)}, u32[]{:S(2)}) copy-start(f32[1024,128]{1,0:T(8,128)} %get-tuple-element.23) | copy-start | bytes 1572868
  (5 other events, 5.1 us)
Sparse Core Ops, SparseCore 0:
  117.5 50.3 reduce-scatter.1

commit v5 on v4

--- a/solution.py
+++ b/solution.py
@@ -43,9 +43,14 @@
     return pieces
 
 
-def reduce_to_owner(parts, axis):
+def together(*values):
+    return lax.optimization_barrier(values)
+
+
+def reduce_to_owner(parts, axis, then=None):
     index = lax.axis_index(axis)
     count = parts.shape[0]
+    after = None
     while count > 1:
         pairs = parts.reshape(count // 2, 2, *parts.shape[1:])
         mask = lax.axis_size(axis) // count
@@ -53,9 +58,11 @@
         sent = lax.dynamic_index_in_dim(pairs, 1 - bit, 1, keepdims=False)
         kept = lax.dynamic_index_in_dim(pairs, bit, 1, keepdims=False)
         came = swap(sent.astype(jnp.bfloat16), axis, mask)
+        if after is None and then is not None:
+            came, *after = together(came, *then)
         parts = kept.astype(jnp.float32) + came.astype(jnp.float32)
         count //= 2
-    return parts[0]
+    return parts[0], after
 
 
 def along_line(x, axis):
@@ -287,22 +294,16 @@
     pieces = [act] + [swap(act, "tp", m) for m in range(1, n_tp)]
     pieces = [p.reshape(n_seq, sub, features) for p in pieces]
 
-    images = []
-    for first, last in ((0, 1), (1, 2), (2, n_tp)):
-        blocks = last - first
-        chunk = jnp.stack(pieces[first:last], 1).reshape(blocks * part_rows, features)
+    def product(blocks):
+        chunk = jnp.stack(blocks, 1).reshape(len(blocks) * part_rows, features)
         partial = jnp.dot(chunk, proj_weight, preferred_element_type=f32).astype(bf16)
-        summed = reduce_to_owner(partial.reshape(n_seq, blocks * sub, columns), "seq")
-        images += list((summed + proj_bias).astype(bf16).reshape(blocks, sub, columns))
-    image_mine = jnp.concatenate(in_order(images, t), 0)
-    low, high = image_mine[:, :col_half], image_mine[:, col_half:]
-    first_core = core == 0
-    came = swap(jnp.where(first_core, high, low), "sec", 1)
-    image = jnp.concatenate(in_order([jnp.where(first_core, low, high), came], core), 0)
-
-    act, text_embed, key_cotangent = lax.optimization_barrier((act, text_embed, key_cotangent))
+        return partial.reshape(n_seq, len(blocks) * sub, columns)
+
+    partials = [product(pieces[:1]), product(pieces[1:2])]
+
     text_values = text_embed.astype(f32)
-    text_sq = total(jnp.sum(text_values * text_values, 1), "tp")
+    text_sq, *pieces = together(jnp.sum(text_values * text_values, 1), *pieces)
+    text_sq = total(text_sq, "tp")
     is_mine = owner_map == z
     image_count = TILE * jnp.sum(jnp.where(is_mine, tile_counts, 0))
     text_count = jnp.sum(jnp.where(is_mine, text_counts, 0))
@@ -318,8 +319,6 @@
         share = key_half // n_seq
         moment = moment.reshape(-1, columns, LANES // share, share).transpose(0, 2, 1, 3)
         moment = moment.reshape(n_seq, columns, share)
-    moment, image_mine = lax.optimization_barrier((moment, image_mine))
-    moment = lax.psum_scatter(moment, "seq", scatter_dimension=0, tiled=False)
 
     starts = jnp.cumsum(tile_counts) - tile_counts
     tile_ids = jnp.arange(tiles, dtype=jnp.int32)[:, None]
@@ -335,7 +334,24 @@
         chosen = (tile_owner == z) & (tile_place == place)
         given = jnp.where(chosen[:, None, None], front[place][None], given)
     given = given.reshape(n_tp, n_sec, n_seq, sub, share).transpose(2, 1, 0, 3, 4)
-    taken = butterfly(given.reshape(stream, share), ("seq",))
+    given = given.reshape(stream, share)
+    given, partials[0] = together(given, partials[0])
+    taken = butterfly(given, ("seq",))
+
+    partials.append(product(pieces[2:]))
+    images = []
+    for i, partial in enumerate(partials):
+        held_back = (moment, taken) if i == len(partials) - 1 else None
+        summed, after = reduce_to_owner(partial, "seq", held_back)
+        images += list((summed + proj_bias).astype(bf16).reshape(-1, sub, columns))
+    moment, taken = after
+    moment = lax.psum_scatter(moment, "seq", scatter_dimension=0, tiled=False)
+    image_mine = jnp.concatenate(in_order(images, t), 0)
+    low, high = image_mine[:, :col_half], image_mine[:, col_half:]
+    first_core = core == 0
+    came = swap(jnp.where(first_core, high, low), "sec", 1)
+    image = jnp.concatenate(in_order([jnp.where(first_core, low, high), came], core), 0)
+
     taken = [taken] + [swap(taken, "tp", m) for m in range(1, n_tp)]
     half_cot = jnp.concatenate(in_order(taken, t), 1)
     other_cot = swap(half_cot, "sec", 1)
@@ -353,6 +369,10 @@
     act_pair = in_order([act_half, swap(act_half, "sec", 1)], core)
     act_full = jnp.stack(act_pair, 1).reshape(stream, features)
 
+    key_bias_part = jnp.sum(key_cotangent.astype(f32), 0)
+    early = jnp.concatenate([gain_text[0], jnp.where(core == 0, key_bias_part, 0.0)])
+    early = total(early, "sec")
+
     own_cot = lax.dynamic_slice_in_dim(image_cot, (z * n_sec + core) * (own // n_sec), own // n_sec, 0)
     own_grad = lax.dot_general(
         own_cot, key_weight, (((1,), (1,)), ((), ())), preferred_element_type=f32
@@ -361,6 +381,7 @@
     gain_half = lax.dynamic_slice_in_dim(norm_gain, core * col_half, col_half, 0)[None]
     if n_seq <= 4:
         up, down = along_line(image, "seq")
+        sums, up[-2], down[-2] = together(sums, up[-2], down[-2])
         sums = jnp.stack(in_order([sums] + [swap(sums, "seq", m) for m in range(1, n_seq)], z), 0)
         others = up + down
     else:
@@ -372,19 +393,17 @@
     embed_grad, here, there, small = image_grads(
         z[None], normed_grad, gain_half, cot_own, sums, image, others
     )
+    early, embed_grad = together(early, embed_grad)
+    early = total(early, "seq") if n_seq <= 4 else butterfly(early, ("seq",))
     there = swap(there, "sec", 1)
     small_other = swap(small, "sec", 1)
-    product = weight_product(act_full, embed_grad)
-    proj_weight_grad = product.reshape(features, 1, 1, col_half)
+    weight_grad = weight_product(act_full, embed_grad)
+    proj_weight_grad = weight_grad.reshape(features, 1, 1, col_half)
 
     both = in_order([here, there.astype(f32)], core)
     key_weight_grad = (moment.astype(f32) + jnp.concatenate(both, 0)) * norm_gain[:, None]
     gain_image, proj_bias_grad = jnp.concatenate(in_order([small, small_other], core), 1)
 
-    key_bias_part = jnp.sum(key_cotangent.astype(f32), 0)
-    early = jnp.concatenate([gain_text[0], jnp.where(core == 0, key_bias_part, 0.0)])
-    early = total(early, "seq") if n_seq <= 4 else butterfly(early, ("seq",))
-    early = total(early, "sec")
     gain_grad = early[:columns] + gain_image
     key_bias_grad = early[columns:]
     return (proj_weight_grad, proj_bias_grad, key_weight_grad, key_bias_grad, gain_grad)

time: 217 us -> 196 us (0.903)
  waiting for transfers between devices: 72.2 us -> 46.1 us
  local copies, waits for them, and re-layouts: 13 us -> 15.7 us
    ppermute x33, waiting for transfers between devices: 52.3 us -> 20.2 us  [swap(): return lax.ppermute(x, axis, [(i, i ^ mask) for i in range(count)])]
    ppermute x3, waiting for transfers between devices: 19.9 us -> 25.8 us  [along_line(): lax.ppermute(left, axis, [(j, j - 1) for j in range(1, count - i + 1)])]
    ppermute x3, starting transfers between devices: 2.67 us -> 6.69 us  [along_line(): lax.ppermute(right, axis, [(j, j + 1) for j in range(i - 1, count - 1)])]
    select_n x9 -> x7, other arithmetic: 5.89 us -> 2.85 us  [in_order(): jnp.where(odd, pieces[m ^ mask], pieces[m])]
    ppermute x33, starting transfers between devices: 40.4 us -> 38.1 us  [swap(): return lax.ppermute(x, axis, [(i, i ^ mask) for i in range(count)])]
    another operation x1 -> x2, other arithmetic: 1.35 us -> 3.6 us  [on_device(): act_half = jnp.stack(in_order(pieces, t), 1)]
    unnamed x56 -> x52, local copies, waits for them, and re-layouts: 5.09 us -> 3.99 us
  transfers between devices with their start and end apart: 40 -> 40, of which waited for: 13 -> 10; matrix products, arithmetic and copies ran while one was open for 22% -> 28% of each run, Pallas kernels for 9% -> 10%
where the time goes in v5:
time: 196 us
  starting transfers between devices  48.7 us (25%)
  waiting for transfers between devices  46.1 us (24%)
  other arithmetic  29 us (15%)
  matrix products  20.9 us (11%)
  Pallas kernels  19.8 us (10%)
  local copies, waits for them, and re-layouts  15.7 us (8%)
  between operations  15.4 us (8%)
    ppermute x33, starting transfers between devices, swap(): return lax.ppermute(x, axis, [(i, i ^ mask) for i in range(count)])  38.1 us
    ppermute x3, waiting for transfers between devices, along_line(): lax.ppermute(left, axis, [(j, j - 1) for j in range(1, count - i + 1)])  25.8 us
    ppermute x33, waiting for transfers between devices, swap(): return lax.ppermute(x, axis, [(i, i ^ mask) for i in range(count)])  20.2 us
    dot_general x3, matrix products, product(): jnp.dot(chunk, proj_weight, preferred_element_type=f32).astype(bf16)  13.6 us
    pallas_call x1, Pallas kernels, weight_product(): pl.pallas_call(weight_kernel, grid=(features // step,), in_specs=[pl.Bloc...  7.39 us
    ppermute x3, starting transfers between devices, along_line(): lax.ppermute(right, axis, [(j, j + 1) for j in range(i - 1, count - 1)])  6.69 us
    pallas_call x1, Pallas kernels, image_grads(): pl.pallas_call(image_kernel, in_specs=[pl.BlockSpec(memory_space=pltpu.SM...  6.16 us
    pallas_call x1, Pallas kernels, text_product(): pl.pallas_call(text_kernel, grid=(columns // step,), in_specs=[pl.BlockSp...  6.04 us
  transfers between devices with their start and end apart: 40, of which 10 were waited for; matrix products, arithmetic and copies ran while one was open for 28% of the time, Pallas kernels for 10%

profile of v5, /device:TPU:0, one launch (start us, length us, event | category | flops | bytes accessed | tf_op | source)
XLA Modules:
  0.0 195.6 jit_solution(637455351551954933)
XLA Ops:
  7.2 2.7 %fusion.4 = bf16[96,2048]{1,0:T(8,128)(2,1)S(1)} fusion(bf16[192,2048]{1,0:T(8,128)(2,1)} %param.10, s32[]{:T(128)S(6)} %select_n.349), kind=kLoop, calls=%fused_computation.22 | loop fusion | flops 12976128 | bytes 786436 | tf_op jit(solution)/shard_map/convert_element_type | solution.py:293
  9.9 4.0 %collective-permute-start.2 = (bf16[96,2048]{1,0:T(8,128)(2,1)S(1)}, bf16[96,2048]{1,0:T(8,128)(2,1)}, u32[]{:S(2)}, u32[]{:S(2)}) collective-permute-start(bf16[96,2048]{1,0:T(8,128)(2,1)S(1)} %fusion.4), channel_id=1, source_target_pairs={{0,3},{1,2},{2,1},{3,0},{4,7},{5,6},{6,5},{7,4},{8,11},{9,10},{10,... | collective-permute-start | bytes 1179656 | tf_op jit(solution)/shard_map/ppermute | solution.py:17
  14.5 0.8 reduce-window.8
  15.3 1.3 fusion.45
  16.7 0.8 select_reduce_fusion.1
  17.8 5.6 %convolution_convert_fusion.2 = bf16[96,2048]{1,0:T(8,128)(2,1)} fusion(bf16[96,2048]{1,0:T(8,128)(2,1)S(1)} %fusion.4, bf16[2048,2048]{1,0:T(8,128)(2,1)} %param.11), kind=kOutput, calls=%fused_computation.5 | convolution fusion | flops 805502976 | bytes 9175040 | tf_op jit(solution)/shard_map/dot_general | solution.py:299
  23.4 1.2 slice-done.2
  25.0 0.7 copy.31
  25.7 1.6 dynamic-slice_bitcast_fusion.1
  27.4 2.0 %collective-permute-start.18 = (bf16[2,24,2048]{2,1,0:T(8,128)(2,1)}, bf16[2,24,2048]{2,1,0:T(8,128)(2,1)}, u32[]{:S(2)}, u32[]{:S(2)}) collective-permute-start(bf16[2,24,2048]{2,1,0:T(8,128)(2,1)} %dynamic-slice_bitcast_fusion.1), channel_id=1, source_target_pairs={{0,4},{4,0},{8,12},{12,8},{1,5},{5,1},{9,13},{13,9},{2,6},{6,2},{1... | collective-permute-start | bytes 589832 | tf_op jit(solution)/shard_map/ppermute | solution.py:17
  30.4 3.1 %multiply_reduce_fusion = f32[1024]{0:T(1024)S(1)} fusion(bf16[1024,2048]{1,0:T(8,128)(2,1)} %text_ref.1), kind=kLoop, calls=%fused_computation | loop fusion | flops 6290432 | bytes 4198400 | tf_op jit(solution)/shard_map/reduce_sum | solution.py:305
  33.5 1.1 constant_dynamic-slice_fusion.4
  34.6 1.8 constant_dynamic-slice_fusion.3.weight_ref
  37.0 1.0 convert_add_fusion.1
  38.0 0.7 dynamic-slice_convert_fusion.1
  38.7 3.0 %collective-permute-start.19 = (bf16[1,24,2048]{2,1,0:T(8,128)(2,1)}, bf16[1,24,2048]{2,1,0:T(8,128)(2,1)}, u32[]{:S(2)}, u32[]{:S(2)}) collective-permute-start(bf16[1,24,2048]{2,1,0:T(8,128)(2,1)} %dynamic-slice_convert_fusion.1), channel_id=1, source_target_pairs={{0,8},{4,12},{8,0},{12,4},{1,9},{5,13},{9,1},{13,5},{2,10},{6,14},... | collective-permute-start | bytes 294920 | tf_op jit(solution)/shard_map/ppermute | solution.py:17
  41.7 1.1 add.175
  42.9 2.8 %collective-permute-start.6 = (f32[1024]{0:T(1024)S(1)}, f32[1024]{0:T(1024)S(1)}, u32[]{:S(2)}, u32[]{:S(2)}) collective-permute-start(f32[1024]{0:T(1024)S(1)} %multiply_reduce_fusion), channel_id=1, source_target_pairs={{0,3},{1,2},{2,1},{3,0},{4,7},{5,6},{6,5},{7,4},{8,11},{9,10},{10,... | collective-permute-start | bytes 12296 | tf_op jit(solution)/shard_map/ppermute | solution.py:17
  46.4 1.3 pad_maximum_fusion.4
  47.8 5.4 %convolution_convert_fusion = bf16[192,2048]{1,0:T(8,128)(2,1)S(1)} fusion(bf16[192,2048]{1,0:T(8,128)(2,1)S(1)} %bitcast.111, bf16[2048,2048]{1,0:T(8,128)(2,1)} %param.11), kind=kOutput, calls=%fused_computation.3 | convolution fusion | flops 1611005952 | bytes 9961472 | tf_op jit(solution)/shard_map/dot_general | solution.py:299
  53.2 0.8 copy-done.13
  54.0 2.2 %select_bitcast_fusion.5 = (bf16[4,1,24,2048]{3,2,0,1:T(8,128)(2,1)S(1)}, bf16[4,1,24,2048]{3,2,0,1:T(8,128)(2,1)S(1)}, bf16[4,1,24,2048]{3,2,0,1:T(8,128)(2,1)}, bf16[4,1,24,2048]{3,2,0,1:T(8,128)(2,1)}) fusion(pred[]{:T(512)S(6)} %ne.59, bf16[4,24,2048]{2,1,0:T(8,128)(2,1)} %bitcast.3, bf16[4,24,2048]{2,1,0:T(8,128)(2,1)} %bitcast.2, pred[]{:T(512)S(6)} %ne.60, ...), kind=kLoop, calls=%fused_computation.71 | loop fusion | flops 1572864 | bytes 3145730 | tf_op jit(solution)/shard_map/stack | solution.py:368
  56.3 2.6 %convolution_convert_fusion.1 = bf16[96,2048]{1,0:T(8,128)(2,1)S(1)} fusion(bf16[96,2048]{1,0:T(8,128)(2,1)} %collective-permute-done, bf16[2048,2048]{1,0:T(8,128)(2,1)S(1)} %bitcast.104), kind=kOutput, calls=%fused_computation.4 | convolution fusion | flops 805502976 | bytes 9175040 | tf_op jit(solution)/shard_map/dot_general | solution.py:299
  59.0 1.9 collective-permute-start.16
  62.3 6.0 %shard_map.137 = (bf16[4,2048,128]{2,1,0:T(8,128)(2,1)}, f32[1,2048]{1,0:T(1,128)S(1)}) custom-call(bf16[1024,2048]{1,0:T(8,128)(2,1)S(1)} %copy-done, bf16[1024,512]{1,0:T(8,128)(2,1)S(1)} %multiply_convert_fusion.cot_ref, bf16[2048,512]{1,0:T(8,128)(2,1)S(1)} %constant_dynamic-slice_fusion.3.weight_ref), custom_call_target="tpu_custom_call" | custom-call | flops 2147483648 | bytes 9437184 | tf_op jit(solution)/shard_map/pallas_call | solution.py:119
  68.4 3.2 %collective-permute-done.8 = bf16[2,48,2048]{2,1,0:T(8,128)(2,1)S(1)} collective-permute-done((bf16[2,48,2048]{2,1,0:T(8,128)(2,1)S(1)}, bf16[2,48,2048]{2,1,0:T(8,128)(2,1)S(1)}, u32[]{:S(2)}, u32[]{:S(2)}) %collective-permute-start.8) | collective-permute-done | bytes 393248 | tf_op jit(solution)/shard_map/ppermute | solution.py:17
  71.6 0.7 copy-done.21
  72.4 1.2 convert_add_fusion
  73.6 2.7 %collective-permute-start.15 = (bf16[1,48,2048]{2,1,0:T(8,128)(2,1)S(1)}, bf16[1,48,2048]{2,1,0:T(8,128)(2,1)S(1)}, u32[]{:S(2)}, u32[]{:S(2)}) collective-permute-start(bf16[1,48,2048]{2,1,0:T(8,128)(2,1)S(1)} %dynamic-slice_convert_fusion), channel_id=1, source_target_pairs={{0,8},{4,12},{8,0},{12,4},{1,9},{5,13},{9,1},{13,5},{2,10},{6,14},... | collective-permute-start | bytes 589832 | tf_op jit(solution)/shard_map/ppermute | solution.py:17
  76.7 1.5 collective-permute-start.13
  78.2 8.1 %collective-permute-done.15 = bf16[1,48,2048]{2,1,0:T(8,128)(2,1)S(1)} collective-permute-done((bf16[1,48,2048]{2,1,0:T(8,128)(2,1)S(1)}, bf16[1,48,2048]{2,1,0:T(8,128)(2,1)S(1)}, u32[]{:S(2)}, u32[]{:S(2)}) %collective-permute-start.15) | collective-permute-done | bytes 196640 | tf_op jit(solution)/shard_map/ppermute | solution.py:17
  86.3 1.6 collective-permute-start.12
  88.0 1.5 collective-permute-start.11
  89.5 1.0 broadcast_select_fusion.25
  90.7 4.6 %collective-permute-done.12 = bf16[768,128]{1,0:T(8,128)(2,1)S(1)} collective-permute-done((bf16[768,128]{1,0:T(8,128)(2,1)S(1)}, bf16[768,128]{1,0:T(8,128)(2,1)S(1)}, u32[]{:S(2)}, u32[]{:S(2)}) %collective-permute-start.12) | collective-permute-done | bytes 196640 | tf_op jit(solution)/shard_map/ppermute | solution.py:17
  95.4 1.0 pad_maximum_fusion.5
  96.4 1.3 collective-permute-start.26
  97.7 5.3 %collective-permute-start.24 = (bf16[192,1024]{1,0:T(8,128)(2,1)S(1)}, bf16[192,1024]{1,0:T(8,128)(2,1)}, u32[]{:S(2)}, u32[]{:S(2)}) collective-permute-start(bf16[192,1024]{1,0:T(8,128)(2,1)S(1)} %pad_maximum_fusion.8.refs_5_), channel_id=1, source_target_pairs={{0,4},{4,8},{8,12},{1,5},{5,9},{9,13},{2,6},{6,10},{10,14},{3,7},{... | collective-permute-start | bytes 1179656 | tf_op jit(solution)/shard_map/ppermute | solution.py:73
  103.1 1.3 pad_maximum_fusion.3
  104.5 0.9 constant_dynamic-slice_fusion.1
  105.4 4.5 %collective-permute-done.26.refs_9_ = bf16[192,1024]{1,0:T(8,128)(2,1)} collective-permute-done((bf16[192,1024]{1,0:T(8,128)(2,1)S(1)}, bf16[192,1024]{1,0:T(8,128)(2,1)}, u32[]{:S(2)}, u32[]{:S(2)}) %collective-permute-start.26) | collective-permute-done | bytes 393248 | tf_op jit(solution)/shard_map/ppermute | solution.py:74
  110.0 1.3 collective-permute-start.27
  112.1 1.6 broadcast_select_fusion.1
  113.7 3.8 %fusion.36.grad_ref = f32[96,2048]{1,0:T(8,128)S(1)} fusion(bf16[2048,1024]{1,0:T(8,128)(2,1)} %param.15, s32[]{:T(128)S(6)} %select_n.407, bf16[768,512]{1,0:T(8,128)(2,1)S(1)} %get-tuple-element.71, bf16[768,512]{1,0:T(8,128)(2,1)S(1)} %get-tuple-element.72), kind=kOutput, calls=%fused_computation.77 | convolution fusion | flops 403046400 | bytes 6553604 | tf_op jit(solution)/shard_map/dot_general | solution.py:377
  117.7 2.2 %collective-permute-start.22 = (f32[2,128]{1,0:T(2,128)S(1)}, f32[2,128]{1,0:T(2,128)S(1)}, u32[]{:S(2)}, u32[]{:S(2)}) collective-permute-start(f32[2,128]{1,0:T(2,128)S(1)} %shard_map.138), channel_id=1, source_target_pairs={{0,3},{1,2},{2,1},{3,0},{4,7},{5,6},{6,5},{7,4},{8,11},{9,10},{10,... | collective-permute-start | bytes 3080 | tf_op jit(solution)/shard_map/ppermute | solution.py:17
  120.7 3.5 %fusion.refs_1_ = f32[768,1024]{1,0:T(8,128)} fusion(bf16[2048,1024]{1,0:T(8,128)(2,1)S(1)} %copy-done.3, s32[]{:T(128)S(6)} %select_n.387, bf16[768,512]{1,0:T(8,128)(2,1)S(1)} %get-tuple-element.72, bf16[768,512]{1,0:T(8,128)(2,1)S(1)} %get-tuple-element.71), kind=kOutput, calls=%fused_computation.6 | convolution fusion | flops 1613758464 | bytes 6815748 | tf_op jit(solution)/shard_map/dot_general | solution.py:360
  124.2 0.9 constant_dynamic-slice_fusion
  125.1 0.7 collective-permute-start.20
  125.8 0.8 pad_maximum_fusion.6.refs_3_
  126.6 2.1 %collective-permute-done.20 = f32[2,128]{1,0:T(2,128)S(1)} collective-permute-done((f32[2,128]{1,0:T(2,128)S(1)}, f32[2,128]{1,0:T(2,128)S(1)}, u32[]{:S(2)}, u32[]{:S(2)}) %collective-permute-start.20) | collective-permute-done | bytes 1056 | tf_op jit(solution)/shard_map/ppermute | solution.py:17
  128.8 16.8 %collective-permute-done.27.refs_10_ = bf16[192,1024]{1,0:T(8,128)(2,1)S(1)} collective-permute-done((bf16[192,1024]{1,0:T(8,128)(2,1)}, bf16[192,1024]{1,0:T(8,128)(2,1)S(1)}, u32[]{:S(2)}, u32[]{:S(2)}) %collective-permute-start.27) | collective-permute-done | bytes 393248 | tf_op jit(solution)/shard_map/ppermute | solution.py:74
  145.6 1.8 collective-permute-start.30
  147.4 4.6 %collective-permute-start.29 = (f32[2,128]{1,0:T(2,128)S(1)}, f32[2,128]{1,0:T(2,128)S(1)}, u32[]{:S(2)}, u32[]{:S(2)}) collective-permute-start(f32[2,128]{1,0:T(2,128)S(1)} %add_add_fusion.1), channel_id=1, source_target_pairs={{0,8},{4,12},{8,0},{12,4},{1,9},{5,13},{9,1},{13,5},{2,10},{6,14},... | collective-permute-start | bytes 3080 | tf_op jit(solution)/shard_map/ppermute | solution.py:17
  152.0 1.3 collective-permute-start.33
  154.0 1.7 select_bitcast_fusion.1
  155.7 1.6 collective-permute-done.28
  159.2 4.4 %collective-permute-done.33.refs_11_ = bf16[192,1024]{1,0:T(8,128)(2,1)S(1)} collective-permute-done((bf16[192,1024]{1,0:T(8,128)(2,1)S(1)}, bf16[192,1024]{1,0:T(8,128)(2,1)S(1)}, u32[]{:S(2)}, u32[]{:S(2)}) %collective-permute-start.33) | collective-permute-done | bytes 393248 | tf_op jit(solution)/shard_map/ppermute | solution.py:74
  163.6 0.8 copy-done.19
  164.5 6.2 %shard_map.139 = (bf16[768,1024]{1,0:T(8,128)(2,1)}, f32[1024,128]{1,0:T(8,128)}, bf16[1024,128]{1,0:T(8,128)(2,1)}, f32[2,1024]{1,0:T(2,128)}) custom-call(s32[1]{0:T(128)} %bitcast.12.refs_0_, f32[768,1024]{1,0:T(8,128)} %fusion.refs_1_, f32[1,1024]{1,0:T(1,128)} %bitcast.118, bf16[768,256]{1,0:T(8,128)(2,1)} %pad_maximum_fusion.6.refs_3_, ...), custom_call_target="tpu_custom_call" | custom-call | flops 402653184 | bytes 6291456 | tf_op jit(solution)/shard_map/pallas_call | solution.py:214
  170.7 3.2 %collective-permute-start.38 = (f32[3072]{0:T(1024)S(1)}, f32[3072]{0:T(1024)S(1)}, u32[]{:S(2)}, u32[]{:S(2)}) collective-permute-start(f32[3072]{0:T(1024)S(1)} %fusion.48), channel_id=1, source_target_pairs={{0,12},{4,8},{8,4},{12,0},{1,13},{5,9},{9,5},{13,1},{2,14},{6,10},... | collective-permute-start | bytes 36872 | tf_op jit(solution)/shard_map/ppermute | solution.py:17
  173.9 1.2 collective-permute-start.36
  175.6 1.4 copy-done.1
  177.0 7.4 %shard_map.140 = f32[16384,128]{1,0:T(8,128)} custom-call(bf16[768,2048]{1,0:T(8,128)(2,1)S(1)} %bitcast.99, bf16[768,1024]{1,0:T(8,128)(2,1)S(1)} %copy-done.1), custom_call_target="tpu_custom_call" | custom-call | flops 3221225472 | bytes 13107200 | tf_op jit(solution)/shard_map/pallas_call | solution.py:247
  186.4 2.4 %fusion.2 = f32[2048,128]{1,0:T(8,128)} fusion(f32[1024,128]{1,0:T(8,128)S(1)} %get-tuple-element.80, f32[1024,128]{1,0:T(8,128)S(1)} %get-tuple-element.79, bf16[1,2048,128]{2,1,0:T(8,128)(2,1)} %reduce-scatter.2.cloned.1.call-done, f32[2048]{0:T(1024)S(1)} %copy-done.2), kind=kLoop, calls=%fused_computation.18 | loop fusion | flops 1048576 | bytes 2629632 | tf_op jit(solution)/shard_map/mul | solution.py:404
  (148 shorter events, 12.4 us)
Async XLA Ops:
  7.2 179.2 %reduce-scatter.2.cloned.1.call-start = ((), (), s32[]{:S(2)}) async-start(), calls=%async_computation.1 | async-start | bytes 2621440 | tf_op jit(solution)/shard_map/reduce_scatter | solution.py:348
  9.9 32.9 %collective-permute-start.2 = (bf16[96,2048]{1,0:T(8,128)(2,1)S(1)}, bf16[96,2048]{1,0:T(8,128)(2,1)}, u32[]{:S(2)}, u32[]{:S(2)}) collective-permute-start(bf16[96,2048]{1,0:T(8,128)(2,1)S(1)} %fusion.4), channel_id=1, source_target_pairs={{0,3},{1,2},{2,1},{3,0},{4,7},{5,6},{6,5},{7,4},{8,11},{9,10},{10,... | collective-permute-start | bytes 1179656 | tf_op jit(solution)/shard_map/ppermute | solution.py:17
  13.9 29.0 %collective-permute-start.1 = (bf16[96,2048]{1,0:T(8,128)(2,1)S(1)}, bf16[96,2048]{1,0:T(8,128)(2,1)}, u32[]{:S(2)}, u32[]{:S(2)}) collective-permute-start(bf16[96,2048]{1,0:T(8,128)(2,1)S(1)} %fusion.4), channel_id=1, source_target_pairs={{0,2},{1,3},{2,0},{3,1},{4,6},{5,7},{6,4},{7,5},{8,10},{9,11},{10,... | collective-permute-start | bytes 1179656 | tf_op jit(solution)/shard_map/ppermute | solution.py:17
  14.4 28.5 %collective-permute-start = (bf16[96,2048]{1,0:T(8,128)(2,1)S(1)}, bf16[96,2048]{1,0:T(8,128)(2,1)}, u32[]{:S(2)}, u32[]{:S(2)}) collective-permute-start(bf16[96,2048]{1,0:T(8,128)(2,1)S(1)} %fusion.4), channel_id=1, source_target_pairs={{0,1},{1,0},{2,3},{3,2},{4,5},{5,4},{6,7},{7,6},{8,9},{9,8},{10,11... | collective-permute-start | bytes 1179656 | tf_op jit(solution)/shard_map/ppermute | solution.py:17
  23.4 1.2 slice-start.2
  23.4 5.9 %copy-start.4 = (bf16[1024,1024]{1,0:T(8,128)(2,1)S(1)}, bf16[1024,1024]{1,0:T(8,128)(2,1)}, u32[]{:S(2)}) copy-start(bf16[1024,1024]{1,0:T(8,128)(2,1)} %param.16) | copy-start | bytes 6291460
  27.4 9.6 %collective-permute-start.18 = (bf16[2,24,2048]{2,1,0:T(8,128)(2,1)}, bf16[2,24,2048]{2,1,0:T(8,128)(2,1)}, u32[]{:S(2)}, u32[]{:S(2)}) collective-permute-start(bf16[2,24,2048]{2,1,0:T(8,128)(2,1)} %dynamic-slice_bitcast_fusion.1), channel_id=1, source_target_pairs={{0,4},{4,0},{8,12},{12,8},{1,5},{5,1},{9,13},{13,9},{2,6},{6,2},{1... | collective-permute-start | bytes 589832 | tf_op jit(solution)/shard_map/ppermute | solution.py:17
  29.3 12.4 %collective-permute-start.9 = (bf16[768,128]{1,0:T(8,128)(2,1)}, bf16[768,128]{1,0:T(8,128)(2,1)}, u32[]{:S(2)}, u32[]{:S(2)}) collective-permute-start(bf16[768,128]{1,0:T(8,128)(2,1)} %bitcast.24), channel_id=1, source_target_pairs={{0,4},{4,0},{8,12},{12,8},{1,5},{5,1},{9,13},{13,9},{2,6},{6,2},{1... | collective-permute-start | bytes 589832 | tf_op jit(solution)/shard_map/ppermute | solution.py:17
  34.6 1.8 copy-start.2
  34.6 2.4 %copy-start.10 = (bf16[96,2048]{1,0:T(8,128)(2,1)S(1)}, bf16[96,2048]{1,0:T(8,128)(2,1)}, u32[]{:S(2)}) copy-start(bf16[96,2048]{1,0:T(8,128)(2,1)} %convolution_convert_fusion.2) | copy-start | bytes 1179652
  38.0 15.2 %copy-start.11 = (f32[2,24,2048]{2,1,0:T(8,128)}, f32[2,24,2048]{2,1,0:T(8,128)S(1)}, u32[]{:S(2)}) copy-start(f32[2,24,2048]{2,1,0:T(8,128)S(1)} %convert_add_fusion.1) | copy-start | bytes 1179652
  38.7 49.2 %collective-permute-start.19 = (bf16[1,24,2048]{2,1,0:T(8,128)(2,1)}, bf16[1,24,2048]{2,1,0:T(8,128)(2,1)}, u32[]{:S(2)}, u32[]{:S(2)}) collective-permute-start(bf16[1,24,2048]{2,1,0:T(8,128)(2,1)} %dynamic-slice_convert_fusion.1), channel_id=1, source_target_pairs={{0,8},{4,12},{8,0},{12,4},{1,9},{5,13},{9,1},{13,5},{2,10},{6,14},... | collective-permute-start | bytes 294920 | tf_op jit(solution)/shard_map/ppermute | solution.py:17
  42.8 16.2 %collective-permute-start.10 = (bf16[768,128]{1,0:T(8,128)(2,1)S(1)}, bf16[768,128]{1,0:T(8,128)(2,1)S(1)}, u32[]{:S(2)}, u32[]{:S(2)}) collective-permute-start(bf16[768,128]{1,0:T(8,128)(2,1)S(1)} %add.175), channel_id=1, source_target_pairs={{0,8},{4,12},{8,0},{12,4},{1,9},{5,13},{9,1},{13,5},{2,10},{6,14},... | collective-permute-start | bytes 589832 | tf_op jit(solution)/shard_map/ppermute | solution.py:17
  42.9 18.1 %collective-permute-start.6 = (f32[1024]{0:T(1024)S(1)}, f32[1024]{0:T(1024)S(1)}, u32[]{:S(2)}, u32[]{:S(2)}) collective-permute-start(f32[1024]{0:T(1024)S(1)} %multiply_reduce_fusion), channel_id=1, source_target_pairs={{0,3},{1,2},{2,1},{3,0},{4,7},{5,6},{6,5},{7,4},{8,11},{9,10},{10,... | collective-permute-start | bytes 12296 | tf_op jit(solution)/shard_map/ppermute | solution.py:17
  45.7 15.5 %collective-permute-start.5 = (f32[1024]{0:T(1024)S(1)}, f32[1024]{0:T(1024)S(1)}, u32[]{:S(2)}, u32[]{:S(2)}) collective-permute-start(f32[1024]{0:T(1024)S(1)} %multiply_reduce_fusion), channel_id=1, source_target_pairs={{0,2},{1,3},{2,0},{3,1},{4,6},{5,7},{6,4},{7,5},{8,10},{9,11},{10,... | collective-permute-start | bytes 12296 | tf_op jit(solution)/shard_map/ppermute | solution.py:17
  46.2 15.0 %collective-permute-start.4 = (f32[1024]{0:T(1024)S(1)}, f32[1024]{0:T(1024)S(1)}, u32[]{:S(2)}, u32[]{:S(2)}) collective-permute-start(f32[1024]{0:T(1024)S(1)} %multiply_reduce_fusion), channel_id=1, source_target_pairs={{0,1},{1,0},{2,3},{3,2},{4,5},{5,4},{6,7},{7,6},{8,9},{9,8},{10,11... | collective-permute-start | bytes 12296 | tf_op jit(solution)/shard_map/ppermute | solution.py:17
  46.4 9.9 %slice-start = ((s8[8388608]{0:T(1024)(128)(4,1)}), s8[4194304]{0:T(1024)(128)(4,1)S(1)}, s32[]{:S(2)}) async-start(s8[8388608]{0:T(1024)(128)(4,1)} %bitcast.103), calls=%async_computation.2 | async-start | bytes 8388608
  47.8 8.5 %slice-start.1 = ((s8[8388608]{0:T(1024)(128)(4,1)}), s8[4194304]{0:T(1024)(128)(4,1)S(1)}, s32[]{:S(2)}) async-start(s8[8388608]{0:T(1024)(128)(4,1)} %bitcast.103), calls=%async_computation.3 | async-start | bytes 8388608
  56.3 5.6 %copy-start.5 = (bf16[1024,512]{1,0:T(8,128)(2,1)S(1)}, bf16[1024,512]{1,0:T(8,128)(2,1)}, u32[]{:S(2)}) copy-start(bf16[1024,512]{1,0:T(8,128)(2,1)} %constant_dynamic-slice_fusion.4) | copy-start | bytes 3145732
  56.3 6.0 %copy-start = (bf16[1024,2048]{1,0:T(8,128)(2,1)S(1)}, bf16[1024,2048]{1,0:T(8,128)(2,1)}, u32[]{:S(2)}) copy-start(bf16[1024,2048]{1,0:T(8,128)(2,1)} %text_ref.1) | copy-start | bytes 12582916
  59.0 9.3 %collective-permute-start.16 = (bf16[2,24,2048]{2,1,0:T(8,128)(2,1)S(1)}, bf16[2,24,2048]{2,1,0:T(8,128)(2,1)S(1)}, u32[]{:S(2)}, u32[]{:S(2)}) collective-permute-start(bf16[2,24,2048]{2,1,0:T(8,128)(2,1)S(1)} %dynamic-slice_bitcast_fusion.2), channel_id=1, source_target_pairs={{0,4},{4,0},{8,12},{12,8},{1,5},{5,1},{9,13},{13,9},{2,6},{6,2},{1... | collective-permute-start | bytes 589832 | tf_op jit(solution)/shard_map/ppermute | solution.py:17
  61.0 27.0 %copy-start.14 = (bf16[768,128]{1,0:T(8,128)(2,1)}, bf16[768,128]{1,0:T(8,128)(2,1)S(1)}, u32[]{:S(2)}) copy-start(bf16[768,128]{1,0:T(8,128)(2,1)S(1)} %add.176) | copy-start | bytes 589828
  61.0 10.6 %collective-permute-start.8 = (bf16[2,48,2048]{2,1,0:T(8,128)(2,1)S(1)}, bf16[2,48,2048]{2,1,0:T(8,128)(2,1)S(1)}, u32[]{:S(2)}, u32[]{:S(2)}) collective-permute-start(bf16[2,48,2048]{2,1,0:T(8,128)(2,1)S(1)} %dynamic-slice_bitcast_fusion), channel_id=1, source_target_pairs={{0,4},{4,0},{8,12},{12,8},{1,5},{5,1},{9,13},{13,9},{2,6},{6,2},{1... | collective-permute-start | bytes 1179656 | tf_op jit(solution)/shard_map/ppermute | solution.py:17
  68.3 19.6 %copy-start.22 = (f32[2048]{0:T(1024)S(1)}, f32[2048]{0:T(1024)}, u32[]{:S(2)}) copy-start(f32[2048]{0:T(1024)} %param.12) | copy-start | bytes 24580
  68.3 36.1 %collective-permute-start.7 = (f32[3072]{0:T(1024)S(1)}, f32[3072]{0:T(1024)S(1)}, u32[]{:S(2)}, u32[]{:S(2)}) collective-permute-start(f32[3072]{0:T(1024)S(1)} %pad_maximum_fusion.9), channel_id=1, source_target_pairs={{0,16},{16,0},{1,17},{17,1},{2,18},{18,2},{3,19},{19,3},{4,20},{20... | collective-permute-start | bytes 36872 | tf_op jit(solution)/shard_map/ppermute | solution.py:17
  68.4 21.1 %copy-start.12 = (f32[2,24,2048]{2,1,0:T(8,128)S(1)}, f32[2,24,2048]{2,1,0:T(8,128)}, u32[]{:S(2)}) copy-start(f32[2,24,2048]{2,1,0:T(8,128)} %copy-done.11) | copy-start | bytes 1179652
  73.6 12.7 %collective-permute-start.15 = (bf16[1,48,2048]{2,1,0:T(8,128)(2,1)S(1)}, bf16[1,48,2048]{2,1,0:T(8,128)(2,1)S(1)}, u32[]{:S(2)}, u32[]{:S(2)}) collective-permute-start(bf16[1,48,2048]{2,1,0:T(8,128)(2,1)S(1)} %dynamic-slice_convert_fusion), channel_id=1, source_target_pairs={{0,8},{4,12},{8,0},{12,4},{1,9},{5,13},{9,1},{13,5},{2,10},{6,14},... | collective-permute-start | bytes 589832 | tf_op jit(solution)/shard_map/ppermute | solution.py:17
  76.3 13.2 %collective-permute-start.17 = (bf16[1,24,2048]{2,1,0:T(8,128)(2,1)S(1)}, bf16[1,24,2048]{2,1,0:T(8,128)(2,1)S(1)}, u32[]{:S(2)}, u32[]{:S(2)}) collective-permute-start(bf16[1,24,2048]{2,1,0:T(8,128)(2,1)S(1)} %dynamic-slice_convert_fusion.2), channel_id=1, source_target_pairs={{0,8},{4,12},{8,0},{12,4},{1,9},{5,13},{9,1},{13,5},{2,10},{6,14},... | collective-permute-start | bytes 294920 | tf_op jit(solution)/shard_map/ppermute | solution.py:17
  76.7 14.0 %collective-permute-start.13 = (bf16[768,128]{1,0:T(8,128)(2,1)S(1)}, bf16[768,128]{1,0:T(8,128)(2,1)S(1)}, u32[]{:S(2)}, u32[]{:S(2)}) collective-permute-start(bf16[768,128]{1,0:T(8,128)(2,1)S(1)} %add.176), channel_id=1, source_target_pairs={{0,1},{1,0},{2,3},{3,2},{4,5},{5,4},{6,7},{7,6},{8,9},{9,8},{10,11... | collective-permute-start | bytes 589832 | tf_op jit(solution)/shard_map/ppermute | solution.py:17
  86.3 9.0 %collective-permute-start.12 = (bf16[768,128]{1,0:T(8,128)(2,1)S(1)}, bf16[768,128]{1,0:T(8,128)(2,1)S(1)}, u32[]{:S(2)}, u32[]{:S(2)}) collective-permute-start(bf16[768,128]{1,0:T(8,128)(2,1)S(1)} %add.176), channel_id=1, source_target_pairs={{0,2},{1,3},{2,0},{3,1},{4,6},{5,7},{6,4},{7,5},{8,10},{9,11},{10,... | collective-permute-start | bytes 589832 | tf_op jit(solution)/shard_map/ppermute | solution.py:17
  88.0 7.3 %collective-permute-start.11 = (bf16[768,128]{1,0:T(8,128)(2,1)S(1)}, bf16[768,128]{1,0:T(8,128)(2,1)S(1)}, u32[]{:S(2)}, u32[]{:S(2)}) collective-permute-start(bf16[768,128]{1,0:T(8,128)(2,1)S(1)} %add.176), channel_id=1, source_target_pairs={{0,3},{1,2},{2,1},{3,0},{4,7},{5,6},{6,5},{7,4},{8,11},{9,10},{10,... | collective-permute-start | bytes 589832 | tf_op jit(solution)/shard_map/ppermute | solution.py:17
  89.4 5.8 %copy-start.15 = (bf16[768,128]{1,0:T(8,128)(2,1)S(1)}, bf16[768,128]{1,0:T(8,128)(2,1)}, u32[]{:S(2)}) copy-start(bf16[768,128]{1,0:T(8,128)(2,1)} %copy-done.14) | copy-start | bytes 589828
  90.6 5.8 %collective-permute-start.23 = (bf16[96,1024]{1,0:T(8,128)(2,1)S(1)}, bf16[96,1024]{1,0:T(8,128)(2,1)S(1)}, u32[]{:S(2)}, u32[]{:S(2)}) collective-permute-start(bf16[96,1024]{1,0:T(8,128)(2,1)S(1)} %broadcast_select_fusion.7), channel_id=1, source_target_pairs={{0,16},{16,0},{1,17},{17,1},{2,18},{18,2},{3,19},{19,3},{4,20},{20... | collective-permute-start | bytes 589832 | tf_op jit(solution)/shard_map/ppermute | solution.py:17
  95.3 1.1 copy-start.8
  95.4 7.7 %copy-start.6 = (bf16[4,1,24,2048]{3,2,0,1:T(8,128)(2,1)S(1)}, bf16[4,1,24,2048]{3,2,0,1:T(8,128)(2,1)}, u32[]{:S(2)}) copy-start(bf16[4,1,24,2048]{3,2,0,1:T(8,128)(2,1)} %get-tuple-element.75) | copy-start | bytes 1179652
  95.4 7.7 %copy-start.7 = (bf16[4,1,24,2048]{3,2,0,1:T(8,128)(2,1)S(1)}, bf16[4,1,24,2048]{3,2,0,1:T(8,128)(2,1)}, u32[]{:S(2)}) copy-start(bf16[4,1,24,2048]{3,2,0,1:T(8,128)(2,1)} %get-tuple-element.76) | copy-start | bytes 1179652
  96.3 15.7 %collective-permute-start.14 = (bf16[768,512]{1,0:T(8,128)(2,1)}, bf16[768,512]{1,0:T(8,128)(2,1)}, u32[]{:S(2)}, u32[]{:S(2)}) collective-permute-start(bf16[768,512]{1,0:T(8,128)(2,1)} %pad_maximum_fusion.5), channel_id=1, source_target_pairs={{0,16},{16,0},{1,17},{17,1},{2,18},{18,2},{3,19},{19,3},{4,20},{20... | collective-permute-start | bytes 2359304 | tf_op jit(solution)/shard_map/ppermute | solution.py:17
  96.4 8.0 %copy-start.9 = (bf16[192,1024]{1,0:T(8,128)(2,1)}, bf16[192,1024]{1,0:T(8,128)(2,1)S(1)}, u32[]{:S(2)}) copy-start(bf16[192,1024]{1,0:T(8,128)(2,1)S(1)} %pad_maximum_fusion.8.refs_5_) | copy-start | bytes 1179652
  96.4 13.5 %collective-permute-start.26 = (bf16[192,1024]{1,0:T(8,128)(2,1)S(1)}, bf16[192,1024]{1,0:T(8,128)(2,1)}, u32[]{:S(2)}, u32[]{:S(2)}) collective-permute-start(bf16[192,1024]{1,0:T(8,128)(2,1)S(1)} %pad_maximum_fusion.8.refs_5_), channel_id=1, source_target_pairs={{4,0},{8,4},{12,8},{5,1},{9,5},{13,9},{6,2},{10,6},{14,10},{7,3},{... | collective-permute-start | bytes 1179656 | tf_op jit(solution)/shard_map/ppermute | solution.py:74
  97.7 13.6 %collective-permute-start.24 = (bf16[192,1024]{1,0:T(8,128)(2,1)S(1)}, bf16[192,1024]{1,0:T(8,128)(2,1)}, u32[]{:S(2)}, u32[]{:S(2)}) collective-permute-start(bf16[192,1024]{1,0:T(8,128)(2,1)S(1)} %pad_maximum_fusion.8.refs_5_), channel_id=1, source_target_pairs={{0,4},{4,8},{8,12},{1,5},{5,9},{9,13},{2,6},{6,10},{10,14},{3,7},{... | collective-permute-start | bytes 1179656 | tf_op jit(solution)/shard_map/ppermute | solution.py:73
  104.4 48.8 %collective-permute-start.3 = (bf16[4,4,24,2048]{3,2,0,1:T(8,128)(2,1)}, bf16[4,4,24,2048]{3,2,0,1:T(8,128)(2,1)}, u32[]{:S(2)}, u32[]{:S(2)}) collective-permute-start(bf16[4,4,24,2048]{3,2,0,1:T(8,128)(2,1)} %pad_maximum_fusion.3), channel_id=1, source_target_pairs={{0,16},{16,0},{1,17},{17,1},{2,18},{18,2},{3,19},{19,3},{4,20},{20... | collective-permute-start | bytes 4718600 | tf_op jit(solution)/shard_map/ppermute | solution.py:17
  110.0 35.6 %collective-permute-start.27 = (bf16[192,1024]{1,0:T(8,128)(2,1)}, bf16[192,1024]{1,0:T(8,128)(2,1)S(1)}, u32[]{:S(2)}, u32[]{:S(2)}) collective-permute-start(bf16[192,1024]{1,0:T(8,128)(2,1)} %collective-permute-done.26.refs_9_), channel_id=1, source_target_pairs={{4,0},{8,4},{5,1},{9,5},{6,2},{10,6},{7,3},{11,7},{20,16},{24,20},... | collective-permute-start | bytes 1179656 | tf_op jit(solution)/shard_map/ppermute | solution.py:74
  111.4 34.2 %collective-permute-start.25 = (bf16[192,1024]{1,0:T(8,128)(2,1)}, bf16[192,1024]{1,0:T(8,128)(2,1)S(1)}, u32[]{:S(2)}, u32[]{:S(2)}) collective-permute-start(bf16[192,1024]{1,0:T(8,128)(2,1)} %collective-permute-done.24.refs_6_), channel_id=1, source_target_pairs={{4,8},{8,12},{5,9},{9,13},{6,10},{10,14},{7,11},{11,15},{20,24},{2... | collective-permute-start | bytes 1179656 | tf_op jit(solution)/shard_map/ppermute | solution.py:73
  113.7 7.0 %copy-start.3 = (bf16[2048,1024]{1,0:T(8,128)(2,1)S(1)}, bf16[2048,1024]{1,0:T(8,128)(2,1)}, u32[]{:S(2)}) copy-start(bf16[2048,1024]{1,0:T(8,128)(2,1)} %param.15) | copy-start | bytes 12582916
  117.7 7.4 %collective-permute-start.22 = (f32[2,128]{1,0:T(2,128)S(1)}, f32[2,128]{1,0:T(2,128)S(1)}, u32[]{:S(2)}, u32[]{:S(2)}) collective-permute-start(f32[2,128]{1,0:T(2,128)S(1)} %shard_map.138), channel_id=1, source_target_pairs={{0,3},{1,2},{2,1},{3,0},{4,7},{5,6},{6,5},{7,4},{8,11},{9,10},{10,... | collective-permute-start | bytes 3080 | tf_op jit(solution)/shard_map/ppermute | solution.py:17
  120.0 6.6 %collective-permute-start.21 = (f32[2,128]{1,0:T(2,128)S(1)}, f32[2,128]{1,0:T(2,128)S(1)}, u32[]{:S(2)}, u32[]{:S(2)}) collective-permute-start(f32[2,128]{1,0:T(2,128)S(1)} %shard_map.138), channel_id=1, source_target_pairs={{0,2},{1,3},{2,0},{3,1},{4,6},{5,7},{6,4},{7,5},{8,10},{9,11},{10,... | collective-permute-start | bytes 3080 | tf_op jit(solution)/shard_map/ppermute | solution.py:17
  125.1 3.6 %collective-permute-start.20 = (f32[2,128]{1,0:T(2,128)S(1)}, f32[2,128]{1,0:T(2,128)S(1)}, u32[]{:S(2)}, u32[]{:S(2)}) collective-permute-start(f32[2,128]{1,0:T(2,128)S(1)} %shard_map.138), channel_id=1, source_target_pairs={{0,1},{1,0},{2,3},{3,2},{4,5},{5,4},{6,7},{7,6},{8,9},{9,8},{10,11... | collective-permute-start | bytes 3080 | tf_op jit(solution)/shard_map/ppermute | solution.py:17
  145.6 10.1 %copy-start.17 = (bf16[192,1024]{1,0:T(8,128)(2,1)}, bf16[192,1024]{1,0:T(8,128)(2,1)S(1)}, u32[]{:S(2)}) copy-start(bf16[192,1024]{1,0:T(8,128)(2,1)S(1)} %collective-permute-done.27.refs_10_) | copy-start | bytes 1179652
  145.6 10.1 %copy-start.18 = (bf16[192,1024]{1,0:T(8,128)(2,1)}, bf16[192,1024]{1,0:T(8,128)(2,1)S(1)}, u32[]{:S(2)}) copy-start(bf16[192,1024]{1,0:T(8,128)(2,1)S(1)} %collective-permute-done.25.refs_7_) | copy-start | bytes 1179652
  145.6 10.1 %collective-permute-start.30 = (f32[2,128]{1,0:T(2,128)S(1)}, f32[2,128]{1,0:T(2,128)S(1)}, u32[]{:S(2)}, u32[]{:S(2)}) collective-permute-start(f32[2,128]{1,0:T(2,128)S(1)} %add_add_fusion.1), channel_id=1, source_target_pairs={{0,4},{4,0},{8,12},{12,8},{1,5},{5,1},{9,13},{13,9},{2,6},{6,2},{1... | collective-permute-start | bytes 3080 | tf_op jit(solution)/shard_map/ppermute | solution.py:17
  147.4 8.3 %collective-permute-start.29 = (f32[2,128]{1,0:T(2,128)S(1)}, f32[2,128]{1,0:T(2,128)S(1)}, u32[]{:S(2)}, u32[]{:S(2)}) collective-permute-start(f32[2,128]{1,0:T(2,128)S(1)} %add_add_fusion.1), channel_id=1, source_target_pairs={{0,8},{4,12},{8,0},{12,4},{1,9},{5,13},{9,1},{13,5},{2,10},{6,14},... | collective-permute-start | bytes 3080 | tf_op jit(solution)/shard_map/ppermute | solution.py:17
  152.0 5.4 %collective-permute-start.28 = (f32[2,128]{1,0:T(2,128)S(1)}, f32[2,128]{1,0:T(2,128)S(1)}, u32[]{:S(2)}, u32[]{:S(2)}) collective-permute-start(f32[2,128]{1,0:T(2,128)S(1)} %add_add_fusion.1), channel_id=1, source_target_pairs={{0,12},{4,8},{8,4},{12,0},{1,13},{5,9},{9,5},{13,1},{2,14},{6,10},... | collective-permute-start | bytes 3080 | tf_op jit(solution)/shard_map/ppermute | solution.py:17
  152.0 11.6 %collective-permute-start.33 = (bf16[192,1024]{1,0:T(8,128)(2,1)S(1)}, bf16[192,1024]{1,0:T(8,128)(2,1)S(1)}, u32[]{:S(2)}, u32[]{:S(2)}) collective-permute-start(bf16[192,1024]{1,0:T(8,128)(2,1)S(1)} %collective-permute-done.27.refs_10_), channel_id=1, source_target_pairs={{4,0},{5,1},{6,2},{7,3},{20,16},{21,17},{22,18},{23,19}} | collective-permute-start | bytes 1179656 | tf_op jit(solution)/shard_map/ppermute | solution.py:74
  153.3 10.3 %collective-permute-start.32 = (bf16[192,1024]{1,0:T(8,128)(2,1)S(1)}, bf16[192,1024]{1,0:T(8,128)(2,1)S(1)}, u32[]{:S(2)}, u32[]{:S(2)}) collective-permute-start(bf16[192,1024]{1,0:T(8,128)(2,1)S(1)} %collective-permute-done.25.refs_7_), channel_id=1, source_target_pairs={{8,12},{9,13},{10,14},{11,15},{24,28},{25,29},{26,30},{27,31}} | collective-permute-start | bytes 1179656 | tf_op jit(solution)/shard_map/ppermute | solution.py:73
  157.4 1.2 collective-permute-start.31
  163.6 0.9 copy-start.20
  170.7 14.3 %collective-permute-start.38 = (f32[3072]{0:T(1024)S(1)}, f32[3072]{0:T(1024)S(1)}, u32[]{:S(2)}, u32[]{:S(2)}) collective-permute-start(f32[3072]{0:T(1024)S(1)} %fusion.48), channel_id=1, source_target_pairs={{0,12},{4,8},{8,4},{12,0},{1,13},{5,9},{9,5},{13,1},{2,14},{6,10},... | collective-permute-start | bytes 36872 | tf_op jit(solution)/shard_map/ppermute | solution.py:17
  173.9 11.1 %collective-permute-start.37 = (f32[3072]{0:T(1024)S(1)}, f32[3072]{0:T(1024)S(1)}, u32[]{:S(2)}, u32[]{:S(2)}) collective-permute-start(f32[3072]{0:T(1024)S(1)} %fusion.48), channel_id=1, source_target_pairs={{0,8},{4,12},{8,0},{12,4},{1,9},{5,13},{9,1},{13,5},{2,10},{6,14},... | collective-permute-start | bytes 36872 | tf_op jit(solution)/shard_map/ppermute | solution.py:17
  173.9 11.1 %collective-permute-start.36 = (f32[3072]{0:T(1024)S(1)}, f32[3072]{0:T(1024)S(1)}, u32[]{:S(2)}, u32[]{:S(2)}) collective-permute-start(f32[3072]{0:T(1024)S(1)} %fusion.48), channel_id=1, source_target_pairs={{0,4},{4,0},{8,12},{12,8},{1,5},{5,1},{9,13},{13,9},{2,6},{6,2},{1... | collective-permute-start | bytes 36872 | tf_op jit(solution)/shard_map/ppermute | solution.py:17
  175.1 9.3 %collective-permute-start.34 = (f32[2,1024]{1,0:T(2,128)}, f32[2,1024]{1,0:T(2,128)S(1)}, u32[]{:S(2)}, u32[]{:S(2)}) collective-permute-start(f32[2,1024]{1,0:T(2,128)} %get-tuple-element.42), channel_id=1, source_target_pairs={{0,16},{16,0},{1,17},{17,1},{2,18},{18,2},{3,19},{19,3},{4,20},{20... | collective-permute-start | bytes 24584 | tf_op jit(solution)/shard_map/ppermute | solution.py:17
  175.1 11.2 %collective-permute-start.35 = (bf16[1024,128]{1,0:T(8,128)(2,1)}, bf16[1024,128]{1,0:T(8,128)(2,1)S(1)}, u32[]{:S(2)}, u32[]{:S(2)}) collective-permute-start(bf16[1024,128]{1,0:T(8,128)(2,1)} %get-tuple-element.44), channel_id=1, source_target_pairs={{0,16},{16,0},{1,17},{17,1},{2,18},{18,2},{3,19},{19,3},{4,20},{20... | collective-permute-start | bytes 786440 | tf_op jit(solution)/shard_map/ppermute | solution.py:17
  175.6 1.4 copy-start.1
  177.0 7.4 %copy-start.23 = (f32[2,1024]{1,0:T(2,128)S(1)}, f32[2,1024]{1,0:T(2,128)}, u32[]{:S(2)}) copy-start(f32[2,1024]{1,0:T(2,128)} %get-tuple-element.42) | copy-start | bytes 24580
  177.0 9.2 %copy-start.16 = (f32[1024,128]{1,0:T(8,128)S(1)}, f32[1024,128]{1,0:T(8,128)}, u32[]{:S(2)}) copy-start(f32[1024,128]{1,0:T(8,128)} %get-tuple-element.45) | copy-start | bytes 1572868
  (3 other events, 2.4 us)
Sparse Core Ops, SparseCore 0:
  104.6 52.5 reduce-scatter.1

commit v6 on v4

--- a/solution.py
+++ b/solution.py
@@ -41,6 +41,10 @@
         pieces = [jnp.where(odd, pieces[m ^ mask], pieces[m]) for m in range(len(pieces))]
         mask *= 2
     return pieces
+
+
+def together(*values):
+    return lax.optimization_barrier(values)
 
 
 def reduce_to_owner(parts, axis):
@@ -58,18 +62,6 @@
     return parts[0]
 
 
-def along_line(x, axis):
-    count = lax.axis_size(axis)
-    up, down = [], []
-    right = left = x
-    for i in range(1, count):
-        right = lax.ppermute(right, axis, [(j, j + 1) for j in range(i - 1, count - 1)])
-        left = lax.ppermute(left, axis, [(j, j - 1) for j in range(1, count - i + 1)])
-        up.append(right)
-        down.append(left)
-    return up, down
-
-
 def columns_of(row, count):
     parts = []
     for i in range(count // LANES):
@@ -93,6 +85,52 @@
     for i in range(1, width // LANES):
         out = out + values[:, i * LANES : (i + 1) * LANES]
     return out
+
+
+def project_kernel(*refs):
+    index_ref, weight_ref = refs[:2]
+    partial_ref, act_ref = refs[-2:]
+    pieces = refs[2:-2]
+    rows = pieces[0].shape[0]
+
+    @pl.when(pl.program_id(0) == 0)
+    def _():
+        for m, piece in enumerate(pieces):
+            at = jnp.bitwise_xor(index_ref[0], m) * rows
+            act_ref[pl.ds(pl.multiple_of(at, rows), rows), :] = piece[...]
+
+    product = jnp.dot(act_ref[...], weight_ref[...], preferred_element_type=jnp.float32)
+    partial_ref[...] = product.astype(jnp.bfloat16)
+
+
+def project(index, pieces, weight):
+    rows, features = pieces[0].shape
+    columns = weight.shape[1]
+    total_rows = rows * len(pieces)
+    step = 512
+    return pl.pallas_call(
+        project_kernel,
+        grid=(columns // step,),
+        in_specs=[
+            pl.BlockSpec(memory_space=pltpu.SMEM),
+            pl.BlockSpec((features, step), lambda i: (0, i)),
+        ]
+        + [pl.BlockSpec((rows, features), lambda i: (0, 0))] * len(pieces),
+        out_specs=[
+            pl.BlockSpec((total_rows, step), lambda i: (0, i)),
+            pl.BlockSpec((total_rows, features), lambda i: (0, 0)),
+        ],
+        out_shape=[
+            jax.ShapeDtypeStruct((total_rows, columns), jnp.bfloat16),
+            jax.ShapeDtypeStruct((total_rows, features), jnp.bfloat16),
+        ],
+        compiler_params=pltpu.CompilerParams(vmem_limit_bytes=40 * 1024 * 1024),
+        cost_estimate=pl.CostEstimate(
+            flops=2 * total_rows * features * columns,
+            bytes_accessed=2 * (features * columns + total_rows * (columns + 2 * features)),
+            transcendentals=0,
+        ),
+    )(index, weight, *pieces)
 
 
 def text_kernel(text_ref, cot_ref, weight_ref, moment_ref, gain_ref):
@@ -158,39 +196,36 @@
     )(rows, grad, gain)
 
 
-def image_kernel(*refs):
-    order_ref, grad_ref, gain_ref, cot_ref, sums_ref, own_ref = refs[:6]
-    embed_ref, here_ref, there_ref, small_ref, rows_ref = refs[-5:]
-    others = refs[6:-5]
-    count = len(others) // 2
-    rows = own_ref.shape[0]
-    stream, width = embed_ref.shape
-    for i in range(count + 1):
-        at = lax.rem(order_ref[0] + count + 1 - i, count + 1) * rows
-        if i == 0:
-            piece = own_ref[...]
-        else:
-            piece = others[i - 1][...] + others[2 * count - i][...]
-        rows_ref[pl.ds(pl.multiple_of(at, rows), rows), :] = piece
+def image_kernel(core_ref, grad_ref, gain_ref, cot_ref, sums_ref, rows_ref, *out):
+    embed_ref, here_ref, there_ref, small_ref = out
+    stream, width = rows_ref.shape
     groups = sums_ref.shape[0]
+    size = stream // groups
     inv, mean = [], []
     for i in range(groups):
         inv_row = lax.rsqrt(sums_ref[i, 0:1, :] / D + EPSILON)
         mean_row = inv_row * inv_row * inv_row * sums_ref[i, 1:2, :] / D
-        inv.append(columns_of(inv_row, inv_row.shape[1])[: stream // groups])
-        mean.append(columns_of(mean_row, mean_row.shape[1])[: stream // groups])
-    inv = jnp.concatenate(inv, 0)
-    mean = jnp.concatenate(mean, 0)
-    for i in range(width // LANES):
-        at = slice(i * LANES, (i + 1) * LANES)
-        values = rows_ref[:, at].astype(jnp.float32)
-        scaled = grad_ref[:, at] * inv
-        embed = (scaled * gain_ref[:, at] - values * mean).astype(jnp.bfloat16)
-        embed_ref[:, at] = embed
-        small_ref[0:1, at] = jnp.sum(scaled * values, 0, keepdims=True)
-        small_ref[1:2, at] = jnp.sum(embed.astype(jnp.float32), 0, keepdims=True)
+        inv.append(columns_of(inv_row, inv_row.shape[1])[:size])
+        mean.append(columns_of(mean_row, mean_row.shape[1])[:size])
+    all_inv = jnp.concatenate(inv, 0)
+    gain_parts = [jnp.zeros((1, LANES), jnp.float32)] * (width // LANES)
+    bias_parts = list(gain_parts)
+    for g in range(groups):
+        rows = slice(g * size, (g + 1) * size)
+        to_rows = slice((g // 2) * size, (g // 2 + 1) * size)
+        side = jnp.bitwise_xor(core_ref[0], g % 2)
+        for i in range(width // LANES):
+            at = slice(i * LANES, (i + 1) * LANES)
+            values = rows_ref[rows, at].astype(jnp.float32)
+            scaled = grad_ref[rows, at] * inv[g]
+            embed = (scaled * gain_ref[:, at] - values * mean[g]).astype(jnp.bfloat16)
+            embed_ref[side, to_rows, at] = embed
+            gain_parts[i] = gain_parts[i] + jnp.sum(scaled * values, 0, keepdims=True)
+            bias_parts[i] = bias_parts[i] + jnp.sum(embed.astype(jnp.float32), 0, keepdims=True)
+    small_ref[0:1, :] = jnp.concatenate(gain_parts, 1)
+    small_ref[1:2, :] = jnp.concatenate(bias_parts, 1)
     lanes = cot_ref.shape[1]
-    wide = [inv] * (lanes // LANES) if lanes >= LANES else [inv[:, :lanes]]
+    wide = [all_inv] * (lanes // LANES) if lanes >= LANES else [all_inv[:, :lanes]]
     cot = (cot_ref[...].astype(jnp.float32) * jnp.concatenate(wide, 1)).astype(jnp.bfloat16)
     moment = lax.dot_general(
         rows_ref[...], cot, (((0,), (0,)), ((), ())), preferred_element_type=jnp.float32
@@ -200,41 +235,43 @@
     there_ref[...] = moment[:, share:].astype(jnp.bfloat16)
 
 
-def image_grads(z, grad, gain, cot, sums, own, others):
+def image_grads(core, grad, gain, cot, sums, rows):
     stream, width = grad.shape
     share = cot.shape[1] // 2
     whole = pl.BlockSpec(memory_space=pltpu.VMEM)
     return pl.pallas_call(
         image_kernel,
-        in_specs=[pl.BlockSpec(memory_space=pltpu.SMEM)] + [whole] * (5 + len(others)),
+        in_specs=[pl.BlockSpec(memory_space=pltpu.SMEM)] + [whole] * 5,
         out_specs=[whole] * 4,
         out_shape=[
-            jax.ShapeDtypeStruct((stream, width), jnp.bfloat16),
+            jax.ShapeDtypeStruct((2, stream // 2, width), jnp.bfloat16),
             jax.ShapeDtypeStruct((width, share), jnp.float32),
             jax.ShapeDtypeStruct((width, share), jnp.bfloat16),
             jax.ShapeDtypeStruct((2, width), jnp.float32),
         ],
-        scratch_shapes=[pltpu.VMEM((stream, width), jnp.bfloat16)],
         compiler_params=pltpu.CompilerParams(vmem_limit_bytes=56 * 1024 * 1024),
         cost_estimate=pl.CostEstimate(
             flops=4 * stream * width * share, bytes_accessed=8 * stream * width, transcendentals=0
         ),
-    )(z, grad, gain, cot, sums, own, *others)
-
-
-def weight_kernel(act_ref, grad_ref, out_ref):
-    step = act_ref.shape[1]
-    groups = grad_ref.shape[1] // LANES
+    )(core, grad, gain, cot, sums, rows)
+
+
+def weight_kernel(mine_ref, other_ref, grad_ref, out_ref):
+    step = mine_ref.shape[1]
+    groups = grad_ref.shape[2] // LANES
+    rows_first = (((0,), (0,)), ((), ()))
     product = lax.dot_general(
-        act_ref[...], grad_ref[...], (((0,), (0,)), ((), ())), preferred_element_type=jnp.float32
+        mine_ref[...], grad_ref[0], rows_first, preferred_element_type=jnp.float32
+    ) + lax.dot_general(
+        other_ref[...], grad_ref[1], rows_first, preferred_element_type=jnp.float32
     )
     for c in range(groups):
         out_ref[pl.ds(c, step, stride=groups), :] = product[:, c * LANES : (c + 1) * LANES]
 
 
-def weight_product(act, grad):
-    rows, features = act.shape
-    width = grad.shape[1]
+def weight_product(mine, other, grad):
+    rows, features = mine.shape
+    width = grad.shape[2]
     groups = width // LANES
     step = 256
     return pl.pallas_call(
@@ -242,17 +279,18 @@
         grid=(features // step,),
         in_specs=[
             pl.BlockSpec((rows, step), lambda i: (0, i)),
-            pl.BlockSpec((rows, width), lambda i: (0, 0)),
+            pl.BlockSpec((rows, step), lambda i: (0, i)),
+            pl.BlockSpec(grad.shape, lambda i: (0, 0, 0)),
         ],
         out_specs=pl.BlockSpec((step * groups, LANES), lambda i: (i, 0)),
         out_shape=jax.ShapeDtypeStruct((features * groups, LANES), jnp.float32),
         compiler_params=pltpu.CompilerParams(vmem_limit_bytes=32 * 1024 * 1024),
         cost_estimate=pl.CostEstimate(
-            flops=2 * rows * features * width,
-            bytes_accessed=4 * features * width + 2 * rows * (features + width),
+            flops=4 * rows * features * width,
+            bytes_accessed=4 * features * width + 4 * rows * (features + width),
             transcendentals=0,
         ),
-    )(act, grad)
+    )(mine, other, grad)
 
 
 def on_device(
@@ -275,34 +313,23 @@
     col_half = columns // n_sec
     stream = block_rows * n_tp
     own = stream // n_seq
-    part_rows = block_rows // n_sec
-    sub = part_rows // n_seq
+    half = own // n_sec
+    groups = block_rows // own
     keys = key_weight.shape[1]
     key_half = keys // n_sec
     seq_len = text_embed.shape[0]
     tiles = stream // TILE
 
-    mine = lax.dynamic_slice_in_dim(vis_hidden, core * part_rows, part_rows, 0)
-    act = jax.nn.gelu(mine.astype(f32), approximate=False).astype(bf16)
-    pieces = [act] + [swap(act, "tp", m) for m in range(1, n_tp)]
-    pieces = [p.reshape(n_seq, sub, features) for p in pieces]
-
-    images = []
-    for first, last in ((0, 1), (1, 2), (2, n_tp)):
-        blocks = last - first
-        chunk = jnp.stack(pieces[first:last], 1).reshape(blocks * part_rows, features)
-        partial = jnp.dot(chunk, proj_weight, preferred_element_type=f32).astype(bf16)
-        summed = reduce_to_owner(partial.reshape(n_seq, blocks * sub, columns), "seq")
-        images += list((summed + proj_bias).astype(bf16).reshape(blocks, sub, columns))
-    image_mine = jnp.concatenate(in_order(images, t), 0)
-    low, high = image_mine[:, :col_half], image_mine[:, col_half:]
-    first_core = core == 0
-    came = swap(jnp.where(first_core, high, low), "sec", 1)
-    image = jnp.concatenate(in_order([jnp.where(first_core, low, high), came], core), 0)
-
-    act, text_embed, key_cotangent = lax.optimization_barrier((act, text_embed, key_cotangent))
     text_values = text_embed.astype(f32)
     text_sq = total(jnp.sum(text_values * text_values, 1), "tp")
+
+    grouped = vis_hidden.reshape(groups, n_sec, half, features)
+    mine = lax.dynamic_index_in_dim(grouped, core, 1, keepdims=False)
+    act = jax.nn.gelu(mine.astype(f32), approximate=False).astype(bf16)
+    act = act.reshape(groups * half, features)
+    pieces = [act] + [swap(act, "tp", m) for m in range(1, n_tp)]
+    partial, act_mine = project(t[None], pieces, proj_weight)
+
     is_mine = owner_map == z
     image_count = TILE * jnp.sum(jnp.where(is_mine, tile_counts, 0))
     text_count = jnp.sum(jnp.where(is_mine, text_counts, 0))
@@ -318,8 +345,7 @@
         share = key_half // n_seq
         moment = moment.reshape(-1, columns, LANES // share, share).transpose(0, 2, 1, 3)
         moment = moment.reshape(n_seq, columns, share)
-    moment, image_mine = lax.optimization_barrier((moment, image_mine))
-    moment = lax.psum_scatter(moment, "seq", scatter_dimension=0, tiled=False)
+    moment = reduce_to_owner(moment, "seq")
 
     starts = jnp.cumsum(tile_counts) - tile_counts
     tile_ids = jnp.arange(tiles, dtype=jnp.int32)[:, None]
@@ -334,8 +360,15 @@
     for place in range(MAXT):
         chosen = (tile_owner == z) & (tile_place == place)
         given = jnp.where(chosen[:, None, None], front[place][None], given)
-    given = given.reshape(n_tp, n_sec, n_seq, sub, share).transpose(2, 1, 0, 3, 4)
     taken = butterfly(given.reshape(stream, share), ("seq",))
+    key_bias_part = jnp.sum(key_cotangent.astype(f32), 0)
+    early = jnp.concatenate([gain_text[0], jnp.where(core == 0, key_bias_part, 0.0)])
+
+    taken, early, act_mine, partial = together(taken, early, act_mine, partial)
+    summed = lax.psum_scatter(partial, "seq", scatter_dimension=0, tiled=True)
+    early = total(early, "seq") if n_seq <= 4 else butterfly(early, ("seq",))
+    early = total(early, "sec")
+    act_other = swap(act_mine, "sec", 1)
     taken = [taken] + [swap(taken, "tp", m) for m in range(1, n_tp)]
     half_cot = jnp.concatenate(in_order(taken, t), 1)
     other_cot = swap(half_cot, "sec", 1)
@@ -344,47 +377,42 @@
     normed_grad = lax.dot_general(
         image_cot, weight_rows, (((1,), (1,)), ((), ())), preferred_element_type=f32
     )
+    own_cot = lax.dynamic_slice_in_dim(image_cot, (z * n_sec + core) * half, half, 0)
+    own_grad = lax.dot_general(
+        own_cot, key_weight, (((1,), (1,)), ((), ())), preferred_element_type=f32
+    )
     key_share = key_half // n_seq
     cot_own = jnp.concatenate(
         [lax.dynamic_slice_in_dim(c, z * key_share, key_share, 1) for c in (half_cot, other_cot)], 1
     )
 
-    act_half = jnp.stack(in_order(pieces, t), 1)
-    act_pair = in_order([act_half, swap(act_half, "sec", 1)], core)
-    act_full = jnp.stack(act_pair, 1).reshape(stream, features)
-
-    own_cot = lax.dynamic_slice_in_dim(image_cot, (z * n_sec + core) * (own // n_sec), own // n_sec, 0)
-    own_grad = lax.dot_general(
-        own_cot, key_weight, (((1,), (1,)), ((), ())), preferred_element_type=f32
-    )
+    image_mine = (summed.astype(f32) + proj_bias).astype(bf16)
+    low, high = image_mine[:, :col_half], image_mine[:, col_half:]
+    first_core = core == 0
+    came = swap(jnp.where(first_core, high, low), "sec", 1)
+    image = jnp.concatenate(in_order([jnp.where(first_core, low, high), came], core), 0)
+    rows = lax.all_gather(image, "seq", axis=0, tiled=True)
+
     sums = total(row_sums(image_mine, own_grad, norm_gain[None]), "tp")
-    gain_half = lax.dynamic_slice_in_dim(norm_gain, core * col_half, col_half, 0)[None]
     if n_seq <= 4:
-        up, down = along_line(image, "seq")
         sums = jnp.stack(in_order([sums] + [swap(sums, "seq", m) for m in range(1, n_seq)], z), 0)
-        others = up + down
     else:
-        image = lax.all_gather(image, "seq", axis=0, tiled=True)
         sums = lax.all_gather(sums, "seq", axis=0, tiled=False)
-        others = []
     sums = jnp.stack(in_order([sums, swap(sums, "sec", 1)], core), 1)
     sums = sums.reshape(n_seq * n_sec, *sums.shape[2:])
+
+    gain_half = lax.dynamic_slice_in_dim(norm_gain, core * col_half, col_half, 0)[None]
     embed_grad, here, there, small = image_grads(
-        z[None], normed_grad, gain_half, cot_own, sums, image, others
+        core[None], normed_grad, gain_half, cot_own, sums, rows
     )
     there = swap(there, "sec", 1)
     small_other = swap(small, "sec", 1)
-    product = weight_product(act_full, embed_grad)
-    proj_weight_grad = product.reshape(features, 1, 1, col_half)
+    weight_grad = weight_product(act_mine, act_other, embed_grad)
+    proj_weight_grad = weight_grad.reshape(features, 1, 1, col_half)
 
     both = in_order([here, there.astype(f32)], core)
-    key_weight_grad = (moment.astype(f32) + jnp.concatenate(both, 0)) * norm_gain[:, None]
+    key_weight_grad = (moment + jnp.concatenate(both, 0)) * norm_gain[:, None]
     gain_image, proj_bias_grad = jnp.concatenate(in_order([small, small_other], core), 1)
-
-    key_bias_part = jnp.sum(key_cotangent.astype(f32), 0)
-    early = jnp.concatenate([gain_text[0], jnp.where(core == 0, key_bias_part, 0.0)])
-    early = total(early, "seq") if n_seq <= 4 else butterfly(early, ("seq",))
-    early = total(early, "sec")
     gain_grad = early[:columns] + gain_image
     key_bias_grad = early[columns:]
     return (proj_weight_grad, proj_bias_grad, key_weight_grad, key_bias_grad, gain_grad)

time: 217 us -> 192 us (0.88)
  matrix products: 20.1 us -> 4.91 us
  starting transfers between devices: 47.2 us -> 34 us
  other arithmetic: 28.4 us -> 17.4 us
  Pallas kernels: 19.7 us -> 27.2 us
  waiting for transfers between devices: 72.2 us -> 78.8 us
    reduce_scatter x1, waiting for transfers between devices: 0.02 us -> 41.5 us  [on_device(): summed = lax.psum_scatter(partial, 'seq', scatter_dimension=0, tiled=True)]
    ppermute x6 -> x0, waiting for transfers between devices: 19.9 us -> none  [the longest x3 19.9 us: along_line(): lax.ppermute(left, axis, [(j, j - 1) for j in range(1, count - i + 1)])]
    ppermute x33 -> x29, waiting for transfers between devices: 52.3 us -> 36.5 us  [swap(): return lax.ppermute(x, axis, [(i, i ^ mask) for i in range(count)])]
    dot_general x3 -> x0, matrix products: 12.5 us -> none  [on_device(): jnp.dot(chunk, proj_weight, preferred_element_type=f32).astype(bf16)]
    ppermute x6 -> x0, starting transfers between devices: 6.76 us -> none  [the longest x3 4.09 us: along_line(): lax.ppermute(left, axis, [(j, j - 1) for j in range(1, count - i + 1)])]
    ppermute x33 -> x29, starting transfers between devices: 40.4 us -> 33.8 us  [swap(): return lax.ppermute(x, axis, [(i, i ^ mask) for i in range(count)])]
    pallas_call x0 -> x1, Pallas kernels: none -> 5.95 us  [project(): pl.pallas_call(project_kernel, grid=(columns // step,), in_specs=[pl.Bloc...]
    another operation x5 -> x1, other arithmetic: 5.4 us -> 0.18 us  [the longest x2 2.03 us: on_device(): act_full = jnp.stack(act_pair, 1).reshape(stream, features)]
  transfers between devices with their start and end apart: 40 -> 31, of which waited for: 13 -> 8; matrix products, arithmetic and copies ran while one was open for 22% -> 14% of each run, Pallas kernels for 9% -> 11%
where the time goes in v6:
time: 192 us
  waiting for transfers between devices  78.8 us (41%)
  starting transfers between devices  34 us (18%)
  Pallas kernels  27.2 us (14%)
  other arithmetic  17.4 us (9%)
  between operations  15.1 us (8%)
  local copies, waits for them, and re-layouts  14.4 us (8%)
  matrix products  4.91 us (3%)
    reduce_scatter x1, waiting for transfers between devices, on_device(): summed = lax.psum_scatter(partial, 'seq', scatter_dimension=0, tiled=True)  41.5 us
    ppermute x29, waiting for transfers between devices, swap(): return lax.ppermute(x, axis, [(i, i ^ mask) for i in range(count)])  36.5 us
    ppermute x29, starting transfers between devices, swap(): return lax.ppermute(x, axis, [(i, i ^ mask) for i in range(count)])  33.8 us
    pallas_call x1, Pallas kernels, weight_product(): pl.pallas_call(weight_kernel, grid=(features // step,), in_specs=[pl.Bloc...  10.3 us
    pallas_call x1, Pallas kernels, project(): pl.pallas_call(project_kernel, grid=(columns // step,), in_specs=[pl.Bloc...  5.95 us
    pallas_call x1, Pallas kernels, image_grads(): pl.pallas_call(image_kernel, in_specs=[pl.BlockSpec(memory_space=pltpu.SM...  5.6 us
    unnamed x36, local copies, waits for them, and re-layouts  5.09 us
    pallas_call x1, Pallas kernels, text_product(): pl.pallas_call(text_kernel, grid=(columns // step,), in_specs=[pl.BlockSp...  5.08 us
  transfers between devices with their start and end apart: 31, of which 8 were waited for; matrix products, arithmetic and copies ran while one was open for 14% of the time, Pallas kernels for 11%

profile of v6, /device:TPU:0, one launch (start us, length us, event | category | flops | bytes accessed | tf_op | source)
XLA Modules:
  0.0 191.8 jit_solution(8873867571980087856)
XLA Ops:
  7.2 3.2 %multiply_reduce_fusion = f32[1024]{0:T(1024)S(1)} fusion(bf16[1024,2048]{1,0:T(8,128)(2,1)} %text_ref.1), kind=kLoop, calls=%fused_computation | loop fusion | flops 6290432 | bytes 4198400 | tf_op jit(solution)/shard_map/reduce_sum | solution.py:324
  10.5 4.0 %collective-permute-start.4 = (f32[1024]{0:T(1024)S(1)}, f32[1024]{0:T(1024)S(1)}, u32[]{:S(2)}, u32[]{:S(2)}) collective-permute-start(f32[1024]{0:T(1024)S(1)} %multiply_reduce_fusion), channel_id=1, source_target_pairs={{0,3},{1,2},{2,1},{3,0},{4,7},{5,6},{6,5},{7,4},{8,11},{9,10},{10,... | collective-permute-start | bytes 12296 | tf_op jit(solution)/shard_map/ppermute | solution.py:17
  14.4 0.5 collective-permute-start.3
  15.1 1.7 fusion.5.refs_2_
  16.8 2.9 %collective-permute-start.7 = (bf16[96,2048]{1,0:T(8,128)(2,1)S(1)}, bf16[96,2048]{1,0:T(8,128)(2,1)S(1)}, u32[]{:S(2)}, u32[]{:S(2)}) collective-permute-start(bf16[96,2048]{1,0:T(8,128)(2,1)S(1)} %fusion.5.refs_2_), channel_id=1, source_target_pairs={{0,3},{1,2},{2,1},{3,0},{4,7},{5,6},{6,5},{7,4},{8,11},{9,10},{10,... | collective-permute-start | bytes 1179656 | tf_op jit(solution)/shard_map/ppermute | solution.py:17
  19.7 0.5 collective-permute-start.6
  20.2 0.4 convert_reduce_fusion
  20.6 0.3 copy-done.16
  21.0 1.1 constant_dynamic-slice_fusion.3
  22.1 3.2 %constant_dynamic-slice_fusion.2.weight_ref = bf16[2048,512]{1,0:T(8,128)(2,1)} fusion(bf16[2048,1024]{1,0:T(8,128)(2,1)} %param.15, s32[]{:T(128)S(6)} %select_n.242), kind=kLoop, calls=%fused_computation.93 | loop fusion | bytes 4194308 | tf_op jit(solution)/shard_map/dynamic_slice | solution.py:342
  25.3 0.6 fusion.45
  27.0 0.3 fusion.39
  27.5 2.0 %collective-permute-start = (bf16[768,128]{1,0:T(8,128)(2,1)S(1)}, bf16[768,128]{1,0:T(8,128)(2,1)S(1)}, u32[]{:S(2)}, u32[]{:S(2)}) collective-permute-start(bf16[768,128]{1,0:T(8,128)(2,1)S(1)} %fusion.39), channel_id=1, source_target_pairs={{0,4},{4,0},{8,12},{12,8},{1,5},{5,1},{9,13},{13,9},{2,6},{6,2},{1... | collective-permute-start | bytes 589832 | tf_op jit(solution)/shard_map/ppermute | solution.py:17
  29.5 0.7 rsqrt_select_fusion
  30.2 0.3 multiply_convert_fusion.cot_ref
  30.5 2.7 %collective-permute-done = bf16[768,128]{1,0:T(8,128)(2,1)S(1)} collective-permute-done((bf16[768,128]{1,0:T(8,128)(2,1)S(1)}, bf16[768,128]{1,0:T(8,128)(2,1)S(1)}, u32[]{:S(2)}, u32[]{:S(2)}) %collective-permute-start) | collective-permute-done | bytes 196640 | tf_op jit(solution)/shard_map/ppermute | solution.py:17
  33.2 0.3 fusion.48
  33.5 3.1 %collective-permute-start.1 = (bf16[768,128]{1,0:T(8,128)(2,1)S(1)}, bf16[768,128]{1,0:T(8,128)(2,1)S(1)}, u32[]{:S(2)}, u32[]{:S(2)}) collective-permute-start(bf16[768,128]{1,0:T(8,128)(2,1)S(1)} %fusion.48), channel_id=1, source_target_pairs={{0,8},{4,12},{8,0},{12,4},{1,9},{5,13},{9,1},{13,5},{2,10},{6,14},... | collective-permute-start | bytes 589832 | tf_op jit(solution)/shard_map/ppermute | solution.py:17
  36.5 2.2 %copy-done = bf16[1024,2048]{1,0:T(8,128)(2,1)S(1)} copy-done((bf16[1024,2048]{1,0:T(8,128)(2,1)S(1)}, bf16[1024,2048]{1,0:T(8,128)(2,1)}, u32[]{:S(2)}) %copy-start) | copy-done | bytes 4194328
  38.7 5.1 %shard_map.137 = (bf16[4,2048,128]{2,1,0:T(8,128)(2,1)S(1)}, f32[1,2048]{1,0:T(1,128)S(1)}) custom-call(bf16[1024,2048]{1,0:T(8,128)(2,1)S(1)} %copy-done, bf16[1024,512]{1,0:T(8,128)(2,1)S(1)} %multiply_convert_fusion.cot_ref, bf16[2048,512]{1,0:T(8,128)(2,1)S(1)} %copy-done.1), custom_call_target="tpu_custom_call" | custom-call | flops 2147483648 | bytes 9437184 | tf_op jit(solution)/shard_map/pallas_call | solution.py:150
  43.9 6.0 %shard_map.138 = (bf16[384,2048]{1,0:T(8,128)(2,1)S(1)}, bf16[384,2048]{1,0:T(8,128)(2,1)}) custom-call(s32[1]{0:T(128)} %bitcast.5.refs_0_, bf16[2048,2048]{1,0:T(8,128)(2,1)S(1)} %copy-done.5, bf16[96,2048]{1,0:T(8,128)(2,1)S(1)} %fusion.5.refs_2_, bf16[96,2048]{1,0:T(8,128)(2,1)S(1)} %collective-permute-done.5.refs_3_, ...), custom_call_target="tpu_custom_call" | custom-call | flops 3221225472 | bytes 13107200 | tf_op jit(solution)/shard_map/pallas_call | solution.py:111
  49.9 1.1 copy-done.3
  51.3 2.9 %collective-permute-start.27 = (f32[3072]{0:T(1024)S(1)}, f32[3072]{0:T(1024)S(1)}, u32[]{:S(2)}, u32[]{:S(2)}) collective-permute-start(f32[3072]{0:T(1024)S(1)} %pad_maximum_fusion.5), channel_id=1, source_target_pairs={{0,12},{4,8},{8,4},{12,0},{1,13},{5,9},{9,5},{13,1},{2,14},{6,10},... | collective-permute-start | bytes 36872 | tf_op jit(solution)/shard_map/ppermute | solution.py:17
  54.4 1.3 collective-permute-start.25
  55.8 0.6 dynamic_slice.47
  56.3 1.5 collective-permute-start.11
  57.8 1.5 collective-permute-start.10
  59.4 0.5 collective-permute-start.9
  59.9 1.0 dynamic-slice_bitcast_fusion
  61.0 0.7 collective-permute-start.22
  61.9 0.6 slice.32
  62.5 2.2 %collective-permute-done.10 = bf16[768,128]{1,0:T(8,128)(2,1)S(1)} collective-permute-done((bf16[768,128]{1,0:T(8,128)(2,1)S(1)}, bf16[768,128]{1,0:T(8,128)(2,1)S(1)}, u32[]{:S(2)}, u32[]{:S(2)}) %collective-permute-start.10) | collective-permute-done | bytes 196640 | tf_op jit(solution)/shard_map/ppermute | solution.py:17
  64.7 1.2 collective-permute-done.9
  66.0 41.5 %reduce-scatter.2.cloned.1.call-done = bf16[96,2048]{1,0:T(8,128)(2,1)} async-done(((bf16[384,2048]{1,0:T(8,128)(2,1)}), bf16[96,2048]{1,0:T(8,128)(2,1)}) %reduce-scatter.2.cloned.1.call-update) | async-done | bytes 393232 | tf_op jit(solution)/shard_map/reduce_scatter | solution.py:368
  107.5 1.1 add_convert_fusion.rows_ref
  108.7 1.0 pad_maximum_fusion.2
  109.7 0.5 collective-permute-start.12
  110.2 0.9 constant_dynamic-slice_fusion.1
  111.2 0.8 pad_maximum_fusion.4
  112.0 1.4 convert_add_fusion
  113.6 2.5 %collective-permute-start.23 = (bf16[1,2048,128]{2,1,0:T(8,128)(2,1)S(1)}, bf16[1,2048,128]{2,1,0:T(8,128)(2,1)S(1)}, u32[]{:S(2)}, u32[]{:S(2)}) collective-permute-start(bf16[1,2048,128]{2,1,0:T(8,128)(2,1)S(1)} %dynamic-slice_convert_fusion), channel_id=1, source_target_pairs={{0,8},{4,12},{8,0},{12,4},{1,9},{5,13},{9,1},{13,5},{2,10},{6,14},... | collective-permute-start | bytes 1572872 | tf_op jit(solution)/shard_map/ppermute | solution.py:17
  116.1 1.6 broadcast_select_fusion.1
  117.7 1.4 fusion.37.grad_ref
  119.1 0.2 shard_map.139
  119.3 2.4 %collective-permute-start.15 = (f32[2,128]{1,0:T(2,128)S(1)}, f32[2,128]{1,0:T(2,128)S(1)}, u32[]{:S(2)}, u32[]{:S(2)}) collective-permute-start(f32[2,128]{1,0:T(2,128)S(1)} %shard_map.139), channel_id=1, source_target_pairs={{0,3},{1,2},{2,1},{3,0},{4,7},{5,6},{6,5},{7,4},{8,11},{9,10},{10,... | collective-permute-start | bytes 3080 | tf_op jit(solution)/shard_map/ppermute | solution.py:17
  121.7 0.6 collective-permute-start.14
  122.3 0.6 collective-permute-start.13
  122.9 3.5 %fusion.grad_ref = f32[768,1024]{1,0:T(8,128)} fusion(bf16[2048,1024]{1,0:T(8,128)(2,1)S(1)} %copy-done.6, s32[]{:T(128)S(6)} %select_n.263, bf16[768,512]{1,0:T(8,128)(2,1)S(1)} %get-tuple-element.49, bf16[768,512]{1,0:T(8,128)(2,1)S(1)} %get-tuple-element.48), kind=kOutput, calls=%fused_computation.3 | convolution fusion | flops 1613758464 | bytes 6815748 | tf_op jit(solution)/shard_map/dot_general | solution.py:377
  126.5 1.6 collective-permute-start.17
  128.1 2.7 %collective-permute-start.16 = (f32[2,128]{1,0:T(2,128)S(1)}, f32[2,128]{1,0:T(2,128)S(1)}, u32[]{:S(2)}, u32[]{:S(2)}) collective-permute-start(f32[2,128]{1,0:T(2,128)S(1)} %add_add_fusion.1), channel_id=1, source_target_pairs={{0,12},{4,8},{8,4},{12,0},{1,13},{5,9},{9,5},{13,1},{2,14},{6,10},... | collective-permute-start | bytes 3080 | tf_op jit(solution)/shard_map/ppermute | solution.py:17
  130.9 0.9 constant_dynamic-slice_fusion
  131.8 3.8 %collective-permute-done.18 = f32[2,128]{1,0:T(2,128)S(1)} collective-permute-done((f32[2,128]{1,0:T(2,128)S(1)}, f32[2,128]{1,0:T(2,128)S(1)}, u32[]{:S(2)}, u32[]{:S(2)}) %collective-permute-start.18) | collective-permute-done | bytes 1056 | tf_op jit(solution)/shard_map/ppermute | solution.py:17
  135.6 26.3 %collective-permute-done.17 = f32[2,128]{1,0:T(2,128)S(1)} collective-permute-done((f32[2,128]{1,0:T(2,128)S(1)}, f32[2,128]{1,0:T(2,128)S(1)}, u32[]{:S(2)}, u32[]{:S(2)}) %collective-permute-start.17) | collective-permute-done | bytes 1056 | tf_op jit(solution)/shard_map/ppermute | solution.py:17
  161.9 0.8 pad_maximum_fusion.3.cot_ref
  162.8 0.3 collective-permute-done.19
  163.1 0.6 copy.20
  163.7 0.7 all-gather.2.cloned.1.call-done.rows_ref
  164.4 5.6 %shard_map.140 = (bf16[2,384,1024]{2,1,0:T(8,128)(2,1)}, f32[1024,128]{1,0:T(8,128)}, bf16[1024,128]{1,0:T(8,128)(2,1)}, f32[2,1024]{1,0:T(2,128)}) custom-call(s32[1]{0:T(128)} %bitcast.9.core_ref, f32[768,1024]{1,0:T(8,128)} %fusion.grad_ref, f32[1,1024]{1,0:T(1,128)} %bitcast.148, bf16[768,256]{1,0:T(8,128)(2,1)} %pad_maximum_fusion.3.cot_ref, ...), custom_call_target="tpu_custom_call" | custom-call | flops 402653184 | bytes 6291456 | tf_op jit(solution)/shard_map/pallas_call | solution.py:242
  170.1 0.4 collective-permute-start.24
  170.5 1.4 copy-done.2
  171.9 10.3 %shard_map.141 = f32[16384,128]{1,0:T(8,128)} custom-call(bf16[384,2048]{1,0:T(8,128)(2,1)} %get-tuple-element.20.mine_ref, bf16[384,2048]{1,0:T(8,128)(2,1)} %collective-permute-done.8.other_ref, bf16[2,384,1024]{2,1,0:T(8,128)(2,1)S(1)} %copy-done.2), custom_call_target="tpu_custom_call" | custom-call | flops 3221225472 | bytes 13107200 | tf_op jit(solution)/shard_map/pallas_call | solution.py:277
  182.3 0.6 pad_maximum_fusion.6
  182.9 0.6 slice_add_fusion
  183.6 1.4 fusion.2
  (94 shorter events, 2.5 us)
Async XLA Ops:
  7.2 7.9 %copy-start.12 = (bf16[192,2048]{1,0:T(8,128)(2,1)S(1)}, bf16[192,2048]{1,0:T(8,128)(2,1)}, u32[]{:S(2)}) copy-start(bf16[192,2048]{1,0:T(8,128)(2,1)} %param.10) | copy-start | bytes 2359300
  7.2 13.0 %copy-start.7 = (bf16[1024,1024]{1,0:T(8,128)(2,1)S(1)}, bf16[1024,1024]{1,0:T(8,128)(2,1)}, u32[]{:S(2)}) copy-start(bf16[1024,1024]{1,0:T(8,128)(2,1)} %param.16) | copy-start | bytes 6291460
  7.2 100.3 %reduce-scatter.2.cloned.1.call-start = ((), (), s32[]{:S(2)}) async-start(), calls=%async_computation.1 | async-start | bytes 1966080 | tf_op jit(solution)/shard_map/reduce_scatter | solution.py:368
  10.5 16.8 %collective-permute-start.4 = (f32[1024]{0:T(1024)S(1)}, f32[1024]{0:T(1024)S(1)}, u32[]{:S(2)}, u32[]{:S(2)}) collective-permute-start(f32[1024]{0:T(1024)S(1)} %multiply_reduce_fusion), channel_id=1, source_target_pairs={{0,3},{1,2},{2,1},{3,0},{4,7},{5,6},{6,5},{7,4},{8,11},{9,10},{10,... | collective-permute-start | bytes 12296 | tf_op jit(solution)/shard_map/ppermute | solution.py:17
  14.4 13.1 %collective-permute-start.3 = (f32[1024]{0:T(1024)S(1)}, f32[1024]{0:T(1024)S(1)}, u32[]{:S(2)}, u32[]{:S(2)}) collective-permute-start(f32[1024]{0:T(1024)S(1)} %multiply_reduce_fusion), channel_id=1, source_target_pairs={{0,2},{1,3},{2,0},{3,1},{4,6},{5,7},{6,4},{7,5},{8,10},{9,11},{10,... | collective-permute-start | bytes 12296 | tf_op jit(solution)/shard_map/ppermute | solution.py:17
  14.9 14.6 %collective-permute-start.2 = (f32[1024]{0:T(1024)S(1)}, f32[1024]{0:T(1024)S(1)}, u32[]{:S(2)}, u32[]{:S(2)}) collective-permute-start(f32[1024]{0:T(1024)S(1)} %multiply_reduce_fusion), channel_id=1, source_target_pairs={{0,1},{1,0},{2,3},{3,2},{4,5},{5,4},{6,7},{7,6},{8,9},{9,8},{10,11... | collective-permute-start | bytes 12296 | tf_op jit(solution)/shard_map/ppermute | solution.py:17
  16.8 27.1 %collective-permute-start.7 = (bf16[96,2048]{1,0:T(8,128)(2,1)S(1)}, bf16[96,2048]{1,0:T(8,128)(2,1)S(1)}, u32[]{:S(2)}, u32[]{:S(2)}) collective-permute-start(bf16[96,2048]{1,0:T(8,128)(2,1)S(1)} %fusion.5.refs_2_), channel_id=1, source_target_pairs={{0,3},{1,2},{2,1},{3,0},{4,7},{5,6},{6,5},{7,4},{8,11},{9,10},{10,... | collective-permute-start | bytes 1179656 | tf_op jit(solution)/shard_map/ppermute | solution.py:17
  19.7 24.2 %collective-permute-start.6 = (bf16[96,2048]{1,0:T(8,128)(2,1)S(1)}, bf16[96,2048]{1,0:T(8,128)(2,1)S(1)}, u32[]{:S(2)}, u32[]{:S(2)}) collective-permute-start(bf16[96,2048]{1,0:T(8,128)(2,1)S(1)} %fusion.5.refs_2_), channel_id=1, source_target_pairs={{0,2},{1,3},{2,0},{3,1},{4,6},{5,7},{6,4},{7,5},{8,10},{9,11},{10,... | collective-permute-start | bytes 1179656 | tf_op jit(solution)/shard_map/ppermute | solution.py:17
  20.2 0.7 copy-start.16
  22.1 3.2 %copy-start.15 = (s32[4]{0:T(128)S(1)}, s32[4]{0:T(128)}, u32[]{:S(2)}) copy-start(s32[4]{0:T(128)} %param.19) | copy-start | bytes 52
  22.1 3.2 %copy-start.17 = (s32[4]{0:T(128)S(1)}, s32[4]{0:T(128)}, u32[]{:S(2)}) copy-start(s32[4]{0:T(128)} %param.18) | copy-start | bytes 52
  22.1 4.0 %slice-start = ((bf16[1024,1024]{1,0:T(8,128)(2,1)}), bf16[512,1024]{1,0:T(8,128)(2,1)S(1)}, s32[]{:S(2)}) async-start(bf16[1024,1024]{1,0:T(8,128)(2,1)} %param.16), calls=%async_computation.3 | async-start | bytes 2097152 | tf_op jit(solution)/shard_map/slice | solution.py:357
  22.1 8.1 %copy-start.10 = (bf16[1024,512]{1,0:T(8,128)(2,1)S(1)}, bf16[1024,512]{1,0:T(8,128)(2,1)}, u32[]{:S(2)}) copy-start(bf16[1024,512]{1,0:T(8,128)(2,1)} %constant_dynamic-slice_fusion.3) | copy-start | bytes 3145732
  27.0 9.5 %copy-start.1 = (bf16[2048,512]{1,0:T(8,128)(2,1)S(1)}, bf16[2048,512]{1,0:T(8,128)(2,1)}, u32[]{:S(2)}) copy-start(bf16[2048,512]{1,0:T(8,128)(2,1)} %constant_dynamic-slice_fusion.2.weight_ref) | copy-start | bytes 6291460
  27.3 16.6 %collective-permute-start.5 = (bf16[96,2048]{1,0:T(8,128)(2,1)S(1)}, bf16[96,2048]{1,0:T(8,128)(2,1)S(1)}, u32[]{:S(2)}, u32[]{:S(2)}) collective-permute-start(bf16[96,2048]{1,0:T(8,128)(2,1)S(1)} %fusion.5.refs_2_), channel_id=1, source_target_pairs={{0,1},{1,0},{2,3},{3,2},{4,5},{5,4},{6,7},{7,6},{8,9},{9,8},{10,11... | collective-permute-start | bytes 1179656 | tf_op jit(solution)/shard_map/ppermute | solution.py:17
  27.5 5.7 %collective-permute-start = (bf16[768,128]{1,0:T(8,128)(2,1)S(1)}, bf16[768,128]{1,0:T(8,128)(2,1)S(1)}, u32[]{:S(2)}, u32[]{:S(2)}) collective-permute-start(bf16[768,128]{1,0:T(8,128)(2,1)S(1)} %fusion.39), channel_id=1, source_target_pairs={{0,4},{4,0},{8,12},{12,8},{1,5},{5,1},{9,13},{13,9},{2,6},{6,2},{1... | collective-permute-start | bytes 589832 | tf_op jit(solution)/shard_map/ppermute | solution.py:17
  33.5 10.3 %collective-permute-start.1 = (bf16[768,128]{1,0:T(8,128)(2,1)S(1)}, bf16[768,128]{1,0:T(8,128)(2,1)S(1)}, u32[]{:S(2)}, u32[]{:S(2)}) collective-permute-start(bf16[768,128]{1,0:T(8,128)(2,1)S(1)} %fusion.48), channel_id=1, source_target_pairs={{0,8},{4,12},{8,0},{12,4},{1,9},{5,13},{9,1},{13,5},{2,10},{6,14},... | collective-permute-start | bytes 589832 | tf_op jit(solution)/shard_map/ppermute | solution.py:17
  36.5 2.2 %copy-start = (bf16[1024,2048]{1,0:T(8,128)(2,1)S(1)}, bf16[1024,2048]{1,0:T(8,128)(2,1)}, u32[]{:S(2)}) copy-start(bf16[1024,2048]{1,0:T(8,128)(2,1)} %text_ref.1) | copy-start | bytes 12582916
  38.7 5.2 %copy-start.5 = (bf16[2048,2048]{1,0:T(8,128)(2,1)S(1)}, bf16[2048,2048]{1,0:T(8,128)(2,1)}, u32[]{:S(2)}) copy-start(bf16[2048,2048]{1,0:T(8,128)(2,1)} %refs_1_.1) | copy-start | bytes 25165828
  43.9 11.8 %copy-start.4 = (f32[2048]{0:T(1024)S(1)}, f32[2048]{0:T(1024)}, u32[]{:S(2)}) copy-start(f32[2048]{0:T(1024)} %param.14) | copy-start | bytes 24580
  49.9 1.1 copy-start.3
  51.1 56.5 %copy-start.13 = (f32[2048]{0:T(1024)S(1)}, f32[2048]{0:T(1024)}, u32[]{:S(2)}) copy-start(f32[2048]{0:T(1024)} %param.12) | copy-start | bytes 24580
  51.1 113.3 %all-gather.2.cloned.1.call-start = ((), (), s32[]{:S(2)}) async-start(), calls=%async_computation.2 | async-start | bytes 1966080 | tf_op jit(solution)/shard_map/all_gather | solution.py:394
  51.3 8.1 %collective-permute-start.27 = (f32[3072]{0:T(1024)S(1)}, f32[3072]{0:T(1024)S(1)}, u32[]{:S(2)}, u32[]{:S(2)}) collective-permute-start(f32[3072]{0:T(1024)S(1)} %pad_maximum_fusion.5), channel_id=1, source_target_pairs={{0,12},{4,8},{8,4},{12,0},{1,13},{5,9},{9,5},{13,1},{2,14},{6,10},... | collective-permute-start | bytes 36872 | tf_op jit(solution)/shard_map/ppermute | solution.py:17
  54.2 5.7 %collective-permute-start.26 = (f32[3072]{0:T(1024)S(1)}, f32[3072]{0:T(1024)S(1)}, u32[]{:S(2)}, u32[]{:S(2)}) collective-permute-start(f32[3072]{0:T(1024)S(1)} %pad_maximum_fusion.5), channel_id=1, source_target_pairs={{0,8},{4,12},{8,0},{12,4},{1,9},{5,13},{9,1},{13,5},{2,10},{6,14},... | collective-permute-start | bytes 36872 | tf_op jit(solution)/shard_map/ppermute | solution.py:17
  54.4 5.4 %collective-permute-start.25 = (f32[3072]{0:T(1024)S(1)}, f32[3072]{0:T(1024)S(1)}, u32[]{:S(2)}, u32[]{:S(2)}) collective-permute-start(f32[3072]{0:T(1024)S(1)} %pad_maximum_fusion.5), channel_id=1, source_target_pairs={{0,4},{4,0},{8,12},{12,8},{1,5},{5,1},{9,13},{13,9},{2,6},{6,2},{1... | collective-permute-start | bytes 36872 | tf_op jit(solution)/shard_map/ppermute | solution.py:17
  56.3 6.1 %collective-permute-start.11 = (bf16[768,128]{1,0:T(8,128)(2,1)S(1)}, bf16[768,128]{1,0:T(8,128)(2,1)S(1)}, u32[]{:S(2)}, u32[]{:S(2)}) collective-permute-start(bf16[768,128]{1,0:T(8,128)(2,1)S(1)} %add.126), channel_id=1, source_target_pairs={{0,1},{1,0},{2,3},{3,2},{4,5},{5,4},{6,7},{7,6},{8,9},{9,8},{10,11... | collective-permute-start | bytes 589832 | tf_op jit(solution)/shard_map/ppermute | solution.py:17
  57.8 6.8 %collective-permute-start.10 = (bf16[768,128]{1,0:T(8,128)(2,1)S(1)}, bf16[768,128]{1,0:T(8,128)(2,1)S(1)}, u32[]{:S(2)}, u32[]{:S(2)}) collective-permute-start(bf16[768,128]{1,0:T(8,128)(2,1)S(1)} %add.126), channel_id=1, source_target_pairs={{0,2},{1,3},{2,0},{3,1},{4,6},{5,7},{6,4},{7,5},{8,10},{9,11},{10,... | collective-permute-start | bytes 589832 | tf_op jit(solution)/shard_map/ppermute | solution.py:17
  59.4 6.6 %collective-permute-start.9 = (bf16[768,128]{1,0:T(8,128)(2,1)S(1)}, bf16[768,128]{1,0:T(8,128)(2,1)S(1)}, u32[]{:S(2)}, u32[]{:S(2)}) collective-permute-start(bf16[768,128]{1,0:T(8,128)(2,1)S(1)} %add.126), channel_id=1, source_target_pairs={{0,3},{1,2},{2,1},{3,0},{4,7},{5,6},{6,5},{7,4},{8,11},{9,10},{10,... | collective-permute-start | bytes 589832 | tf_op jit(solution)/shard_map/ppermute | solution.py:17
  59.9 1.8 collective-permute-start.28
  61.0 51.0 %collective-permute-start.22 = (bf16[2,2048,128]{2,1,0:T(8,128)(2,1)}, bf16[2,2048,128]{2,1,0:T(8,128)(2,1)}, u32[]{:S(2)}, u32[]{:S(2)}) collective-permute-start(bf16[2,2048,128]{2,1,0:T(8,128)(2,1)} %dynamic-slice_bitcast_fusion), channel_id=1, source_target_pairs={{0,4},{4,0},{8,12},{12,8},{1,5},{5,1},{9,13},{13,9},{2,6},{6,2},{1... | collective-permute-start | bytes 3145736 | tf_op jit(solution)/shard_map/ppermute | solution.py:17
  61.7 108.8 %collective-permute-start.8 = (bf16[384,2048]{1,0:T(8,128)(2,1)}, bf16[384,2048]{1,0:T(8,128)(2,1)}, u32[]{:S(2)}, u32[]{:S(2)}) collective-permute-start(bf16[384,2048]{1,0:T(8,128)(2,1)} %get-tuple-element.20.mine_ref), channel_id=1, source_target_pairs={{0,16},{16,0},{1,17},{17,1},{2,18},{18,2},{3,19},{19,3},{4,20},{20... | collective-permute-start | bytes 4718600 | tf_op jit(solution)/shard_map/ppermute | solution.py:17
  108.6 2.5 %collective-permute-start.20 = (bf16[96,1024]{1,0:T(8,128)(2,1)S(1)}, bf16[96,1024]{1,0:T(8,128)(2,1)S(1)}, u32[]{:S(2)}, u32[]{:S(2)}) collective-permute-start(bf16[96,1024]{1,0:T(8,128)(2,1)S(1)} %broadcast_select_fusion.3), channel_id=1, source_target_pairs={{0,16},{16,0},{1,17},{17,1},{2,18},{18,2},{3,19},{19,3},{4,20},{20... | collective-permute-start | bytes 589832 | tf_op jit(solution)/shard_map/ppermute | solution.py:17
  109.7 6.4 %collective-permute-start.12 = (bf16[768,512]{1,0:T(8,128)(2,1)}, bf16[768,512]{1,0:T(8,128)(2,1)}, u32[]{:S(2)}, u32[]{:S(2)}) collective-permute-start(bf16[768,512]{1,0:T(8,128)(2,1)} %pad_maximum_fusion.2), channel_id=1, source_target_pairs={{0,16},{16,0},{1,17},{17,1},{2,18},{18,2},{3,19},{19,3},{4,20},{20... | collective-permute-start | bytes 2359304 | tf_op jit(solution)/shard_map/ppermute | solution.py:17
  113.5 4.2 %copy-start.8 = (f32[2,2048,128]{2,1,0:T(8,128)}, f32[2,2048,128]{2,1,0:T(8,128)S(1)}, u32[]{:S(2)}) copy-start(f32[2,2048,128]{2,1,0:T(8,128)S(1)} %convert_add_fusion) | copy-start | bytes 6291460
  113.5 4.2 %copy-start.6 = (bf16[2048,1024]{1,0:T(8,128)(2,1)S(1)}, bf16[2048,1024]{1,0:T(8,128)(2,1)}, u32[]{:S(2)}) copy-start(bf16[2048,1024]{1,0:T(8,128)(2,1)} %param.15) | copy-start | bytes 12582916
  113.6 70.0 %collective-permute-start.23 = (bf16[1,2048,128]{2,1,0:T(8,128)(2,1)S(1)}, bf16[1,2048,128]{2,1,0:T(8,128)(2,1)S(1)}, u32[]{:S(2)}, u32[]{:S(2)}) collective-permute-start(bf16[1,2048,128]{2,1,0:T(8,128)(2,1)S(1)} %dynamic-slice_convert_fusion), channel_id=1, source_target_pairs={{0,8},{4,12},{8,0},{12,4},{1,9},{5,13},{9,1},{13,5},{2,10},{6,14},... | collective-permute-start | bytes 1572872 | tf_op jit(solution)/shard_map/ppermute | solution.py:17
  119.3 7.0 %collective-permute-start.15 = (f32[2,128]{1,0:T(2,128)S(1)}, f32[2,128]{1,0:T(2,128)S(1)}, u32[]{:S(2)}, u32[]{:S(2)}) collective-permute-start(f32[2,128]{1,0:T(2,128)S(1)} %shard_map.139), channel_id=1, source_target_pairs={{0,3},{1,2},{2,1},{3,0},{4,7},{5,6},{6,5},{7,4},{8,11},{9,10},{10,... | collective-permute-start | bytes 3080 | tf_op jit(solution)/shard_map/ppermute | solution.py:17
  121.7 4.7 %collective-permute-start.14 = (f32[2,128]{1,0:T(2,128)S(1)}, f32[2,128]{1,0:T(2,128)S(1)}, u32[]{:S(2)}, u32[]{:S(2)}) collective-permute-start(f32[2,128]{1,0:T(2,128)S(1)} %shard_map.139), channel_id=1, source_target_pairs={{0,2},{1,3},{2,0},{3,1},{4,6},{5,7},{6,4},{7,5},{8,10},{9,11},{10,... | collective-permute-start | bytes 3080 | tf_op jit(solution)/shard_map/ppermute | solution.py:17
  122.3 4.1 %collective-permute-start.13 = (f32[2,128]{1,0:T(2,128)S(1)}, f32[2,128]{1,0:T(2,128)S(1)}, u32[]{:S(2)}, u32[]{:S(2)}) collective-permute-start(f32[2,128]{1,0:T(2,128)S(1)} %shard_map.139), channel_id=1, source_target_pairs={{0,1},{1,0},{2,3},{3,2},{4,5},{5,4},{6,7},{7,6},{8,9},{9,8},{10,11... | collective-permute-start | bytes 3080 | tf_op jit(solution)/shard_map/ppermute | solution.py:17
  126.4 9.2 %collective-permute-start.18 = (f32[2,128]{1,0:T(2,128)S(1)}, f32[2,128]{1,0:T(2,128)S(1)}, u32[]{:S(2)}, u32[]{:S(2)}) collective-permute-start(f32[2,128]{1,0:T(2,128)S(1)} %add_add_fusion.1), channel_id=1, source_target_pairs={{0,4},{4,0},{8,12},{12,8},{1,5},{5,1},{9,13},{13,9},{2,6},{6,2},{1... | collective-permute-start | bytes 3080 | tf_op jit(solution)/shard_map/ppermute | solution.py:17
  126.5 35.3 %collective-permute-start.17 = (f32[2,128]{1,0:T(2,128)S(1)}, f32[2,128]{1,0:T(2,128)S(1)}, u32[]{:S(2)}, u32[]{:S(2)}) collective-permute-start(f32[2,128]{1,0:T(2,128)S(1)} %add_add_fusion.1), channel_id=1, source_target_pairs={{0,8},{4,12},{8,0},{12,4},{1,9},{5,13},{9,1},{13,5},{2,10},{6,14},... | collective-permute-start | bytes 3080 | tf_op jit(solution)/shard_map/ppermute | solution.py:17
  128.1 33.7 %collective-permute-start.16 = (f32[2,128]{1,0:T(2,128)S(1)}, f32[2,128]{1,0:T(2,128)S(1)}, u32[]{:S(2)}, u32[]{:S(2)}) collective-permute-start(f32[2,128]{1,0:T(2,128)S(1)} %add_add_fusion.1), channel_id=1, source_target_pairs={{0,12},{4,8},{8,4},{12,0},{1,13},{5,9},{9,5},{13,1},{2,14},{6,10},... | collective-permute-start | bytes 3080 | tf_op jit(solution)/shard_map/ppermute | solution.py:17
  161.9 1.2 collective-permute-start.19
  170.0 12.3 %collective-permute-start.21 = (f32[2,1024]{1,0:T(2,128)}, f32[2,1024]{1,0:T(2,128)S(1)}, u32[]{:S(2)}, u32[]{:S(2)}) collective-permute-start(f32[2,1024]{1,0:T(2,128)} %get-tuple-element.24), channel_id=1, source_target_pairs={{0,16},{16,0},{1,17},{17,1},{2,18},{18,2},{3,19},{19,3},{4,20},{20... | collective-permute-start | bytes 24584 | tf_op jit(solution)/shard_map/ppermute | solution.py:17
  170.1 13.4 %collective-permute-start.24 = (bf16[1024,128]{1,0:T(8,128)(2,1)}, bf16[1024,128]{1,0:T(8,128)(2,1)S(1)}, u32[]{:S(2)}, u32[]{:S(2)}) collective-permute-start(bf16[1024,128]{1,0:T(8,128)(2,1)} %get-tuple-element.26), channel_id=1, source_target_pairs={{0,16},{16,0},{1,17},{17,1},{2,18},{18,2},{3,19},{19,3},{4,20},{20... | collective-permute-start | bytes 786440 | tf_op jit(solution)/shard_map/ppermute | solution.py:17
  170.5 1.4 copy-start.2
  171.9 10.3 %copy-start.14 = (f32[2,1024]{1,0:T(2,128)S(1)}, f32[2,1024]{1,0:T(2,128)}, u32[]{:S(2)}) copy-start(f32[2,1024]{1,0:T(2,128)} %get-tuple-element.24) | copy-start | bytes 24580
  171.9 11.6 %copy-start.11 = (f32[1024,128]{1,0:T(8,128)S(1)}, f32[1024,128]{1,0:T(8,128)}, u32[]{:S(2)}) copy-start(f32[1024,128]{1,0:T(8,128)} %get-tuple-element.27) | copy-start | bytes 1572868
  171.9 11.7 %copy-start.9 = (f32[2,2048,128]{2,1,0:T(8,128)S(1)}, f32[2,2048,128]{2,1,0:T(8,128)}, u32[]{:S(2)}) copy-start(f32[2,2048,128]{2,1,0:T(8,128)} %copy-done.8) | copy-start | bytes 6291460
Sparse Core Ops, SparseCore 0:
  51.2 56.3 reduce-scatter.1
  112.1 52.2 all-gather.1

commit v7 on v6

--- a/solution.py
+++ b/solution.py
@@ -60,6 +60,22 @@
         parts = kept.astype(jnp.float32) + came.astype(jnp.float32)
         count //= 2
     return parts[0]
+
+
+def line_step(parts, axis, step, before):
+    count = lax.axis_size(axis)
+    index = lax.axis_index(axis)
+    out = []
+    for sign in (1, -1):
+        place = index + sign * (count - step)
+        place = jnp.clip(place, 0, count - 1)
+        sent = lax.dynamic_index_in_dim(parts, place, 0, keepdims=False)
+        if before is not None:
+            sent = (sent.astype(jnp.float32) + before[len(out)].astype(jnp.float32)).astype(sent.dtype)
+        first = 0 if sign > 0 else count - 1
+        pairs = [(first + sign * j, first + sign * (j + 1)) for j in range(step)]
+        out.append(lax.ppermute(sent, axis, pairs))
+    return out
 
 
 def columns_of(row, count):
@@ -133,32 +149,109 @@
     )(index, weight, *pieces)
 
 
-def text_kernel(text_ref, cot_ref, weight_ref, moment_ref, gain_ref):
+def opening_kernel(core_ref, text_ref, *refs):
+    del core_ref
+    sums_ref, act_ref = refs[-2:]
+    groups = refs[:-2]
+
+    @pl.when(pl.program_id(0) == 0)
+    def _():
+        rows = groups[0].shape[0]
+        for i, group in enumerate(groups):
+            hidden = group[...].astype(jnp.float32)
+            act = 0.5 * hidden * (1.0 + lax.erf(hidden * 0.7071067811865476))
+            act_ref[i * rows : (i + 1) * rows, :] = act.astype(jnp.bfloat16)
+
+    values = text_ref[...].astype(jnp.float32)
+    sums_ref[...] = row_of(fold(values * values))
+
+
+def opening(core, text, hidden, groups, n_sec):
+    seq_len, columns = text.shape
+    rows, features = hidden.shape
+    half = rows // (groups * n_sec)
+    step = 256
+    part = [
+        pl.BlockSpec((half, features), lambda i, c, q=q: (q * n_sec + c[0], 0)) for q in range(groups)
+    ]
+    return pl.pallas_call(
+        opening_kernel,
+        grid_spec=pltpu.PrefetchScalarGridSpec(
+            num_scalar_prefetch=1,
+            grid=(seq_len // step,),
+            in_specs=[pl.BlockSpec((step, columns), lambda i, c: (i, 0))] + part,
+            out_specs=[
+                pl.BlockSpec((1, step), lambda i, c: (0, i)),
+                pl.BlockSpec((groups * half, features), lambda i, c: (0, 0)),
+            ],
+        ),
+        out_shape=[
+            jax.ShapeDtypeStruct((1, seq_len), jnp.float32),
+            jax.ShapeDtypeStruct((groups * half, features), jnp.bfloat16),
+        ],
+        compiler_params=pltpu.CompilerParams(vmem_limit_bytes=24 * 1024 * 1024),
+        cost_estimate=pl.CostEstimate(
+            flops=2 * seq_len * columns + 40 * groups * half * features,
+            bytes_accessed=2 * seq_len * columns,
+            transcendentals=0,
+        ),
+    )(core, text, *[hidden] * groups)
+
+
+def text_kernel(
+    at_ref, text_ref, weight_ref, cot_ref, *refs
+):
+    moment_ref, gain_ref, long_ref, scaled_ref = refs[-4:]
+    squares = refs[:-4]
+    seq_len, width = cot_ref.shape
+
+    @pl.when(pl.program_id(0) == 0)
+    def _():
+        parts = [r[...] for r in squares]
+        while len(parts) > 1:
+            parts = [parts[i] + parts[i + 1] for i in range(0, len(parts), 2)]
+        places = lax.broadcasted_iota(jnp.int32, (1, seq_len), 1)
+        scale = lax.rsqrt(parts[0] / D + EPSILON)
+        scale = columns_of(jnp.where(places < at_ref[2], scale, 0.0), seq_len)
+        long_ref[:seq_len, :] = cot_ref[...]
+        long_ref[seq_len:, :] = jnp.zeros((MAXT * TILE, width), jnp.bfloat16)
+        for i in range(width // LANES):
+            lanes = slice(i * LANES, (i + 1) * LANES)
+            shifted = long_ref[pl.ds(pl.multiple_of(at_ref[1] * TILE, TILE), seq_len), lanes]
+            scaled_ref[:, lanes] = (shifted.astype(jnp.float32) * scale).astype(jnp.bfloat16)
+
     moment = lax.dot_general(
-        text_ref[...], cot_ref[...], (((0,), (0,)), ((), ())), preferred_element_type=jnp.float32
+        text_ref[...], scaled_ref[...], (((0,), (0,)), ((), ())), preferred_element_type=jnp.float32
     )
     for i in range(moment_ref.shape[0]):
         moment_ref[i] = moment[:, i * LANES : (i + 1) * LANES].astype(jnp.bfloat16)
     gain_ref[...] = row_of(fold(moment * weight_ref[...].astype(jnp.float32)))
 
 
-def text_product(text, cot, weight):
+def text_product(at, text, weight, cot, squares, width):
     seq_len, columns = text.shape
-    width = cot.shape[1]
     groups = width // LANES
     step = 256
     return pl.pallas_call(
         text_kernel,
-        grid=(columns // step,),
-        in_specs=[
-            pl.BlockSpec((seq_len, step), lambda i: (0, i)),
-            pl.BlockSpec((seq_len, width), lambda i: (0, 0)),
-            pl.BlockSpec((step, width), lambda i: (i, 0)),
-        ],
-        out_specs=[
-            pl.BlockSpec((groups, step, LANES), lambda i: (0, i, 0)),
-            pl.BlockSpec((1, step), lambda i: (0, i)),
-        ],
+        grid_spec=pltpu.PrefetchScalarGridSpec(
+            num_scalar_prefetch=1,
+            grid=(columns // step,),
+            in_specs=[
+                pl.BlockSpec((seq_len, step), lambda i, a: (0, i)),
+                pl.BlockSpec((step, width), lambda i, a: (i, a[0])),
+                pl.BlockSpec((seq_len, width), lambda i, a: (0, a[0])),
+            ]
+            + [pl.BlockSpec((1, seq_len), lambda i, a: (0, 0))] * len(squares),
+            out_specs=[
+                pl.BlockSpec((groups, step, LANES), lambda i, a: (0, i, 0)),
+                pl.BlockSpec((1, step), lambda i, a: (0, i)),
+            ],
+            scratch_shapes=[
+                pltpu.VMEM((seq_len + MAXT * TILE, width), jnp.bfloat16),
+                pltpu.VMEM((seq_len, width), jnp.bfloat16),
+            ],
+        ),
         out_shape=[
             jax.ShapeDtypeStruct((groups, columns, LANES), jnp.bfloat16),
             jax.ShapeDtypeStruct((1, columns), jnp.float32),
@@ -169,7 +262,7 @@
             bytes_accessed=2 * (seq_len * (columns + width) + 2 * columns * width),
             transcendentals=0,
         ),
-    )(text, cot, weight)
+    )(at, text, weight, cot, *squares)
 
 
 def sums_kernel(rows_ref, grad_ref, gain_ref, sums_ref):
@@ -212,14 +305,14 @@
     bias_parts = list(gain_parts)
     for g in range(groups):
         rows = slice(g * size, (g + 1) * size)
-        to_rows = slice((g // 2) * size, (g // 2 + 1) * size)
-        side = jnp.bitwise_xor(core_ref[0], g % 2)
+        to = jnp.bitwise_xor(core_ref[0], g % 2) * (stream // 2) + (g // 2) * size
+        to_rows = pl.ds(pl.multiple_of(to, 16), size)
         for i in range(width // LANES):
             at = slice(i * LANES, (i + 1) * LANES)
             values = rows_ref[rows, at].astype(jnp.float32)
             scaled = grad_ref[rows, at] * inv[g]
             embed = (scaled * gain_ref[:, at] - values * mean[g]).astype(jnp.bfloat16)
-            embed_ref[side, to_rows, at] = embed
+            embed_ref[to_rows, at] = embed
             gain_parts[i] = gain_parts[i] + jnp.sum(scaled * values, 0, keepdims=True)
             bias_parts[i] = bias_parts[i] + jnp.sum(embed.astype(jnp.float32), 0, keepdims=True)
     small_ref[0:1, :] = jnp.concatenate(gain_parts, 1)
@@ -244,7 +337,7 @@
         in_specs=[pl.BlockSpec(memory_space=pltpu.SMEM)] + [whole] * 5,
         out_specs=[whole] * 4,
         out_shape=[
-            jax.ShapeDtypeStruct((2, stream // 2, width), jnp.bfloat16),
+            jax.ShapeDtypeStruct((stream, width), jnp.bfloat16),
             jax.ShapeDtypeStruct((width, share), jnp.float32),
             jax.ShapeDtypeStruct((width, share), jnp.bfloat16),
             jax.ShapeDtypeStruct((2, width), jnp.float32),
@@ -256,41 +349,35 @@
     )(core, grad, gain, cot, sums, rows)
 
 
-def weight_kernel(mine_ref, other_ref, grad_ref, out_ref):
-    step = mine_ref.shape[1]
-    groups = grad_ref.shape[2] // LANES
-    rows_first = (((0,), (0,)), ((), ()))
-    product = lax.dot_general(
-        mine_ref[...], grad_ref[0], rows_first, preferred_element_type=jnp.float32
-    ) + lax.dot_general(
-        other_ref[...], grad_ref[1], rows_first, preferred_element_type=jnp.float32
-    )
+def weight_kernel(act_ref, grad_ref, out_ref):
+    step = act_ref.shape[0]
+    groups = grad_ref.shape[1] // LANES
+    product = jnp.dot(act_ref[...], grad_ref[...], preferred_element_type=jnp.float32)
     for c in range(groups):
         out_ref[pl.ds(c, step, stride=groups), :] = product[:, c * LANES : (c + 1) * LANES]
 
 
-def weight_product(mine, other, grad):
-    rows, features = mine.shape
-    width = grad.shape[2]
+def weight_product(act, grad):
+    features, rows = act.shape
+    width = grad.shape[1]
     groups = width // LANES
     step = 256
     return pl.pallas_call(
         weight_kernel,
         grid=(features // step,),
         in_specs=[
-            pl.BlockSpec((rows, step), lambda i: (0, i)),
-            pl.BlockSpec((rows, step), lambda i: (0, i)),
-            pl.BlockSpec(grad.shape, lambda i: (0, 0, 0)),
+            pl.BlockSpec((step, rows), lambda i: (i, 0)),
+            pl.BlockSpec((rows, width), lambda i: (0, 0)),
         ],
         out_specs=pl.BlockSpec((step * groups, LANES), lambda i: (i, 0)),
         out_shape=jax.ShapeDtypeStruct((features * groups, LANES), jnp.float32),
         compiler_params=pltpu.CompilerParams(vmem_limit_bytes=32 * 1024 * 1024),
         cost_estimate=pl.CostEstimate(
-            flops=4 * rows * features * width,
-            bytes_accessed=4 * features * width + 4 * rows * (features + width),
+            flops=2 * rows * features * width,
+            bytes_accessed=4 * features * width + 2 * rows * (features + width),
             transcendentals=0,
         ),
-    )(mine, other, grad)
+    )(act, grad)
 
 
 def on_device(
@@ -320,32 +407,24 @@
     seq_len = text_embed.shape[0]
     tiles = stream // TILE
 
-    text_values = text_embed.astype(f32)
-    text_sq = total(jnp.sum(text_values * text_values, 1), "tp")
-
-    grouped = vis_hidden.reshape(groups, n_sec, half, features)
-    mine = lax.dynamic_index_in_dim(grouped, core, 1, keepdims=False)
-    act = jax.nn.gelu(mine.astype(f32), approximate=False).astype(bf16)
-    act = act.reshape(groups * half, features)
+    text_sq, act = opening(core[None], text_embed, vis_hidden, groups, n_sec)
+    text_sq = [text_sq] + [swap(text_sq, "tp", m) for m in range(1, n_tp)]
     pieces = [act] + [swap(act, "tp", m) for m in range(1, n_tp)]
-    partial, act_mine = project(t[None], pieces, proj_weight)
 
     is_mine = owner_map == z
-    image_count = TILE * jnp.sum(jnp.where(is_mine, tile_counts, 0))
+    image_tiles = jnp.sum(jnp.where(is_mine, tile_counts, 0))
     text_count = jnp.sum(jnp.where(is_mine, text_counts, 0))
-    text_inv = lax.rsqrt(text_sq / D + EPSILON)
-    text_scale = jnp.where(jnp.arange(seq_len) < text_count, text_inv, 0.0)
-    cot_half = lax.dynamic_slice_in_dim(key_cotangent, core * key_half, key_half, 1)
-    cot_padded = jnp.concatenate([cot_half, jnp.zeros((MAXT * TILE, key_half), bf16)], 0)
-    cot_text = lax.dynamic_slice_in_dim(cot_padded, image_count, seq_len, 0)
-    cot_text = (cot_text.astype(f32) * text_scale[:, None]).astype(bf16)
-    weight_half = lax.dynamic_slice_in_dim(key_weight, core * key_half, key_half, 1)
-    moment, gain_text = text_product(text_embed, cot_text, weight_half)
-    if n_seq != moment.shape[0]:
+    at = jnp.stack([core, image_tiles, text_count]).astype(jnp.int32)
+    moment, gain_text = text_product(at, text_embed, key_weight, key_cotangent, text_sq, key_half)
+    if n_seq <= 4:
+        way = line_step(moment, "seq", 1, None)
+        way[0], way[1], *pieces = together(*way, *pieces)
+        way = line_step(moment, "seq", 2, way)
+    else:
         share = key_half // n_seq
         moment = moment.reshape(-1, columns, LANES // share, share).transpose(0, 2, 1, 3)
-        moment = moment.reshape(n_seq, columns, share)
-    moment = reduce_to_owner(moment, "seq")
+        moment = reduce_to_owner(moment.reshape(n_seq, columns, share), "seq")
+    partial, act_mine = project(t[None], pieces, proj_weight)
 
     starts = jnp.cumsum(tile_counts) - tile_counts
     tile_ids = jnp.arange(tiles, dtype=jnp.int32)[:, None]
@@ -366,8 +445,6 @@
 
     taken, early, act_mine, partial = together(taken, early, act_mine, partial)
     summed = lax.psum_scatter(partial, "seq", scatter_dimension=0, tiled=True)
-    early = total(early, "seq") if n_seq <= 4 else butterfly(early, ("seq",))
-    early = total(early, "sec")
     act_other = swap(act_mine, "sec", 1)
     taken = [taken] + [swap(taken, "tp", m) for m in range(1, n_tp)]
     half_cot = jnp.concatenate(in_order(taken, t), 1)
@@ -387,6 +464,12 @@
     )
 
     image_mine = (summed.astype(f32) + proj_bias).astype(bf16)
+    if n_seq <= 4:
+        way[0], way[1], image_mine = together(*way, image_mine)
+        for step in range(3, n_seq):
+            way = line_step(moment, "seq", step, way)
+        moment = lax.dynamic_index_in_dim(moment, z, 0, keepdims=False).astype(f32)
+        moment = moment + way[0].astype(f32) + way[1].astype(f32)
     low, high = image_mine[:, :col_half], image_mine[:, col_half:]
     first_core = core == 0
     came = swap(jnp.where(first_core, high, low), "sec", 1)
@@ -394,12 +477,18 @@
     rows = lax.all_gather(image, "seq", axis=0, tiled=True)
 
     sums = total(row_sums(image_mine, own_grad, norm_gain[None]), "tp")
+    size = sums.size
+    sums = jnp.concatenate([sums.reshape(-1), early])
     if n_seq <= 4:
         sums = jnp.stack(in_order([sums] + [swap(sums, "seq", m) for m in range(1, n_seq)], z), 0)
     else:
         sums = lax.all_gather(sums, "seq", axis=0, tiled=False)
-    sums = jnp.stack(in_order([sums, swap(sums, "sec", 1)], core), 1)
-    sums = sums.reshape(n_seq * n_sec, *sums.shape[2:])
+    early = jnp.sum(sums[:, size:], 0)
+    sums = jnp.concatenate([sums[:, :size].reshape(-1), early])
+    sums = jnp.stack(in_order([sums, swap(sums, "sec", 1)], core), 0)
+    early = jnp.sum(sums[:, n_seq * size :], 0)
+    sums = sums[:, : n_seq * size].reshape(n_sec, n_seq, 2, -1).transpose(1, 0, 2, 3)
+    sums = sums.reshape(n_seq * n_sec, 2, -1)
 
     gain_half = lax.dynamic_slice_in_dim(norm_gain, core * col_half, col_half, 0)[None]
     embed_grad, here, there, small = image_grads(
@@ -407,7 +496,8 @@
     )
     there = swap(there, "sec", 1)
     small_other = swap(small, "sec", 1)
-    weight_grad = weight_product(act_mine, act_other, embed_grad)
+    act_turned = jnp.concatenate([act_mine, act_other], 0).T
+    weight_grad = weight_product(act_turned, embed_grad)
     proj_weight_grad = weight_grad.reshape(features, 1, 1, col_half)
 
     both = in_order([here, there.astype(f32)], core)

time: 192 us -> 197 us (1.026)
  waiting for transfers between devices: 78.8 us -> 53 us
  local copies, waits for them, and re-layouts: 14.4 us -> 25.9 us
  other arithmetic: 17.4 us -> 25.6 us
  starting transfers between devices: 34 us -> 40.3 us
  matrix products: 4.91 us -> 9.33 us
    reduce_scatter x1, waiting for transfers between devices: 41.5 us -> 16.8 us  [on_device(): summed = lax.psum_scatter(partial, 'seq', scatter_dimension=0, tiled=True)]
    ppermute x29 -> x23, waiting for transfers between devices: 36.5 us -> 15 us  [swap(): return lax.ppermute(x, axis, [(i, i ^ mask) for i in range(count)])]
    ppermute x0 -> x6, starting transfers between devices: none -> 15 us  [line_step(): out.append(lax.ppermute(sent, axis, pairs))]
    all_gather x1, waiting for transfers between devices: 0.68 us -> 11.8 us  [on_device(): rows = lax.all_gather(image, 'seq', axis=0, tiled=True)]
    unnamed x36 -> x57, local copies, waits for them, and re-layouts: 5.09 us -> 16.2 us
    ppermute x0 -> x6, waiting for transfers between devices: none -> 9.42 us  [line_step(): out.append(lax.ppermute(sent, axis, pairs))]
    ppermute x29 -> x23, starting transfers between devices: 33.8 us -> 25.3 us  [swap(): return lax.ppermute(x, axis, [(i, i ^ mask) for i in range(count)])]
    dynamic_slice x2 -> x0, local copies, waits for them, and re-layouts: 4.28 us -> none  [the longest x1 3.2 us: on_device(): lax.dynamic_slice_in_dim(key_weight, core * key_half, key_half, 1)]
  transfers between devices with their start and end apart: 31 -> 31, of which waited for: 8 -> 11; matrix products, arithmetic and copies ran while one was open for 14% -> 21% of each run, Pallas kernels for 11% -> 10%
where the time goes in v7:
time: 197 us; the launch traced here: 195 us
  waiting for transfers between devices  53 us (27%)
  starting transfers between devices  40.3 us (20%)
  Pallas kernels  26.4 us (13%)
  local copies, waits for them, and re-layouts  25.9 us (13%)
  other arithmetic  25.6 us (13%)
  between operations  14.6 us (7%)
  matrix products  9.33 us (5%)
    ppermute x23, starting transfers between devices, swap(): return lax.ppermute(x, axis, [(i, i ^ mask) for i in range(count)])  25.3 us
    reduce_scatter x1, waiting for transfers between devices, on_device(): summed = lax.psum_scatter(partial, 'seq', scatter_dimension=0, tiled=True)  16.8 us
    unnamed x57, local copies, waits for them, and re-layouts  16.2 us
    ppermute x23, waiting for transfers between devices, swap(): return lax.ppermute(x, axis, [(i, i ^ mask) for i in range(count)])  15 us
    ppermute x6, starting transfers between devices, line_step(): out.append(lax.ppermute(sent, axis, pairs))  15 us
    all_gather x1, waiting for transfers between devices, on_device(): rows = lax.all_gather(image, 'seq', axis=0, tiled=True)  11.8 us
    ppermute x6, waiting for transfers between devices, line_step(): out.append(lax.ppermute(sent, axis, pairs))  9.42 us
    pallas_call x1, Pallas kernels, weight_product(): pl.pallas_call(weight_kernel, grid=(features // step,), in_specs=[pl.Bloc...  6.91 us
  transfers between devices with their start and end apart: 31, of which 11 were waited for; matrix products, arithmetic and copies ran while one was open for 21% of the time, Pallas kernels for 10%

profile of v7, /device:TPU:0, one launch (start us, length us, event | category | flops | bytes accessed | tf_op | source)
XLA Modules:
  0.0 195.2 jit_solution(7170209073411605195)
XLA Ops:
  7.2 2.2 %copy-done = bf16[1024,2048]{1,0:T(8,128)(2,1)S(1)} copy-done((bf16[1024,2048]{1,0:T(8,128)(2,1)S(1)}, bf16[1024,2048]{1,0:T(8,128)(2,1)}, u32[]{:S(2)}) %copy-start) | copy-done | bytes 4194328
  9.4 1.1 copy-done.10
  10.5 1.3 shard_map.137
  11.9 4.0 %collective-permute-start.4 = (f32[1,1024]{1,0:T(1,128)S(1)}, f32[1,1024]{1,0:T(1,128)S(1)}, u32[]{:S(2)}, u32[]{:S(2)}) collective-permute-start(f32[1,1024]{1,0:T(1,128)S(1)} %get-tuple-element.28.refs_0_), channel_id=1, source_target_pairs={{0,3},{1,2},{2,1},{3,0},{4,7},{5,6},{6,5},{7,4},{8,11},{9,10},{10,... | collective-permute-start | bytes 12296 | tf_op jit(solution)/shard_map/ppermute | solution.py:17
  16.5 2.8 %collective-permute-start.9 = (bf16[96,2048]{1,0:T(8,128)(2,1)S(1)}, bf16[96,2048]{1,0:T(8,128)(2,1)}, u32[]{:S(2)}, u32[]{:S(2)}) collective-permute-start(bf16[96,2048]{1,0:T(8,128)(2,1)S(1)} %get-tuple-element.32.refs_2_), channel_id=1, source_target_pairs={{0,3},{1,2},{2,1},{3,0},{4,7},{5,6},{6,5},{7,4},{8,11},{9,10},{10,... | collective-permute-start | bytes 1179656 | tf_op jit(solution)/shard_map/ppermute | solution.py:17
  19.9 1.3 reduce-window.8
  21.2 1.4 fusion.18
  22.6 0.8 select_reduce_fusion.1
  24.0 0.7 fusion.23
  24.7 1.3 pad_add_fusion.at_ref
  26.0 0.7 broadcast_in_dim.86
  26.7 0.7 broadcast_in_dim.91
  27.5 1.2 fusion.11
  28.9 2.0 %collective-permute-start = (bf16[768,128]{1,0:T(8,128)(2,1)S(1)}, bf16[768,128]{1,0:T(8,128)(2,1)S(1)}, u32[]{:S(2)}, u32[]{:S(2)}) collective-permute-start(bf16[768,128]{1,0:T(8,128)(2,1)S(1)} %fusion.11), channel_id=1, source_target_pairs={{0,4},{4,0},{8,12},{12,8},{1,5},{5,1},{9,13},{13,9},{2,6},{6,2},{1... | collective-permute-start | bytes 589832 | tf_op jit(solution)/shard_map/ppermute | solution.py:17
  30.9 2.2 %copy-done.1 = bf16[1024,2048]{1,0:T(8,128)(2,1)S(1)} copy-done((bf16[1024,2048]{1,0:T(8,128)(2,1)S(1)}, bf16[1024,2048]{1,0:T(8,128)(2,1)}, u32[]{:S(2)}) %copy-start.1) | copy-done | bytes 4194328
  33.1 2.2 %copy-done.2 = bf16[2048,1024]{1,0:T(8,128)(2,1)S(1)} copy-done((bf16[2048,1024]{1,0:T(8,128)(2,1)S(1)}, bf16[2048,1024]{1,0:T(8,128)(2,1)}, u32[]{:S(2)}) %copy-start.2) | copy-done | bytes 4194328
  35.2 6.5 %shard_map.138 = (bf16[4,2048,128]{2,1,0:T(8,128)(2,1)S(1)}, f32[1,2048]{1,0:T(1,128)S(1)}) custom-call(s32[3]{0:T(128)S(1)} %pad_add_fusion.at_ref, bf16[1024,2048]{1,0:T(8,128)(2,1)S(1)} %copy-done.1, bf16[2048,1024]{1,0:T(8,128)(2,1)S(1)} %copy-done.2, bf16[1024,1024]{1,0:T(8,128)(2,1)S(1)} %copy-done.3, f32[1,1024]{1,0:T(1,128)S(1)} %get-tuple-element.28.refs_0_, ...), custom_call_target="tpu_custom_call" | custom-call | flops 2147483648 | bytes 9437184 | tf_op jit(solution)/shard_map/pallas_call | solution.py:235
  42.0 2.7 %collective-permute-start.1 = (bf16[768,128]{1,0:T(8,128)(2,1)S(1)}, bf16[768,128]{1,0:T(8,128)(2,1)S(1)}, u32[]{:S(2)}, u32[]{:S(2)}) collective-permute-start(bf16[768,128]{1,0:T(8,128)(2,1)S(1)} %fusion.22), channel_id=1, source_target_pairs={{0,8},{4,12},{8,0},{12,4},{1,9},{5,13},{9,1},{13,5},{2,10},{6,14},... | collective-permute-start | bytes 589832 | tf_op jit(solution)/shard_map/ppermute | solution.py:17
  44.7 1.0 dynamic-slice_bitcast_fusion
  45.7 1.5 collective-permute-start.6
  47.2 4.5 %collective-permute-done.1 = bf16[768,128]{1,0:T(8,128)(2,1)S(1)} collective-permute-done((bf16[768,128]{1,0:T(8,128)(2,1)S(1)}, bf16[768,128]{1,0:T(8,128)(2,1)S(1)}, u32[]{:S(2)}, u32[]{:S(2)}) %collective-permute-start.1) | collective-permute-done | bytes 196640 | tf_op jit(solution)/shard_map/ppermute | solution.py:17
  51.7 2.5 %collective-permute-start.5 = (bf16[2048,128]{1,0:T(8,128)(2,1)}, bf16[2048,128]{1,0:T(8,128)(2,1)}, u32[]{:S(2)}, u32[]{:S(2)}) collective-permute-start(bf16[2048,128]{1,0:T(8,128)(2,1)} %get-tuple-element.75), channel_id=1, source_target_pairs={{0,4},{1,5},{2,6},{3,7},{16,20},{17,21},{18,22},{19,23}} | collective-permute-start | bytes 1572872 | tf_op jit(solution)/shard_map/ppermute | solution.py:77
  54.8 9.4 %collective-permute-done.5 = bf16[2048,128]{1,0:T(8,128)(2,1)} collective-permute-done((bf16[2048,128]{1,0:T(8,128)(2,1)}, bf16[2048,128]{1,0:T(8,128)(2,1)}, u32[]{:S(2)}, u32[]{:S(2)}) %collective-permute-start.5) | collective-permute-done | bytes 524320 | tf_op jit(solution)/shard_map/ppermute | solution.py:77
  64.2 3.4 %copy-done.12 = bf16[2048,2048]{1,0:T(8,128)(2,1)S(1)} copy-done((bf16[2048,2048]{1,0:T(8,128)(2,1)S(1)}, bf16[2048,2048]{1,0:T(8,128)(2,1)}, u32[]{:S(2)}) %copy-start.12) | copy-done | bytes 8388632
  67.5 5.7 %shard_map.139 = (bf16[384,2048]{1,0:T(8,128)(2,1)S(1)}, bf16[384,2048]{1,0:T(8,128)(2,1)S(1)}) custom-call(s32[1]{0:T(128)} %bitcast.8.refs_0_, bf16[2048,2048]{1,0:T(8,128)(2,1)S(1)} %copy-done.12, bf16[96,2048]{1,0:T(8,128)(2,1)S(1)} %get-tuple-element.32.refs_2_, bf16[96,2048]{1,0:T(8,128)(2,1)S(1)} %collective-permute-done.7.refs_3_, ...), custom_call_target="tpu_custom_call" | custom-call | flops 3221225472 | bytes 13107200 | tf_op jit(solution)/shard_map/pallas_call | solution.py:127
  73.3 1.1 copy-done.8
  74.4 1.1 copy-done.9
  75.7 1.4 collective-permute-start.13
  77.1 1.5 collective-permute-start.12
  78.6 0.6 collective-permute-start.11
  79.2 3.6 %collective-permute-done.13 = bf16[768,128]{1,0:T(8,128)(2,1)S(1)} collective-permute-done((bf16[768,128]{1,0:T(8,128)(2,1)S(1)}, bf16[768,128]{1,0:T(8,128)(2,1)S(1)}, u32[]{:S(2)}, u32[]{:S(2)}) %collective-permute-start.13) | collective-permute-done | bytes 196640 | tf_op jit(solution)/shard_map/ppermute | solution.py:17
  82.8 3.4 %collective-permute-done.12 = bf16[768,128]{1,0:T(8,128)(2,1)S(1)} collective-permute-done((bf16[768,128]{1,0:T(8,128)(2,1)S(1)}, bf16[768,128]{1,0:T(8,128)(2,1)S(1)}, u32[]{:S(2)}, u32[]{:S(2)}) %collective-permute-start.12) | collective-permute-done | bytes 196640 | tf_op jit(solution)/shard_map/ppermute | solution.py:17
  86.2 0.7 copy-done.23
  86.9 1.1 broadcast_select_fusion.13
  88.0 1.0 pad_maximum_fusion.2
  89.5 2.5 %fusion.6 = (bf16[2048,128]{1,0:T(8,128)(2,1)}, bf16[2048,128]{1,0:T(8,128)(2,1)}) fusion(bf16[2048,128]{1,0:T(8,128)(2,1)} %collective-permute-done.6, bf16[4,2048,128]{2,1,0:T(8,128)(2,1)S(1)} %copy-done.5, s32[]{:T(128)S(6)} %min.22, bf16[2048,128]{1,0:T(8,128)(2,1)} %collective-permute-done.5, s32[]{:T(128)S(6)} %min.21), kind=kLoop, calls=%fused_computation.16 | loop fusion | flops 2097152 | bytes 3145736 | tf_op jit(solution)/shard_map/convert_element_type | solution.py:74
  92.0 0.8 collective-permute-start.16
  92.9 5.8 %collective-permute-start.15 = (bf16[2048,128]{1,0:T(8,128)(2,1)}, bf16[2048,128]{1,0:T(8,128)(2,1)}, u32[]{:S(2)}, u32[]{:S(2)}) collective-permute-start(bf16[2048,128]{1,0:T(8,128)(2,1)} %get-tuple-element.73), channel_id=1, source_target_pairs={{0,4},{4,8},{1,5},{5,9},{2,6},{6,10},{3,7},{7,11},{16,20},{20,24},... | collective-permute-start | bytes 1572872 | tf_op jit(solution)/shard_map/ppermute | solution.py:77
  98.6 1.9 copy.23
  100.8 1.9 constant_dynamic-slice_fusion.1
  102.7 2.8 %broadcast_select_fusion.1 = (bf16[768,512]{1,0:T(8,128)(2,1)}, bf16[768,512]{1,0:T(8,128)(2,1)}) fusion(bf16[768,512]{1,0:T(8,128)(2,1)} %collective-permute-done.14, pred[]{:T(512)S(6)} %ne.19, bf16[768,128]{1,0:T(8,128)(2,1)S(1)} %copy-done.16, bf16[768,128]{1,0:T(8,128)(2,1)S(1)} %get-tuple-element.84, bf16[768,128]{1,0:T(8,128)(2,1)S(1)} %get-tuple-element.83, ...), kind=kLoop, calls=%fused_computation.22 | loop fusion | flops 3932160 | bytes 3145729 | tf_op jit(solution)/shard_map/jit(_where)/select_n | solution.py:41
  105.5 16.8 %reduce-scatter.2.cloned.1.call-done = bf16[96,2048]{1,0:T(8,128)(2,1)} async-done(((bf16[384,2048]{1,0:T(8,128)(2,1)}), bf16[96,2048]{1,0:T(8,128)(2,1)}) %reduce-scatter.2.cloned.1.call-update) | async-done | bytes 393232 | tf_op jit(solution)/shard_map/reduce_scatter | solution.py:447
  122.3 1.1 add_convert_fusion.rows_ref
  123.5 0.7 copy-done.20
  124.2 3.7 %fusion.9.grad_ref = f32[96,2048]{1,0:T(8,128)S(1)} fusion(bf16[2048,1024]{1,0:T(8,128)(2,1)} %weight_ref.1, s32[]{:T(128)S(6)} %select_n.229, bf16[768,512]{1,0:T(8,128)(2,1)} %get-tuple-element.76, bf16[768,512]{1,0:T(8,128)(2,1)} %get-tuple-element.77), kind=kOutput, calls=%fused_computation.30 | convolution fusion | flops 403046400 | bytes 6553604 | tf_op jit(solution)/shard_map/dot_general | solution.py:458
  128.0 0.8 pad_maximum_fusion.4
  128.8 0.9 constant_dynamic-slice_fusion
  129.8 5.6 %fusion.grad_ref = f32[768,1024]{1,0:T(8,128)} fusion(bf16[2048,1024]{1,0:T(8,128)(2,1)} %weight_ref.1, s32[]{:T(128)S(6)} %select_n.224, bf16[768,512]{1,0:T(8,128)(2,1)} %get-tuple-element.77, bf16[768,512]{1,0:T(8,128)(2,1)} %get-tuple-element.76), kind=kOutput, calls=%fused_computation.2 | convolution fusion | flops 1613758464 | bytes 6815748 | tf_op jit(solution)/shard_map/dot_general | solution.py:454
  135.6 2.5 %collective-permute-start.19 = (f32[2,128]{1,0:T(2,128)S(1)}, f32[2,128]{1,0:T(2,128)S(1)}, u32[]{:S(2)}, u32[]{:S(2)}) collective-permute-start(f32[2,128]{1,0:T(2,128)S(1)} %shard_map.140), channel_id=1, source_target_pairs={{0,3},{1,2},{2,1},{3,0},{4,7},{5,6},{6,5},{7,4},{8,11},{9,10},{10,... | collective-permute-start | bytes 3080 | tf_op jit(solution)/shard_map/ppermute | solution.py:17
  139.2 0.8 pad_maximum_fusion.3.cot_ref
  140.1 1.5 collective-permute-done.18
  142.3 1.5 collective-permute-start.21
  143.8 2.9 %collective-permute-start.20 = (f32[3328]{0:T(1024)S(1)}, f32[3328]{0:T(1024)S(1)}, u32[]{:S(2)}, u32[]{:S(2)}) collective-permute-start(f32[3328]{0:T(1024)S(1)} %pad_maximum_fusion.9), channel_id=1, source_target_pairs={{0,12},{4,8},{8,4},{12,0},{1,13},{5,9},{9,5},{13,1},{2,14},{6,10},... | collective-permute-start | bytes 39944 | tf_op jit(solution)/shard_map/ppermute | solution.py:17
  146.7 1.7 maximum_bitcast_fusion.act_ref
  148.4 1.2 collective-permute-done.20
  149.9 2.3 %fusion.4 = (bf16[2048,128]{1,0:T(8,128)(2,1)}, bf16[2048,128]{1,0:T(8,128)(2,1)}) fusion(bf16[2048,128]{1,0:T(8,128)(2,1)} %collective-permute-done.15, bf16[4,2048,128]{2,1,0:T(8,128)(2,1)S(1)} %copy-done.6, s32[]{:T(128)S(6)} %min.23, bf16[2048,128]{1,0:T(8,128)(2,1)S(1)} %copy-done.21, s32[]{:T(128)S(6)} %min.24), kind=kLoop, calls=%fused_computation.12 | loop fusion | flops 2097152 | bytes 3145736 | tf_op jit(solution)/shard_map/convert_element_type | solution.py:74
  152.3 2.9 %collective-permute-start.26 = (bf16[2048,128]{1,0:T(8,128)(2,1)}, bf16[2048,128]{1,0:T(8,128)(2,1)}, u32[]{:S(2)}, u32[]{:S(2)}) collective-permute-start(bf16[2048,128]{1,0:T(8,128)(2,1)} %get-tuple-element.70), channel_id=1, source_target_pairs={{0,4},{4,8},{8,12},{1,5},{5,9},{9,13},{2,6},{6,10},{10,14},{3,7},{... | collective-permute-start | bytes 1572872 | tf_op jit(solution)/shard_map/ppermute | solution.py:77
  155.2 1.5 collective-permute-start.27
  158.0 11.8 %all-gather.2.cloned.1.call-done.rows_ref = bf16[768,1024]{1,0:T(8,128)(2,1)} async-done(((bf16[192,1024]{1,0:T(8,128)(2,1)}), bf16[768,1024]{1,0:T(8,128)(2,1)}) %all-gather.2.cloned.1.call-update) | async-done | bytes 1572880 | tf_op jit(solution)/shard_map/all_gather | solution.py:477
  169.8 5.7 %shard_map.141 = (bf16[768,1024]{1,0:T(8,128)(2,1)}, f32[1024,128]{1,0:T(8,128)}, bf16[1024,128]{1,0:T(8,128)(2,1)}, f32[2,1024]{1,0:T(2,128)}) custom-call(s32[1]{0:T(128)} %bitcast.4.core_ref, f32[768,1024]{1,0:T(8,128)} %fusion.grad_ref, f32[1,1024]{1,0:T(1,128)} %bitcast.66, bf16[768,256]{1,0:T(8,128)(2,1)} %pad_maximum_fusion.3.cot_ref, ...), custom_call_target="tpu_custom_call" | custom-call | flops 402653184 | bytes 6291456 | tf_op jit(solution)/shard_map/pallas_call | solution.py:335
  176.0 1.4 copy-done.7
  177.4 6.9 %shard_map.142 = f32[16384,128]{1,0:T(8,128)} custom-call(bf16[2048,768]{1,0:T(8,128)(2,1)S(1)} %maximum_bitcast_fusion.act_ref, bf16[768,1024]{1,0:T(8,128)(2,1)S(1)} %copy-done.7), custom_call_target="tpu_custom_call" | custom-call | flops 3221225472 | bytes 13107200 | tf_op jit(solution)/shard_map/pallas_call | solution.py:365
  184.3 0.6 pad_maximum_fusion.12
  185.6 2.7 %fusion.2 = f32[2048,128]{1,0:T(8,128)} fusion(f32[1024,128]{1,0:T(8,128)S(1)} %get-tuple-element.81, f32[1024,128]{1,0:T(8,128)S(1)} %get-tuple-element.80, bf16[2048,128]{1,0:T(8,128)(2,1)} %collective-permute-done.27, bf16[2048,128]{1,0:T(8,128)(2,1)} %collective-permute-done.26, f32[2048]{0:T(1024)S(1)} %copy-done.11, bf16[4,2048,128]{2,1,0:T(8,128)(2,1)} %copy-done.4, ...), kind=kLoop, calls=%fused_computation.8 | loop fusion | flops 2097152 | bytes 3678212 | tf_op jit(solution)/shard_map/mul | solution.py:504
  (120 shorter events, 8.8 us)
Async XLA Ops:
  7.2 115.1 %reduce-scatter.2.cloned.1.call-start = ((), (), s32[]{:S(2)}) async-start(), calls=%async_computation.1 | async-start | bytes 1966080 | tf_op jit(solution)/shard_map/reduce_scatter | solution.py:447
  7.2 2.2 %copy-start = (bf16[1024,2048]{1,0:T(8,128)(2,1)S(1)}, bf16[1024,2048]{1,0:T(8,128)(2,1)}, u32[]{:S(2)}) copy-start(bf16[1024,2048]{1,0:T(8,128)(2,1)} %text_ref.3) | copy-start | bytes 12582916
  9.4 1.1 copy-start.10
  10.5 20.3 %copy-start.3 = (bf16[1024,1024]{1,0:T(8,128)(2,1)S(1)}, bf16[1024,1024]{1,0:T(8,128)(2,1)}, u32[]{:S(2)}) copy-start(bf16[1024,1024]{1,0:T(8,128)(2,1)} %cot_ref.1) | copy-start | bytes 6291460
  11.9 12.1 %slice-start = ((bf16[1024,1024]{1,0:T(8,128)(2,1)}), bf16[512,1024]{1,0:T(8,128)(2,1)S(1)}, s32[]{:S(2)}) async-start(bf16[1024,1024]{1,0:T(8,128)(2,1)} %cot_ref.1), calls=%async_computation.3 | async-start | bytes 2097152 | tf_op jit(solution)/shard_map/slice | solution.py:436
  11.9 16.8 %collective-permute-start.4 = (f32[1,1024]{1,0:T(1,128)S(1)}, f32[1,1024]{1,0:T(1,128)S(1)}, u32[]{:S(2)}, u32[]{:S(2)}) collective-permute-start(f32[1,1024]{1,0:T(1,128)S(1)} %get-tuple-element.28.refs_0_), channel_id=1, source_target_pairs={{0,3},{1,2},{2,1},{3,0},{4,7},{5,6},{6,5},{7,4},{8,11},{9,10},{10,... | collective-permute-start | bytes 12296 | tf_op jit(solution)/shard_map/ppermute | solution.py:17
  15.9 13.0 %collective-permute-start.3 = (f32[1,1024]{1,0:T(1,128)S(1)}, f32[1,1024]{1,0:T(1,128)S(1)}, u32[]{:S(2)}, u32[]{:S(2)}) collective-permute-start(f32[1,1024]{1,0:T(1,128)S(1)} %get-tuple-element.28.refs_0_), channel_id=1, source_target_pairs={{0,2},{1,3},{2,0},{3,1},{4,6},{5,7},{6,4},{7,5},{8,10},{9,11},{10,... | collective-permute-start | bytes 12296 | tf_op jit(solution)/shard_map/ppermute | solution.py:17
  16.4 14.5 %collective-permute-start.2 = (f32[1,1024]{1,0:T(1,128)S(1)}, f32[1,1024]{1,0:T(1,128)S(1)}, u32[]{:S(2)}, u32[]{:S(2)}) collective-permute-start(f32[1,1024]{1,0:T(1,128)S(1)} %get-tuple-element.28.refs_0_), channel_id=1, source_target_pairs={{0,1},{1,0},{2,3},{3,2},{4,5},{5,4},{6,7},{7,6},{8,9},{9,8},{10,11... | collective-permute-start | bytes 12296 | tf_op jit(solution)/shard_map/ppermute | solution.py:17
  16.5 38.2 %collective-permute-start.9 = (bf16[96,2048]{1,0:T(8,128)(2,1)S(1)}, bf16[96,2048]{1,0:T(8,128)(2,1)}, u32[]{:S(2)}, u32[]{:S(2)}) collective-permute-start(bf16[96,2048]{1,0:T(8,128)(2,1)S(1)} %get-tuple-element.32.refs_2_), channel_id=1, source_target_pairs={{0,3},{1,2},{2,1},{3,0},{4,7},{5,6},{6,5},{7,4},{8,11},{9,10},{10,... | collective-permute-start | bytes 1179656 | tf_op jit(solution)/shard_map/ppermute | solution.py:17
  19.3 35.4 %collective-permute-start.8 = (bf16[96,2048]{1,0:T(8,128)(2,1)S(1)}, bf16[96,2048]{1,0:T(8,128)(2,1)}, u32[]{:S(2)}, u32[]{:S(2)}) collective-permute-start(bf16[96,2048]{1,0:T(8,128)(2,1)S(1)} %get-tuple-element.32.refs_2_), channel_id=1, source_target_pairs={{0,2},{1,3},{2,0},{3,1},{4,6},{5,7},{6,4},{7,5},{8,10},{9,11},{10,... | collective-permute-start | bytes 1179656 | tf_op jit(solution)/shard_map/ppermute | solution.py:17
  27.5 14.3 %copy-start.18 = (bf16[256,128]{1,0:T(8,128)(2,1)S(1)}, bf16[256,128]{1,0:T(8,128)(2,1)}, u32[]{:S(2)}) copy-start(bf16[256,128]{1,0:T(8,128)(2,1)} %get-tuple-element.78) | copy-start | bytes 196612
  27.5 14.3 %copy-start.19 = (bf16[256,128]{1,0:T(8,128)(2,1)S(1)}, bf16[256,128]{1,0:T(8,128)(2,1)}, u32[]{:S(2)}) copy-start(bf16[256,128]{1,0:T(8,128)(2,1)} %get-tuple-element.79) | copy-start | bytes 196612
  28.7 26.1 %collective-permute-start.7 = (bf16[96,2048]{1,0:T(8,128)(2,1)S(1)}, bf16[96,2048]{1,0:T(8,128)(2,1)S(1)}, u32[]{:S(2)}, u32[]{:S(2)}) collective-permute-start(bf16[96,2048]{1,0:T(8,128)(2,1)S(1)} %get-tuple-element.32.refs_2_), channel_id=1, source_target_pairs={{0,1},{1,0},{2,3},{3,2},{4,5},{5,4},{6,7},{7,6},{8,9},{9,8},{10,11... | collective-permute-start | bytes 1179656 | tf_op jit(solution)/shard_map/ppermute | solution.py:17
  28.9 12.8 %collective-permute-start = (bf16[768,128]{1,0:T(8,128)(2,1)S(1)}, bf16[768,128]{1,0:T(8,128)(2,1)S(1)}, u32[]{:S(2)}, u32[]{:S(2)}) collective-permute-start(bf16[768,128]{1,0:T(8,128)(2,1)S(1)} %fusion.11), channel_id=1, source_target_pairs={{0,4},{4,0},{8,12},{12,8},{1,5},{5,1},{9,13},{13,9},{2,6},{6,2},{1... | collective-permute-start | bytes 589832 | tf_op jit(solution)/shard_map/ppermute | solution.py:17
  30.9 2.2 %copy-start.1 = (bf16[1024,2048]{1,0:T(8,128)(2,1)S(1)}, bf16[1024,2048]{1,0:T(8,128)(2,1)}, u32[]{:S(2)}) copy-start(bf16[1024,2048]{1,0:T(8,128)(2,1)} %text_ref.3) | copy-start | bytes 12582916
  33.0 2.2 %copy-start.2 = (bf16[2048,1024]{1,0:T(8,128)(2,1)S(1)}, bf16[2048,1024]{1,0:T(8,128)(2,1)}, u32[]{:S(2)}) copy-start(bf16[2048,1024]{1,0:T(8,128)(2,1)} %weight_ref.1) | copy-start | bytes 12582916
  41.7 3.0 %copy-start.4 = (bf16[4,2048,128]{2,1,0:T(8,128)(2,1)}, bf16[4,2048,128]{2,1,0:T(8,128)(2,1)S(1)}, u32[]{:S(2)}) copy-start(bf16[4,2048,128]{2,1,0:T(8,128)(2,1)S(1)} %get-tuple-element.30) | copy-start | bytes 6291460
  42.0 9.7 %collective-permute-start.1 = (bf16[768,128]{1,0:T(8,128)(2,1)S(1)}, bf16[768,128]{1,0:T(8,128)(2,1)S(1)}, u32[]{:S(2)}, u32[]{:S(2)}) collective-permute-start(bf16[768,128]{1,0:T(8,128)(2,1)S(1)} %fusion.22), channel_id=1, source_target_pairs={{0,8},{4,12},{8,0},{12,4},{1,9},{5,13},{9,1},{13,5},{2,10},{6,14},... | collective-permute-start | bytes 589832 | tf_op jit(solution)/shard_map/ppermute | solution.py:17
  45.7 9.0 %collective-permute-start.6 = (bf16[2048,128]{1,0:T(8,128)(2,1)}, bf16[2048,128]{1,0:T(8,128)(2,1)}, u32[]{:S(2)}, u32[]{:S(2)}) collective-permute-start(bf16[2048,128]{1,0:T(8,128)(2,1)} %get-tuple-element.74), channel_id=1, source_target_pairs={{12,8},{13,9},{14,10},{15,11},{28,24},{29,25},{30,26},{31,27}} | collective-permute-start | bytes 1572872 | tf_op jit(solution)/shard_map/ppermute | solution.py:77
  51.7 12.4 %collective-permute-start.5 = (bf16[2048,128]{1,0:T(8,128)(2,1)}, bf16[2048,128]{1,0:T(8,128)(2,1)}, u32[]{:S(2)}, u32[]{:S(2)}) collective-permute-start(bf16[2048,128]{1,0:T(8,128)(2,1)} %get-tuple-element.75), channel_id=1, source_target_pairs={{0,4},{1,5},{2,6},{3,7},{16,20},{17,21},{18,22},{19,23}} | collective-permute-start | bytes 1572872 | tf_op jit(solution)/shard_map/ppermute | solution.py:77
  54.6 87.5 %copy-start.24 = (f32[3072]{0:T(1024)}, f32[3072]{0:T(1024)S(1)}, u32[]{:S(2)}) copy-start(f32[3072]{0:T(1024)S(1)} %pad_maximum_fusion.11) | copy-start | bytes 36868
  64.2 3.4 %copy-start.12 = (bf16[2048,2048]{1,0:T(8,128)(2,1)S(1)}, bf16[2048,2048]{1,0:T(8,128)(2,1)}, u32[]{:S(2)}) copy-start(bf16[2048,2048]{1,0:T(8,128)(2,1)} %refs_1_.1) | copy-start | bytes 25165828
  73.3 1.1 copy-start.8
  74.4 1.1 copy-start.9
  75.6 13.4 %copy-start.11 = (f32[2048]{0:T(1024)S(1)}, f32[2048]{0:T(1024)}, u32[]{:S(2)}) copy-start(f32[2048]{0:T(1024)} %param.14) | copy-start | bytes 24580
  75.6 14.0 %copy-start.5 = (bf16[4,2048,128]{2,1,0:T(8,128)(2,1)S(1)}, bf16[4,2048,128]{2,1,0:T(8,128)(2,1)}, u32[]{:S(2)}) copy-start(bf16[4,2048,128]{2,1,0:T(8,128)(2,1)} %copy-done.4) | copy-start | bytes 6291460
  75.6 94.2 %all-gather.2.cloned.1.call-start = ((), (), s32[]{:S(2)}) async-start(), calls=%async_computation.2 | async-start | bytes 1966080 | tf_op jit(solution)/shard_map/all_gather | solution.py:477
  75.7 7.2 %collective-permute-start.13 = (bf16[768,128]{1,0:T(8,128)(2,1)S(1)}, bf16[768,128]{1,0:T(8,128)(2,1)S(1)}, u32[]{:S(2)}, u32[]{:S(2)}) collective-permute-start(bf16[768,128]{1,0:T(8,128)(2,1)S(1)} %add.101), channel_id=1, source_target_pairs={{0,1},{1,0},{2,3},{3,2},{4,5},{5,4},{6,7},{7,6},{8,9},{9,8},{10,11... | collective-permute-start | bytes 589832 | tf_op jit(solution)/shard_map/ppermute | solution.py:17
  77.1 9.1 %collective-permute-start.12 = (bf16[768,128]{1,0:T(8,128)(2,1)S(1)}, bf16[768,128]{1,0:T(8,128)(2,1)S(1)}, u32[]{:S(2)}, u32[]{:S(2)}) collective-permute-start(bf16[768,128]{1,0:T(8,128)(2,1)S(1)} %add.101), channel_id=1, source_target_pairs={{0,2},{1,3},{2,0},{3,1},{4,6},{5,7},{6,4},{7,5},{8,10},{9,11},{10,... | collective-permute-start | bytes 589832 | tf_op jit(solution)/shard_map/ppermute | solution.py:17
  78.6 8.2 %collective-permute-start.11 = (bf16[768,128]{1,0:T(8,128)(2,1)S(1)}, bf16[768,128]{1,0:T(8,128)(2,1)}, u32[]{:S(2)}, u32[]{:S(2)}) collective-permute-start(bf16[768,128]{1,0:T(8,128)(2,1)S(1)} %add.101), channel_id=1, source_target_pairs={{0,3},{1,2},{2,1},{3,0},{4,7},{5,6},{6,5},{7,4},{8,11},{9,10},{10,... | collective-permute-start | bytes 589832 | tf_op jit(solution)/shard_map/ppermute | solution.py:17
  86.2 0.7 copy-start.23
  88.0 4.1 %copy-start.15 = (bf16[768,128]{1,0:T(8,128)(2,1)}, bf16[768,128]{1,0:T(8,128)(2,1)S(1)}, u32[]{:S(2)}) copy-start(bf16[768,128]{1,0:T(8,128)(2,1)S(1)} %get-tuple-element.85) | copy-start | bytes 589828
  88.9 13.8 %collective-permute-start.14 = (bf16[768,512]{1,0:T(8,128)(2,1)}, bf16[768,512]{1,0:T(8,128)(2,1)}, u32[]{:S(2)}, u32[]{:S(2)}) collective-permute-start(bf16[768,512]{1,0:T(8,128)(2,1)} %pad_maximum_fusion.2), channel_id=1, source_target_pairs={{0,16},{16,0},{1,17},{17,1},{2,18},{18,2},{3,19},{19,3},{4,20},{20... | collective-permute-start | bytes 2359304 | tf_op jit(solution)/shard_map/ppermute | solution.py:17
  92.0 10.7 %copy-start.16 = (bf16[768,128]{1,0:T(8,128)(2,1)S(1)}, bf16[768,128]{1,0:T(8,128)(2,1)}, u32[]{:S(2)}) copy-start(bf16[768,128]{1,0:T(8,128)(2,1)} %copy-done.15) | copy-start | bytes 589828
  92.0 31.3 %collective-permute-start.16 = (bf16[2048,128]{1,0:T(8,128)(2,1)}, bf16[2048,128]{1,0:T(8,128)(2,1)S(1)}, u32[]{:S(2)}, u32[]{:S(2)}) collective-permute-start(bf16[2048,128]{1,0:T(8,128)(2,1)} %get-tuple-element.72), channel_id=1, source_target_pairs={{12,8},{8,4},{13,9},{9,5},{14,10},{10,6},{15,11},{11,7},{28,24},{2... | collective-permute-start | bytes 1572872 | tf_op jit(solution)/shard_map/ppermute | solution.py:77
  92.9 30.5 %collective-permute-start.15 = (bf16[2048,128]{1,0:T(8,128)(2,1)}, bf16[2048,128]{1,0:T(8,128)(2,1)}, u32[]{:S(2)}, u32[]{:S(2)}) collective-permute-start(bf16[2048,128]{1,0:T(8,128)(2,1)} %get-tuple-element.73), channel_id=1, source_target_pairs={{0,4},{4,8},{1,5},{5,9},{2,6},{6,10},{3,7},{7,11},{16,20},{20,24},... | collective-permute-start | bytes 1572872 | tf_op jit(solution)/shard_map/ppermute | solution.py:77
  100.5 22.8 %copy-start.13 = (bf16[384,2048]{0,1:T(8,128)(2,1)}, bf16[384,2048]{0,1:T(8,128)(2,1)S(1)}, u32[]{:S(2)}) copy-start(bf16[384,2048]{0,1:T(8,128)(2,1)S(1)} %copy.23) | copy-start | bytes 4718596
  100.5 21.8 %copy-start.26 = (f32[2048]{0:T(1024)S(1)}, f32[2048]{0:T(1024)}, u32[]{:S(2)}) copy-start(f32[2048]{0:T(1024)} %param.12) | copy-start | bytes 24580
  100.5 46.1 %collective-permute-start.10 = (bf16[384,2048]{0,1:T(8,128)(2,1)S(1)}, bf16[384,2048]{0,1:T(8,128)(2,1)}, u32[]{:S(2)}, u32[]{:S(2)}) collective-permute-start(bf16[384,2048]{0,1:T(8,128)(2,1)S(1)} %copy.23), channel_id=1, source_target_pairs={{0,16},{16,0},{1,17},{17,1},{2,18},{18,2},{3,19},{19,3},{4,20},{20... | collective-permute-start | bytes 4718600 | tf_op jit(solution)/shard_map/ppermute | solution.py:17
  123.4 0.8 copy-start.20
  123.4 4.5 %collective-permute-start.24 = (bf16[96,1024]{1,0:T(8,128)(2,1)S(1)}, bf16[96,1024]{1,0:T(8,128)(2,1)S(1)}, u32[]{:S(2)}, u32[]{:S(2)}) collective-permute-start(bf16[96,1024]{1,0:T(8,128)(2,1)S(1)} %broadcast_select_fusion.3), channel_id=1, source_target_pairs={{0,16},{16,0},{1,17},{17,1},{2,18},{18,2},{3,19},{19,3},{4,20},{20... | collective-permute-start | bytes 589832 | tf_op jit(solution)/shard_map/ppermute | solution.py:17
  129.8 9.4 %copy-start.17 = (bf16[768,128]{1,0:T(8,128)(2,1)S(1)}, bf16[768,128]{1,0:T(8,128)(2,1)}, u32[]{:S(2)}) copy-start(bf16[768,128]{1,0:T(8,128)(2,1)} %constant_dynamic-slice_fusion.1) | copy-start | bytes 589828
  135.4 11.3 %copy-start.14 = (bf16[384,2048]{0,1:T(8,128)(2,1)S(1)}, bf16[384,2048]{0,1:T(8,128)(2,1)}, u32[]{:S(2)}) copy-start(bf16[384,2048]{0,1:T(8,128)(2,1)} %copy-done.13) | copy-start | bytes 4718596
  135.6 4.5 %collective-permute-start.19 = (f32[2,128]{1,0:T(2,128)S(1)}, f32[2,128]{1,0:T(2,128)S(1)}, u32[]{:S(2)}, u32[]{:S(2)}) collective-permute-start(f32[2,128]{1,0:T(2,128)S(1)} %shard_map.140), channel_id=1, source_target_pairs={{0,3},{1,2},{2,1},{3,0},{4,7},{5,6},{6,5},{7,4},{8,11},{9,10},{10,... | collective-permute-start | bytes 3080 | tf_op jit(solution)/shard_map/ppermute | solution.py:17
  138.1 3.6 %collective-permute-start.18 = (f32[2,128]{1,0:T(2,128)S(1)}, f32[2,128]{1,0:T(2,128)S(1)}, u32[]{:S(2)}, u32[]{:S(2)}) collective-permute-start(f32[2,128]{1,0:T(2,128)S(1)} %shard_map.140), channel_id=1, source_target_pairs={{0,2},{1,3},{2,0},{3,1},{4,6},{5,7},{6,4},{7,5},{8,10},{9,11},{10,... | collective-permute-start | bytes 3080 | tf_op jit(solution)/shard_map/ppermute | solution.py:17
  138.6 3.6 %collective-permute-start.17 = (f32[2,128]{1,0:T(2,128)S(1)}, f32[2,128]{1,0:T(2,128)S(1)}, u32[]{:S(2)}, u32[]{:S(2)}) collective-permute-start(f32[2,128]{1,0:T(2,128)S(1)} %shard_map.140), channel_id=1, source_target_pairs={{0,1},{1,0},{2,3},{3,2},{4,5},{5,4},{6,7},{7,6},{8,9},{9,8},{10,11... | collective-permute-start | bytes 3080 | tf_op jit(solution)/shard_map/ppermute | solution.py:17
  142.2 7.4 %copy-start.25 = (f32[3072]{0:T(1024)S(1)}, f32[3072]{0:T(1024)}, u32[]{:S(2)}) copy-start(f32[3072]{0:T(1024)} %copy-done.24) | copy-start | bytes 36868
  142.2 7.7 %copy-start.6 = (bf16[4,2048,128]{2,1,0:T(8,128)(2,1)S(1)}, bf16[4,2048,128]{2,1,0:T(8,128)(2,1)}, u32[]{:S(2)}) copy-start(bf16[4,2048,128]{2,1,0:T(8,128)(2,1)} %copy-done.4) | copy-start | bytes 6291460
  142.2 7.7 %copy-start.21 = (bf16[2048,128]{1,0:T(8,128)(2,1)S(1)}, bf16[2048,128]{1,0:T(8,128)(2,1)}, u32[]{:S(2)}) copy-start(bf16[2048,128]{1,0:T(8,128)(2,1)} %copy-done.20) | copy-start | bytes 1572868
  142.2 6.1 %collective-permute-start.22 = (f32[3328]{0:T(1024)S(1)}, f32[3328]{0:T(1024)S(1)}, u32[]{:S(2)}, u32[]{:S(2)}) collective-permute-start(f32[3328]{0:T(1024)S(1)} %pad_maximum_fusion.9), channel_id=1, source_target_pairs={{0,4},{4,0},{8,12},{12,8},{1,5},{5,1},{9,13},{13,9},{2,6},{6,2},{1... | collective-permute-start | bytes 39944 | tf_op jit(solution)/shard_map/ppermute | solution.py:17
  142.3 6.1 %collective-permute-start.21 = (f32[3328]{0:T(1024)S(1)}, f32[3328]{0:T(1024)S(1)}, u32[]{:S(2)}, u32[]{:S(2)}) collective-permute-start(f32[3328]{0:T(1024)S(1)} %pad_maximum_fusion.9), channel_id=1, source_target_pairs={{0,8},{4,12},{8,0},{12,4},{1,9},{5,13},{9,1},{13,5},{2,10},{6,14},... | collective-permute-start | bytes 39944 | tf_op jit(solution)/shard_map/ppermute | solution.py:17
  143.8 5.9 %collective-permute-start.20 = (f32[3328]{0:T(1024)S(1)}, f32[3328]{0:T(1024)S(1)}, u32[]{:S(2)}, u32[]{:S(2)}) collective-permute-start(f32[3328]{0:T(1024)S(1)} %pad_maximum_fusion.9), channel_id=1, source_target_pairs={{0,12},{4,8},{8,4},{12,0},{1,13},{5,9},{9,5},{13,1},{2,14},{6,10},... | collective-permute-start | bytes 39944 | tf_op jit(solution)/shard_map/ppermute | solution.py:17
  149.8 6.8 %collective-permute-start.23 = (f32[4096]{0:T(1024)S(1)}, f32[4096]{0:T(1024)S(1)}, u32[]{:S(2)}, u32[]{:S(2)}) collective-permute-start(f32[4096]{0:T(1024)S(1)} %pad_maximum_fusion.10), channel_id=1, source_target_pairs={{0,16},{16,0},{1,17},{17,1},{2,18},{18,2},{3,19},{19,3},{4,20},{20... | collective-permute-start | bytes 49160 | tf_op jit(solution)/shard_map/ppermute | solution.py:17
  152.3 33.3 %collective-permute-start.26 = (bf16[2048,128]{1,0:T(8,128)(2,1)}, bf16[2048,128]{1,0:T(8,128)(2,1)}, u32[]{:S(2)}, u32[]{:S(2)}) collective-permute-start(bf16[2048,128]{1,0:T(8,128)(2,1)} %get-tuple-element.70), channel_id=1, source_target_pairs={{0,4},{4,8},{8,12},{1,5},{5,9},{9,13},{2,6},{6,10},{10,14},{3,7},{... | collective-permute-start | bytes 1572872 | tf_op jit(solution)/shard_map/ppermute | solution.py:77
  155.2 30.4 %collective-permute-start.27 = (bf16[2048,128]{1,0:T(8,128)(2,1)}, bf16[2048,128]{1,0:T(8,128)(2,1)}, u32[]{:S(2)}, u32[]{:S(2)}) collective-permute-start(bf16[2048,128]{1,0:T(8,128)(2,1)} %get-tuple-element.71), channel_id=1, source_target_pairs={{12,8},{8,4},{4,0},{13,9},{9,5},{5,1},{14,10},{10,6},{6,2},{15,11}... | collective-permute-start | bytes 1572872 | tf_op jit(solution)/shard_map/ppermute | solution.py:77
  175.5 8.8 %collective-permute-start.25 = (f32[2,1024]{1,0:T(2,128)}, f32[2,1024]{1,0:T(2,128)S(1)}, u32[]{:S(2)}, u32[]{:S(2)}) collective-permute-start(f32[2,1024]{1,0:T(2,128)} %get-tuple-element.46), channel_id=1, source_target_pairs={{0,16},{16,0},{1,17},{17,1},{2,18},{18,2},{3,19},{19,3},{4,20},{20... | collective-permute-start | bytes 24584 | tf_op jit(solution)/shard_map/ppermute | solution.py:17
  175.5 10.1 %collective-permute-start.28 = (bf16[1024,128]{1,0:T(8,128)(2,1)}, bf16[1024,128]{1,0:T(8,128)(2,1)S(1)}, u32[]{:S(2)}, u32[]{:S(2)}) collective-permute-start(bf16[1024,128]{1,0:T(8,128)(2,1)} %get-tuple-element.49), channel_id=1, source_target_pairs={{0,16},{16,0},{1,17},{17,1},{2,18},{18,2},{3,19},{19,3},{4,20},{20... | collective-permute-start | bytes 786440 | tf_op jit(solution)/shard_map/ppermute | solution.py:17
  176.0 1.4 copy-start.7
  177.4 6.9 %copy-start.27 = (f32[2,1024]{1,0:T(2,128)S(1)}, f32[2,1024]{1,0:T(2,128)}, u32[]{:S(2)}) copy-start(f32[2,1024]{1,0:T(2,128)} %get-tuple-element.46) | copy-start | bytes 24580
  177.4 8.1 %copy-start.22 = (f32[1024,128]{1,0:T(8,128)S(1)}, f32[1024,128]{1,0:T(8,128)}, u32[]{:S(2)}) copy-start(f32[1024,128]{1,0:T(8,128)} %get-tuple-element.50) | copy-start | bytes 1572868
Sparse Core Ops, SparseCore 0:
  75.7 46.5 reduce-scatter.1
  128.9 40.8 all-gather.1

commit v8 on v7

--- a/solution.py
+++ b/solution.py
@@ -10,6 +10,7 @@
 MAXT = 2
 LANES = 128
 EPSILON = 1e-06
+VMEM = 60 * 1024 * 1024
 
 
 def swap(x, axis, mask):
@@ -140,7 +141,7 @@
             jax.ShapeDtypeStruct((total_rows, columns), jnp.bfloat16),
             jax.ShapeDtypeStruct((total_rows, features), jnp.bfloat16),
         ],
-        compiler_params=pltpu.CompilerParams(vmem_limit_bytes=40 * 1024 * 1024),
+        compiler_params=pltpu.CompilerParams(vmem_limit_bytes=VMEM),
         cost_estimate=pl.CostEstimate(
             flops=2 * total_rows * features * columns,
             bytes_accessed=2 * (features * columns + total_rows * (columns + 2 * features)),
@@ -149,10 +150,12 @@
     )(index, weight, *pieces)
 
 
-def opening_kernel(core_ref, text_ref, *refs):
-    del core_ref
-    sums_ref, act_ref = refs[-2:]
-    groups = refs[:-2]
+def opening_kernel(
+    core_ref, z_ref, t_ref, tiles_ref, owners_ref, text_ref, cot_ref, *refs
+):
+    del core_ref, t_ref
+    sums_ref, act_ref, given_ref = refs[-3:]
+    groups = refs[:-3]
 
     @pl.when(pl.program_id(0) == 0)
     def _():
@@ -161,46 +164,66 @@
             hidden = group[...].astype(jnp.float32)
             act = 0.5 * hidden * (1.0 + lax.erf(hidden * 0.7071067811865476))
             act_ref[i * rows : (i + 1) * rows, :] = act.astype(jnp.bfloat16)
+        for tile in range(given_ref.shape[0] // TILE):
+            start = owner = place = jnp.int32(0)
+            for s in range(tiles_ref.shape[0]):
+                inside = (tile >= start) & (tile < start + tiles_ref[s])
+                owner = jnp.where(inside, owners_ref[s], owner)
+                place = jnp.where(inside, tile - start, place)
+                start = start + tiles_ref[s]
+            at = pl.multiple_of(jnp.clip(place, 0, MAXT - 1) * TILE, TILE)
+            here = jnp.where(owner == z_ref[0], 1.0, 0.0)
+            rows_of_tile = cot_ref[pl.ds(at, TILE), :].astype(jnp.float32) * here
+            given_ref[tile * TILE : (tile + 1) * TILE, :] = rows_of_tile.astype(jnp.bfloat16)
 
     values = text_ref[...].astype(jnp.float32)
     sums_ref[...] = row_of(fold(values * values))
 
 
-def opening(core, text, hidden, groups, n_sec):
+def opening(core, z, t, tile_counts, owner_map, text, hidden, cot, groups, n_sec, n_tp, stream):
     seq_len, columns = text.shape
     rows, features = hidden.shape
     half = rows // (groups * n_sec)
+    share = cot.shape[1] // (n_sec * n_tp)
     step = 256
     part = [
-        pl.BlockSpec((half, features), lambda i, c, q=q: (q * n_sec + c[0], 0)) for q in range(groups)
+        pl.BlockSpec((half, features), lambda i, c, *_, q=q: (q * n_sec + c[0], 0))
+        for q in range(groups)
     ]
     return pl.pallas_call(
         opening_kernel,
         grid_spec=pltpu.PrefetchScalarGridSpec(
-            num_scalar_prefetch=1,
+            num_scalar_prefetch=5,
             grid=(seq_len // step,),
-            in_specs=[pl.BlockSpec((step, columns), lambda i, c: (i, 0))] + part,
+            in_specs=[
+                pl.BlockSpec((step, columns), lambda i, *_: (i, 0)),
+                pl.BlockSpec((MAXT * TILE, share), lambda i, c, z, t, *_: (0, c[0] * n_tp + t[0])),
+            ]
+            + part,
             out_specs=[
-                pl.BlockSpec((1, step), lambda i, c: (0, i)),
-                pl.BlockSpec((groups * half, features), lambda i, c: (0, 0)),
+                pl.BlockSpec((1, step), lambda i, *_: (0, i)),
+                pl.BlockSpec((groups * half, features), lambda i, *_: (0, 0)),
+                pl.BlockSpec((stream, share), lambda i, *_: (0, 0)),
             ],
         ),
         out_shape=[
             jax.ShapeDtypeStruct((1, seq_len), jnp.float32),
             jax.ShapeDtypeStruct((groups * half, features), jnp.bfloat16),
+            jax.ShapeDtypeStruct((stream, share), jnp.bfloat16),
         ],
-        compiler_params=pltpu.CompilerParams(vmem_limit_bytes=24 * 1024 * 1024),
+        compiler_params=pltpu.CompilerParams(vmem_limit_bytes=VMEM),
         cost_estimate=pl.CostEstimate(
             flops=2 * seq_len * columns + 40 * groups * half * features,
             bytes_accessed=2 * seq_len * columns,
             transcendentals=0,
         ),
-    )(core, text, *[hidden] * groups)
+    )(core, z, t, tile_counts, owner_map, text, cot, *[hidden] * groups)
 
 
 def text_kernel(
-    at_ref, text_ref, weight_ref, cot_ref, *refs
+    core_ref, z_ref, tiles_ref, texts_ref, owners_ref, text_ref, weight_ref, cot_ref, *refs
 ):
+    del core_ref
     moment_ref, gain_ref, long_ref, scaled_ref = refs[-4:]
     squares = refs[:-4]
     seq_len, width = cot_ref.shape
@@ -210,14 +233,20 @@
         parts = [r[...] for r in squares]
         while len(parts) > 1:
             parts = [parts[i] + parts[i + 1] for i in range(0, len(parts), 2)]
+        image_tiles = text_count = jnp.int32(0)
+        for s in range(owners_ref.shape[0]):
+            mine = owners_ref[s] == z_ref[0]
+            image_tiles = jnp.where(mine, tiles_ref[s], image_tiles)
+            text_count = jnp.where(mine, texts_ref[s], text_count)
+        begin = pl.multiple_of(jnp.clip(image_tiles, 0, MAXT) * TILE, TILE)
         places = lax.broadcasted_iota(jnp.int32, (1, seq_len), 1)
         scale = lax.rsqrt(parts[0] / D + EPSILON)
-        scale = columns_of(jnp.where(places < at_ref[2], scale, 0.0), seq_len)
+        scale = columns_of(jnp.where(places < text_count, scale, 0.0), seq_len)
         long_ref[:seq_len, :] = cot_ref[...]
         long_ref[seq_len:, :] = jnp.zeros((MAXT * TILE, width), jnp.bfloat16)
         for i in range(width // LANES):
             lanes = slice(i * LANES, (i + 1) * LANES)
-            shifted = long_ref[pl.ds(pl.multiple_of(at_ref[1] * TILE, TILE), seq_len), lanes]
+            shifted = long_ref[pl.ds(begin, seq_len), lanes]
             scaled_ref[:, lanes] = (shifted.astype(jnp.float32) * scale).astype(jnp.bfloat16)
 
     moment = lax.dot_general(
@@ -228,24 +257,24 @@
     gain_ref[...] = row_of(fold(moment * weight_ref[...].astype(jnp.float32)))
 
 
-def text_product(at, text, weight, cot, squares, width):
+def text_product(scalars, text, weight, cot, squares, width):
     seq_len, columns = text.shape
     groups = width // LANES
     step = 256
     return pl.pallas_call(
         text_kernel,
         grid_spec=pltpu.PrefetchScalarGridSpec(
-            num_scalar_prefetch=1,
+            num_scalar_prefetch=len(scalars),
             grid=(columns // step,),
             in_specs=[
-                pl.BlockSpec((seq_len, step), lambda i, a: (0, i)),
-                pl.BlockSpec((step, width), lambda i, a: (i, a[0])),
-                pl.BlockSpec((seq_len, width), lambda i, a: (0, a[0])),
+                pl.BlockSpec((seq_len, step), lambda i, *_: (0, i)),
+                pl.BlockSpec((step, width), lambda i, c, *_: (i, c[0])),
+                pl.BlockSpec((seq_len, width), lambda i, c, *_: (0, c[0])),
             ]
-            + [pl.BlockSpec((1, seq_len), lambda i, a: (0, 0))] * len(squares),
+            + [pl.BlockSpec((1, seq_len), lambda i, *_: (0, 0))] * len(squares),
             out_specs=[
-                pl.BlockSpec((groups, step, LANES), lambda i, a: (0, i, 0)),
-                pl.BlockSpec((1, step), lambda i, a: (0, i)),
+                pl.BlockSpec((groups, step, LANES), lambda i, *_: (0, i, 0)),
+                pl.BlockSpec((1, step), lambda i, *_: (0, i)),
             ],
             scratch_shapes=[
                 pltpu.VMEM((seq_len + MAXT * TILE, width), jnp.bfloat16),
@@ -256,13 +285,13 @@
             jax.ShapeDtypeStruct((groups, columns, LANES), jnp.bfloat16),
             jax.ShapeDtypeStruct((1, columns), jnp.float32),
         ],
-        compiler_params=pltpu.CompilerParams(vmem_limit_bytes=32 * 1024 * 1024),
+        compiler_params=pltpu.CompilerParams(vmem_limit_bytes=VMEM),
         cost_estimate=pl.CostEstimate(
             flops=2 * seq_len * columns * width,
             bytes_accessed=2 * (seq_len * (columns + width) + 2 * columns * width),
             transcendentals=0,
         ),
-    )(at, text, weight, cot, *squares)
+    )(*scalars, text, weight, cot, *squares)
 
 
 def sums_kernel(rows_ref, grad_ref, gain_ref, sums_ref):
@@ -371,7 +400,7 @@
         ],
         out_specs=pl.BlockSpec((step * groups, LANES), lambda i: (i, 0)),
         out_shape=jax.ShapeDtypeStruct((features * groups, LANES), jnp.float32),
-        compiler_params=pltpu.CompilerParams(vmem_limit_bytes=32 * 1024 * 1024),
+        compiler_params=pltpu.CompilerParams(vmem_limit_bytes=VMEM),
         cost_estimate=pl.CostEstimate(
             flops=2 * rows * features * width,
             bytes_accessed=4 * features * width + 2 * rows * (features + width),
@@ -405,46 +434,33 @@
     keys = key_weight.shape[1]
     key_half = keys // n_sec
     seq_len = text_embed.shape[0]
-    tiles = stream // TILE
-
-    text_sq, act = opening(core[None], text_embed, vis_hidden, groups, n_sec)
+
+    text_sq, act, given = opening(
+        core[None], z[None], t[None], tile_counts, owner_map,
+        text_embed, vis_hidden, key_cotangent, groups, n_sec, n_tp, stream,
+    )
+    pieces = [act] + [swap(act, "tp", m) for m in range(1, n_tp)]
+    pieces[1], text_sq = together(pieces[1], text_sq)
     text_sq = [text_sq] + [swap(text_sq, "tp", m) for m in range(1, n_tp)]
-    pieces = [act] + [swap(act, "tp", m) for m in range(1, n_tp)]
-
-    is_mine = owner_map == z
-    image_tiles = jnp.sum(jnp.where(is_mine, tile_counts, 0))
-    text_count = jnp.sum(jnp.where(is_mine, text_counts, 0))
-    at = jnp.stack([core, image_tiles, text_count]).astype(jnp.int32)
-    moment, gain_text = text_product(at, text_embed, key_weight, key_cotangent, text_sq, key_half)
+    partial, act_mine = project(t[None], pieces, proj_weight)
+    text_sq[0], given, act_mine, partial = together(text_sq[0], given, act_mine, partial)
+    summed = lax.psum_scatter(partial, "seq", scatter_dimension=0, tiled=True)
+
+    scalars = (core[None], z[None], tile_counts, text_counts, owner_map)
+    moment, gain_text = text_product(
+        scalars, text_embed, key_weight, key_cotangent, text_sq, key_half
+    )
     if n_seq <= 4:
         way = line_step(moment, "seq", 1, None)
-        way[0], way[1], *pieces = together(*way, *pieces)
-        way = line_step(moment, "seq", 2, way)
     else:
         share = key_half // n_seq
         moment = moment.reshape(-1, columns, LANES // share, share).transpose(0, 2, 1, 3)
         moment = reduce_to_owner(moment.reshape(n_seq, columns, share), "seq")
-    partial, act_mine = project(t[None], pieces, proj_weight)
-
-    starts = jnp.cumsum(tile_counts) - tile_counts
-    tile_ids = jnp.arange(tiles, dtype=jnp.int32)[:, None]
-    held = (tile_ids >= starts[None]) & (tile_ids < (starts + tile_counts)[None])
-    tile_owner = jnp.sum(jnp.where(held, owner_map[None], 0), 1)
-    tile_place = jnp.sum(jnp.where(held, tile_ids - starts[None], 0), 1)
-    share = key_half // n_tp
-    from_col = (core * n_tp + t) * share
-    front = lax.dynamic_slice_in_dim(key_cotangent[: MAXT * TILE], from_col, share, 1)
-    front = front.reshape(MAXT, TILE, share)
-    given = jnp.zeros((tiles, TILE, share), bf16)
-    for place in range(MAXT):
-        chosen = (tile_owner == z) & (tile_place == place)
-        given = jnp.where(chosen[:, None, None], front[place][None], given)
-    taken = butterfly(given.reshape(stream, share), ("seq",))
+
+    taken = butterfly(given, ("seq",))
     key_bias_part = jnp.sum(key_cotangent.astype(f32), 0)
     early = jnp.concatenate([gain_text[0], jnp.where(core == 0, key_bias_part, 0.0)])
 
-    taken, early, act_mine, partial = together(taken, early, act_mine, partial)
-    summed = lax.psum_scatter(partial, "seq", scatter_dimension=0, tiled=True)
     act_other = swap(act_mine, "sec", 1)
     taken = [taken] + [swap(taken, "tp", m) for m in range(1, n_tp)]
     half_cot = jnp.concatenate(in_order(taken, t), 1)
@@ -466,10 +482,7 @@
     image_mine = (summed.astype(f32) + proj_bias).astype(bf16)
     if n_seq <= 4:
         way[0], way[1], image_mine = together(*way, image_mine)
-        for step in range(3, n_seq):
-            way = line_step(moment, "seq", step, way)
-        moment = lax.dynamic_index_in_dim(moment, z, 0, keepdims=False).astype(f32)
-        moment = moment + way[0].astype(f32) + way[1].astype(f32)
+        way = line_step(moment, "seq", 2, way)
     low, high = image_mine[:, :col_half], image_mine[:, col_half:]
     first_core = core == 0
     came = swap(jnp.where(first_core, high, low), "sec", 1)
@@ -490,6 +503,12 @@
     sums = sums[:, : n_seq * size].reshape(n_sec, n_seq, 2, -1).transpose(1, 0, 2, 3)
     sums = sums.reshape(n_seq * n_sec, 2, -1)
 
+    if n_seq <= 4:
+        way[0], way[1], rows = together(*way, rows)
+        for step in range(3, n_seq):
+            way = line_step(moment, "seq", step, way)
+        moment = lax.dynamic_index_in_dim(moment, z, 0, keepdims=False).astype(f32)
+        moment = moment + way[0].astype(f32) + way[1].astype(f32)
     gain_half = lax.dynamic_slice_in_dim(norm_gain, core * col_half, col_half, 0)[None]
     embed_grad, here, there, small = image_grads(
         core[None], normed_grad, gain_half, cot_own, sums, rows

time: 197 us -> 203 us (1.030)
  waiting for transfers between devices: 53 us -> 71.7 us
  local copies, waits for them, and re-layouts: 25.9 us -> 8.83 us
  Pallas kernels: 26.4 us -> 38.9 us
  other arithmetic: 25.6 us -> 15.4 us
  starting transfers between devices: 40.3 us -> 43.9 us
    ppermute x23, waiting for transfers between devices: 15 us -> 44 us  [swap(): return lax.ppermute(x, axis, [(i, i ^ mask) for i in range(count)])]
    ppermute x6, waiting for transfers between devices: 9.42 us -> 27.7 us  [line_step(): out.append(lax.ppermute(sent, axis, pairs))]
    reduce_scatter x1, waiting for transfers between devices: 16.8 us -> 0.02 us  [on_device(): summed = lax.psum_scatter(partial, 'seq', scatter_dimension=0, tiled=True)]
    unnamed x57 -> x33, local copies, waits for them, and re-layouts: 16.2 us -> 1.98 us
    all_gather x1, waiting for transfers between devices: 11.8 us -> 0.01 us  [on_device(): rows = lax.all_gather(image, 'seq', axis=0, tiled=True)]
    pallas_call x1, Pallas kernels: 1.34 us -> 5.34 us  [opening(): pl.pallas_call(opening_kernel, grid_spec=pltpu.PrefetchScalarGridSpec(num...]
    pallas_call x1, Pallas kernels: 6.47 us -> 9.94 us  [text_product(): pl.pallas_call(text_kernel, grid_spec=pltpu.PrefetchScalarGridSpec(num_sc...]
    ppermute x6, starting transfers between devices: 15 us -> 18.1 us  [line_step(): out.append(lax.ppermute(sent, axis, pairs))]
  transfers between devices with their start and end apart: 31 -> 31, of which waited for: 11 -> 12; matrix products, arithmetic and copies ran while one was open for 21% -> 15% of each run, Pallas kernels for 10% -> 10%
where the time goes in v8:
time: 203 us; the launch traced here: 202 us
  waiting for transfers between devices  71.7 us (35%)
  starting transfers between devices  43.9 us (22%)
  Pallas kernels  38.9 us (19%)
  other arithmetic  15.4 us (8%)
  between operations  14.5 us (7%)
  local copies, waits for them, and re-layouts  8.83 us (4%)
  matrix products  8.7 us (4%)
    ppermute x23, waiting for transfers between devices, swap(): return lax.ppermute(x, axis, [(i, i ^ mask) for i in range(count)])  44 us
    ppermute x6, waiting for transfers between devices, line_step(): out.append(lax.ppermute(sent, axis, pairs))  27.7 us
    ppermute x23, starting transfers between devices, swap(): return lax.ppermute(x, axis, [(i, i ^ mask) for i in range(count)])  25.7 us
    ppermute x6, starting transfers between devices, line_step(): out.append(lax.ppermute(sent, axis, pairs))  18.1 us
    pallas_call x1, Pallas kernels, text_product(): pl.pallas_call(text_kernel, grid_spec=pltpu.PrefetchScalarGridSpec(num_sc...  9.94 us
    pallas_call x1, Pallas kernels, weight_product(): pl.pallas_call(weight_kernel, grid=(features // step,), in_specs=[pl.Bloc...  9.82 us
    pallas_call x1, Pallas kernels, project(): pl.pallas_call(project_kernel, grid=(columns // step,), in_specs=[pl.Bloc...  7.94 us
    pallas_call x1, Pallas kernels, image_grads(): pl.pallas_call(image_kernel, in_specs=[pl.BlockSpec(memory_space=pltpu.SM...  5.63 us
  transfers between devices with their start and end apart: 31, of which 12 were waited for; matrix products, arithmetic and copies ran while one was open for 15% of the time, Pallas kernels for 10%

profile of v8, /device:TPU:0, one launch (start us, length us, event | category | flops | bytes accessed | tf_op | source)
XLA Modules:
  0.0 202.0 jit_solution(2867851165678599970)
XLA Ops:
  7.2 5.3 %shard_map.137 = (f32[1,1024]{1,0:T(1,128)}, bf16[96,2048]{1,0:T(8,128)(2,1)}, bf16[768,128]{1,0:T(8,128)(2,1)}) custom-call(s32[1]{0:T(128)} %bitcast.core_ref, s32[1]{0:T(128)} %bitcast.1.z_ref, s32[1]{0:T(128)} %bitcast.2.t_ref.refs_0_, s32[4]{0:T(128)} %tiles_ref.3, s32[4]{0:T(128)} %owners_ref.3, bf16[1024,2048]{1,0:T(8,128)(2,1)} %text_ref.3, ...), custom_call_target="tpu_custom_call" | custom-call | flops 12058624 | bytes 4194304 | tf_op jit(solution)/shard_map/pallas_call | solution.py:193
  12.6 2.9 %collective-permute-start = (bf16[96,2048]{1,0:T(8,128)(2,1)}, bf16[96,2048]{1,0:T(8,128)(2,1)S(1)}, u32[]{:S(2)}, u32[]{:S(2)}) collective-permute-start(bf16[96,2048]{1,0:T(8,128)(2,1)} %get-tuple-element.28.refs_2_), channel_id=1, source_target_pairs={{0,1},{1,0},{2,3},{3,2},{4,5},{5,4},{6,7},{7,6},{8,9},{9,8},{10,11... | collective-permute-start | bytes 1179656 | tf_op jit(solution)/shard_map/ppermute | solution.py:18
  15.5 1.5 collective-permute-start.2
  17.0 8.6 %collective-permute-done.refs_3_ = bf16[96,2048]{1,0:T(8,128)(2,1)S(1)} collective-permute-done((bf16[96,2048]{1,0:T(8,128)(2,1)}, bf16[96,2048]{1,0:T(8,128)(2,1)S(1)}, u32[]{:S(2)}, u32[]{:S(2)}) %collective-permute-start) | collective-permute-done | bytes 393248 | tf_op jit(solution)/shard_map/ppermute | solution.py:18
  25.7 8.9 %collective-permute-done.2.refs_5_ = bf16[96,2048]{1,0:T(8,128)(2,1)S(1)} collective-permute-done((bf16[96,2048]{1,0:T(8,128)(2,1)}, bf16[96,2048]{1,0:T(8,128)(2,1)S(1)}, u32[]{:S(2)}, u32[]{:S(2)}) %collective-permute-start.2) | collective-permute-done | bytes 393248 | tf_op jit(solution)/shard_map/ppermute | solution.py:18
  34.6 1.4 collective-permute-done.1.refs_4_
  35.9 0.8 copy-done.15
  36.7 7.9 %shard_map.138 = (bf16[384,2048]{1,0:T(8,128)(2,1)}, bf16[384,2048]{1,0:T(8,128)(2,1)}) custom-call(s32[1]{0:T(128)} %bitcast.2.t_ref.refs_0_, bf16[2048,2048]{1,0:T(8,128)(2,1)} %refs_1_.1, bf16[96,2048]{1,0:T(8,128)(2,1)} %get-tuple-element.28.refs_2_, bf16[96,2048]{1,0:T(8,128)(2,1)} %copy-done.13, bf16[96,2048]{1,0:T(8,128)(2,1)} %copy-done.15, ...), custom_call_target="tpu_custom_call" | custom-call | flops 3221225472 | bytes 13107200 | tf_op jit(solution)/shard_map/pallas_call | solution.py:128
  44.7 1.6 collective-permute-start.4
  46.4 4.1 %collective-permute-done.4 = bf16[768,128]{1,0:T(8,128)(2,1)S(1)} collective-permute-done((bf16[768,128]{1,0:T(8,128)(2,1)S(1)}, bf16[768,128]{1,0:T(8,128)(2,1)S(1)}, u32[]{:S(2)}, u32[]{:S(2)}) %collective-permute-start.4) | collective-permute-done | bytes 196640 | tf_op jit(solution)/shard_map/ppermute | solution.py:18
  50.5 2.8 %collective-permute-start.5 = (bf16[768,128]{1,0:T(8,128)(2,1)S(1)}, bf16[768,128]{1,0:T(8,128)(2,1)S(1)}, u32[]{:S(2)}, u32[]{:S(2)}) collective-permute-start(bf16[768,128]{1,0:T(8,128)(2,1)S(1)} %add.91), channel_id=1, source_target_pairs={{0,8},{4,12},{8,0},{12,4},{1,9},{5,13},{9,1},{13,5},{2,10},{6,14},... | collective-permute-start | bytes 589832 | tf_op jit(solution)/shard_map/ppermute | solution.py:18
  53.3 17.9 %collective-permute-done.5 = bf16[768,128]{1,0:T(8,128)(2,1)S(1)} collective-permute-done((bf16[768,128]{1,0:T(8,128)(2,1)S(1)}, bf16[768,128]{1,0:T(8,128)(2,1)S(1)}, u32[]{:S(2)}, u32[]{:S(2)}) %collective-permute-start.5) | collective-permute-done | bytes 196640 | tf_op jit(solution)/shard_map/ppermute | solution.py:18
  71.3 1.6 collective-permute-start.8
  72.9 2.0 collective-permute-start.6
  74.9 0.4 convert_reduce_fusion
  75.3 1.0 collective-permute-start.12
  76.3 2.0 %collective-permute-start.11 = (f32[1,1024]{1,0:T(1,128)S(1)}, f32[1,1024]{1,0:T(1,128)S(1)}, u32[]{:S(2)}, u32[]{:S(2)}) collective-permute-start(f32[1,1024]{1,0:T(1,128)S(1)} %copy-done.9), channel_id=1, source_target_pairs={{0,2},{1,3},{2,0},{3,1},{4,6},{5,7},{6,4},{7,5},{8,10},{9,11},{10,... | collective-permute-start | bytes 12296 | tf_op jit(solution)/shard_map/ppermute | solution.py:18
  78.3 0.5 collective-permute-start.10
  78.8 1.9 collective-permute-done.7
  80.8 0.1 pad_maximum_fusion.2
  81.0 0.6 dynamic_slice.38
  81.6 1.6 copy.23
  83.2 0.4 collective-permute-start.3
  83.6 0.6 copy-done.10
  84.2 0.6 copy-done.12
  84.8 9.9 %shard_map.139 = (bf16[4,2048,128]{2,1,0:T(8,128)(2,1)}, f32[1,2048]{1,0:T(1,128)}) custom-call(s32[1]{0:T(128)} %bitcast.core_ref, s32[1]{0:T(128)} %bitcast.1.z_ref, s32[4]{0:T(128)} %tiles_ref.3, s32[4]{0:T(128)} %texts_ref.1, s32[4]{0:T(128)} %owners_ref.3, bf16[1024,2048]{1,0:T(8,128)(2,1)} %text_ref.3, bf16[2048,1024]{1,0:T(8,128)(2,1)} %weight_ref.1, ...), custom_call_target="tpu_custom_call" | custom-call | flops 2147483648 | bytes 9437184 | tf_op jit(solution)/shard_map/pallas_call | solution.py:264
  94.7 2.3 %dynamic-slice_bitcast_fusion = (bf16[2048,128]{1,0:T(8,128)(2,1)}, bf16[2048,128]{1,0:T(8,128)(2,1)}) fusion(bf16[4,2048,128]{2,1,0:T(8,128)(2,1)} %get-tuple-element.38, s32[]{:T(128)S(6)} %min.20, s32[]{:T(128)S(6)} %min.19), kind=kLoop, calls=%fused_computation.25 | loop fusion | bytes 2097160 | tf_op jit(solution)/shard_map/jit(dynamic_index_in_dim)/squeeze | solution.py:73
  97.0 1.6 collective-permute-start.14
  98.7 4.7 %collective-permute-start.13 = (bf16[2048,128]{1,0:T(8,128)(2,1)}, bf16[2048,128]{1,0:T(8,128)(2,1)}, u32[]{:S(2)}, u32[]{:S(2)}) collective-permute-start(bf16[2048,128]{1,0:T(8,128)(2,1)} %get-tuple-element.71), channel_id=1, source_target_pairs={{0,4},{1,5},{2,6},{3,7},{16,20},{17,21},{18,22},{19,23}} | collective-permute-start | bytes 1572872 | tf_op jit(solution)/shard_map/ppermute | solution.py:78
  103.4 1.6 broadcast_select_fusion.1
  105.0 1.1 add_convert_fusion.rows_ref
  106.1 8.2 %collective-permute-done.13 = bf16[2048,128]{1,0:T(8,128)(2,1)} collective-permute-done((bf16[2048,128]{1,0:T(8,128)(2,1)}, bf16[2048,128]{1,0:T(8,128)(2,1)}, u32[]{:S(2)}, u32[]{:S(2)}) %collective-permute-start.13) | collective-permute-done | bytes 524320 | tf_op jit(solution)/shard_map/ppermute | solution.py:78
  114.4 3.6 %fusion.9.grad_ref = f32[96,2048]{1,0:T(8,128)S(1)} fusion(bf16[2048,1024]{1,0:T(8,128)(2,1)} %weight_ref.1, s32[]{:T(128)S(6)} %select_n.193, bf16[768,512]{1,0:T(8,128)(2,1)S(1)} %get-tuple-element.72, bf16[768,512]{1,0:T(8,128)(2,1)S(1)} %get-tuple-element.73), kind=kOutput, calls=%fused_computation.30 | convolution fusion | flops 403046400 | bytes 6553604 | tf_op jit(solution)/shard_map/dot_general | solution.py:474
  118.1 0.8 pad_maximum_fusion.4
  118.9 5.1 %fusion.grad_ref = f32[768,1024]{1,0:T(8,128)} fusion(bf16[2048,1024]{1,0:T(8,128)(2,1)} %weight_ref.1, s32[]{:T(128)S(6)} %select_n.188, bf16[768,512]{1,0:T(8,128)(2,1)S(1)} %get-tuple-element.73, bf16[768,512]{1,0:T(8,128)(2,1)S(1)} %get-tuple-element.72), kind=kOutput, calls=%fused_computation.2 | convolution fusion | flops 1613758464 | bytes 6815748 | tf_op jit(solution)/shard_map/dot_general | solution.py:470
  124.0 1.1 constant_dynamic-slice_fusion
  125.1 0.2 shard_map.140
  125.3 1.2 collective-permute-start.17
  126.6 0.8 collective-permute-start.16
  127.4 1.5 collective-permute-start.15
  128.9 0.8 pad_maximum_fusion.3.cot_ref
  129.7 0.2 collective-permute-done.17
  129.9 0.3 collective-permute-done.16
  130.1 0.8 collective-permute-done.15
  131.0 2.5 %collective-permute-start.20 = (f32[3328]{0:T(1024)S(1)}, f32[3328]{0:T(1024)S(1)}, u32[]{:S(2)}, u32[]{:S(2)}) collective-permute-start(f32[3328]{0:T(1024)S(1)} %pad_maximum_fusion.9), channel_id=1, source_target_pairs={{0,4},{4,0},{8,12},{12,8},{1,5},{5,1},{9,13},{13,9},{2,6},{6,2},{1... | collective-permute-start | bytes 39944 | tf_op jit(solution)/shard_map/ppermute | solution.py:18
  133.5 0.9 collective-permute-start.19
  134.4 1.6 collective-permute-start.18
  136.0 2.5 %fusion.6 = (bf16[2048,128]{1,0:T(8,128)(2,1)}, bf16[2048,128]{1,0:T(8,128)(2,1)}) fusion(bf16[2048,128]{1,0:T(8,128)(2,1)} %collective-permute-done.14, bf16[4,2048,128]{2,1,0:T(8,128)(2,1)S(1)} %copy-done.2, s32[]{:T(128)S(6)} %min.22, bf16[2048,128]{1,0:T(8,128)(2,1)} %collective-permute-done.13, s32[]{:T(128)S(6)} %min.21), kind=kLoop, calls=%fused_computation.16 | loop fusion | flops 2097152 | bytes 3145736 | tf_op jit(solution)/shard_map/convert_element_type | solution.py:75
  138.5 0.7 collective-permute-start.23
  139.2 3.8 %collective-permute-start.22 = (bf16[2048,128]{1,0:T(8,128)(2,1)}, bf16[2048,128]{1,0:T(8,128)(2,1)S(1)}, u32[]{:S(2)}, u32[]{:S(2)}) collective-permute-start(bf16[2048,128]{1,0:T(8,128)(2,1)} %get-tuple-element.69), channel_id=1, source_target_pairs={{0,4},{4,8},{1,5},{5,9},{2,6},{6,10},{3,7},{7,11},{16,20},{20,24},... | collective-permute-start | bytes 1572872 | tf_op jit(solution)/shard_map/ppermute | solution.py:78
  143.3 3.9 %maximum_bitcast_fusion.act_ref = bf16[2048,768]{1,0:T(8,128)(2,1)} fusion(bf16[384,2048]{0,1:T(8,128)(2,1)} %collective-permute-done.3, bf16[384,2048]{0,1:T(8,128)(2,1)} %copy.23), kind=kLoop, calls=%fused_computation.1 | loop fusion | flops 6291456 | bytes 6291456 | tf_op jit(solution)/shard_map/transpose | solution.py:518
  147.2 0.6 copy.24
  147.9 0.6 slice.32
  148.5 16.3 %collective-permute-done.22 = bf16[2048,128]{1,0:T(8,128)(2,1)S(1)} collective-permute-done((bf16[2048,128]{1,0:T(8,128)(2,1)}, bf16[2048,128]{1,0:T(8,128)(2,1)S(1)}, u32[]{:S(2)}, u32[]{:S(2)}) %collective-permute-start.22) | collective-permute-done | bytes 524320 | tf_op jit(solution)/shard_map/ppermute | solution.py:78
  164.8 5.6 %shard_map.141 = (bf16[768,1024]{1,0:T(8,128)(2,1)}, f32[1024,128]{1,0:T(8,128)}, bf16[1024,128]{1,0:T(8,128)(2,1)}, f32[2,1024]{1,0:T(2,128)}) custom-call(s32[1]{0:T(128)} %bitcast.core_ref, f32[768,1024]{1,0:T(8,128)} %fusion.grad_ref, f32[1,1024]{1,0:T(1,128)} %bitcast.53, bf16[768,256]{1,0:T(8,128)(2,1)} %pad_maximum_fusion.3.cot_ref, ...), custom_call_target="tpu_custom_call" | custom-call | flops 402653184 | bytes 6291456 | tf_op jit(solution)/shard_map/pallas_call | solution.py:364
  170.4 0.5 collective-permute-start.28
  170.9 1.2 fusion.4
  172.1 6.0 %collective-permute-start.26 = (bf16[2048,128]{1,0:T(8,128)(2,1)}, bf16[2048,128]{1,0:T(8,128)(2,1)S(1)}, u32[]{:S(2)}, u32[]{:S(2)}) collective-permute-start(bf16[2048,128]{1,0:T(8,128)(2,1)} %get-tuple-element.66), channel_id=1, source_target_pairs={{0,4},{4,8},{8,12},{1,5},{5,9},{9,13},{2,6},{6,10},{10,14},{3,7},{... | collective-permute-start | bytes 1572872 | tf_op jit(solution)/shard_map/ppermute | solution.py:78
  178.1 1.3 collective-permute-start.27
  179.5 9.8 %shard_map.142 = f32[16384,128]{1,0:T(8,128)} custom-call(bf16[2048,768]{1,0:T(8,128)(2,1)} %maximum_bitcast_fusion.act_ref, bf16[768,1024]{1,0:T(8,128)(2,1)} %get-tuple-element.45.grad_ref), custom_call_target="tpu_custom_call" | custom-call | flops 3221225472 | bytes 13107200 | tf_op jit(solution)/shard_map/pallas_call | solution.py:394
  189.3 0.6 pad_maximum_fusion.11
  189.9 0.6 slice_add_fusion
  190.6 3.2 %collective-permute-done.27 = bf16[2048,128]{1,0:T(8,128)(2,1)S(1)} collective-permute-done((bf16[2048,128]{1,0:T(8,128)(2,1)}, bf16[2048,128]{1,0:T(8,128)(2,1)S(1)}, u32[]{:S(2)}, u32[]{:S(2)}) %collective-permute-start.27) | collective-permute-done | bytes 524320 | tf_op jit(solution)/shard_map/ppermute | solution.py:78
  193.8 1.3 fusion.2
  (82 shorter events, 1.1 us)
Async XLA Ops:
  7.2 97.8 %reduce-scatter.2.cloned.1.call-start = ((), (), s32[]{:S(2)}) async-start(), calls=%async_computation.1 | async-start | bytes 1966080 | tf_op jit(solution)/shard_map/reduce_scatter | solution.py:447
  12.6 13.1 %collective-permute-start = (bf16[96,2048]{1,0:T(8,128)(2,1)}, bf16[96,2048]{1,0:T(8,128)(2,1)S(1)}, u32[]{:S(2)}, u32[]{:S(2)}) collective-permute-start(bf16[96,2048]{1,0:T(8,128)(2,1)} %get-tuple-element.28.refs_2_), channel_id=1, source_target_pairs={{0,1},{1,0},{2,3},{3,2},{4,5},{5,4},{6,7},{7,6},{8,9},{9,8},{10,11... | collective-permute-start | bytes 1179656 | tf_op jit(solution)/shard_map/ppermute | solution.py:18
  15.5 19.1 %collective-permute-start.2 = (bf16[96,2048]{1,0:T(8,128)(2,1)}, bf16[96,2048]{1,0:T(8,128)(2,1)S(1)}, u32[]{:S(2)}, u32[]{:S(2)}) collective-permute-start(bf16[96,2048]{1,0:T(8,128)(2,1)} %get-tuple-element.28.refs_2_), channel_id=1, source_target_pairs={{0,3},{1,2},{2,1},{3,0},{4,7},{5,6},{6,5},{7,4},{8,11},{9,10},{10,... | collective-permute-start | bytes 1179656 | tf_op jit(solution)/shard_map/ppermute | solution.py:18
  17.0 18.9 %collective-permute-start.1 = (bf16[96,2048]{1,0:T(8,128)(2,1)}, bf16[96,2048]{1,0:T(8,128)(2,1)S(1)}, u32[]{:S(2)}, u32[]{:S(2)}) collective-permute-start(bf16[96,2048]{1,0:T(8,128)(2,1)} %get-tuple-element.28.refs_2_), channel_id=1, source_target_pairs={{0,2},{1,3},{2,0},{3,1},{4,6},{5,7},{6,4},{7,5},{8,10},{9,11},{10,... | collective-permute-start | bytes 1179656 | tf_op jit(solution)/shard_map/ppermute | solution.py:18
  25.7 10.3 %copy-start.13 = (bf16[96,2048]{1,0:T(8,128)(2,1)}, bf16[96,2048]{1,0:T(8,128)(2,1)S(1)}, u32[]{:S(2)}) copy-start(bf16[96,2048]{1,0:T(8,128)(2,1)S(1)} %collective-permute-done.refs_3_) | copy-start | bytes 1179652
  25.7 19.1 %copy-start.5 = (bf16[768,128]{1,0:T(8,128)(2,1)S(1)}, bf16[768,128]{1,0:T(8,128)(2,1)}, u32[]{:S(2)}) copy-start(bf16[768,128]{1,0:T(8,128)(2,1)} %get-tuple-element.36) | copy-start | bytes 589828
  34.6 1.4 copy-start.14
  35.9 0.8 copy-start.15
  44.6 30.2 %copy-start.1 = (bf16[1024,1024]{1,0:T(8,128)(2,1)S(1)}, bf16[1024,1024]{1,0:T(8,128)(2,1)}, u32[]{:S(2)}) copy-start(bf16[1024,1024]{1,0:T(8,128)(2,1)} %cot_ref.3) | copy-start | bytes 6291460
  44.6 30.6 %copy-start.9 = (f32[1,1024]{1,0:T(1,128)S(1)}, f32[1,1024]{1,0:T(1,128)}, u32[]{:S(2)}) copy-start(f32[1,1024]{1,0:T(1,128)} %get-tuple-element.37.refs_0_) | copy-start | bytes 12292
  44.7 120.1 %all-gather.2.cloned.1.call-start = ((), (), s32[]{:S(2)}) async-start(), calls=%async_computation.2 | async-start | bytes 1966080 | tf_op jit(solution)/shard_map/all_gather | solution.py:490
  44.7 5.7 %collective-permute-start.4 = (bf16[768,128]{1,0:T(8,128)(2,1)S(1)}, bf16[768,128]{1,0:T(8,128)(2,1)S(1)}, u32[]{:S(2)}, u32[]{:S(2)}) collective-permute-start(bf16[768,128]{1,0:T(8,128)(2,1)S(1)} %copy-done.5), channel_id=1, source_target_pairs={{0,4},{4,0},{8,12},{12,8},{1,5},{5,1},{9,13},{13,9},{2,6},{6,2},{1... | collective-permute-start | bytes 589832 | tf_op jit(solution)/shard_map/ppermute | solution.py:18
  50.5 20.7 %collective-permute-start.5 = (bf16[768,128]{1,0:T(8,128)(2,1)S(1)}, bf16[768,128]{1,0:T(8,128)(2,1)S(1)}, u32[]{:S(2)}, u32[]{:S(2)}) collective-permute-start(bf16[768,128]{1,0:T(8,128)(2,1)S(1)} %add.91), channel_id=1, source_target_pairs={{0,8},{4,12},{8,0},{12,4},{1,9},{5,13},{9,1},{13,5},{2,10},{6,14},... | collective-permute-start | bytes 589832 | tf_op jit(solution)/shard_map/ppermute | solution.py:18
  71.3 7.0 %collective-permute-start.8 = (bf16[768,128]{1,0:T(8,128)(2,1)S(1)}, bf16[768,128]{1,0:T(8,128)(2,1)S(1)}, u32[]{:S(2)}, u32[]{:S(2)}) collective-permute-start(bf16[768,128]{1,0:T(8,128)(2,1)S(1)} %add.92), channel_id=1, source_target_pairs={{0,1},{1,0},{2,3},{3,2},{4,5},{5,4},{6,7},{7,6},{8,9},{9,8},{10,11... | collective-permute-start | bytes 589832 | tf_op jit(solution)/shard_map/ppermute | solution.py:18
  72.9 7.8 %collective-permute-start.7 = (bf16[768,128]{1,0:T(8,128)(2,1)S(1)}, bf16[768,128]{1,0:T(8,128)(2,1)S(1)}, u32[]{:S(2)}, u32[]{:S(2)}) collective-permute-start(bf16[768,128]{1,0:T(8,128)(2,1)S(1)} %add.92), channel_id=1, source_target_pairs={{0,2},{1,3},{2,0},{3,1},{4,6},{5,7},{6,4},{7,5},{8,10},{9,11},{10,... | collective-permute-start | bytes 589832 | tf_op jit(solution)/shard_map/ppermute | solution.py:18
  72.9 7.8 %collective-permute-start.6 = (bf16[768,128]{1,0:T(8,128)(2,1)S(1)}, bf16[768,128]{1,0:T(8,128)(2,1)S(1)}, u32[]{:S(2)}, u32[]{:S(2)}) collective-permute-start(bf16[768,128]{1,0:T(8,128)(2,1)S(1)} %add.92), channel_id=1, source_target_pairs={{0,3},{1,2},{2,1},{3,0},{4,7},{5,6},{6,5},{7,4},{8,11},{9,10},{10,... | collective-permute-start | bytes 589832 | tf_op jit(solution)/shard_map/ppermute | solution.py:18
  75.2 5.7 %copy-start = (f32[2048]{0:T(1024)S(1)}, f32[2048]{0:T(1024)}, u32[]{:S(2)}) copy-start(f32[2048]{0:T(1024)} %param.14) | copy-start | bytes 24580
  75.2 6.3 %copy-start.3 = (bf16[384,2048]{1,0:T(8,128)(2,1)S(1)}, bf16[384,2048]{1,0:T(8,128)(2,1)}, u32[]{:S(2)}) copy-start(bf16[384,2048]{1,0:T(8,128)(2,1)} %get-tuple-element.35) | copy-start | bytes 4718596
  75.3 8.4 %collective-permute-start.12 = (f32[1,1024]{1,0:T(1,128)S(1)}, f32[1,1024]{1,0:T(1,128)S(1)}, u32[]{:S(2)}, u32[]{:S(2)}) collective-permute-start(f32[1,1024]{1,0:T(1,128)S(1)} %copy-done.9), channel_id=1, source_target_pairs={{0,3},{1,2},{2,1},{3,0},{4,7},{5,6},{6,5},{7,4},{8,11},{9,10},{10,... | collective-permute-start | bytes 12296 | tf_op jit(solution)/shard_map/ppermute | solution.py:18
  76.3 7.4 %collective-permute-start.11 = (f32[1,1024]{1,0:T(1,128)S(1)}, f32[1,1024]{1,0:T(1,128)S(1)}, u32[]{:S(2)}, u32[]{:S(2)}) collective-permute-start(f32[1,1024]{1,0:T(1,128)S(1)} %copy-done.9), channel_id=1, source_target_pairs={{0,2},{1,3},{2,0},{3,1},{4,6},{5,7},{6,4},{7,5},{8,10},{9,11},{10,... | collective-permute-start | bytes 12296 | tf_op jit(solution)/shard_map/ppermute | solution.py:18
  78.3 5.4 %collective-permute-start.10 = (f32[1,1024]{1,0:T(1,128)S(1)}, f32[1,1024]{1,0:T(1,128)S(1)}, u32[]{:S(2)}, u32[]{:S(2)}) collective-permute-start(f32[1,1024]{1,0:T(1,128)S(1)} %copy-done.9), channel_id=1, source_target_pairs={{0,1},{1,0},{2,3},{3,2},{4,5},{5,4},{6,7},{7,6},{8,9},{9,8},{10,11... | collective-permute-start | bytes 12296 | tf_op jit(solution)/shard_map/ppermute | solution.py:18
  80.9 22.5 %collective-permute-start.9 = (bf16[768,512]{1,0:T(8,128)(2,1)S(1)}, bf16[768,512]{1,0:T(8,128)(2,1)}, u32[]{:S(2)}, u32[]{:S(2)}) collective-permute-start(bf16[768,512]{1,0:T(8,128)(2,1)S(1)} %pad_maximum_fusion.2), channel_id=1, source_target_pairs={{0,16},{16,0},{1,17},{17,1},{2,18},{18,2},{3,19},{19,3},{4,20},{20... | collective-permute-start | bytes 2359304 | tf_op jit(solution)/shard_map/ppermute | solution.py:18
  83.2 60.1 %collective-permute-start.3 = (bf16[384,2048]{0,1:T(8,128)(2,1)}, bf16[384,2048]{0,1:T(8,128)(2,1)}, u32[]{:S(2)}, u32[]{:S(2)}) collective-permute-start(bf16[384,2048]{0,1:T(8,128)(2,1)} %copy.23), channel_id=1, source_target_pairs={{0,16},{16,0},{1,17},{17,1},{2,18},{18,2},{3,19},{19,3},{4,20},{20... | collective-permute-start | bytes 4718600 | tf_op jit(solution)/shard_map/ppermute | solution.py:18
  83.6 0.6 copy-start.10
  83.6 0.6 copy-start.11
  84.2 0.6 copy-start.12
  97.0 8.0 %copy-start.7 = (f32[2048]{0:T(1024)S(1)}, f32[2048]{0:T(1024)}, u32[]{:S(2)}) copy-start(f32[2048]{0:T(1024)} %param.12) | copy-start | bytes 24580
  97.0 9.1 %collective-permute-start.14 = (bf16[2048,128]{1,0:T(8,128)(2,1)}, bf16[2048,128]{1,0:T(8,128)(2,1)}, u32[]{:S(2)}, u32[]{:S(2)}) collective-permute-start(bf16[2048,128]{1,0:T(8,128)(2,1)} %get-tuple-element.70), channel_id=1, source_target_pairs={{12,8},{13,9},{14,10},{15,11},{28,24},{29,25},{30,26},{31,27}} | collective-permute-start | bytes 1572872 | tf_op jit(solution)/shard_map/ppermute | solution.py:78
  98.7 15.6 %collective-permute-start.13 = (bf16[2048,128]{1,0:T(8,128)(2,1)}, bf16[2048,128]{1,0:T(8,128)(2,1)}, u32[]{:S(2)}, u32[]{:S(2)}) collective-permute-start(bf16[2048,128]{1,0:T(8,128)(2,1)} %get-tuple-element.71), channel_id=1, source_target_pairs={{0,4},{1,5},{2,6},{3,7},{16,20},{17,21},{18,22},{19,23}} | collective-permute-start | bytes 1572872 | tf_op jit(solution)/shard_map/ppermute | solution.py:78
  114.3 3.7 %collective-permute-start.24 = (bf16[96,1024]{1,0:T(8,128)(2,1)S(1)}, bf16[96,1024]{1,0:T(8,128)(2,1)S(1)}, u32[]{:S(2)}, u32[]{:S(2)}) collective-permute-start(bf16[96,1024]{1,0:T(8,128)(2,1)S(1)} %broadcast_select_fusion.3), channel_id=1, source_target_pairs={{0,16},{16,0},{1,17},{17,1},{2,18},{18,2},{3,19},{19,3},{4,20},{20... | collective-permute-start | bytes 589832 | tf_op jit(solution)/shard_map/ppermute | solution.py:18
  124.0 7.0 %copy-start.6 = (f32[1,2048]{1,0:T(1,128)S(1)}, f32[1,2048]{1,0:T(1,128)}, u32[]{:S(2)}) copy-start(f32[1,2048]{1,0:T(1,128)} %get-tuple-element.41) | copy-start | bytes 24580
  124.0 12.0 %copy-start.2 = (bf16[4,2048,128]{2,1,0:T(8,128)(2,1)S(1)}, bf16[4,2048,128]{2,1,0:T(8,128)(2,1)}, u32[]{:S(2)}) copy-start(bf16[4,2048,128]{2,1,0:T(8,128)(2,1)} %get-tuple-element.38) | copy-start | bytes 6291460
  125.3 4.5 %collective-permute-start.17 = (f32[2,128]{1,0:T(2,128)S(1)}, f32[2,128]{1,0:T(2,128)S(1)}, u32[]{:S(2)}, u32[]{:S(2)}) collective-permute-start(f32[2,128]{1,0:T(2,128)S(1)} %shard_map.140), channel_id=1, source_target_pairs={{0,3},{1,2},{2,1},{3,0},{4,7},{5,6},{6,5},{7,4},{8,11},{9,10},{10,... | collective-permute-start | bytes 3080 | tf_op jit(solution)/shard_map/ppermute | solution.py:18
  126.6 3.6 %collective-permute-start.16 = (f32[2,128]{1,0:T(2,128)S(1)}, f32[2,128]{1,0:T(2,128)S(1)}, u32[]{:S(2)}, u32[]{:S(2)}) collective-permute-start(f32[2,128]{1,0:T(2,128)S(1)} %shard_map.140), channel_id=1, source_target_pairs={{0,2},{1,3},{2,0},{3,1},{4,6},{5,7},{6,4},{7,5},{8,10},{9,11},{10,... | collective-permute-start | bytes 3080 | tf_op jit(solution)/shard_map/ppermute | solution.py:18
  127.4 3.6 %collective-permute-start.15 = (f32[2,128]{1,0:T(2,128)S(1)}, f32[2,128]{1,0:T(2,128)S(1)}, u32[]{:S(2)}, u32[]{:S(2)}) collective-permute-start(f32[2,128]{1,0:T(2,128)S(1)} %shard_map.140), channel_id=1, source_target_pairs={{0,1},{1,0},{2,3},{3,2},{4,5},{5,4},{6,7},{7,6},{8,9},{9,8},{10,11... | collective-permute-start | bytes 3080 | tf_op jit(solution)/shard_map/ppermute | solution.py:18
  131.0 8.2 %collective-permute-start.20 = (f32[3328]{0:T(1024)S(1)}, f32[3328]{0:T(1024)S(1)}, u32[]{:S(2)}, u32[]{:S(2)}) collective-permute-start(f32[3328]{0:T(1024)S(1)} %pad_maximum_fusion.9), channel_id=1, source_target_pairs={{0,4},{4,0},{8,12},{12,8},{1,5},{5,1},{9,13},{13,9},{2,6},{6,2},{1... | collective-permute-start | bytes 39944 | tf_op jit(solution)/shard_map/ppermute | solution.py:18
  133.5 9.4 %collective-permute-start.19 = (f32[3328]{0:T(1024)S(1)}, f32[3328]{0:T(1024)S(1)}, u32[]{:S(2)}, u32[]{:S(2)}) collective-permute-start(f32[3328]{0:T(1024)S(1)} %pad_maximum_fusion.9), channel_id=1, source_target_pairs={{0,8},{4,12},{8,0},{12,4},{1,9},{5,13},{9,1},{13,5},{2,10},{6,14},... | collective-permute-start | bytes 39944 | tf_op jit(solution)/shard_map/ppermute | solution.py:18
  134.4 8.6 %collective-permute-start.18 = (f32[3328]{0:T(1024)S(1)}, f32[3328]{0:T(1024)S(1)}, u32[]{:S(2)}, u32[]{:S(2)}) collective-permute-start(f32[3328]{0:T(1024)S(1)} %pad_maximum_fusion.9), channel_id=1, source_target_pairs={{0,12},{4,8},{8,4},{12,0},{1,13},{5,9},{9,5},{13,1},{2,14},{6,10},... | collective-permute-start | bytes 39944 | tf_op jit(solution)/shard_map/ppermute | solution.py:18
  138.5 10.0 %collective-permute-start.23 = (bf16[2048,128]{1,0:T(8,128)(2,1)}, bf16[2048,128]{1,0:T(8,128)(2,1)S(1)}, u32[]{:S(2)}, u32[]{:S(2)}) collective-permute-start(bf16[2048,128]{1,0:T(8,128)(2,1)} %get-tuple-element.68), channel_id=1, source_target_pairs={{12,8},{8,4},{13,9},{9,5},{14,10},{10,6},{15,11},{11,7},{28,24},{2... | collective-permute-start | bytes 1572872 | tf_op jit(solution)/shard_map/ppermute | solution.py:78
  139.2 25.6 %collective-permute-start.22 = (bf16[2048,128]{1,0:T(8,128)(2,1)}, bf16[2048,128]{1,0:T(8,128)(2,1)S(1)}, u32[]{:S(2)}, u32[]{:S(2)}) collective-permute-start(bf16[2048,128]{1,0:T(8,128)(2,1)} %get-tuple-element.69), channel_id=1, source_target_pairs={{0,4},{4,8},{1,5},{5,9},{2,6},{6,10},{3,7},{7,11},{16,20},{20,24},... | collective-permute-start | bytes 1572872 | tf_op jit(solution)/shard_map/ppermute | solution.py:78
  143.2 4.0 %collective-permute-start.21 = (f32[4096]{0:T(1024)S(1)}, f32[4096]{0:T(1024)S(1)}, u32[]{:S(2)}, u32[]{:S(2)}) collective-permute-start(f32[4096]{0:T(1024)S(1)} %pad_maximum_fusion.10), channel_id=1, source_target_pairs={{0,16},{16,0},{1,17},{17,1},{2,18},{18,2},{3,19},{19,3},{4,20},{20... | collective-permute-start | bytes 49160 | tf_op jit(solution)/shard_map/ppermute | solution.py:18
  170.4 18.9 %collective-permute-start.25 = (f32[2,1024]{1,0:T(2,128)}, f32[2,1024]{1,0:T(2,128)S(1)}, u32[]{:S(2)}, u32[]{:S(2)}) collective-permute-start(f32[2,1024]{1,0:T(2,128)} %get-tuple-element.46), channel_id=1, source_target_pairs={{0,16},{16,0},{1,17},{17,1},{2,18},{18,2},{3,19},{19,3},{4,20},{20... | collective-permute-start | bytes 24584 | tf_op jit(solution)/shard_map/ppermute | solution.py:18
  170.4 20.1 %collective-permute-start.28 = (bf16[1024,128]{1,0:T(8,128)(2,1)}, bf16[1024,128]{1,0:T(8,128)(2,1)S(1)}, u32[]{:S(2)}, u32[]{:S(2)}) collective-permute-start(bf16[1024,128]{1,0:T(8,128)(2,1)} %get-tuple-element.49), channel_id=1, source_target_pairs={{0,16},{16,0},{1,17},{17,1},{2,18},{18,2},{3,19},{19,3},{4,20},{20... | collective-permute-start | bytes 786440 | tf_op jit(solution)/shard_map/ppermute | solution.py:18
  172.1 18.5 %collective-permute-start.26 = (bf16[2048,128]{1,0:T(8,128)(2,1)}, bf16[2048,128]{1,0:T(8,128)(2,1)S(1)}, u32[]{:S(2)}, u32[]{:S(2)}) collective-permute-start(bf16[2048,128]{1,0:T(8,128)(2,1)} %get-tuple-element.66), channel_id=1, source_target_pairs={{0,4},{4,8},{8,12},{1,5},{5,9},{9,13},{2,6},{6,10},{10,14},{3,7},{... | collective-permute-start | bytes 1572872 | tf_op jit(solution)/shard_map/ppermute | solution.py:78
  178.1 15.7 %collective-permute-start.27 = (bf16[2048,128]{1,0:T(8,128)(2,1)}, bf16[2048,128]{1,0:T(8,128)(2,1)S(1)}, u32[]{:S(2)}, u32[]{:S(2)}) collective-permute-start(bf16[2048,128]{1,0:T(8,128)(2,1)} %get-tuple-element.67), channel_id=1, source_target_pairs={{12,8},{8,4},{4,0},{13,9},{9,5},{5,1},{14,10},{10,6},{6,2},{15,11}... | collective-permute-start | bytes 1572872 | tf_op jit(solution)/shard_map/ppermute | solution.py:78
  179.4 9.8 %copy-start.8 = (f32[2,1024]{1,0:T(2,128)S(1)}, f32[2,1024]{1,0:T(2,128)}, u32[]{:S(2)}) copy-start(f32[2,1024]{1,0:T(2,128)} %get-tuple-element.46) | copy-start | bytes 24580
  179.5 11.1 %copy-start.4 = (f32[1024,128]{1,0:T(8,128)S(1)}, f32[1024,128]{1,0:T(8,128)}, u32[]{:S(2)}) copy-start(f32[1024,128]{1,0:T(8,128)} %get-tuple-element.50) | copy-start | bytes 1572868
Sparse Core Ops, SparseCore 0:
  44.8 38.8 reduce-scatter.1
  119.0 45.2 all-gather.1

commit v9 on v8

--- a/solution.py
+++ b/solution.py
@@ -10,7 +10,7 @@
 MAXT = 2
 LANES = 128
 EPSILON = 1e-06
-VMEM = 60 * 1024 * 1024
+VMEM = 32 * 1024 * 1024
 
 
 def swap(x, axis, mask):
@@ -440,16 +440,15 @@
         text_embed, vis_hidden, key_cotangent, groups, n_sec, n_tp, stream,
     )
     pieces = [act] + [swap(act, "tp", m) for m in range(1, n_tp)]
-    pieces[1], text_sq = together(pieces[1], text_sq)
     text_sq = [text_sq] + [swap(text_sq, "tp", m) for m in range(1, n_tp)]
-    partial, act_mine = project(t[None], pieces, proj_weight)
-    text_sq[0], given, act_mine, partial = together(text_sq[0], given, act_mine, partial)
-    summed = lax.psum_scatter(partial, "seq", scatter_dimension=0, tiled=True)
+    text_sq[0], pieces[1] = together(text_sq[0], pieces[1])
 
     scalars = (core[None], z[None], tile_counts, text_counts, owner_map)
     moment, gain_text = text_product(
         scalars, text_embed, key_weight, key_cotangent, text_sq, key_half
     )
+    given, moment = together(given, moment)
+    taken = butterfly(given, ("seq",))
     if n_seq <= 4:
         way = line_step(moment, "seq", 1, None)
     else:
@@ -457,7 +456,13 @@
         moment = moment.reshape(-1, columns, LANES // share, share).transpose(0, 2, 1, 3)
         moment = reduce_to_owner(moment.reshape(n_seq, columns, share), "seq")
 
-    taken = butterfly(given, ("seq",))
+    partial, act_mine = project(t[None], pieces, proj_weight)
+    if n_seq <= 4:
+        way[0], way[1], act_mine, partial = together(*way, act_mine, partial)
+        way = line_step(moment, "seq", 2, way)
+    taken, act_mine, partial = together(taken, act_mine, partial)
+    summed = lax.psum_scatter(partial, "seq", scatter_dimension=0, tiled=True)
+
     key_bias_part = jnp.sum(key_cotangent.astype(f32), 0)
     early = jnp.concatenate([gain_text[0], jnp.where(core == 0, key_bias_part, 0.0)])
 
@@ -479,16 +484,17 @@
         [lax.dynamic_slice_in_dim(c, z * key_share, key_share, 1) for c in (half_cot, other_cot)], 1
     )
 
+    summed, normed_grad, own_grad = together(summed, normed_grad, own_grad)
     image_mine = (summed.astype(f32) + proj_bias).astype(bf16)
     if n_seq <= 4:
         way[0], way[1], image_mine = together(*way, image_mine)
-        way = line_step(moment, "seq", 2, way)
     low, high = image_mine[:, :col_half], image_mine[:, col_half:]
     first_core = core == 0
     came = swap(jnp.where(first_core, high, low), "sec", 1)
     image = jnp.concatenate(in_order([jnp.where(first_core, low, high), came], core), 0)
     rows = lax.all_gather(image, "seq", axis=0, tiled=True)
 
+    image_mine, came = together(image_mine, came)
     sums = total(row_sums(image_mine, own_grad, norm_gain[None]), "tp")
     size = sums.size
     sums = jnp.concatenate([sums.reshape(-1), early])
@@ -504,7 +510,6 @@
     sums = sums.reshape(n_seq * n_sec, 2, -1)
 
     if n_seq <= 4:
-        way[0], way[1], rows = together(*way, rows)
         for step in range(3, n_seq):
             way = line_step(moment, "seq", step, way)
         moment = lax.dynamic_index_in_dim(moment, z, 0, keepdims=False).astype(f32)

time: 203 us -> 193 us (0.951)
  local copies, waits for them, and re-layouts: 8.83 us -> 22.1 us
  Pallas kernels: 38.9 us -> 26.9 us
  waiting for transfers between devices: 71.7 us -> 65.6 us
  starting transfers between devices: 43.9 us -> 39.4 us
  matrix products: 8.7 us -> 4.92 us
  other arithmetic: 15.4 us -> 18.5 us
    ppermute x6, waiting for transfers between devices: 27.7 us -> 0.02 us  [line_step(): out.append(lax.ppermute(sent, axis, pairs))]
    all_gather x1, waiting for transfers between devices: 0.01 us -> 19.5 us  [on_device(): rows = lax.all_gather(image, 'seq', axis=0, tiled=True)]
    reduce_scatter x1, waiting for transfers between devices: 0.02 us -> 18 us  [on_device(): summed = lax.psum_scatter(partial, 'seq', scatter_dimension=0, tiled=True)]
    ppermute x23, waiting for transfers between devices: 44 us -> 28.1 us  [swap(): return lax.ppermute(x, axis, [(i, i ^ mask) for i in range(count)])]
    unnamed x33 -> x45, local copies, waits for them, and re-layouts: 1.98 us -> 15.7 us
    pallas_call x1, Pallas kernels: 9.94 us -> 6.34 us  [text_product(): pl.pallas_call(text_kernel, grid_spec=pltpu.PrefetchScalarGridSpec(num_sc...]
    pallas_call x1, Pallas kernels: 5.34 us -> 2 us  [opening(): pl.pallas_call(opening_kernel, grid_spec=pltpu.PrefetchScalarGridSpec(num...]
    pallas_call x1, Pallas kernels: 9.82 us -> 7.01 us  [weight_product(): pl.pallas_call(weight_kernel, grid=(features // step,), in_specs=[pl.Bloc...]
  transfers between devices with their start and end apart: 31 -> 31, of which waited for: 12 -> 11; matrix products, arithmetic and copies ran while one was open for 15% -> 14% of each run, Pallas kernels for 10% -> 13%
where the time goes in v9:
time: 193 us; the launch traced here: 192 us
  waiting for transfers between devices  65.6 us (34%)
  starting transfers between devices  39.4 us (20%)
  Pallas kernels  26.9 us (14%)
  local copies, waits for them, and re-layouts  22.1 us (11%)
  other arithmetic  18.5 us (10%)
  between operations  14.5 us (8%)
  matrix products  4.92 us (3%)
    ppermute x23, waiting for transfers between devices, swap(): return lax.ppermute(x, axis, [(i, i ^ mask) for i in range(count)])  28.1 us
    ppermute x23, starting transfers between devices, swap(): return lax.ppermute(x, axis, [(i, i ^ mask) for i in range(count)])  23.6 us
    all_gather x1, waiting for transfers between devices, on_device(): rows = lax.all_gather(image, 'seq', axis=0, tiled=True)  19.5 us
    reduce_scatter x1, waiting for transfers between devices, on_device(): summed = lax.psum_scatter(partial, 'seq', scatter_dimension=0, tiled=True)  18 us
    unnamed x45, local copies, waits for them, and re-layouts  15.7 us
    ppermute x6, starting transfers between devices, line_step(): out.append(lax.ppermute(sent, axis, pairs))  15.7 us
    pallas_call x1, Pallas kernels, weight_product(): pl.pallas_call(weight_kernel, grid=(features // step,), in_specs=[pl.Bloc...  7.01 us
    pallas_call x1, Pallas kernels, text_product(): pl.pallas_call(text_kernel, grid_spec=pltpu.PrefetchScalarGridSpec(num_sc...  6.34 us
  transfers between devices with their start and end apart: 31, of which 11 were waited for; matrix products, arithmetic and copies ran while one was open for 14% of the time, Pallas kernels for 13%

profile of v9, /device:TPU:0, one launch (start us, length us, event | category | flops | bytes accessed | tf_op | source)
XLA Modules:
  0.0 191.9 jit_solution(6069525306627714466)
XLA Ops:
  7.2 1.6 copy-done
  8.8 2.2 %copy-done.2 = bf16[1024,2048]{1,0:T(8,128)(2,1)S(1)} copy-done((bf16[1024,2048]{1,0:T(8,128)(2,1)S(1)}, bf16[1024,2048]{1,0:T(8,128)(2,1)}, u32[]{:S(2)}) %copy-start.2) | copy-done | bytes 4194328
  11.0 1.1 copy-done.11
  12.1 0.7 copy-done.13
  12.8 0.7 copy-done.15
  13.5 2.0 %shard_map.137 = (f32[1,1024]{1,0:T(1,128)S(1)}, bf16[96,2048]{1,0:T(8,128)(2,1)S(1)}, bf16[768,128]{1,0:T(8,128)(2,1)S(1)}) custom-call(s32[1]{0:T(128)} %bitcast.core_ref, s32[1]{0:T(128)} %bitcast.1.z_ref, s32[1]{0:T(128)} %bitcast.2.t_ref.refs_0_, s32[4]{0:T(128)S(1)} %copy-done.13, s32[4]{0:T(128)S(1)} %copy-done.15, bf16[1024,2048]{1,0:T(8,128)(2,1)S(1)} %copy-done.2, ...), custom_call_target="tpu_custom_call" | custom-call | flops 12058624 | bytes 4194304 | tf_op jit(solution)/shard_map/pallas_call | solution.py:193
  15.5 3.0 %collective-permute-start = (bf16[96,2048]{1,0:T(8,128)(2,1)S(1)}, bf16[96,2048]{1,0:T(8,128)(2,1)S(1)}, u32[]{:S(2)}, u32[]{:S(2)}) collective-permute-start(bf16[96,2048]{1,0:T(8,128)(2,1)S(1)} %get-tuple-element.36.refs_2_), channel_id=1, source_target_pairs={{0,1},{1,0},{2,3},{3,2},{4,5},{5,4},{6,7},{7,6},{8,9},{9,8},{10,11... | collective-permute-start | bytes 1179656 | tf_op jit(solution)/shard_map/ppermute | solution.py:18
  18.5 1.5 collective-permute-start.3
  20.0 1.9 %collective-permute-start.1 = (f32[1,1024]{1,0:T(1,128)S(1)}, f32[1,1024]{1,0:T(1,128)S(1)}, u32[]{:S(2)}, u32[]{:S(2)}) collective-permute-start(f32[1,1024]{1,0:T(1,128)S(1)} %get-tuple-element.37.refs_0_), channel_id=1, source_target_pairs={{0,1},{1,0},{2,3},{3,2},{4,5},{5,4},{6,7},{7,6},{8,9},{9,8},{10,11... | collective-permute-start | bytes 12296 | tf_op jit(solution)/shard_map/ppermute | solution.py:18
  22.0 1.5 collective-permute-start.9
  23.4 5.0 %collective-permute-done.refs_3_ = bf16[96,2048]{1,0:T(8,128)(2,1)S(1)} collective-permute-done((bf16[96,2048]{1,0:T(8,128)(2,1)S(1)}, bf16[96,2048]{1,0:T(8,128)(2,1)S(1)}, u32[]{:S(2)}, u32[]{:S(2)}) %collective-permute-start) | collective-permute-done | bytes 393248 | tf_op jit(solution)/shard_map/ppermute | solution.py:18
  28.4 2.1 %collective-permute-start.8 = (bf16[96,2048]{1,0:T(8,128)(2,1)S(1)}, bf16[96,2048]{1,0:T(8,128)(2,1)S(1)}, u32[]{:S(2)}, u32[]{:S(2)}) collective-permute-start(bf16[96,2048]{1,0:T(8,128)(2,1)S(1)} %get-tuple-element.36.refs_2_), channel_id=1, source_target_pairs={{0,2},{1,3},{2,0},{3,1},{4,6},{5,7},{6,4},{7,5},{8,10},{9,11},{10,... | collective-permute-start | bytes 1179656 | tf_op jit(solution)/shard_map/ppermute | solution.py:18
  30.6 2.2 %copy-done.3 = bf16[1024,2048]{1,0:T(8,128)(2,1)S(1)} copy-done((bf16[1024,2048]{1,0:T(8,128)(2,1)S(1)}, bf16[1024,2048]{1,0:T(8,128)(2,1)}, u32[]{:S(2)}) %copy-start.3) | copy-done | bytes 4194328
  32.7 2.2 %copy-done.4 = bf16[2048,1024]{1,0:T(8,128)(2,1)S(1)} copy-done((bf16[2048,1024]{1,0:T(8,128)(2,1)S(1)}, bf16[2048,1024]{1,0:T(8,128)(2,1)}, u32[]{:S(2)}) %copy-start.4) | copy-done | bytes 4194328
  34.9 6.3 %shard_map.138 = (bf16[4,2048,128]{2,1,0:T(8,128)(2,1)S(1)}, f32[1,2048]{1,0:T(1,128)S(1)}) custom-call(s32[1]{0:T(128)} %bitcast.core_ref, s32[1]{0:T(128)} %bitcast.1.z_ref, s32[4]{0:T(128)S(1)} %copy-done.14, s32[4]{0:T(128)S(1)} %copy-done.17, s32[4]{0:T(128)S(1)} %copy-done.16, bf16[1024,2048]{1,0:T(8,128)(2,1)S(1)} %copy-done.3, ...), custom_call_target="tpu_custom_call" | custom-call | flops 2147483648 | bytes 9437184 | tf_op jit(solution)/shard_map/pallas_call | solution.py:264
  41.3 1.3 copy-done.6
  42.7 1.5 collective-permute-start.7
  44.2 4.3 %collective-permute-start.6 = (bf16[2048,128]{1,0:T(8,128)(2,1)S(1)}, bf16[2048,128]{1,0:T(8,128)(2,1)}, u32[]{:S(2)}, u32[]{:S(2)}) collective-permute-start(bf16[2048,128]{1,0:T(8,128)(2,1)S(1)} %get-tuple-element.83), channel_id=1, source_target_pairs={{0,4},{1,5},{2,6},{3,7},{16,20},{17,21},{18,22},{19,23}} | collective-permute-start | bytes 1572872 | tf_op jit(solution)/shard_map/ppermute | solution.py:78
  48.5 13.2 %collective-permute-done.4 = bf16[768,128]{1,0:T(8,128)(2,1)S(1)} collective-permute-done((bf16[768,128]{1,0:T(8,128)(2,1)S(1)}, bf16[768,128]{1,0:T(8,128)(2,1)S(1)}, u32[]{:S(2)}, u32[]{:S(2)}) %collective-permute-start.4) | collective-permute-done | bytes 196640 | tf_op jit(solution)/shard_map/ppermute | solution.py:18
  61.8 1.1 collective-permute-start.5
  62.9 5.6 %shard_map.139 = (bf16[384,2048]{1,0:T(8,128)(2,1)S(1)}, bf16[384,2048]{1,0:T(8,128)(2,1)S(1)}) custom-call(s32[1]{0:T(128)} %bitcast.2.t_ref.refs_0_, bf16[2048,2048]{1,0:T(8,128)(2,1)S(1)} %copy-done.18, bf16[96,2048]{1,0:T(8,128)(2,1)S(1)} %get-tuple-element.36.refs_2_, bf16[96,2048]{1,0:T(8,128)(2,1)S(1)} %collective-permute-done.refs_3_, ...), custom_call_target="tpu_custom_call" | custom-call | flops 3221225472 | bytes 13107200 | tf_op jit(solution)/shard_map/pallas_call | solution.py:128
  68.6 1.2 copy-done.9
  69.7 1.1 copy-done.10
  71.0 1.6 collective-permute-start.13
  73.1 1.5 collective-permute-start.11
  74.6 2.2 %collective-permute-done.13 = bf16[768,128]{1,0:T(8,128)(2,1)S(1)} collective-permute-done((bf16[768,128]{1,0:T(8,128)(2,1)S(1)}, bf16[768,128]{1,0:T(8,128)(2,1)S(1)}, u32[]{:S(2)}, u32[]{:S(2)}) %collective-permute-start.13) | collective-permute-done | bytes 196640 | tf_op jit(solution)/shard_map/ppermute | solution.py:18
  76.8 3.6 %collective-permute-done.12 = bf16[768,128]{1,0:T(8,128)(2,1)S(1)} collective-permute-done((bf16[768,128]{1,0:T(8,128)(2,1)S(1)}, bf16[768,128]{1,0:T(8,128)(2,1)S(1)}, u32[]{:S(2)}, u32[]{:S(2)}) %collective-permute-start.12) | collective-permute-done | bytes 196640 | tf_op jit(solution)/shard_map/ppermute | solution.py:18
  80.4 1.0 broadcast_select_fusion.13
  81.4 1.0 pad_maximum_fusion.2
  82.3 2.6 %copy.23 = bf16[384,2048]{0,1:T(8,128)(2,1)} copy(bf16[384,2048]{1,0:T(8,128)(2,1)} %copy-done.10) | data formatting | bytes 3145728 | tf_op jit(solution)/shard_map/optimization_barrier | solution.py:48
  84.9 2.9 %fusion.6 = (bf16[2048,128]{1,0:T(8,128)(2,1)}, bf16[2048,128]{1,0:T(8,128)(2,1)}) fusion(bf16[2048,128]{1,0:T(8,128)(2,1)} %collective-permute-done.7, bf16[4,2048,128]{2,1,0:T(8,128)(2,1)} %copy-done.6, s32[]{:T(128)S(6)} %min.22, bf16[2048,128]{1,0:T(8,128)(2,1)} %collective-permute-done.6, s32[]{:T(128)S(6)} %min.21), kind=kLoop, calls=%fused_computation.16 | loop fusion | flops 2097152 | bytes 3145736 | tf_op jit(solution)/shard_map/convert_element_type | solution.py:75
  87.8 1.5 collective-permute-start.16
  89.3 4.0 %collective-permute-start.15 = (bf16[2048,128]{1,0:T(8,128)(2,1)}, bf16[2048,128]{1,0:T(8,128)(2,1)}, u32[]{:S(2)}, u32[]{:S(2)}) collective-permute-start(bf16[2048,128]{1,0:T(8,128)(2,1)} %get-tuple-element.81), channel_id=1, source_target_pairs={{0,4},{4,8},{1,5},{5,9},{2,6},{6,10},{3,7},{7,11},{16,20},{20,24},... | collective-permute-start | bytes 1572872 | tf_op jit(solution)/shard_map/ppermute | solution.py:78
  93.5 1.6 broadcast_select_fusion.1
  95.1 1.4 fusion.9.grad_ref
  96.6 3.5 %fusion.grad_ref = f32[768,1024]{1,0:T(8,128)} fusion(bf16[2048,1024]{1,0:T(8,128)(2,1)S(1)} %copy-done.5, s32[]{:T(128)S(6)} %select_n.188, bf16[768,512]{1,0:T(8,128)(2,1)S(1)} %get-tuple-element.85, bf16[768,512]{1,0:T(8,128)(2,1)S(1)} %get-tuple-element.84), kind=kOutput, calls=%fused_computation.2 | convolution fusion | flops 1613758464 | bytes 6815748 | tf_op jit(solution)/shard_map/dot_general | solution.py:475
  100.1 18.0 %reduce-scatter.2.cloned.1.call-done = bf16[96,2048]{1,0:T(8,128)(2,1)} async-done(((bf16[384,2048]{1,0:T(8,128)(2,1)}), bf16[96,2048]{1,0:T(8,128)(2,1)}) %reduce-scatter.2.cloned.1.call-update) | async-done | bytes 393232 | tf_op jit(solution)/shard_map/reduce_scatter | solution.py:464
  118.1 1.1 add_convert_fusion.rows_ref
  119.6 1.1 collective-permute-done.17
  120.8 0.8 pad_maximum_fusion.4
  121.6 0.6 dynamic_slice.41
  122.2 0.9 constant_dynamic-slice_fusion.1
  123.1 0.9 constant_dynamic-slice_fusion
  124.3 2.5 %collective-permute-start.20 = (f32[2,128]{1,0:T(2,128)S(1)}, f32[2,128]{1,0:T(2,128)S(1)}, u32[]{:S(2)}, u32[]{:S(2)}) collective-permute-start(f32[2,128]{1,0:T(2,128)S(1)} %shard_map.140), channel_id=1, source_target_pairs={{0,3},{1,2},{2,1},{3,0},{4,7},{5,6},{6,5},{7,4},{8,11},{9,10},{10,... | collective-permute-start | bytes 3080 | tf_op jit(solution)/shard_map/ppermute | solution.py:18
  126.8 0.5 collective-permute-start.19
  127.9 0.8 pad_maximum_fusion.3.cot_ref
  128.9 1.5 collective-permute-done.19
  130.4 0.5 collective-permute-done.18
  131.0 1.5 collective-permute-start.22
  132.5 2.9 %collective-permute-start.21 = (f32[3328]{0:T(1024)S(1)}, f32[3328]{0:T(1024)S(1)}, u32[]{:S(2)}, u32[]{:S(2)}) collective-permute-start(f32[3328]{0:T(1024)S(1)} %pad_maximum_fusion.9), channel_id=1, source_target_pairs={{0,12},{4,8},{8,4},{12,0},{1,13},{5,9},{9,5},{13,1},{2,14},{6,10},... | collective-permute-start | bytes 39944 | tf_op jit(solution)/shard_map/ppermute | solution.py:18
  135.4 2.2 %maximum_bitcast_fusion.act_ref = bf16[2048,768]{1,0:T(8,128)(2,1)S(1)} fusion(bf16[384,2048]{0,1:T(8,128)(2,1)} %collective-permute-done.10, bf16[384,2048]{0,1:T(8,128)(2,1)} %copy.23), kind=kLoop, calls=%fused_computation.1 | loop fusion | flops 6291456 | bytes 6291456 | tf_op jit(solution)/shard_map/transpose | solution.py:523
  137.6 0.8 collective-permute-done.21
  138.7 2.5 %fusion.4 = (bf16[2048,128]{1,0:T(8,128)(2,1)}, bf16[2048,128]{1,0:T(8,128)(2,1)}) fusion(bf16[2048,128]{1,0:T(8,128)(2,1)} %collective-permute-done.15, bf16[4,2048,128]{2,1,0:T(8,128)(2,1)S(1)} %copy-done.7, s32[]{:T(128)S(6)} %min.23, bf16[2048,128]{1,0:T(8,128)(2,1)} %collective-permute-done.16, s32[]{:T(128)S(6)} %min.24), kind=kLoop, calls=%fused_computation.12 | loop fusion | flops 2097152 | bytes 3145736 | tf_op jit(solution)/shard_map/convert_element_type | solution.py:75
  141.2 3.0 %collective-permute-start.26 = (bf16[2048,128]{1,0:T(8,128)(2,1)}, bf16[2048,128]{1,0:T(8,128)(2,1)}, u32[]{:S(2)}, u32[]{:S(2)}) collective-permute-start(bf16[2048,128]{1,0:T(8,128)(2,1)} %get-tuple-element.78), channel_id=1, source_target_pairs={{0,4},{4,8},{8,12},{1,5},{5,9},{9,13},{2,6},{6,10},{10,14},{3,7},{... | collective-permute-start | bytes 1572872 | tf_op jit(solution)/shard_map/ppermute | solution.py:78
  144.1 1.5 collective-permute-start.27
  145.7 0.6 copy.24
  146.3 0.6 slice.32
  146.9 19.5 %all-gather.2.cloned.1.call-done.rows_ref = bf16[768,1024]{1,0:T(8,128)(2,1)} async-done(((bf16[192,1024]{1,0:T(8,128)(2,1)}), bf16[768,1024]{1,0:T(8,128)(2,1)}) %all-gather.2.cloned.1.call-update) | async-done | bytes 1572880 | tf_op jit(solution)/shard_map/all_gather | solution.py:495
  166.4 5.7 %shard_map.141 = (bf16[768,1024]{1,0:T(8,128)(2,1)}, f32[1024,128]{1,0:T(8,128)}, bf16[1024,128]{1,0:T(8,128)(2,1)}, f32[2,1024]{1,0:T(2,128)}) custom-call(s32[1]{0:T(128)} %bitcast.core_ref, f32[768,1024]{1,0:T(8,128)} %fusion.grad_ref, f32[1,1024]{1,0:T(1,128)} %bitcast.53, bf16[768,256]{1,0:T(8,128)(2,1)} %pad_maximum_fusion.3.cot_ref, ...), custom_call_target="tpu_custom_call" | custom-call | flops 402653184 | bytes 6291456 | tf_op jit(solution)/shard_map/pallas_call | solution.py:364
  172.6 1.4 copy-done.8
  174.0 7.0 %shard_map.142 = f32[16384,128]{1,0:T(8,128)} custom-call(bf16[2048,768]{1,0:T(8,128)(2,1)S(1)} %maximum_bitcast_fusion.act_ref, bf16[768,1024]{1,0:T(8,128)(2,1)S(1)} %copy-done.8), custom_call_target="tpu_custom_call" | custom-call | flops 3221225472 | bytes 13107200 | tf_op jit(solution)/shard_map/pallas_call | solution.py:394
  181.0 0.6 pad_maximum_fusion.11
  181.7 0.6 slice_add_fusion
  182.4 2.7 %fusion.2 = f32[2048,128]{1,0:T(8,128)} fusion(f32[1024,128]{1,0:T(8,128)S(1)} %get-tuple-element.87, f32[1024,128]{1,0:T(8,128)S(1)} %get-tuple-element.86, bf16[2048,128]{1,0:T(8,128)(2,1)} %collective-permute-done.27, bf16[2048,128]{1,0:T(8,128)(2,1)} %collective-permute-done.26, f32[2048]{0:T(1024)S(1)} %copy-done.12, bf16[4,2048,128]{2,1,0:T(8,128)(2,1)} %copy-done.6, ...), kind=kLoop, calls=%fused_computation.8 | loop fusion | flops 2097152 | bytes 3678212 | tf_op jit(solution)/shard_map/mul | solution.py:528
  (94 shorter events, 3.6 us)
Async XLA Ops:
  7.2 110.9 %reduce-scatter.2.cloned.1.call-start = ((), (), s32[]{:S(2)}) async-start(), calls=%async_computation.1 | async-start | bytes 1966080 | tf_op jit(solution)/shard_map/reduce_scatter | solution.py:464
  7.2 1.6 copy-start
  8.8 2.2 %copy-start.2 = (bf16[1024,2048]{1,0:T(8,128)(2,1)S(1)}, bf16[1024,2048]{1,0:T(8,128)(2,1)}, u32[]{:S(2)}) copy-start(bf16[1024,2048]{1,0:T(8,128)(2,1)} %text_ref.3) | copy-start | bytes 12582916
  11.0 1.1 copy-start.11
  12.1 0.7 copy-start.13
  12.8 0.7 copy-start.15
  13.4 17.1 %copy-start.1 = (bf16[1024,1024]{1,0:T(8,128)(2,1)S(1)}, bf16[1024,1024]{1,0:T(8,128)(2,1)}, u32[]{:S(2)}) copy-start(bf16[1024,1024]{1,0:T(8,128)(2,1)} %cot_ref.3) | copy-start | bytes 6291460
  13.4 17.1 %copy-start.14 = (s32[4]{0:T(128)S(1)}, s32[4]{0:T(128)}, u32[]{:S(2)}) copy-start(s32[4]{0:T(128)} %tiles_ref.3) | copy-start | bytes 52
  13.4 17.1 %copy-start.16 = (s32[4]{0:T(128)S(1)}, s32[4]{0:T(128)}, u32[]{:S(2)}) copy-start(s32[4]{0:T(128)} %owners_ref.3) | copy-start | bytes 52
  13.5 17.1 %copy-start.17 = (s32[4]{0:T(128)S(1)}, s32[4]{0:T(128)}, u32[]{:S(2)}) copy-start(s32[4]{0:T(128)} %texts_ref.1) | copy-start | bytes 52
  15.5 12.9 %collective-permute-start = (bf16[96,2048]{1,0:T(8,128)(2,1)S(1)}, bf16[96,2048]{1,0:T(8,128)(2,1)S(1)}, u32[]{:S(2)}, u32[]{:S(2)}) collective-permute-start(bf16[96,2048]{1,0:T(8,128)(2,1)S(1)} %get-tuple-element.36.refs_2_), channel_id=1, source_target_pairs={{0,1},{1,0},{2,3},{3,2},{4,5},{5,4},{6,7},{7,6},{8,9},{9,8},{10,11... | collective-permute-start | bytes 1179656 | tf_op jit(solution)/shard_map/ppermute | solution.py:18
  18.5 12.0 %collective-permute-start.3 = (f32[1,1024]{1,0:T(1,128)S(1)}, f32[1,1024]{1,0:T(1,128)S(1)}, u32[]{:S(2)}, u32[]{:S(2)}) collective-permute-start(f32[1,1024]{1,0:T(1,128)S(1)} %get-tuple-element.37.refs_0_), channel_id=1, source_target_pairs={{0,3},{1,2},{2,1},{3,0},{4,7},{5,6},{6,5},{7,4},{8,11},{9,10},{10,... | collective-permute-start | bytes 12296 | tf_op jit(solution)/shard_map/ppermute | solution.py:18
  20.0 10.5 %collective-permute-start.2 = (f32[1,1024]{1,0:T(1,128)S(1)}, f32[1,1024]{1,0:T(1,128)S(1)}, u32[]{:S(2)}, u32[]{:S(2)}) collective-permute-start(f32[1,1024]{1,0:T(1,128)S(1)} %get-tuple-element.37.refs_0_), channel_id=1, source_target_pairs={{0,2},{1,3},{2,0},{3,1},{4,6},{5,7},{6,4},{7,5},{8,10},{9,11},{10,... | collective-permute-start | bytes 12296 | tf_op jit(solution)/shard_map/ppermute | solution.py:18
  20.0 10.5 %collective-permute-start.1 = (f32[1,1024]{1,0:T(1,128)S(1)}, f32[1,1024]{1,0:T(1,128)S(1)}, u32[]{:S(2)}, u32[]{:S(2)}) collective-permute-start(f32[1,1024]{1,0:T(1,128)S(1)} %get-tuple-element.37.refs_0_), channel_id=1, source_target_pairs={{0,1},{1,0},{2,3},{3,2},{4,5},{5,4},{6,7},{7,6},{8,9},{9,8},{10,11... | collective-permute-start | bytes 12296 | tf_op jit(solution)/shard_map/ppermute | solution.py:18
  22.0 40.9 %collective-permute-start.9 = (bf16[96,2048]{1,0:T(8,128)(2,1)S(1)}, bf16[96,2048]{1,0:T(8,128)(2,1)}, u32[]{:S(2)}, u32[]{:S(2)}) collective-permute-start(bf16[96,2048]{1,0:T(8,128)(2,1)S(1)} %get-tuple-element.36.refs_2_), channel_id=1, source_target_pairs={{0,3},{1,2},{2,1},{3,0},{4,7},{5,6},{6,5},{7,4},{8,11},{9,10},{10,... | collective-permute-start | bytes 1179656 | tf_op jit(solution)/shard_map/ppermute | solution.py:18
  28.4 34.5 %collective-permute-start.8 = (bf16[96,2048]{1,0:T(8,128)(2,1)S(1)}, bf16[96,2048]{1,0:T(8,128)(2,1)S(1)}, u32[]{:S(2)}, u32[]{:S(2)}) collective-permute-start(bf16[96,2048]{1,0:T(8,128)(2,1)S(1)} %get-tuple-element.36.refs_2_), channel_id=1, source_target_pairs={{0,2},{1,3},{2,0},{3,1},{4,6},{5,7},{6,4},{7,5},{8,10},{9,11},{10,... | collective-permute-start | bytes 1179656 | tf_op jit(solution)/shard_map/ppermute | solution.py:18
  30.5 2.2 %copy-start.3 = (bf16[1024,2048]{1,0:T(8,128)(2,1)S(1)}, bf16[1024,2048]{1,0:T(8,128)(2,1)}, u32[]{:S(2)}) copy-start(bf16[1024,2048]{1,0:T(8,128)(2,1)} %text_ref.3) | copy-start | bytes 12582916
  32.7 2.2 %copy-start.4 = (bf16[2048,1024]{1,0:T(8,128)(2,1)S(1)}, bf16[2048,1024]{1,0:T(8,128)(2,1)}, u32[]{:S(2)}) copy-start(bf16[2048,1024]{1,0:T(8,128)(2,1)} %weight_ref.1) | copy-start | bytes 12582916
  34.9 28.0 %copy-start.18 = (bf16[2048,2048]{1,0:T(8,128)(2,1)S(1)}, bf16[2048,2048]{1,0:T(8,128)(2,1)}, u32[]{:S(2)}) copy-start(bf16[2048,2048]{1,0:T(8,128)(2,1)} %refs_1_.1) | copy-start | bytes 25165828
  41.3 1.4 copy-start.6
  42.7 28.2 %collective-permute-start.7 = (bf16[2048,128]{1,0:T(8,128)(2,1)S(1)}, bf16[2048,128]{1,0:T(8,128)(2,1)}, u32[]{:S(2)}, u32[]{:S(2)}) collective-permute-start(bf16[2048,128]{1,0:T(8,128)(2,1)S(1)} %get-tuple-element.82), channel_id=1, source_target_pairs={{12,8},{13,9},{14,10},{15,11},{28,24},{29,25},{30,26},{31,27}} | collective-permute-start | bytes 1572872 | tf_op jit(solution)/shard_map/ppermute | solution.py:78
  44.2 26.8 %collective-permute-start.6 = (bf16[2048,128]{1,0:T(8,128)(2,1)S(1)}, bf16[2048,128]{1,0:T(8,128)(2,1)}, u32[]{:S(2)}, u32[]{:S(2)}) collective-permute-start(bf16[2048,128]{1,0:T(8,128)(2,1)S(1)} %get-tuple-element.83), channel_id=1, source_target_pairs={{0,4},{1,5},{2,6},{3,7},{16,20},{17,21},{18,22},{19,23}} | collective-permute-start | bytes 1572872 | tf_op jit(solution)/shard_map/ppermute | solution.py:78
  48.5 13.2 %collective-permute-start.4 = (bf16[768,128]{1,0:T(8,128)(2,1)S(1)}, bf16[768,128]{1,0:T(8,128)(2,1)S(1)}, u32[]{:S(2)}, u32[]{:S(2)}) collective-permute-start(bf16[768,128]{1,0:T(8,128)(2,1)S(1)} %get-tuple-element.39), channel_id=1, source_target_pairs={{0,4},{4,0},{8,12},{12,8},{1,5},{5,1},{9,13},{13,9},{2,6},{6,2},{1... | collective-permute-start | bytes 589832 | tf_op jit(solution)/shard_map/ppermute | solution.py:18
  61.8 9.1 %collective-permute-start.5 = (bf16[768,128]{1,0:T(8,128)(2,1)S(1)}, bf16[768,128]{1,0:T(8,128)(2,1)S(1)}, u32[]{:S(2)}, u32[]{:S(2)}) collective-permute-start(bf16[768,128]{1,0:T(8,128)(2,1)S(1)} %add.91), channel_id=1, source_target_pairs={{0,8},{4,12},{8,0},{12,4},{1,9},{5,13},{9,1},{13,5},{2,10},{6,14},... | collective-permute-start | bytes 589832 | tf_op jit(solution)/shard_map/ppermute | solution.py:18
  68.5 1.2 copy-start.9
  69.7 1.1 copy-start.10
  71.0 95.5 %all-gather.2.cloned.1.call-start = ((), (), s32[]{:S(2)}) async-start(), calls=%async_computation.2 | async-start | bytes 1966080 | tf_op jit(solution)/shard_map/all_gather | solution.py:495
  71.0 5.7 %collective-permute-start.13 = (bf16[768,128]{1,0:T(8,128)(2,1)S(1)}, bf16[768,128]{1,0:T(8,128)(2,1)S(1)}, u32[]{:S(2)}, u32[]{:S(2)}) collective-permute-start(bf16[768,128]{1,0:T(8,128)(2,1)S(1)} %add.92), channel_id=1, source_target_pairs={{0,1},{1,0},{2,3},{3,2},{4,5},{5,4},{6,7},{7,6},{8,9},{9,8},{10,11... | collective-permute-start | bytes 589832 | tf_op jit(solution)/shard_map/ppermute | solution.py:18
  72.6 7.8 %collective-permute-start.12 = (bf16[768,128]{1,0:T(8,128)(2,1)S(1)}, bf16[768,128]{1,0:T(8,128)(2,1)S(1)}, u32[]{:S(2)}, u32[]{:S(2)}) collective-permute-start(bf16[768,128]{1,0:T(8,128)(2,1)S(1)} %add.92), channel_id=1, source_target_pairs={{0,2},{1,3},{2,0},{3,1},{4,6},{5,7},{6,4},{7,5},{8,10},{9,11},{10,... | collective-permute-start | bytes 589832 | tf_op jit(solution)/shard_map/ppermute | solution.py:18
  73.1 7.3 %collective-permute-start.11 = (bf16[768,128]{1,0:T(8,128)(2,1)S(1)}, bf16[768,128]{1,0:T(8,128)(2,1)}, u32[]{:S(2)}, u32[]{:S(2)}) collective-permute-start(bf16[768,128]{1,0:T(8,128)(2,1)S(1)} %add.92), channel_id=1, source_target_pairs={{0,3},{1,2},{2,1},{3,0},{4,7},{5,6},{6,5},{7,4},{8,11},{9,10},{10,... | collective-permute-start | bytes 589832 | tf_op jit(solution)/shard_map/ppermute | solution.py:18
  82.3 11.2 %collective-permute-start.14 = (bf16[768,512]{1,0:T(8,128)(2,1)}, bf16[768,512]{1,0:T(8,128)(2,1)}, u32[]{:S(2)}, u32[]{:S(2)}) collective-permute-start(bf16[768,512]{1,0:T(8,128)(2,1)} %pad_maximum_fusion.2), channel_id=1, source_target_pairs={{0,16},{16,0},{1,17},{17,1},{2,18},{18,2},{3,19},{19,3},{4,20},{20... | collective-permute-start | bytes 2359304 | tf_op jit(solution)/shard_map/ppermute | solution.py:18
  84.9 10.2 %copy-start.5 = (bf16[2048,1024]{1,0:T(8,128)(2,1)S(1)}, bf16[2048,1024]{1,0:T(8,128)(2,1)}, u32[]{:S(2)}) copy-start(bf16[2048,1024]{1,0:T(8,128)(2,1)} %weight_ref.1) | copy-start | bytes 12582916
  87.8 31.3 %collective-permute-start.16 = (bf16[2048,128]{1,0:T(8,128)(2,1)}, bf16[2048,128]{1,0:T(8,128)(2,1)}, u32[]{:S(2)}, u32[]{:S(2)}) collective-permute-start(bf16[2048,128]{1,0:T(8,128)(2,1)} %get-tuple-element.80), channel_id=1, source_target_pairs={{12,8},{8,4},{13,9},{9,5},{14,10},{10,6},{15,11},{11,7},{28,24},{2... | collective-permute-start | bytes 1572872 | tf_op jit(solution)/shard_map/ppermute | solution.py:78
  89.3 29.8 %collective-permute-start.15 = (bf16[2048,128]{1,0:T(8,128)(2,1)}, bf16[2048,128]{1,0:T(8,128)(2,1)}, u32[]{:S(2)}, u32[]{:S(2)}) collective-permute-start(bf16[2048,128]{1,0:T(8,128)(2,1)} %get-tuple-element.81), channel_id=1, source_target_pairs={{0,4},{4,8},{1,5},{5,9},{2,6},{6,10},{3,7},{7,11},{16,20},{20,24},... | collective-permute-start | bytes 1572872 | tf_op jit(solution)/shard_map/ppermute | solution.py:78
  93.3 42.1 %collective-permute-start.10 = (bf16[384,2048]{0,1:T(8,128)(2,1)}, bf16[384,2048]{0,1:T(8,128)(2,1)}, u32[]{:S(2)}, u32[]{:S(2)}) collective-permute-start(bf16[384,2048]{0,1:T(8,128)(2,1)} %copy.23), channel_id=1, source_target_pairs={{0,16},{16,0},{1,17},{17,1},{2,18},{18,2},{3,19},{19,3},{4,20},{20... | collective-permute-start | bytes 4718600 | tf_op jit(solution)/shard_map/ppermute | solution.py:18
  96.6 21.5 %copy-start.20 = (f32[2048]{0:T(1024)S(1)}, f32[2048]{0:T(1024)}, u32[]{:S(2)}) copy-start(f32[2048]{0:T(1024)} %param.12) | copy-start | bytes 24580
  119.2 2.4 %copy-start.12 = (f32[2048]{0:T(1024)S(1)}, f32[2048]{0:T(1024)}, u32[]{:S(2)}) copy-start(f32[2048]{0:T(1024)} %param.14) | copy-start | bytes 24580
  119.2 1.5 collective-permute-start.17
  124.3 4.5 %collective-permute-start.20 = (f32[2,128]{1,0:T(2,128)S(1)}, f32[2,128]{1,0:T(2,128)S(1)}, u32[]{:S(2)}, u32[]{:S(2)}) collective-permute-start(f32[2,128]{1,0:T(2,128)S(1)} %shard_map.140), channel_id=1, source_target_pairs={{0,3},{1,2},{2,1},{3,0},{4,7},{5,6},{6,5},{7,4},{8,11},{9,10},{10,... | collective-permute-start | bytes 3080 | tf_op jit(solution)/shard_map/ppermute | solution.py:18
  126.8 3.6 %collective-permute-start.19 = (f32[2,128]{1,0:T(2,128)S(1)}, f32[2,128]{1,0:T(2,128)S(1)}, u32[]{:S(2)}, u32[]{:S(2)}) collective-permute-start(f32[2,128]{1,0:T(2,128)S(1)} %shard_map.140), channel_id=1, source_target_pairs={{0,2},{1,3},{2,0},{3,1},{4,6},{5,7},{6,4},{7,5},{8,10},{9,11},{10,... | collective-permute-start | bytes 3080 | tf_op jit(solution)/shard_map/ppermute | solution.py:18
  127.4 3.6 %collective-permute-start.18 = (f32[2,128]{1,0:T(2,128)S(1)}, f32[2,128]{1,0:T(2,128)S(1)}, u32[]{:S(2)}, u32[]{:S(2)}) collective-permute-start(f32[2,128]{1,0:T(2,128)S(1)} %shard_map.140), channel_id=1, source_target_pairs={{0,1},{1,0},{2,3},{3,2},{4,5},{5,4},{6,7},{7,6},{8,9},{9,8},{10,11... | collective-permute-start | bytes 3080 | tf_op jit(solution)/shard_map/ppermute | solution.py:18
  131.0 7.7 %copy-start.7 = (bf16[4,2048,128]{2,1,0:T(8,128)(2,1)S(1)}, bf16[4,2048,128]{2,1,0:T(8,128)(2,1)}, u32[]{:S(2)}) copy-start(bf16[4,2048,128]{2,1,0:T(8,128)(2,1)} %copy-done.6) | copy-start | bytes 6291460
  131.0 6.6 %collective-permute-start.23 = (f32[3328]{0:T(1024)S(1)}, f32[3328]{0:T(1024)S(1)}, u32[]{:S(2)}, u32[]{:S(2)}) collective-permute-start(f32[3328]{0:T(1024)S(1)} %pad_maximum_fusion.9), channel_id=1, source_target_pairs={{0,4},{4,0},{8,12},{12,8},{1,5},{5,1},{9,13},{13,9},{2,6},{6,2},{1... | collective-permute-start | bytes 39944 | tf_op jit(solution)/shard_map/ppermute | solution.py:18
  131.0 6.6 %collective-permute-start.22 = (f32[3328]{0:T(1024)S(1)}, f32[3328]{0:T(1024)S(1)}, u32[]{:S(2)}, u32[]{:S(2)}) collective-permute-start(f32[3328]{0:T(1024)S(1)} %pad_maximum_fusion.9), channel_id=1, source_target_pairs={{0,8},{4,12},{8,0},{12,4},{1,9},{5,13},{9,1},{13,5},{2,10},{6,14},... | collective-permute-start | bytes 39944 | tf_op jit(solution)/shard_map/ppermute | solution.py:18
  132.5 5.9 %collective-permute-start.21 = (f32[3328]{0:T(1024)S(1)}, f32[3328]{0:T(1024)S(1)}, u32[]{:S(2)}, u32[]{:S(2)}) collective-permute-start(f32[3328]{0:T(1024)S(1)} %pad_maximum_fusion.9), channel_id=1, source_target_pairs={{0,12},{4,8},{8,4},{12,0},{1,13},{5,9},{9,5},{13,1},{2,14},{6,10},... | collective-permute-start | bytes 39944 | tf_op jit(solution)/shard_map/ppermute | solution.py:18
  138.6 7.0 %collective-permute-start.24 = (f32[4096]{0:T(1024)S(1)}, f32[4096]{0:T(1024)S(1)}, u32[]{:S(2)}, u32[]{:S(2)}) collective-permute-start(f32[4096]{0:T(1024)S(1)} %pad_maximum_fusion.10), channel_id=1, source_target_pairs={{0,16},{16,0},{1,17},{17,1},{2,18},{18,2},{3,19},{19,3},{4,20},{20... | collective-permute-start | bytes 49160 | tf_op jit(solution)/shard_map/ppermute | solution.py:18
  141.2 41.2 %collective-permute-start.26 = (bf16[2048,128]{1,0:T(8,128)(2,1)}, bf16[2048,128]{1,0:T(8,128)(2,1)}, u32[]{:S(2)}, u32[]{:S(2)}) collective-permute-start(bf16[2048,128]{1,0:T(8,128)(2,1)} %get-tuple-element.78), channel_id=1, source_target_pairs={{0,4},{4,8},{8,12},{1,5},{5,9},{9,13},{2,6},{6,10},{10,14},{3,7},{... | collective-permute-start | bytes 1572872 | tf_op jit(solution)/shard_map/ppermute | solution.py:78
  144.1 38.2 %collective-permute-start.27 = (bf16[2048,128]{1,0:T(8,128)(2,1)}, bf16[2048,128]{1,0:T(8,128)(2,1)}, u32[]{:S(2)}, u32[]{:S(2)}) collective-permute-start(bf16[2048,128]{1,0:T(8,128)(2,1)} %get-tuple-element.79), channel_id=1, source_target_pairs={{12,8},{8,4},{4,0},{13,9},{9,5},{5,1},{14,10},{10,6},{6,2},{15,11}... | collective-permute-start | bytes 1572872 | tf_op jit(solution)/shard_map/ppermute | solution.py:78
  172.1 8.9 %collective-permute-start.25 = (f32[2,1024]{1,0:T(2,128)}, f32[2,1024]{1,0:T(2,128)S(1)}, u32[]{:S(2)}, u32[]{:S(2)}) collective-permute-start(f32[2,1024]{1,0:T(2,128)} %get-tuple-element.58), channel_id=1, source_target_pairs={{0,16},{16,0},{1,17},{17,1},{2,18},{18,2},{3,19},{19,3},{4,20},{20... | collective-permute-start | bytes 24584 | tf_op jit(solution)/shard_map/ppermute | solution.py:18
  172.1 10.2 %collective-permute-start.28 = (bf16[1024,128]{1,0:T(8,128)(2,1)}, bf16[1024,128]{1,0:T(8,128)(2,1)S(1)}, u32[]{:S(2)}, u32[]{:S(2)}) collective-permute-start(bf16[1024,128]{1,0:T(8,128)(2,1)} %get-tuple-element.61), channel_id=1, source_target_pairs={{0,16},{16,0},{1,17},{17,1},{2,18},{18,2},{3,19},{19,3},{4,20},{20... | collective-permute-start | bytes 786440 | tf_op jit(solution)/shard_map/ppermute | solution.py:18
  172.6 1.4 copy-start.8
  174.0 7.0 %copy-start.21 = (f32[2,1024]{1,0:T(2,128)S(1)}, f32[2,1024]{1,0:T(2,128)}, u32[]{:S(2)}) copy-start(f32[2,1024]{1,0:T(2,128)} %get-tuple-element.58) | copy-start | bytes 24580
  174.0 8.2 %copy-start.19 = (f32[1024,128]{1,0:T(8,128)S(1)}, f32[1024,128]{1,0:T(8,128)}, u32[]{:S(2)}) copy-start(f32[1024,128]{1,0:T(8,128)} %get-tuple-element.62) | copy-start | bytes 1572868
Sparse Core Ops, SparseCore 0:
  71.1 46.9 reduce-scatter.1
  121.7 44.7 all-gather.1

commit v10 on v2

--- a/solution.py
+++ b/solution.py
@@ -218,19 +218,22 @@
     key_bias_part = jnp.sum(key_cotangent.astype(f32), 0)
     bias_part = jnp.sum(embed_grad.astype(f32), 0)
     once = jnp.concatenate([key_bias_part, bias_part])
-    small = butterfly(jnp.concatenate([gain_part, jnp.where(core == 0, once, 0.0)]), ("sec", "seq"))
-    gain_grad = small[:columns]
-    key_bias_grad = small[columns : columns + keys]
-    proj_bias_grad = small[columns + keys :]
+    small = total(jnp.concatenate([gain_part, jnp.where(core == 0, once, 0.0)]), "sec")
 
     if n_seq <= 4:
         up, down = along_line(grad_half, "seq")
+        small, up[-1], down[-1] = lax.optimization_barrier((small, up[-1], down[-1]))
+        small = total(small, "seq")
         around = jnp.concatenate([act_full[::-1], act_full[::-1]], 0)
         act_used = lax.dynamic_slice_in_dim(around, n_seq - 1 - z, n_seq, 0)
         product = weight_product(act_used.reshape(stream, features), grad_half, up + down)
     else:
+        small = butterfly(small, ("seq",))
         grads = lax.all_gather(grad_half, "seq", axis=0, tiled=True)
         product = weight_product(act_full.reshape(stream, features), grads, [])
+    gain_grad = small[:columns]
+    key_bias_grad = small[columns : columns + keys]
+    proj_bias_grad = small[columns + keys :]
     proj_weight_grad = product.reshape(features, 1, 1, col_half)
     return (proj_weight_grad, proj_bias_grad, key_weight_grad, key_bias_grad, gain_grad)
 

time: 186 us -> 193 us (1.038)
  starting transfers between devices: 32 us -> 38.2 us
  waiting for transfers between devices: 65.8 us -> 68.3 us
  other arithmetic: 24.3 us -> 22.3 us
    ppermute x3, waiting for transfers between devices: 10.7 us -> 42.2 us  [along_line(): lax.ppermute(left, axis, [(j, j - 1) for j in range(1, count - i + 1)])]
    ppermute x21 -> x22, waiting for transfers between devices: 55 us -> 26 us  [swap(): return lax.ppermute(x, axis, [(i, i ^ mask) for i in range(count)])]
    ppermute x21 -> x22, starting transfers between devices: 24.9 us -> 28.2 us  [swap(): return lax.ppermute(x, axis, [(i, i ^ mask) for i in range(count)])]
    ppermute x3, starting transfers between devices: 3.03 us -> 5.94 us  [along_line(): lax.ppermute(right, axis, [(j, j + 1) for j in range(i - 1, count - 1)])]
    unnamed x37 -> x43, local copies, waits for them, and re-layouts: 7.27 us -> 7.56 us
  transfers between devices with their start and end apart: 29 -> 30, of which waited for: 10 -> 10; matrix products, arithmetic and copies ran while one was open for 25% -> 23% of each run, Pallas kernels for 4% -> 4%
where the time goes in v10:
time: 193 us
  waiting for transfers between devices  68.3 us (35%)
  starting transfers between devices  38.2 us (20%)
  local copies, waits for them, and re-layouts  23.3 us (12%)
  other arithmetic  22.3 us (12%)
  matrix products  17.3 us (9%)
  between operations  15.4 us (8%)
  Pallas kernels  7.63 us (4%)
    ppermute x3, waiting for transfers between devices, along_line(): lax.ppermute(left, axis, [(j, j - 1) for j in range(1, count - i + 1)])  42.2 us
    ppermute x22, starting transfers between devices, swap(): return lax.ppermute(x, axis, [(i, i ^ mask) for i in range(count)])  28.2 us
    ppermute x22, waiting for transfers between devices, swap(): return lax.ppermute(x, axis, [(i, i ^ mask) for i in range(count)])  26 us
    pallas_call x1, Pallas kernels, weight_product(): pl.pallas_call(weight_kernel, grid=(features // step,), in_specs=[pl.Bloc...  7.63 us
    unnamed x43, local copies, waits for them, and re-layouts  7.56 us
    dot_general x2, matrix products, on_device(): jnp.dot(chunk, proj_weight, preferred_element_type=f32).astype(bf16)  7.24 us
    ppermute x3, starting transfers between devices, along_line(): lax.ppermute(right, axis, [(j, j + 1) for j in range(i - 1, count - 1)])  5.94 us
    dot_general x1, matrix products, on_device(): lax.dot_general(text_embed, cot_text, rows_first, preferred_element_type=...  4.84 us
  transfers between devices with their start and end apart: 30, of which 10 were waited for; matrix products, arithmetic and copies ran while one was open for 23% of the time, Pallas kernels for 4%

profile of v10, /device:TPU:0, one launch (start us, length us, event | category | flops | bytes accessed | tf_op | source)
XLA Modules:
  0.0 192.5 jit_solution(14495515296418599156)
XLA Ops:
  7.3 3.1 %multiply_reduce_fusion = f32[1024]{0:T(1024)S(1)} fusion(bf16[1024,2048]{1,0:T(8,128)(2,1)} %param.13), kind=kLoop, calls=%fused_computation | loop fusion | flops 6290432 | bytes 4198400 | tf_op jit(solution)/shard_map/reduce_sum | solution.py:187
  10.4 4.0 %collective-permute-start.19 = (f32[1024]{0:T(1024)S(1)}, f32[1024]{0:T(1024)S(1)}, u32[]{:S(2)}, u32[]{:S(2)}) collective-permute-start(f32[1024]{0:T(1024)S(1)} %multiply_reduce_fusion), channel_id=1, source_target_pairs={{0,3},{1,2},{2,1},{3,0},{4,7},{5,6},{6,5},{7,4},{8,11},{9,10},{10,... | collective-permute-start | bytes 12296 | tf_op jit(solution)/shard_map/ppermute | solution.py:17
  14.4 0.5 collective-permute-start.18
  15.0 1.7 fusion.9
  16.7 2.0 %collective-permute-start.1 = (bf16[96,2048]{1,0:T(8,128)(2,1)S(1)}, bf16[96,2048]{1,0:T(8,128)(2,1)}, u32[]{:S(2)}, u32[]{:S(2)}) collective-permute-start(bf16[96,2048]{1,0:T(8,128)(2,1)S(1)} %fusion.9), channel_id=1, source_target_pairs={{0,2},{1,3},{2,0},{3,1},{4,6},{5,7},{6,4},{7,5},{8,10},{9,11},{10,... | collective-permute-start | bytes 1179656 | tf_op jit(solution)/shard_map/ppermute | solution.py:17
  18.7 1.4 collective-permute-start
  20.3 0.6 fusion.49
  21.9 0.8 copy.34
  23.6 3.1 %constant_dynamic-slice_fusion = bf16[2048,512]{1,0:T(8,128)(2,1)} fusion(bf16[2048,1024]{1,0:T(8,128)(2,1)} %param.15, s32[]{:T(128)S(6)} %select_n.357), kind=kLoop, calls=%fused_computation.111 | loop fusion | bytes 4194308 | tf_op jit(solution)/shard_map/dynamic_slice | solution.py:211
  26.7 3.0 %copy.40 = bf16[2048,512]{0,1:T(8,128)(2,1)S(1)} copy(bf16[2048,512]{1,0:T(8,128)(2,1)} %constant_dynamic-slice_fusion) | data formatting | bytes 4194304
  29.7 2.3 %constant_dynamic-slice_fusion.1 = bf16[1024,512]{1,0:T(8,128)(2,1)} fusion(bf16[1024,1024]{1,0:T(8,128)(2,1)} %param.16, s32[]{:T(128)S(6)} %select_n.357), kind=kLoop, calls=%fused_computation.114 | loop fusion | bytes 2097156 | tf_op jit(solution)/shard_map/dynamic_slice | solution.py:191
  31.9 3.7 %collective-permute-done.1 = bf16[96,2048]{1,0:T(8,128)(2,1)} collective-permute-done((bf16[96,2048]{1,0:T(8,128)(2,1)S(1)}, bf16[96,2048]{1,0:T(8,128)(2,1)}, u32[]{:S(2)}, u32[]{:S(2)}) %collective-permute-start.1) | collective-permute-done | bytes 393248 | tf_op jit(solution)/shard_map/ppermute | solution.py:17
  35.6 1.6 collective-permute-start.2
  37.2 1.3 pad_maximum_fusion.2
  38.6 5.4 %convolution_convert_fusion.1 = bf16[192,2048]{1,0:T(8,128)(2,1)S(1)} fusion(bf16[192,2048]{1,0:T(8,128)(2,1)S(1)} %bitcast.76, bf16[2048,2048]{1,0:T(8,128)(2,1)} %param.11), kind=kOutput, calls=%fused_computation.11 | convolution fusion | flops 1611005952 | bytes 9961472 | tf_op jit(solution)/shard_map/dot_general | solution.py:173
  44.0 1.7 collective-permute-start.4
  45.8 1.9 convolution_convert_fusion
  47.7 0.8 collective-permute-start.6
  48.5 9.7 %collective-permute-done.4 = bf16[2,48,2048]{2,1,0:T(8,128)(2,1)S(1)} collective-permute-done((bf16[2,48,2048]{2,1,0:T(8,128)(2,1)S(1)}, bf16[2,48,2048]{2,1,0:T(8,128)(2,1)S(1)}, u32[]{:S(2)}, u32[]{:S(2)}) %collective-permute-start.4) | collective-permute-done | bytes 393248 | tf_op jit(solution)/shard_map/ppermute | solution.py:17
  58.4 1.8 collective-permute-start.5
  60.1 3.8 %collective-permute-done.6 = bf16[2,48,2048]{2,1,0:T(8,128)(2,1)S(1)} collective-permute-done((bf16[2,48,2048]{2,1,0:T(8,128)(2,1)S(1)}, bf16[2,48,2048]{2,1,0:T(8,128)(2,1)S(1)}, u32[]{:S(2)}, u32[]{:S(2)}) %collective-permute-start.6) | collective-permute-done | bytes 393248 | tf_op jit(solution)/shard_map/ppermute | solution.py:17
  64.1 0.9 copy-done.6
  65.0 2.1 %collective-permute-start.7 = (bf16[1,48,2048]{2,1,0:T(8,128)(2,1)S(1)}, bf16[1,48,2048]{2,1,0:T(8,128)(2,1)}, u32[]{:S(2)}, u32[]{:S(2)}) collective-permute-start(bf16[1,48,2048]{2,1,0:T(8,128)(2,1)S(1)} %dynamic-slice_convert_fusion), channel_id=1, source_target_pairs={{0,8},{4,12},{8,0},{12,4},{1,9},{5,13},{9,1},{13,5},{2,10},{6,14},... | collective-permute-start | bytes 589832 | tf_op jit(solution)/shard_map/ppermute | solution.py:17
  67.1 0.7 rsqrt_select_fusion
  67.8 0.6 collective-permute-start.11
  68.4 2.3 %collective-permute-start.10 = (bf16[192,256]{1,0:T(8,128)(2,1)}, bf16[192,256]{1,0:T(8,128)(2,1)S(1)}, u32[]{:S(2)}, u32[]{:S(2)}) collective-permute-start(bf16[192,256]{1,0:T(8,128)(2,1)} %reduce-scatter.3.cloned.1.call-done), channel_id=1, source_target_pairs={{0,2},{1,3},{2,0},{3,1},{4,6},{5,7},{6,4},{7,5},{8,10},{9,11},{10,... | collective-permute-start | bytes 294920 | tf_op jit(solution)/shard_map/ppermute | solution.py:17
  70.7 0.9 collective-permute-start.9
  71.6 1.2 collective-permute-done.5
  72.8 3.6 %collective-permute-done.7 = bf16[1,48,2048]{2,1,0:T(8,128)(2,1)} collective-permute-done((bf16[1,48,2048]{2,1,0:T(8,128)(2,1)S(1)}, bf16[1,48,2048]{2,1,0:T(8,128)(2,1)}, u32[]{:S(2)}, u32[]{:S(2)}) %collective-permute-start.7) | collective-permute-done | bytes 196640 | tf_op jit(solution)/shard_map/ppermute | solution.py:17
  76.3 1.2 fusion.39
  77.7 4.8 %fusion.6 = f32[512,2048]{1,0:T(8,128)S(1)} fusion(bf16[1024,2048]{1,0:T(8,128)(2,1)} %param.13, s32[]{:T(128)S(6)} %select_n.359, bf16[1024,512]{1,0:T(8,128)(2,1)S(1)} %copy-done.10, f32[1024]{0:T(1024)S(1)} %rsqrt_select_fusion), kind=kOutput, calls=%fused_computation.27 | convolution fusion | flops 2149056512 | bytes 9441284 | tf_op jit(solution)/shard_map/dot_general | solution.py:196
  82.9 0.4 copy-done.15
  83.3 2.7 %fusion.1 = (f32[192]{0:T(256)S(1)}, f32[192]{0:T(256)S(1)}, f32[192,2048]{1,0:T(8,128)}) fusion(bf16[96,2048]{1,0:T(8,128)(2,1)S(1)} %get-tuple-element.50, bf16[96,2048]{1,0:T(8,128)(2,1)S(1)} %get-tuple-element.49, f32[2048]{0:T(1024)S(1)} %copy-done.15, bf16[2048,1024]{1,0:T(8,128)(2,1)S(1)} %copy-done.11, bf16[192,256]{1,0:T(8,128)(2,1)S(1)} %get-tuple-element.58, ...), kind=kOutput, calls=%fused_computation.16 | convolution fusion | flops 810417792 | bytes 6956544 | tf_op jit(solution)/shard_map/dot_general | solution.py:166
  86.0 2.3 %collective-permute-start.13 = (f32[2,192]{1,0:T(2,128)S(1)}, f32[2,192]{1,0:T(2,128)S(1)}, u32[]{:S(2)}, u32[]{:S(2)}) collective-permute-start(f32[2,192]{1,0:T(2,128)S(1)} %pad_maximum_fusion.8), channel_id=1, source_target_pairs={{0,2},{1,3},{2,0},{3,1},{4,6},{5,7},{6,4},{7,5},{8,10},{9,11},{10,... | collective-permute-start | bytes 4616 | tf_op jit(solution)/shard_map/ppermute | solution.py:17
  88.5 1.5 collective-permute-start.12
  90.0 2.9 %collective-permute-done.14 = f32[2,192]{1,0:T(2,128)S(1)} collective-permute-done((f32[2,192]{1,0:T(2,128)S(1)}, f32[2,192]{1,0:T(2,128)S(1)}, u32[]{:S(2)}, u32[]{:S(2)}) %collective-permute-start.14) | collective-permute-done | bytes 1568 | tf_op jit(solution)/shard_map/ppermute | solution.py:17
  92.9 2.4 %multiply_convert_fusion = (bf16[2048,512]{0,1:T(8,128)(2,1)}, f32[2048]{0:T(1024)S(1)}) fusion(f32[2048]{0:T(1024)S(1)} %copy-done.15, bf16[2048,512]{0,1:T(8,128)(2,1)S(1)} %copy.40, f32[192]{0:T(256)S(1)} %bitcast.82, bf16[192,1024]{1,0:T(8,128)(2,1)S(1)} %pad_maximum_fusion.6, s32[]{:T(128)S(6)} %select_n.357, ...), kind=kOutput, calls=%fused_computation.4 | convolution fusion | flops 410810368 | bytes 9389060 | tf_op jit(solution)/shard_map/dot_general | solution.py:208
  95.4 4.0 %copy.36 = bf16[2048,4,128]{2,0,1:T(8,128)(2,1)} copy(bf16[2048,4,128]{0,2,1:T(8,128)(2,1)} %bitcast.67) | data formatting | bytes 4194304 | tf_op jit(solution)/shard_map/reshape | solution.py:214
  99.3 1.0 copy-done.5
  100.4 1.2 broadcast_select_fusion.9
  101.7 0.7 copy-done.1
  102.4 1.3 pad_maximum_fusion.1
  104.4 1.2 copy-done.7
  105.6 0.4 convert_reduce_fusion.1
  106.0 1.3 collective-permute-start.22
  107.3 4.6 %collective-permute-start.15 = (bf16[192,1024]{1,0:T(8,128)(2,1)S(1)}, bf16[192,1024]{1,0:T(8,128)(2,1)S(1)}, u32[]{:S(2)}, u32[]{:S(2)}) collective-permute-start(bf16[192,1024]{1,0:T(8,128)(2,1)S(1)} %constant_dynamic-slice_fusion.2.refs_1_), channel_id=1, source_target_pairs={{0,4},{4,8},{8,12},{1,5},{5,9},{9,13},{2,6},{6,10},{10,14},{3,7},{... | collective-permute-start | bytes 1179656 | tf_op jit(solution)/shard_map/ppermute | solution.py:66
  112.0 1.2 collective-permute-done.20
  113.2 23.3 %collective-permute-done.22.refs_5_ = bf16[192,1024]{1,0:T(8,128)(2,1)S(1)} collective-permute-done((bf16[192,1024]{1,0:T(8,128)(2,1)S(1)}, bf16[192,1024]{1,0:T(8,128)(2,1)S(1)}, u32[]{:S(2)}, u32[]{:S(2)}) %collective-permute-start.22) | collective-permute-done | bytes 393248 | tf_op jit(solution)/shard_map/ppermute | solution.py:67
  136.5 1.3 collective-permute-start.23
  137.8 0.7 collective-permute-start.16
  138.5 2.0 %select_bitcast_fusion.1 = (bf16[4,1,4,24,2048]{4,3,2,1,0:T(8,128)(2,1)S(1)}, bf16[4,1,4,24,2048]{4,3,2,1,0:T(8,128)(2,1)S(1)}) fusion(bf16[4,4,24,2048]{3,2,1,0:T(8,128)(2,1)} %collective-permute-done.3, pred[]{:T(512)S(6)} %ne.40, bf16[4,1,24,2048]{3,2,1,0:T(8,128)(2,1)} %copy-done.3, bf16[4,1,24,2048]{3,2,1,0:T(8,128)(2,1)} %copy-done.2, ...), kind=kLoop, calls=%fused_computation.25 | loop fusion | flops 3932160 | bytes 6291457 | tf_op jit(solution)/shard_map/stack | solution.py:181
  140.5 17.3 %collective-permute-done.23.refs_6_ = bf16[192,1024]{1,0:T(8,128)(2,1)S(1)} collective-permute-done((bf16[192,1024]{1,0:T(8,128)(2,1)S(1)}, bf16[192,1024]{1,0:T(8,128)(2,1)S(1)}, u32[]{:S(2)}, u32[]{:S(2)}) %collective-permute-start.23) | collective-permute-done | bytes 393248 | tf_op jit(solution)/shard_map/ppermute | solution.py:67
  157.8 1.3 collective-permute-start.24
  159.1 0.7 collective-permute-start.21
  159.7 1.9 %pad_maximum_fusion = bf16[4,2,4,24,2048]{4,3,2,1,0:T(8,128)(2,1)} fusion(bf16[4,1,4,24,2048]{4,3,2,1,0:T(8,128)(2,1)S(1)} %get-tuple-element.42, bf16[4,1,4,24,2048]{4,3,2,1,0:T(8,128)(2,1)S(1)} %get-tuple-element.41), kind=kLoop, calls=%fused_computation.8 | loop fusion | flops 1572864 | bytes 6291456 | tf_op jit(solution)/shard_map/stack | solution.py:181
  161.7 3.9 %rev.4 = bf16[4,192,2048]{2,1,0:T(8,128)(2,1)} reverse(bf16[4,192,2048]{2,1,0:T(8,128)(2,1)} %bitcast.65), dimensions={0} | reverse | bytes 6291456 | tf_op jit(solution)/shard_map/rev | solution.py:227
  165.6 3.0 %fusion = bf16[4,192,2048]{2,1,0:T(8,128)(2,1)S(1)} fusion(s32[]{:T(128)S(6)} %select_n.320, bf16[4,192,2048]{2,1,0:T(8,128)(2,1)} %rev.4), kind=kLoop, calls=%fused_computation.7 | loop fusion | flops 1572864 | bytes 6291460 | tf_op jit(solution)/shard_map/concatenate | solution.py:227
  168.7 1.7 collective-permute-done.24.refs_7_
  170.3 2.5 %collective-permute-start.27 = (f32[5120]{0:T(1024)S(1)}, f32[5120]{0:T(1024)S(1)}, u32[]{:S(2)}, u32[]{:S(2)}) collective-permute-start(f32[5120]{0:T(1024)S(1)} %fusion.51), channel_id=1, source_target_pairs={{0,12},{4,8},{8,4},{12,0},{1,13},{5,9},{9,5},{13,1},{2,14},{6,10},... | collective-permute-start | bytes 61448 | tf_op jit(solution)/shard_map/ppermute | solution.py:17
  172.9 1.9 collective-permute-start.25
  174.7 7.6 %shard_map.137 = f32[16384,128]{1,0:T(8,128)} custom-call(bf16[768,2048]{1,0:T(8,128)(2,1)S(1)} %bitcast.64, bf16[192,1024]{1,0:T(8,128)(2,1)S(1)} %constant_dynamic-slice_fusion.2.refs_1_, bf16[192,1024]{1,0:T(8,128)(2,1)S(1)} %collective-permute-done.15.refs_2_, bf16[192,1024]{1,0:T(8,128)(2,1)S(1)} %collective-permute-done.16.refs_3_, ...), custom_call_target="tpu_custom_call" | custom-call | flops 3221225472 | bytes 13107200 | tf_op jit(solution)/shard_map/pallas_call | solution.py:102
  182.4 0.6 slice.41
  183.0 0.6 fusion.53
  183.6 2.1 %bitcast_convert_fusion = f32[2048,128]{1,0:T(8,128)} fusion(bf16[1,2048,128]{2,1,0:T(8,128)(2,1)} %reduce-scatter.5.cloned.1.call-done), kind=kLoop, calls=%fused_computation.67 | loop fusion | flops 262144 | bytes 1572864 | tf_op jit(solution)/shard_map/convert_element_type | solution.py:216
  (103 shorter events, 3.3 us)
Async XLA Ops:
  7.2 7.8 %copy-start.12 = (bf16[192,2048]{1,0:T(8,128)(2,1)S(1)}, bf16[192,2048]{1,0:T(8,128)(2,1)}, u32[]{:S(2)}) copy-start(bf16[192,2048]{1,0:T(8,128)(2,1)} %param.10) | copy-start | bytes 2359300
  7.2 13.0 %copy-start.17 = (s32[4]{0:T(128)S(1)}, s32[4]{0:T(128)}, u32[]{:S(2)}) copy-start(s32[4]{0:T(128)} %param.17) | copy-start | bytes 52
  7.2 13.1 %copy-start.16 = (s32[4]{0:T(128)S(1)}, s32[4]{0:T(128)}, u32[]{:S(2)}) copy-start(s32[4]{0:T(128)} %param.19) | copy-start | bytes 52
  7.2 13.1 %copy-start.18 = (s32[4]{0:T(128)S(1)}, s32[4]{0:T(128)}, u32[]{:S(2)}) copy-start(s32[4]{0:T(128)} %param.18) | copy-start | bytes 52
  7.2 60.6 %reduce-scatter.3.cloned.1.call-start = ((), (), s32[]{:S(2)}) async-start(), calls=%async_computation.2 | async-start | bytes 491520 | tf_op jit(solution)/shard_map/reduce_scatter | solution.py:161
  10.4 11.1 %slice-start = ((bf16[1024,1024]{1,0:T(8,128)(2,1)}), bf16[512,1024]{1,0:T(8,128)(2,1)S(1)}, s32[]{:S(2)}) async-start(bf16[1024,1024]{1,0:T(8,128)(2,1)} %param.16), calls=%async_computation.4 | async-start | bytes 2097152 | tf_op jit(solution)/shard_map/slice | solution.py:154
  10.4 56.7 %collective-permute-start.19 = (f32[1024]{0:T(1024)S(1)}, f32[1024]{0:T(1024)S(1)}, u32[]{:S(2)}, u32[]{:S(2)}) collective-permute-start(f32[1024]{0:T(1024)S(1)} %multiply_reduce_fusion), channel_id=1, source_target_pairs={{0,3},{1,2},{2,1},{3,0},{4,7},{5,6},{6,5},{7,4},{8,11},{9,10},{10,... | collective-permute-start | bytes 12296 | tf_op jit(solution)/shard_map/ppermute | solution.py:17
  14.4 52.7 %collective-permute-start.18 = (f32[1024]{0:T(1024)S(1)}, f32[1024]{0:T(1024)S(1)}, u32[]{:S(2)}, u32[]{:S(2)}) collective-permute-start(f32[1024]{0:T(1024)S(1)} %multiply_reduce_fusion), channel_id=1, source_target_pairs={{0,2},{1,3},{2,0},{3,1},{4,6},{5,7},{6,4},{7,5},{8,10},{9,11},{10,... | collective-permute-start | bytes 12296 | tf_op jit(solution)/shard_map/ppermute | solution.py:17
  14.9 52.2 %collective-permute-start.17 = (f32[1024]{0:T(1024)S(1)}, f32[1024]{0:T(1024)S(1)}, u32[]{:S(2)}, u32[]{:S(2)}) collective-permute-start(f32[1024]{0:T(1024)S(1)} %multiply_reduce_fusion), channel_id=1, source_target_pairs={{0,1},{1,0},{2,3},{3,2},{4,5},{5,4},{6,7},{7,6},{8,9},{9,8},{10,11... | collective-permute-start | bytes 12296 | tf_op jit(solution)/shard_map/ppermute | solution.py:17
  16.7 29.0 %copy-start.4 = (bf16[96,2048]{1,0:T(8,128)(2,1)}, bf16[96,2048]{1,0:T(8,128)(2,1)S(1)}, u32[]{:S(2)}) copy-start(bf16[96,2048]{1,0:T(8,128)(2,1)S(1)} %fusion.9) | copy-start | bytes 1179652
  16.7 18.9 %collective-permute-start.1 = (bf16[96,2048]{1,0:T(8,128)(2,1)S(1)}, bf16[96,2048]{1,0:T(8,128)(2,1)}, u32[]{:S(2)}, u32[]{:S(2)}) collective-permute-start(bf16[96,2048]{1,0:T(8,128)(2,1)S(1)} %fusion.9), channel_id=1, source_target_pairs={{0,2},{1,3},{2,0},{3,1},{4,6},{5,7},{6,4},{7,5},{8,10},{9,11},{10,... | collective-permute-start | bytes 1179656 | tf_op jit(solution)/shard_map/ppermute | solution.py:17
  18.7 18.5 %collective-permute-start = (bf16[96,2048]{1,0:T(8,128)(2,1)S(1)}, bf16[96,2048]{1,0:T(8,128)(2,1)}, u32[]{:S(2)}, u32[]{:S(2)}) collective-permute-start(bf16[96,2048]{1,0:T(8,128)(2,1)S(1)} %fusion.9), channel_id=1, source_target_pairs={{0,3},{1,2},{2,1},{3,0},{4,7},{5,6},{6,5},{7,4},{8,11},{9,10},{10,... | collective-permute-start | bytes 1179656 | tf_op jit(solution)/shard_map/ppermute | solution.py:17
  22.7 160.9 %reduce-scatter.5.cloned.1.call-start = ((), (), s32[]{:S(2)}) async-start(), calls=%async_computation.3 | async-start | bytes 2621440 | tf_op jit(solution)/shard_map/reduce_scatter | solution.py:215
  35.6 10.1 %collective-permute-start.2 = (bf16[96,2048]{1,0:T(8,128)(2,1)S(1)}, bf16[96,2048]{1,0:T(8,128)(2,1)S(1)}, u32[]{:S(2)}, u32[]{:S(2)}) collective-permute-start(bf16[96,2048]{1,0:T(8,128)(2,1)S(1)} %fusion.9), channel_id=1, source_target_pairs={{0,1},{1,0},{2,3},{3,2},{4,5},{5,4},{6,7},{7,6},{8,9},{9,8},{10,11... | collective-permute-start | bytes 1179656 | tf_op jit(solution)/shard_map/ppermute | solution.py:17
  37.2 8.5 %slice-start.1 = ((s8[8388608]{0:T(1024)(128)(4,1)}), s8[4194304]{0:T(1024)(128)(4,1)S(1)}, s32[]{:S(2)}) async-start(s8[8388608]{0:T(1024)(128)(4,1)} %bitcast.92), calls=%async_computation.5 | async-start | bytes 8388608
  38.6 7.2 %slice-start.2 = ((s8[8388608]{0:T(1024)(128)(4,1)}), s8[4194304]{0:T(1024)(128)(4,1)S(1)}, s32[]{:S(2)}) async-start(s8[8388608]{0:T(1024)(128)(4,1)} %bitcast.92), calls=%async_computation.6 | async-start | bytes 8388608
  44.0 14.2 %collective-permute-start.4 = (bf16[2,48,2048]{2,1,0:T(8,128)(2,1)S(1)}, bf16[2,48,2048]{2,1,0:T(8,128)(2,1)S(1)}, u32[]{:S(2)}, u32[]{:S(2)}) collective-permute-start(bf16[2,48,2048]{2,1,0:T(8,128)(2,1)S(1)} %dynamic-slice_bitcast_fusion.1), channel_id=1, source_target_pairs={{0,4},{4,0},{8,12},{12,8},{1,5},{5,1},{9,13},{13,9},{2,6},{6,2},{1... | collective-permute-start | bytes 1179656 | tf_op jit(solution)/shard_map/ppermute | solution.py:17
  45.7 2.0 %copy-start.8 = (bf16[96,2048]{1,0:T(8,128)(2,1)}, bf16[96,2048]{1,0:T(8,128)(2,1)S(1)}, u32[]{:S(2)}) copy-start(bf16[96,2048]{1,0:T(8,128)(2,1)S(1)} %collective-permute-done.2) | copy-start | bytes 1179652
  47.7 28.6 %copy-start.14 = (f32[2048]{0:T(1024)S(1)}, f32[2048]{0:T(1024)}, u32[]{:S(2)}) copy-start(f32[2048]{0:T(1024)} %param.12) | copy-start | bytes 24580
  47.7 16.2 %collective-permute-start.6 = (bf16[2,48,2048]{2,1,0:T(8,128)(2,1)S(1)}, bf16[2,48,2048]{2,1,0:T(8,128)(2,1)S(1)}, u32[]{:S(2)}, u32[]{:S(2)}) collective-permute-start(bf16[2,48,2048]{2,1,0:T(8,128)(2,1)S(1)} %dynamic-slice_bitcast_fusion), channel_id=1, source_target_pairs={{0,4},{4,0},{8,12},{12,8},{1,5},{5,1},{9,13},{13,9},{2,6},{6,2},{1... | collective-permute-start | bytes 1179656 | tf_op jit(solution)/shard_map/ppermute | solution.py:17
  58.4 14.4 %collective-permute-start.5 = (bf16[1,48,2048]{2,1,0:T(8,128)(2,1)S(1)}, bf16[1,48,2048]{2,1,0:T(8,128)(2,1)S(1)}, u32[]{:S(2)}, u32[]{:S(2)}) collective-permute-start(bf16[1,48,2048]{2,1,0:T(8,128)(2,1)S(1)} %dynamic-slice_convert_fusion.1), channel_id=1, source_target_pairs={{0,8},{4,12},{8,0},{12,4},{1,9},{5,13},{9,1},{13,5},{2,10},{6,14},... | collective-permute-start | bytes 589832 | tf_op jit(solution)/shard_map/ppermute | solution.py:17
  64.1 0.9 copy-start.6
  65.0 11.4 %collective-permute-start.7 = (bf16[1,48,2048]{2,1,0:T(8,128)(2,1)S(1)}, bf16[1,48,2048]{2,1,0:T(8,128)(2,1)}, u32[]{:S(2)}, u32[]{:S(2)}) collective-permute-start(bf16[1,48,2048]{2,1,0:T(8,128)(2,1)S(1)} %dynamic-slice_convert_fusion), channel_id=1, source_target_pairs={{0,8},{4,12},{8,0},{12,4},{1,9},{5,13},{9,1},{13,5},{2,10},{6,14},... | collective-permute-start | bytes 589832 | tf_op jit(solution)/shard_map/ppermute | solution.py:17
  67.8 9.9 %copy-start.10 = (bf16[1024,512]{1,0:T(8,128)(2,1)S(1)}, bf16[1024,512]{1,0:T(8,128)(2,1)}, u32[]{:S(2)}) copy-start(bf16[1024,512]{1,0:T(8,128)(2,1)} %constant_dynamic-slice_fusion.1) | copy-start | bytes 3145732
  67.8 14.8 %collective-permute-start.11 = (bf16[192,256]{1,0:T(8,128)(2,1)}, bf16[192,256]{1,0:T(8,128)(2,1)S(1)}, u32[]{:S(2)}, u32[]{:S(2)}) collective-permute-start(bf16[192,256]{1,0:T(8,128)(2,1)} %reduce-scatter.3.cloned.1.call-done), channel_id=1, source_target_pairs={{0,1},{1,0},{2,3},{3,2},{4,5},{5,4},{6,7},{7,6},{8,9},{9,8},{10,11... | collective-permute-start | bytes 294920 | tf_op jit(solution)/shard_map/ppermute | solution.py:17
  68.4 14.2 %collective-permute-start.10 = (bf16[192,256]{1,0:T(8,128)(2,1)}, bf16[192,256]{1,0:T(8,128)(2,1)S(1)}, u32[]{:S(2)}, u32[]{:S(2)}) collective-permute-start(bf16[192,256]{1,0:T(8,128)(2,1)} %reduce-scatter.3.cloned.1.call-done), channel_id=1, source_target_pairs={{0,2},{1,3},{2,0},{3,1},{4,6},{5,7},{6,4},{7,5},{8,10},{9,11},{10,... | collective-permute-start | bytes 294920 | tf_op jit(solution)/shard_map/ppermute | solution.py:17
  70.7 12.0 %collective-permute-start.9 = (bf16[192,256]{1,0:T(8,128)(2,1)}, bf16[192,256]{1,0:T(8,128)(2,1)S(1)}, u32[]{:S(2)}, u32[]{:S(2)}) collective-permute-start(bf16[192,256]{1,0:T(8,128)(2,1)} %reduce-scatter.3.cloned.1.call-done), channel_id=1, source_target_pairs={{0,3},{1,2},{2,1},{3,0},{4,7},{5,6},{6,5},{7,4},{8,11},{9,10},{10,... | collective-permute-start | bytes 294920 | tf_op jit(solution)/shard_map/ppermute | solution.py:17
  77.6 5.0 %copy-start.13 = (bf16[192,256]{1,0:T(8,128)(2,1)S(1)}, bf16[192,256]{1,0:T(8,128)(2,1)}, u32[]{:S(2)}) copy-start(bf16[192,256]{1,0:T(8,128)(2,1)} %reduce-scatter.3.cloned.1.call-done) | copy-start | bytes 294916
  77.6 5.1 %collective-permute-start.8 = (bf16[96,2048]{1,0:T(8,128)(2,1)S(1)}, bf16[96,2048]{1,0:T(8,128)(2,1)S(1)}, u32[]{:S(2)}, u32[]{:S(2)}) collective-permute-start(bf16[96,2048]{1,0:T(8,128)(2,1)S(1)} %pad_maximum_fusion.5), channel_id=1, source_target_pairs={{0,16},{16,0},{1,17},{17,1},{2,18},{18,2},{3,19},{19,3},{4,20},{20... | collective-permute-start | bytes 1179656 | tf_op jit(solution)/shard_map/ppermute | solution.py:17
  77.7 5.1 %copy-start.11 = (bf16[2048,1024]{1,0:T(8,128)(2,1)S(1)}, bf16[2048,1024]{1,0:T(8,128)(2,1)}, u32[]{:S(2)}) copy-start(bf16[2048,1024]{1,0:T(8,128)(2,1)} %param.15) | copy-start | bytes 12582916
  82.6 0.7 copy-start.15
  86.0 3.9 %collective-permute-start.13 = (f32[2,192]{1,0:T(2,128)S(1)}, f32[2,192]{1,0:T(2,128)S(1)}, u32[]{:S(2)}, u32[]{:S(2)}) collective-permute-start(f32[2,192]{1,0:T(2,128)S(1)} %pad_maximum_fusion.8), channel_id=1, source_target_pairs={{0,2},{1,3},{2,0},{3,1},{4,6},{5,7},{6,4},{7,5},{8,10},{9,11},{10,... | collective-permute-start | bytes 4616 | tf_op jit(solution)/shard_map/ppermute | solution.py:17
  88.4 4.5 %collective-permute-start.14 = (f32[2,192]{1,0:T(2,128)S(1)}, f32[2,192]{1,0:T(2,128)S(1)}, u32[]{:S(2)}, u32[]{:S(2)}) collective-permute-start(f32[2,192]{1,0:T(2,128)S(1)} %pad_maximum_fusion.8), channel_id=1, source_target_pairs={{0,3},{1,2},{2,1},{3,0},{4,7},{5,6},{6,5},{7,4},{8,11},{9,10},{10,... | collective-permute-start | bytes 4616 | tf_op jit(solution)/shard_map/ppermute | solution.py:17
  88.5 4.4 %collective-permute-start.12 = (f32[2,192]{1,0:T(2,128)S(1)}, f32[2,192]{1,0:T(2,128)S(1)}, u32[]{:S(2)}, u32[]{:S(2)}) collective-permute-start(f32[2,192]{1,0:T(2,128)S(1)} %pad_maximum_fusion.8), channel_id=1, source_target_pairs={{0,1},{1,0},{2,3},{3,2},{4,5},{5,4},{6,7},{7,6},{8,9},{9,8},{10,11... | collective-permute-start | bytes 4616 | tf_op jit(solution)/shard_map/ppermute | solution.py:17
  99.3 1.0 copy-start.5
  99.3 1.1 copy-start.9
  101.7 0.8 copy-start.1
  101.7 2.1 %copy-start.2 = (bf16[4,1,24,2048]{3,2,1,0:T(8,128)(2,1)}, bf16[4,1,24,2048]{3,2,1,0:T(8,128)(2,1)S(1)}, u32[]{:S(2)}) copy-start(bf16[4,1,24,2048]{3,2,1,0:T(8,128)(2,1)S(1)} %get-tuple-element.45) | copy-start | bytes 1179652
  101.7 2.1 %copy-start.3 = (bf16[4,1,24,2048]{3,2,1,0:T(8,128)(2,1)}, bf16[4,1,24,2048]{3,2,1,0:T(8,128)(2,1)S(1)}, u32[]{:S(2)}) copy-start(bf16[4,1,24,2048]{3,2,1,0:T(8,128)(2,1)S(1)} %get-tuple-element.46) | copy-start | bytes 1179652
  101.7 2.3 %copy-start = (bf16[1024,1024]{1,0:T(8,128)(2,1)S(1)}, bf16[1024,1024]{1,0:T(8,128)(2,1)}, u32[]{:S(2)}) copy-start(bf16[1024,1024]{1,0:T(8,128)(2,1)} %param.16) | copy-start | bytes 6291460
  103.8 34.7 %collective-permute-start.3 = (bf16[4,4,24,2048]{3,2,1,0:T(8,128)(2,1)}, bf16[4,4,24,2048]{3,2,1,0:T(8,128)(2,1)}, u32[]{:S(2)}, u32[]{:S(2)}) collective-permute-start(bf16[4,4,24,2048]{3,2,1,0:T(8,128)(2,1)} %pad_maximum_fusion.1), channel_id=1, source_target_pairs={{0,16},{16,0},{1,17},{17,1},{2,18},{18,2},{3,19},{19,3},{4,20},{20... | collective-permute-start | bytes 4718600 | tf_op jit(solution)/shard_map/ppermute | solution.py:17
  104.0 1.6 copy-start.7
  106.0 30.5 %collective-permute-start.22 = (bf16[192,1024]{1,0:T(8,128)(2,1)S(1)}, bf16[192,1024]{1,0:T(8,128)(2,1)S(1)}, u32[]{:S(2)}, u32[]{:S(2)}) collective-permute-start(bf16[192,1024]{1,0:T(8,128)(2,1)S(1)} %constant_dynamic-slice_fusion.2.refs_1_), channel_id=1, source_target_pairs={{4,0},{8,4},{12,8},{5,1},{9,5},{13,9},{6,2},{10,6},{14,10},{7,3},{... | collective-permute-start | bytes 1179656 | tf_op jit(solution)/shard_map/ppermute | solution.py:67
  107.3 30.5 %collective-permute-start.15 = (bf16[192,1024]{1,0:T(8,128)(2,1)S(1)}, bf16[192,1024]{1,0:T(8,128)(2,1)S(1)}, u32[]{:S(2)}, u32[]{:S(2)}) collective-permute-start(bf16[192,1024]{1,0:T(8,128)(2,1)S(1)} %constant_dynamic-slice_fusion.2.refs_1_), channel_id=1, source_target_pairs={{0,4},{4,8},{8,12},{1,5},{5,9},{9,13},{2,6},{6,10},{10,14},{3,7},{... | collective-permute-start | bytes 1179656 | tf_op jit(solution)/shard_map/ppermute | solution.py:66
  111.9 1.3 collective-permute-start.20
  136.5 21.3 %collective-permute-start.23 = (bf16[192,1024]{1,0:T(8,128)(2,1)S(1)}, bf16[192,1024]{1,0:T(8,128)(2,1)S(1)}, u32[]{:S(2)}, u32[]{:S(2)}) collective-permute-start(bf16[192,1024]{1,0:T(8,128)(2,1)S(1)} %collective-permute-done.22.refs_5_), channel_id=1, source_target_pairs={{4,0},{8,4},{5,1},{9,5},{6,2},{10,6},{7,3},{11,7},{20,16},{24,20},... | collective-permute-start | bytes 1179656 | tf_op jit(solution)/shard_map/ppermute | solution.py:67
  137.8 21.3 %collective-permute-start.16 = (bf16[192,1024]{1,0:T(8,128)(2,1)S(1)}, bf16[192,1024]{1,0:T(8,128)(2,1)S(1)}, u32[]{:S(2)}, u32[]{:S(2)}) collective-permute-start(bf16[192,1024]{1,0:T(8,128)(2,1)S(1)} %collective-permute-done.15.refs_2_), channel_id=1, source_target_pairs={{4,8},{8,12},{5,9},{9,13},{6,10},{10,14},{7,11},{11,15},{20,24},{2... | collective-permute-start | bytes 1179656 | tf_op jit(solution)/shard_map/ppermute | solution.py:66
  157.8 12.6 %collective-permute-start.24 = (bf16[192,1024]{1,0:T(8,128)(2,1)S(1)}, bf16[192,1024]{1,0:T(8,128)(2,1)S(1)}, u32[]{:S(2)}, u32[]{:S(2)}) collective-permute-start(bf16[192,1024]{1,0:T(8,128)(2,1)S(1)} %collective-permute-done.23.refs_6_), channel_id=1, source_target_pairs={{4,0},{5,1},{6,2},{7,3},{20,16},{21,17},{22,18},{23,19}} | collective-permute-start | bytes 1179656 | tf_op jit(solution)/shard_map/ppermute | solution.py:67
  159.1 11.3 %collective-permute-start.21 = (bf16[192,1024]{1,0:T(8,128)(2,1)S(1)}, bf16[192,1024]{1,0:T(8,128)(2,1)S(1)}, u32[]{:S(2)}, u32[]{:S(2)}) collective-permute-start(bf16[192,1024]{1,0:T(8,128)(2,1)S(1)} %collective-permute-done.16.refs_3_), channel_id=1, source_target_pairs={{8,12},{9,13},{10,14},{11,15},{24,28},{25,29},{26,30},{27,31}} | collective-permute-start | bytes 1179656 | tf_op jit(solution)/shard_map/ppermute | solution.py:66
  170.3 12.0 %collective-permute-start.27 = (f32[5120]{0:T(1024)S(1)}, f32[5120]{0:T(1024)S(1)}, u32[]{:S(2)}, u32[]{:S(2)}) collective-permute-start(f32[5120]{0:T(1024)S(1)} %fusion.51), channel_id=1, source_target_pairs={{0,12},{4,8},{8,4},{12,0},{1,13},{5,9},{9,5},{13,1},{2,14},{6,10},... | collective-permute-start | bytes 61448 | tf_op jit(solution)/shard_map/ppermute | solution.py:17
  172.9 9.5 %collective-permute-start.26 = (f32[5120]{0:T(1024)S(1)}, f32[5120]{0:T(1024)S(1)}, u32[]{:S(2)}, u32[]{:S(2)}) collective-permute-start(f32[5120]{0:T(1024)S(1)} %fusion.51), channel_id=1, source_target_pairs={{0,8},{4,12},{8,0},{12,4},{1,9},{5,13},{9,1},{13,5},{2,10},{6,14},... | collective-permute-start | bytes 61448 | tf_op jit(solution)/shard_map/ppermute | solution.py:17
  172.9 9.5 %collective-permute-start.25 = (f32[5120]{0:T(1024)S(1)}, f32[5120]{0:T(1024)S(1)}, u32[]{:S(2)}, u32[]{:S(2)}) collective-permute-start(f32[5120]{0:T(1024)S(1)} %fusion.51), channel_id=1, source_target_pairs={{0,4},{4,0},{8,12},{12,8},{1,5},{5,1},{9,13},{13,9},{2,6},{6,2},{1... | collective-permute-start | bytes 61448 | tf_op jit(solution)/shard_map/ppermute | solution.py:17
Sparse Core Ops, SparseCore 0:
  22.8 20.8 reduce-scatter.2
  99.5 55.0 reduce-scatter.4

commit v11 on v9

--- a/solution.py
+++ b/solution.py
@@ -25,9 +25,9 @@
     return pieces[0]
 
 
-def butterfly(x, axes):
+def butterfly(x, axes, first=1):
     for axis in axes:
-        mask = 1
+        mask = first
         while mask < lax.axis_size(axis):
             x = x + swap(x, axis, mask)
             mask *= 2
@@ -211,7 +211,7 @@
             jax.ShapeDtypeStruct((groups * half, features), jnp.bfloat16),
             jax.ShapeDtypeStruct((stream, share), jnp.bfloat16),
         ],
-        compiler_params=pltpu.CompilerParams(vmem_limit_bytes=VMEM),
+        compiler_params=pltpu.CompilerParams(vmem_limit_bytes=60 * 1024 * 1024),
         cost_estimate=pl.CostEstimate(
             flops=2 * seq_len * columns + 40 * groups * half * features,
             bytes_accessed=2 * seq_len * columns,
@@ -441,14 +441,14 @@
     )
     pieces = [act] + [swap(act, "tp", m) for m in range(1, n_tp)]
     text_sq = [text_sq] + [swap(text_sq, "tp", m) for m in range(1, n_tp)]
-    text_sq[0], pieces[1] = together(text_sq[0], pieces[1])
+    given = given + swap(given, "seq", 1)
+    text_sq[0], pieces[1], given = together(text_sq[0], pieces[1], given)
 
     scalars = (core[None], z[None], tile_counts, text_counts, owner_map)
     moment, gain_text = text_product(
         scalars, text_embed, key_weight, key_cotangent, text_sq, key_half
     )
-    given, moment = together(given, moment)
-    taken = butterfly(given, ("seq",))
+    taken = butterfly(given, ("seq",), 2)
     if n_seq <= 4:
         way = line_step(moment, "seq", 1, None)
     else:
@@ -458,9 +458,9 @@
 
     partial, act_mine = project(t[None], pieces, proj_weight)
     if n_seq <= 4:
-        way[0], way[1], act_mine, partial = together(*way, act_mine, partial)
+        way[0], way[1], partial = together(*way, partial)
         way = line_step(moment, "seq", 2, way)
-    taken, act_mine, partial = together(taken, act_mine, partial)
+    taken, partial = together(taken, partial)
     summed = lax.psum_scatter(partial, "seq", scatter_dimension=0, tiled=True)
 
     key_bias_part = jnp.sum(key_cotangent.astype(f32), 0)

time: 193 us -> 180 us (0.933)
  waiting for transfers between devices: 65.6 us -> 53.2 us
  local copies, waits for them, and re-layouts: 22.1 us -> 16.5 us
  Pallas kernels: 26.9 us -> 29.4 us
  starting transfers between devices: 39.4 us -> 41.8 us
    ppermute x23, waiting for transfers between devices: 28.1 us -> 18.3 us  [swap(): return lax.ppermute(x, axis, [(i, i ^ mask) for i in range(count)])]
    unnamed x45 -> x39, local copies, waits for them, and re-layouts: 15.7 us -> 10.1 us
    pallas_call x1, Pallas kernels: 2 us -> 5.47 us  [opening(): pl.pallas_call(opening_kernel, grid_spec=pltpu.PrefetchScalarGridSpec(num...]
    reduce_scatter x1, waiting for transfers between devices: 18 us -> 14.8 us  [on_device(): summed = lax.psum_scatter(partial, 'seq', scatter_dimension=0, tiled=True)]
    pallas_call x0 -> x1, local copies, waits for them, and re-layouts: none -> 2.57 us  [project(): pl.pallas_call(project_kernel, grid=(columns // step,), in_specs=[pl.Bloc...]
    optimization_barrier x1 -> x0, local copies, waits for them, and re-layouts: 2.56 us -> none  [together(): return lax.optimization_barrier(values)]
  transfers between devices with their start and end apart: 31 -> 31, of which waited for: 11 -> 12; matrix products, arithmetic and copies ran while one was open for 14% -> 16% of each run, Pallas kernels for 13% -> 13%
where the time goes in v11:
time: 180 us
  waiting for transfers between devices  53.2 us (30%)
  starting transfers between devices  41.8 us (23%)
  Pallas kernels  29.4 us (16%)
  other arithmetic  19.3 us (11%)
  local copies, waits for them, and re-layouts  16.5 us (9%)
  between operations  14.5 us (8%)
  matrix products  4.92 us (3%)
    ppermute x23, starting transfers between devices, swap(): return lax.ppermute(x, axis, [(i, i ^ mask) for i in range(count)])  25.5 us
    all_gather x1, waiting for transfers between devices, on_device(): rows = lax.all_gather(image, 'seq', axis=0, tiled=True)  20.1 us
    ppermute x23, waiting for transfers between devices, swap(): return lax.ppermute(x, axis, [(i, i ^ mask) for i in range(count)])  18.3 us
    ppermute x6, starting transfers between devices, line_step(): out.append(lax.ppermute(sent, axis, pairs))  16.2 us
    reduce_scatter x1, waiting for transfers between devices, on_device(): summed = lax.psum_scatter(partial, 'seq', scatter_dimension=0, tiled=True)  14.8 us
    unnamed x39, local copies, waits for them, and re-layouts  10.1 us
    pallas_call x1, Pallas kernels, weight_product(): pl.pallas_call(weight_kernel, grid=(features // step,), in_specs=[pl.Bloc...  6.91 us
    pallas_call x1, Pallas kernels, text_product(): pl.pallas_call(text_kernel, grid_spec=pltpu.PrefetchScalarGridSpec(num_sc...  6.34 us
  transfers between devices with their start and end apart: 31, of which 12 were waited for; matrix products, arithmetic and copies ran while one was open for 16% of the time, Pallas kernels for 13%

profile of v11, /device:TPU:0, one launch (start us, length us, event | category | flops | bytes accessed | tf_op | source)
XLA Modules:
  0.0 179.7 jit_solution(3674676108967962465)
XLA Ops:
  7.3 5.5 %shard_map.137 = (f32[1,1024]{1,0:T(1,128)}, bf16[96,2048]{1,0:T(8,128)(2,1)}, bf16[768,128]{1,0:T(8,128)(2,1)}) custom-call(s32[1]{0:T(128)} %bitcast.1.core_ref, s32[1]{0:T(128)} %bitcast.2.z_ref, s32[1]{0:T(128)} %bitcast.t_ref.refs_0_, s32[4]{0:T(128)} %tiles_ref.3, s32[4]{0:T(128)} %owners_ref.3, bf16[1024,2048]{1,0:T(8,128)(2,1)} %text_ref.3, ...), custom_call_target="tpu_custom_call" | custom-call | flops 12058624 | bytes 4194304 | tf_op jit(solution)/shard_map/pallas_call | solution.py:193
  12.7 2.9 %collective-permute-start = (bf16[96,2048]{1,0:T(8,128)(2,1)}, bf16[96,2048]{1,0:T(8,128)(2,1)S(1)}, u32[]{:S(2)}, u32[]{:S(2)}) collective-permute-start(bf16[96,2048]{1,0:T(8,128)(2,1)} %get-tuple-element.31.refs_2_), channel_id=1, source_target_pairs={{0,1},{1,0},{2,3},{3,2},{4,5},{5,4},{6,7},{7,6},{8,9},{9,8},{10,11... | collective-permute-start | bytes 1179656 | tf_op jit(solution)/shard_map/ppermute | solution.py:18
  15.7 1.6 collective-permute-start.1
  17.2 1.5 collective-permute-start.8
  18.7 0.5 collective-permute-start.7
  19.2 1.5 collective-permute-start.6
  20.7 1.5 collective-permute-done.1
  22.2 1.5 collective-permute-start.3
  23.7 1.0 add.91
  24.7 0.8 collective-permute-done.refs_3_
  25.5 2.4 %collective-permute-start.2 = (bf16[96,2048]{1,0:T(8,128)(2,1)}, bf16[96,2048]{1,0:T(8,128)(2,1)S(1)}, u32[]{:S(2)}, u32[]{:S(2)}) collective-permute-start(bf16[96,2048]{1,0:T(8,128)(2,1)} %get-tuple-element.31.refs_2_), channel_id=1, source_target_pairs={{0,2},{1,3},{2,0},{3,1},{4,6},{5,7},{6,4},{7,5},{8,10},{9,11},{10,... | collective-permute-start | bytes 1179656 | tf_op jit(solution)/shard_map/ppermute | solution.py:18
  28.0 2.2 %copy-done.1 = bf16[1024,2048]{1,0:T(8,128)(2,1)S(1)} copy-done((bf16[1024,2048]{1,0:T(8,128)(2,1)S(1)}, bf16[1024,2048]{1,0:T(8,128)(2,1)}, u32[]{:S(2)}) %copy-start.1) | copy-done | bytes 4194328
  30.2 2.2 %copy-done.2 = bf16[2048,1024]{1,0:T(8,128)(2,1)S(1)} copy-done((bf16[2048,1024]{1,0:T(8,128)(2,1)S(1)}, bf16[2048,1024]{1,0:T(8,128)(2,1)}, u32[]{:S(2)}) %copy-start.2) | copy-done | bytes 4194328
  32.3 0.7 copy-done.10
  33.0 6.3 %shard_map.139 = (bf16[4,2048,128]{2,1,0:T(8,128)(2,1)S(1)}, f32[1,2048]{1,0:T(1,128)S(1)}) custom-call(s32[1]{0:T(128)} %bitcast.1.core_ref, s32[1]{0:T(128)} %bitcast.2.z_ref, s32[4]{0:T(128)S(1)} %copy-done.11, s32[4]{0:T(128)S(1)} %copy-done.13, s32[4]{0:T(128)S(1)} %copy-done.12, bf16[1024,2048]{1,0:T(8,128)(2,1)S(1)} %copy-done.1, ...), custom_call_target="tpu_custom_call" | custom-call | flops 2147483648 | bytes 9437184 | tf_op jit(solution)/shard_map/pallas_call | solution.py:264
  39.4 1.3 copy-done.4
  40.8 1.5 collective-permute-start.10
  42.3 4.3 %collective-permute-start.9 = (bf16[2048,128]{1,0:T(8,128)(2,1)S(1)}, bf16[2048,128]{1,0:T(8,128)(2,1)}, u32[]{:S(2)}, u32[]{:S(2)}) collective-permute-start(bf16[2048,128]{1,0:T(8,128)(2,1)S(1)} %get-tuple-element.77), channel_id=1, source_target_pairs={{0,4},{1,5},{2,6},{3,7},{16,20},{17,21},{18,22},{19,23}} | collective-permute-start | bytes 1572872 | tf_op jit(solution)/shard_map/ppermute | solution.py:78
  46.7 4.8 %shard_map.138 = (bf16[384,2048]{1,0:T(8,128)(2,1)S(1)}, bf16[384,2048]{1,0:T(8,128)(2,1)S(1)}) custom-call(s32[1]{0:T(128)} %bitcast.t_ref.refs_0_, bf16[2048,2048]{1,0:T(8,128)(2,1)S(1)} %copy-done.14, bf16[96,2048]{1,0:T(8,128)(2,1)S(1)} %copy-done.15, bf16[96,2048]{1,0:T(8,128)(2,1)S(1)} %collective-permute-done.refs_3_, ...), custom_call_target="tpu_custom_call" | custom-call | flops 3221225472 | bytes 13107200 | tf_op jit(solution)/shard_map/pallas_call | solution.py:128
  51.5 1.1 copy-done.7
  52.6 1.1 copy-done.8
  53.8 5.1 %collective-permute-done.5 = bf16[768,128]{1,0:T(8,128)(2,1)S(1)} collective-permute-done((bf16[768,128]{1,0:T(8,128)(2,1)S(1)}, bf16[768,128]{1,0:T(8,128)(2,1)S(1)}, u32[]{:S(2)}, u32[]{:S(2)}) %collective-permute-start.5) | collective-permute-done | bytes 196640 | tf_op jit(solution)/shard_map/ppermute | solution.py:18
  59.0 1.6 collective-permute-start.13
  60.6 0.5 collective-permute-start.12
  61.1 1.5 collective-permute-start.11
  62.6 2.3 %collective-permute-done.13 = bf16[768,128]{1,0:T(8,128)(2,1)S(1)} collective-permute-done((bf16[768,128]{1,0:T(8,128)(2,1)S(1)}, bf16[768,128]{1,0:T(8,128)(2,1)S(1)}, u32[]{:S(2)}, u32[]{:S(2)}) %collective-permute-start.13) | collective-permute-done | bytes 196640 | tf_op jit(solution)/shard_map/ppermute | solution.py:18
  64.9 3.5 %collective-permute-done.12 = bf16[768,128]{1,0:T(8,128)(2,1)S(1)} collective-permute-done((bf16[768,128]{1,0:T(8,128)(2,1)S(1)}, bf16[768,128]{1,0:T(8,128)(2,1)S(1)}, u32[]{:S(2)}, u32[]{:S(2)}) %collective-permute-start.12) | collective-permute-done | bytes 196640 | tf_op jit(solution)/shard_map/ppermute | solution.py:18
  68.4 1.0 broadcast_select_fusion.13
  69.4 1.0 pad_maximum_fusion.2
  70.3 2.6 %copy.23 = bf16[384,2048]{0,1:T(8,128)(2,1)} copy(bf16[384,2048]{1,0:T(8,128)(2,1)} %copy-done.8) | data formatting | bytes 3145728 | tf_op jit(solution)/shard_map/pallas_call | solution.py:128
  72.9 0.5 collective-permute-start.4
  73.4 2.9 %fusion.6 = (bf16[2048,128]{1,0:T(8,128)(2,1)}, bf16[2048,128]{1,0:T(8,128)(2,1)}) fusion(bf16[2048,128]{1,0:T(8,128)(2,1)} %collective-permute-done.10, bf16[4,2048,128]{2,1,0:T(8,128)(2,1)} %copy-done.4, s32[]{:T(128)S(6)} %min.22, bf16[2048,128]{1,0:T(8,128)(2,1)} %collective-permute-done.9, s32[]{:T(128)S(6)} %min.21), kind=kLoop, calls=%fused_computation.16 | loop fusion | flops 2097152 | bytes 3145736 | tf_op jit(solution)/shard_map/convert_element_type | solution.py:75
  76.3 1.5 collective-permute-start.16
  77.8 4.6 %collective-permute-start.15 = (bf16[2048,128]{1,0:T(8,128)(2,1)}, bf16[2048,128]{1,0:T(8,128)(2,1)}, u32[]{:S(2)}, u32[]{:S(2)}) collective-permute-start(bf16[2048,128]{1,0:T(8,128)(2,1)} %get-tuple-element.75), channel_id=1, source_target_pairs={{0,4},{4,8},{1,5},{5,9},{2,6},{6,10},{3,7},{7,11},{16,20},{20,24},... | collective-permute-start | bytes 1572872 | tf_op jit(solution)/shard_map/ppermute | solution.py:78
  82.4 1.6 broadcast_select_fusion.1
  84.0 1.4 fusion.9.grad_ref
  85.4 3.5 %fusion.grad_ref = f32[768,1024]{1,0:T(8,128)} fusion(bf16[2048,1024]{1,0:T(8,128)(2,1)S(1)} %copy-done.3, s32[]{:T(128)S(6)} %select_n.188, bf16[768,512]{1,0:T(8,128)(2,1)S(1)} %get-tuple-element.79, bf16[768,512]{1,0:T(8,128)(2,1)S(1)} %get-tuple-element.78), kind=kOutput, calls=%fused_computation.2 | convolution fusion | flops 1613758464 | bytes 6815748 | tf_op jit(solution)/shard_map/dot_general | solution.py:475
  88.9 14.8 %reduce-scatter.2.cloned.1.call-done = bf16[96,2048]{1,0:T(8,128)(2,1)} async-done(((bf16[384,2048]{1,0:T(8,128)(2,1)}), bf16[96,2048]{1,0:T(8,128)(2,1)}) %reduce-scatter.2.cloned.1.call-update) | async-done | bytes 393232 | tf_op jit(solution)/shard_map/reduce_scatter | solution.py:464
  103.7 1.1 add_convert_fusion.rows_ref
  105.3 1.1 collective-permute-done.17
  106.4 0.8 pad_maximum_fusion.4
  107.2 0.6 dynamic_slice.41
  107.8 0.9 constant_dynamic-slice_fusion.1
  108.7 0.9 constant_dynamic-slice_fusion
  109.9 3.8 %collective-permute-start.20 = (f32[2,128]{1,0:T(2,128)S(1)}, f32[2,128]{1,0:T(2,128)S(1)}, u32[]{:S(2)}, u32[]{:S(2)}) collective-permute-start(f32[2,128]{1,0:T(2,128)S(1)} %shard_map.140), channel_id=1, source_target_pairs={{0,3},{1,2},{2,1},{3,0},{4,7},{5,6},{6,5},{7,4},{8,11},{9,10},{10,... | collective-permute-start | bytes 3080 | tf_op jit(solution)/shard_map/ppermute | solution.py:18
  113.9 0.6 collective-permute-start.18
  114.4 0.8 pad_maximum_fusion.3.cot_ref
  115.3 2.0 %collective-permute-done.19 = f32[2,128]{1,0:T(2,128)S(1)} collective-permute-done((f32[2,128]{1,0:T(2,128)S(1)}, f32[2,128]{1,0:T(2,128)S(1)}, u32[]{:S(2)}, u32[]{:S(2)}) %collective-permute-start.19) | collective-permute-done | bytes 1056 | tf_op jit(solution)/shard_map/ppermute | solution.py:18
  117.5 2.4 %collective-permute-start.22 = (f32[3328]{0:T(1024)S(1)}, f32[3328]{0:T(1024)S(1)}, u32[]{:S(2)}, u32[]{:S(2)}) collective-permute-start(f32[3328]{0:T(1024)S(1)} %pad_maximum_fusion.9), channel_id=1, source_target_pairs={{0,8},{4,12},{8,0},{12,4},{1,9},{5,13},{9,1},{13,5},{2,10},{6,14},... | collective-permute-start | bytes 39944 | tf_op jit(solution)/shard_map/ppermute | solution.py:18
  119.9 2.0 %collective-permute-start.21 = (f32[3328]{0:T(1024)S(1)}, f32[3328]{0:T(1024)S(1)}, u32[]{:S(2)}, u32[]{:S(2)}) collective-permute-start(f32[3328]{0:T(1024)S(1)} %pad_maximum_fusion.9), channel_id=1, source_target_pairs={{0,12},{4,8},{8,4},{12,0},{1,13},{5,9},{9,5},{13,1},{2,14},{6,10},... | collective-permute-start | bytes 39944 | tf_op jit(solution)/shard_map/ppermute | solution.py:18
  121.9 2.1 %maximum_bitcast_fusion.act_ref = bf16[2048,768]{1,0:T(8,128)(2,1)S(1)} fusion(bf16[384,2048]{0,1:T(8,128)(2,1)} %collective-permute-done.4, bf16[384,2048]{0,1:T(8,128)(2,1)} %copy.23), kind=kLoop, calls=%fused_computation.1 | loop fusion | flops 6291456 | bytes 6291456 | tf_op jit(solution)/shard_map/transpose | solution.py:523
  124.1 1.7 collective-permute-done.21
  126.1 2.5 %fusion.4 = (bf16[2048,128]{1,0:T(8,128)(2,1)}, bf16[2048,128]{1,0:T(8,128)(2,1)}) fusion(bf16[2048,128]{1,0:T(8,128)(2,1)} %collective-permute-done.15, bf16[4,2048,128]{2,1,0:T(8,128)(2,1)S(1)} %copy-done.5, s32[]{:T(128)S(6)} %min.23, bf16[2048,128]{1,0:T(8,128)(2,1)} %collective-permute-done.16, s32[]{:T(128)S(6)} %min.24), kind=kLoop, calls=%fused_computation.12 | loop fusion | flops 2097152 | bytes 3145736 | tf_op jit(solution)/shard_map/convert_element_type | solution.py:75
  128.6 2.8 %collective-permute-start.26 = (bf16[2048,128]{1,0:T(8,128)(2,1)}, bf16[2048,128]{1,0:T(8,128)(2,1)}, u32[]{:S(2)}, u32[]{:S(2)}) collective-permute-start(bf16[2048,128]{1,0:T(8,128)(2,1)} %get-tuple-element.72), channel_id=1, source_target_pairs={{0,4},{4,8},{8,12},{1,5},{5,9},{9,13},{2,6},{6,10},{10,14},{3,7},{... | collective-permute-start | bytes 1572872 | tf_op jit(solution)/shard_map/ppermute | solution.py:78
  131.4 1.5 collective-permute-start.27
  133.0 0.6 copy.24
  133.6 0.6 slice.32
  134.2 20.1 %all-gather.2.cloned.1.call-done.rows_ref = bf16[768,1024]{1,0:T(8,128)(2,1)} async-done(((bf16[192,1024]{1,0:T(8,128)(2,1)}), bf16[768,1024]{1,0:T(8,128)(2,1)}) %all-gather.2.cloned.1.call-update) | async-done | bytes 1572880 | tf_op jit(solution)/shard_map/all_gather | solution.py:495
  154.3 5.7 %shard_map.141 = (bf16[768,1024]{1,0:T(8,128)(2,1)}, f32[1024,128]{1,0:T(8,128)}, bf16[1024,128]{1,0:T(8,128)(2,1)}, f32[2,1024]{1,0:T(2,128)}) custom-call(s32[1]{0:T(128)} %bitcast.1.core_ref, f32[768,1024]{1,0:T(8,128)} %fusion.grad_ref, f32[1,1024]{1,0:T(1,128)} %bitcast.53, bf16[768,256]{1,0:T(8,128)(2,1)} %pad_maximum_fusion.3.cot_ref, ...), custom_call_target="tpu_custom_call" | custom-call | flops 402653184 | bytes 6291456 | tf_op jit(solution)/shard_map/pallas_call | solution.py:364
  160.5 1.4 copy-done.6
  161.9 6.9 %shard_map.142 = f32[16384,128]{1,0:T(8,128)} custom-call(bf16[2048,768]{1,0:T(8,128)(2,1)S(1)} %maximum_bitcast_fusion.act_ref, bf16[768,1024]{1,0:T(8,128)(2,1)S(1)} %copy-done.6), custom_call_target="tpu_custom_call" | custom-call | flops 3221225472 | bytes 13107200 | tf_op jit(solution)/shard_map/pallas_call | solution.py:394
  168.8 0.6 pad_maximum_fusion.11
  169.4 0.6 slice_add_fusion
  170.1 2.7 %fusion.2 = f32[2048,128]{1,0:T(8,128)} fusion(f32[1024,128]{1,0:T(8,128)S(1)} %get-tuple-element.81, f32[1024,128]{1,0:T(8,128)S(1)} %get-tuple-element.80, bf16[2048,128]{1,0:T(8,128)(2,1)} %collective-permute-done.27, bf16[2048,128]{1,0:T(8,128)(2,1)} %collective-permute-done.26, f32[2048]{0:T(1024)S(1)} %copy-done.9, bf16[4,2048,128]{2,1,0:T(8,128)(2,1)} %copy-done.4, ...), kind=kLoop, calls=%fused_computation.8 | loop fusion | flops 2097152 | bytes 3678212 | tf_op jit(solution)/shard_map/mul | solution.py:528
  (88 shorter events, 2.4 us)
Async XLA Ops:
  7.2 96.5 %reduce-scatter.2.cloned.1.call-start = ((), (), s32[]{:S(2)}) async-start(), calls=%async_computation.1 | async-start | bytes 1966080 | tf_op jit(solution)/shard_map/reduce_scatter | solution.py:464
  7.2 20.7 %copy-start = (bf16[1024,1024]{1,0:T(8,128)(2,1)S(1)}, bf16[1024,1024]{1,0:T(8,128)(2,1)}, u32[]{:S(2)}) copy-start(bf16[1024,1024]{1,0:T(8,128)(2,1)} %cot_ref.3) | copy-start | bytes 6291460
  7.2 20.7 %copy-start.11 = (s32[4]{0:T(128)S(1)}, s32[4]{0:T(128)}, u32[]{:S(2)}) copy-start(s32[4]{0:T(128)} %tiles_ref.3) | copy-start | bytes 52
  7.2 20.7 %copy-start.12 = (s32[4]{0:T(128)S(1)}, s32[4]{0:T(128)}, u32[]{:S(2)}) copy-start(s32[4]{0:T(128)} %owners_ref.3) | copy-start | bytes 52
  7.2 20.7 %copy-start.13 = (s32[4]{0:T(128)S(1)}, s32[4]{0:T(128)}, u32[]{:S(2)}) copy-start(s32[4]{0:T(128)} %texts_ref.1) | copy-start | bytes 52
  12.7 12.8 %collective-permute-start = (bf16[96,2048]{1,0:T(8,128)(2,1)}, bf16[96,2048]{1,0:T(8,128)(2,1)S(1)}, u32[]{:S(2)}, u32[]{:S(2)}) collective-permute-start(bf16[96,2048]{1,0:T(8,128)(2,1)} %get-tuple-element.31.refs_2_), channel_id=1, source_target_pairs={{0,1},{1,0},{2,3},{3,2},{4,5},{5,4},{6,7},{7,6},{8,9},{9,8},{10,11... | collective-permute-start | bytes 1179656 | tf_op jit(solution)/shard_map/ppermute | solution.py:18
  15.7 6.6 %collective-permute-start.1 = (bf16[768,128]{1,0:T(8,128)(2,1)}, bf16[768,128]{1,0:T(8,128)(2,1)S(1)}, u32[]{:S(2)}, u32[]{:S(2)}) collective-permute-start(bf16[768,128]{1,0:T(8,128)(2,1)} %get-tuple-element.33), channel_id=1, source_target_pairs={{0,4},{4,0},{8,12},{12,8},{1,5},{5,1},{9,13},{13,9},{2,6},{6,2},{1... | collective-permute-start | bytes 589832 | tf_op jit(solution)/shard_map/ppermute | solution.py:18
  17.2 10.7 %collective-permute-start.8 = (f32[1,1024]{1,0:T(1,128)}, f32[1,1024]{1,0:T(1,128)S(1)}, u32[]{:S(2)}, u32[]{:S(2)}) collective-permute-start(f32[1,1024]{1,0:T(1,128)} %get-tuple-element.37.refs_0_), channel_id=1, source_target_pairs={{0,3},{1,2},{2,1},{3,0},{4,7},{5,6},{6,5},{7,4},{8,11},{9,10},{10,... | collective-permute-start | bytes 12296 | tf_op jit(solution)/shard_map/ppermute | solution.py:18
  18.7 9.2 %collective-permute-start.7 = (f32[1,1024]{1,0:T(1,128)}, f32[1,1024]{1,0:T(1,128)S(1)}, u32[]{:S(2)}, u32[]{:S(2)}) collective-permute-start(f32[1,1024]{1,0:T(1,128)} %get-tuple-element.37.refs_0_), channel_id=1, source_target_pairs={{0,2},{1,3},{2,0},{3,1},{4,6},{5,7},{6,4},{7,5},{8,10},{9,11},{10,... | collective-permute-start | bytes 12296 | tf_op jit(solution)/shard_map/ppermute | solution.py:18
  19.2 8.7 %collective-permute-start.6 = (f32[1,1024]{1,0:T(1,128)}, f32[1,1024]{1,0:T(1,128)S(1)}, u32[]{:S(2)}, u32[]{:S(2)}) collective-permute-start(f32[1,1024]{1,0:T(1,128)} %get-tuple-element.37.refs_0_), channel_id=1, source_target_pairs={{0,1},{1,0},{2,3},{3,2},{4,5},{5,4},{6,7},{7,6},{8,9},{9,8},{10,11... | collective-permute-start | bytes 12296 | tf_op jit(solution)/shard_map/ppermute | solution.py:18
  22.2 24.4 %collective-permute-start.3 = (bf16[96,2048]{1,0:T(8,128)(2,1)}, bf16[96,2048]{1,0:T(8,128)(2,1)S(1)}, u32[]{:S(2)}, u32[]{:S(2)}) collective-permute-start(bf16[96,2048]{1,0:T(8,128)(2,1)} %get-tuple-element.31.refs_2_), channel_id=1, source_target_pairs={{0,3},{1,2},{2,1},{3,0},{4,7},{5,6},{6,5},{7,4},{8,11},{9,10},{10,... | collective-permute-start | bytes 1179656 | tf_op jit(solution)/shard_map/ppermute | solution.py:18
  25.5 21.1 %collective-permute-start.2 = (bf16[96,2048]{1,0:T(8,128)(2,1)}, bf16[96,2048]{1,0:T(8,128)(2,1)S(1)}, u32[]{:S(2)}, u32[]{:S(2)}) collective-permute-start(bf16[96,2048]{1,0:T(8,128)(2,1)} %get-tuple-element.31.refs_2_), channel_id=1, source_target_pairs={{0,2},{1,3},{2,0},{3,1},{4,6},{5,7},{6,4},{7,5},{8,10},{9,11},{10,... | collective-permute-start | bytes 1179656 | tf_op jit(solution)/shard_map/ppermute | solution.py:18
  28.0 2.2 %copy-start.1 = (bf16[1024,2048]{1,0:T(8,128)(2,1)S(1)}, bf16[1024,2048]{1,0:T(8,128)(2,1)}, u32[]{:S(2)}) copy-start(bf16[1024,2048]{1,0:T(8,128)(2,1)} %text_ref.3) | copy-start | bytes 12582916
  30.2 2.2 %copy-start.2 = (bf16[2048,1024]{1,0:T(8,128)(2,1)S(1)}, bf16[2048,1024]{1,0:T(8,128)(2,1)}, u32[]{:S(2)}) copy-start(bf16[2048,1024]{1,0:T(8,128)(2,1)} %weight_ref.1) | copy-start | bytes 12582916
  32.3 0.7 copy-start.10
  33.0 13.6 %copy-start.14 = (bf16[2048,2048]{1,0:T(8,128)(2,1)S(1)}, bf16[2048,2048]{1,0:T(8,128)(2,1)}, u32[]{:S(2)}) copy-start(bf16[2048,2048]{1,0:T(8,128)(2,1)} %refs_1_.1) | copy-start | bytes 25165828
  39.4 1.3 copy-start.4
  39.4 7.3 %copy-start.15 = (bf16[96,2048]{1,0:T(8,128)(2,1)S(1)}, bf16[96,2048]{1,0:T(8,128)(2,1)}, u32[]{:S(2)}) copy-start(bf16[96,2048]{1,0:T(8,128)(2,1)} %get-tuple-element.31.refs_2_) | copy-start | bytes 1179652
  40.8 18.1 %collective-permute-start.10 = (bf16[2048,128]{1,0:T(8,128)(2,1)S(1)}, bf16[2048,128]{1,0:T(8,128)(2,1)}, u32[]{:S(2)}, u32[]{:S(2)}) collective-permute-start(bf16[2048,128]{1,0:T(8,128)(2,1)S(1)} %get-tuple-element.76), channel_id=1, source_target_pairs={{12,8},{13,9},{14,10},{15,11},{28,24},{29,25},{30,26},{31,27}} | collective-permute-start | bytes 1572872 | tf_op jit(solution)/shard_map/ppermute | solution.py:78
  42.3 16.6 %collective-permute-start.9 = (bf16[2048,128]{1,0:T(8,128)(2,1)S(1)}, bf16[2048,128]{1,0:T(8,128)(2,1)}, u32[]{:S(2)}, u32[]{:S(2)}) collective-permute-start(bf16[2048,128]{1,0:T(8,128)(2,1)S(1)} %get-tuple-element.77), channel_id=1, source_target_pairs={{0,4},{1,5},{2,6},{3,7},{16,20},{17,21},{18,22},{19,23}} | collective-permute-start | bytes 1572872 | tf_op jit(solution)/shard_map/ppermute | solution.py:78
  46.6 12.3 %collective-permute-start.5 = (bf16[768,128]{1,0:T(8,128)(2,1)S(1)}, bf16[768,128]{1,0:T(8,128)(2,1)S(1)}, u32[]{:S(2)}, u32[]{:S(2)}) collective-permute-start(bf16[768,128]{1,0:T(8,128)(2,1)S(1)} %add.91), channel_id=1, source_target_pairs={{0,8},{4,12},{8,0},{12,4},{1,9},{5,13},{9,1},{13,5},{2,10},{6,14},... | collective-permute-start | bytes 589832 | tf_op jit(solution)/shard_map/ppermute | solution.py:18
  51.5 1.2 copy-start.7
  52.6 1.1 copy-start.8
  59.0 95.3 %all-gather.2.cloned.1.call-start = ((), (), s32[]{:S(2)}) async-start(), calls=%async_computation.2 | async-start | bytes 1966080 | tf_op jit(solution)/shard_map/all_gather | solution.py:495
  59.0 5.9 %collective-permute-start.13 = (bf16[768,128]{1,0:T(8,128)(2,1)S(1)}, bf16[768,128]{1,0:T(8,128)(2,1)S(1)}, u32[]{:S(2)}, u32[]{:S(2)}) collective-permute-start(bf16[768,128]{1,0:T(8,128)(2,1)S(1)} %add.92), channel_id=1, source_target_pairs={{0,1},{1,0},{2,3},{3,2},{4,5},{5,4},{6,7},{7,6},{8,9},{9,8},{10,11... | collective-permute-start | bytes 589832 | tf_op jit(solution)/shard_map/ppermute | solution.py:18
  60.6 7.8 %collective-permute-start.12 = (bf16[768,128]{1,0:T(8,128)(2,1)S(1)}, bf16[768,128]{1,0:T(8,128)(2,1)S(1)}, u32[]{:S(2)}, u32[]{:S(2)}) collective-permute-start(bf16[768,128]{1,0:T(8,128)(2,1)S(1)} %add.92), channel_id=1, source_target_pairs={{0,2},{1,3},{2,0},{3,1},{4,6},{5,7},{6,4},{7,5},{8,10},{9,11},{10,... | collective-permute-start | bytes 589832 | tf_op jit(solution)/shard_map/ppermute | solution.py:18
  61.1 7.3 %collective-permute-start.11 = (bf16[768,128]{1,0:T(8,128)(2,1)S(1)}, bf16[768,128]{1,0:T(8,128)(2,1)}, u32[]{:S(2)}, u32[]{:S(2)}) collective-permute-start(bf16[768,128]{1,0:T(8,128)(2,1)S(1)} %add.92), channel_id=1, source_target_pairs={{0,3},{1,2},{2,1},{3,0},{4,7},{5,6},{6,5},{7,4},{8,11},{9,10},{10,... | collective-permute-start | bytes 589832 | tf_op jit(solution)/shard_map/ppermute | solution.py:18
  70.3 12.1 %collective-permute-start.14 = (bf16[768,512]{1,0:T(8,128)(2,1)}, bf16[768,512]{1,0:T(8,128)(2,1)}, u32[]{:S(2)}, u32[]{:S(2)}) collective-permute-start(bf16[768,512]{1,0:T(8,128)(2,1)} %pad_maximum_fusion.2), channel_id=1, source_target_pairs={{0,16},{16,0},{1,17},{17,1},{2,18},{18,2},{3,19},{19,3},{4,20},{20... | collective-permute-start | bytes 2359304 | tf_op jit(solution)/shard_map/ppermute | solution.py:18
  72.9 49.0 %collective-permute-start.4 = (bf16[384,2048]{0,1:T(8,128)(2,1)}, bf16[384,2048]{0,1:T(8,128)(2,1)}, u32[]{:S(2)}, u32[]{:S(2)}) collective-permute-start(bf16[384,2048]{0,1:T(8,128)(2,1)} %copy.23), channel_id=1, source_target_pairs={{0,16},{16,0},{1,17},{17,1},{2,18},{18,2},{3,19},{19,3},{4,20},{20... | collective-permute-start | bytes 4718600 | tf_op jit(solution)/shard_map/ppermute | solution.py:18
  73.4 10.6 %copy-start.3 = (bf16[2048,1024]{1,0:T(8,128)(2,1)S(1)}, bf16[2048,1024]{1,0:T(8,128)(2,1)}, u32[]{:S(2)}) copy-start(bf16[2048,1024]{1,0:T(8,128)(2,1)} %weight_ref.1) | copy-start | bytes 12582916
  76.3 28.4 %collective-permute-start.16 = (bf16[2048,128]{1,0:T(8,128)(2,1)}, bf16[2048,128]{1,0:T(8,128)(2,1)}, u32[]{:S(2)}, u32[]{:S(2)}) collective-permute-start(bf16[2048,128]{1,0:T(8,128)(2,1)} %get-tuple-element.74), channel_id=1, source_target_pairs={{12,8},{8,4},{13,9},{9,5},{14,10},{10,6},{15,11},{11,7},{28,24},{2... | collective-permute-start | bytes 1572872 | tf_op jit(solution)/shard_map/ppermute | solution.py:78
  77.8 27.0 %collective-permute-start.15 = (bf16[2048,128]{1,0:T(8,128)(2,1)}, bf16[2048,128]{1,0:T(8,128)(2,1)}, u32[]{:S(2)}, u32[]{:S(2)}) collective-permute-start(bf16[2048,128]{1,0:T(8,128)(2,1)} %get-tuple-element.75), channel_id=1, source_target_pairs={{0,4},{4,8},{1,5},{5,9},{2,6},{6,10},{3,7},{7,11},{16,20},{20,24},... | collective-permute-start | bytes 1572872 | tf_op jit(solution)/shard_map/ppermute | solution.py:78
  85.4 18.3 %copy-start.17 = (f32[2048]{0:T(1024)S(1)}, f32[2048]{0:T(1024)}, u32[]{:S(2)}) copy-start(f32[2048]{0:T(1024)} %param.12) | copy-start | bytes 24580
  104.8 2.4 %copy-start.9 = (f32[2048]{0:T(1024)S(1)}, f32[2048]{0:T(1024)}, u32[]{:S(2)}) copy-start(f32[2048]{0:T(1024)} %param.14) | copy-start | bytes 24580
  104.8 1.5 collective-permute-start.17
  109.9 5.4 %collective-permute-start.20 = (f32[2,128]{1,0:T(2,128)S(1)}, f32[2,128]{1,0:T(2,128)S(1)}, u32[]{:S(2)}, u32[]{:S(2)}) collective-permute-start(f32[2,128]{1,0:T(2,128)S(1)} %shard_map.140), channel_id=1, source_target_pairs={{0,3},{1,2},{2,1},{3,0},{4,7},{5,6},{6,5},{7,4},{8,11},{9,10},{10,... | collective-permute-start | bytes 3080 | tf_op jit(solution)/shard_map/ppermute | solution.py:18
  113.8 3.6 %collective-permute-start.19 = (f32[2,128]{1,0:T(2,128)S(1)}, f32[2,128]{1,0:T(2,128)S(1)}, u32[]{:S(2)}, u32[]{:S(2)}) collective-permute-start(f32[2,128]{1,0:T(2,128)S(1)} %shard_map.140), channel_id=1, source_target_pairs={{0,2},{1,3},{2,0},{3,1},{4,6},{5,7},{6,4},{7,5},{8,10},{9,11},{10,... | collective-permute-start | bytes 3080 | tf_op jit(solution)/shard_map/ppermute | solution.py:18
  113.9 3.6 %collective-permute-start.18 = (f32[2,128]{1,0:T(2,128)S(1)}, f32[2,128]{1,0:T(2,128)S(1)}, u32[]{:S(2)}, u32[]{:S(2)}) collective-permute-start(f32[2,128]{1,0:T(2,128)S(1)} %shard_map.140), channel_id=1, source_target_pairs={{0,1},{1,0},{2,3},{3,2},{4,5},{5,4},{6,7},{7,6},{8,9},{9,8},{10,11... | collective-permute-start | bytes 3080 | tf_op jit(solution)/shard_map/ppermute | solution.py:18
  117.4 8.7 %copy-start.5 = (bf16[4,2048,128]{2,1,0:T(8,128)(2,1)S(1)}, bf16[4,2048,128]{2,1,0:T(8,128)(2,1)}, u32[]{:S(2)}) copy-start(bf16[4,2048,128]{2,1,0:T(8,128)(2,1)} %copy-done.4) | copy-start | bytes 6291460
  117.4 6.6 %collective-permute-start.23 = (f32[3328]{0:T(1024)S(1)}, f32[3328]{0:T(1024)S(1)}, u32[]{:S(2)}, u32[]{:S(2)}) collective-permute-start(f32[3328]{0:T(1024)S(1)} %pad_maximum_fusion.9), channel_id=1, source_target_pairs={{0,4},{4,0},{8,12},{12,8},{1,5},{5,1},{9,13},{13,9},{2,6},{6,2},{1... | collective-permute-start | bytes 39944 | tf_op jit(solution)/shard_map/ppermute | solution.py:18
  117.5 6.5 %collective-permute-start.22 = (f32[3328]{0:T(1024)S(1)}, f32[3328]{0:T(1024)S(1)}, u32[]{:S(2)}, u32[]{:S(2)}) collective-permute-start(f32[3328]{0:T(1024)S(1)} %pad_maximum_fusion.9), channel_id=1, source_target_pairs={{0,8},{4,12},{8,0},{12,4},{1,9},{5,13},{9,1},{13,5},{2,10},{6,14},... | collective-permute-start | bytes 39944 | tf_op jit(solution)/shard_map/ppermute | solution.py:18
  119.9 5.9 %collective-permute-start.21 = (f32[3328]{0:T(1024)S(1)}, f32[3328]{0:T(1024)S(1)}, u32[]{:S(2)}, u32[]{:S(2)}) collective-permute-start(f32[3328]{0:T(1024)S(1)} %pad_maximum_fusion.9), channel_id=1, source_target_pairs={{0,12},{4,8},{8,4},{12,0},{1,13},{5,9},{9,5},{13,1},{2,14},{6,10},... | collective-permute-start | bytes 39944 | tf_op jit(solution)/shard_map/ppermute | solution.py:18
  126.0 6.9 %collective-permute-start.24 = (f32[4096]{0:T(1024)S(1)}, f32[4096]{0:T(1024)S(1)}, u32[]{:S(2)}, u32[]{:S(2)}) collective-permute-start(f32[4096]{0:T(1024)S(1)} %pad_maximum_fusion.10), channel_id=1, source_target_pairs={{0,16},{16,0},{1,17},{17,1},{2,18},{18,2},{3,19},{19,3},{4,20},{20... | collective-permute-start | bytes 49160 | tf_op jit(solution)/shard_map/ppermute | solution.py:18
  128.6 41.5 %collective-permute-start.26 = (bf16[2048,128]{1,0:T(8,128)(2,1)}, bf16[2048,128]{1,0:T(8,128)(2,1)}, u32[]{:S(2)}, u32[]{:S(2)}) collective-permute-start(bf16[2048,128]{1,0:T(8,128)(2,1)} %get-tuple-element.72), channel_id=1, source_target_pairs={{0,4},{4,8},{8,12},{1,5},{5,9},{9,13},{2,6},{6,10},{10,14},{3,7},{... | collective-permute-start | bytes 1572872 | tf_op jit(solution)/shard_map/ppermute | solution.py:78
  131.4 38.7 %collective-permute-start.27 = (bf16[2048,128]{1,0:T(8,128)(2,1)}, bf16[2048,128]{1,0:T(8,128)(2,1)}, u32[]{:S(2)}, u32[]{:S(2)}) collective-permute-start(bf16[2048,128]{1,0:T(8,128)(2,1)} %get-tuple-element.73), channel_id=1, source_target_pairs={{12,8},{8,4},{4,0},{13,9},{9,5},{5,1},{14,10},{10,6},{6,2},{15,11}... | collective-permute-start | bytes 1572872 | tf_op jit(solution)/shard_map/ppermute | solution.py:78
  160.0 8.8 %collective-permute-start.25 = (f32[2,1024]{1,0:T(2,128)}, f32[2,1024]{1,0:T(2,128)S(1)}, u32[]{:S(2)}, u32[]{:S(2)}) collective-permute-start(f32[2,1024]{1,0:T(2,128)} %get-tuple-element.52), channel_id=1, source_target_pairs={{0,16},{16,0},{1,17},{17,1},{2,18},{18,2},{3,19},{19,3},{4,20},{20... | collective-permute-start | bytes 24584 | tf_op jit(solution)/shard_map/ppermute | solution.py:18
  160.1 10.0 %collective-permute-start.28 = (bf16[1024,128]{1,0:T(8,128)(2,1)}, bf16[1024,128]{1,0:T(8,128)(2,1)S(1)}, u32[]{:S(2)}, u32[]{:S(2)}) collective-permute-start(bf16[1024,128]{1,0:T(8,128)(2,1)} %get-tuple-element.55), channel_id=1, source_target_pairs={{0,16},{16,0},{1,17},{17,1},{2,18},{18,2},{3,19},{19,3},{4,20},{20... | collective-permute-start | bytes 786440 | tf_op jit(solution)/shard_map/ppermute | solution.py:18
  160.5 1.4 copy-start.6
  161.9 6.9 %copy-start.18 = (f32[2,1024]{1,0:T(2,128)S(1)}, f32[2,1024]{1,0:T(2,128)}, u32[]{:S(2)}) copy-start(f32[2,1024]{1,0:T(2,128)} %get-tuple-element.52) | copy-start | bytes 24580
  161.9 8.1 %copy-start.16 = (f32[1024,128]{1,0:T(8,128)S(1)}, f32[1024,128]{1,0:T(8,128)}, u32[]{:S(2)}) copy-start(f32[1024,128]{1,0:T(8,128)} %get-tuple-element.56) | copy-start | bytes 1572868
Sparse Core Ops, SparseCore 0:
  59.1 44.5 reduce-scatter.1
  107.3 46.9 all-gather.1

commit v12 on v11

--- a/solution.py
+++ b/solution.py
@@ -458,9 +458,8 @@
 
     partial, act_mine = project(t[None], pieces, proj_weight)
     if n_seq <= 4:
-        way[0], way[1], partial = together(*way, partial)
+        way[0], way[1], taken, _ = together(*way, taken, partial)
         way = line_step(moment, "seq", 2, way)
-    taken, partial = together(taken, partial)
     summed = lax.psum_scatter(partial, "seq", scatter_dimension=0, tiled=True)
 
     key_bias_part = jnp.sum(key_cotangent.astype(f32), 0)

time: 180 us -> 205 us (1.14); the launches traced: 180 us -> 202 us
  waiting for transfers between devices: 53.2 us -> 70.5 us
  local copies, waits for them, and re-layouts: 16.5 us -> 20.2 us
    ppermute x23, waiting for transfers between devices: 18.3 us -> 50.8 us  [swap(): return lax.ppermute(x, axis, [(i, i ^ mask) for i in range(count)])]
    reduce_scatter x1, waiting for transfers between devices: 14.8 us -> 0.01 us  [on_device(): summed = lax.psum_scatter(partial, 'seq', scatter_dimension=0, tiled=True)]
    unnamed x39 -> x45, local copies, waits for them, and re-layouts: 10.1 us -> 13.9 us
    all_gather x1, waiting for transfers between devices: 20.1 us -> 16.4 us  [on_device(): rows = lax.all_gather(image, 'seq', axis=0, tiled=True)]
    ppermute x6, waiting for transfers between devices: 0.02 us -> 3.23 us  [line_step(): out.append(lax.ppermute(sent, axis, pairs))]
  transfers between devices with their start and end apart: 31 -> 31, of which waited for: 12 -> 14; matrix products, arithmetic and copies ran while one was open for 16% -> 14% of each run, Pallas kernels for 13% -> 12%
where the time goes in v12:
time: 205 us; the launch traced here: 202 us
  waiting for transfers between devices  70.5 us (34%)
  starting transfers between devices  43.7 us (21%)
  Pallas kernels  29.2 us (14%)
  local copies, waits for them, and re-layouts  20.2 us (10%)
  other arithmetic  19.2 us (9%)
  between operations  14.6 us (7%)
  matrix products  4.92 us (2%)
    ppermute x23, waiting for transfers between devices, swap(): return lax.ppermute(x, axis, [(i, i ^ mask) for i in range(count)])  50.8 us
    ppermute x23, starting transfers between devices, swap(): return lax.ppermute(x, axis, [(i, i ^ mask) for i in range(count)])  27.2 us
    ppermute x6, starting transfers between devices, line_step(): out.append(lax.ppermute(sent, axis, pairs))  16.4 us
    all_gather x1, waiting for transfers between devices, on_device(): rows = lax.all_gather(image, 'seq', axis=0, tiled=True)  16.4 us
    unnamed x45, local copies, waits for them, and re-layouts  13.9 us
    pallas_call x1, Pallas kernels, weight_product(): pl.pallas_call(weight_kernel, grid=(features // step,), in_specs=[pl.Bloc...  6.91 us
    pallas_call x1, Pallas kernels, text_product(): pl.pallas_call(text_kernel, grid_spec=pltpu.PrefetchScalarGridSpec(num_sc...  6.32 us
    pallas_call x1, Pallas kernels, image_grads(): pl.pallas_call(image_kernel, in_specs=[pl.BlockSpec(memory_space=pltpu.SM...  5.65 us
  transfers between devices with their start and end apart: 31, of which 14 were waited for; matrix products, arithmetic and copies ran while one was open for 14% of the time, Pallas kernels for 12%

profile of v12, /device:TPU:0, one launch (start us, length us, event | category | flops | bytes accessed | tf_op | source)
XLA Modules:
  0.0 202.3 jit_solution(68981547393803425)
XLA Ops:
  7.2 5.3 %shard_map.137 = (f32[1,1024]{1,0:T(1,128)}, bf16[96,2048]{1,0:T(8,128)(2,1)}, bf16[768,128]{1,0:T(8,128)(2,1)}) custom-call(s32[1]{0:T(128)} %bitcast.1.core_ref, s32[1]{0:T(128)} %bitcast.2.z_ref, s32[1]{0:T(128)} %bitcast.t_ref.refs_0_, s32[4]{0:T(128)} %tiles_ref.3, s32[4]{0:T(128)} %owners_ref.3, bf16[1024,2048]{1,0:T(8,128)(2,1)} %text_ref.3, ...), custom_call_target="tpu_custom_call" | custom-call | flops 12058624 | bytes 4194304 | tf_op jit(solution)/shard_map/pallas_call | solution.py:193
  12.6 2.9 %collective-permute-start = (bf16[96,2048]{1,0:T(8,128)(2,1)}, bf16[96,2048]{1,0:T(8,128)(2,1)S(1)}, u32[]{:S(2)}, u32[]{:S(2)}) collective-permute-start(bf16[96,2048]{1,0:T(8,128)(2,1)} %get-tuple-element.29.refs_2_), channel_id=1, source_target_pairs={{0,1},{1,0},{2,3},{3,2},{4,5},{5,4},{6,7},{7,6},{8,9},{9,8},{10,11... | collective-permute-start | bytes 1179656 | tf_op jit(solution)/shard_map/ppermute | solution.py:18
  15.5 1.5 collective-permute-start.3
  17.0 2.0 %collective-permute-start.1 = (bf16[768,128]{1,0:T(8,128)(2,1)}, bf16[768,128]{1,0:T(8,128)(2,1)S(1)}, u32[]{:S(2)}, u32[]{:S(2)}) collective-permute-start(bf16[768,128]{1,0:T(8,128)(2,1)} %get-tuple-element.31), channel_id=1, source_target_pairs={{0,4},{4,0},{8,12},{12,8},{1,5},{5,1},{9,13},{13,9},{2,6},{6,2},{1... | collective-permute-start | bytes 589832 | tf_op jit(solution)/shard_map/ppermute | solution.py:18
  19.1 2.4 %collective-permute-start.7 = (f32[1,1024]{1,0:T(1,128)}, f32[1,1024]{1,0:T(1,128)S(1)}, u32[]{:S(2)}, u32[]{:S(2)}) collective-permute-start(f32[1,1024]{1,0:T(1,128)} %get-tuple-element.35.refs_0_), channel_id=1, source_target_pairs={{0,3},{1,2},{2,1},{3,0},{4,7},{5,6},{6,5},{7,4},{8,11},{9,10},{10,... | collective-permute-start | bytes 12296 | tf_op jit(solution)/shard_map/ppermute | solution.py:18
  21.5 1.8 collective-permute-done.1
  23.3 1.7 collective-permute-start.6
  25.0 1.0 add.91
  26.1 1.6 collective-permute-start.5
  27.7 6.9 %collective-permute-done.3.refs_5_ = bf16[96,2048]{1,0:T(8,128)(2,1)S(1)} collective-permute-done((bf16[96,2048]{1,0:T(8,128)(2,1)}, bf16[96,2048]{1,0:T(8,128)(2,1)S(1)}, u32[]{:S(2)}, u32[]{:S(2)}) %collective-permute-start.3) | collective-permute-done | bytes 393248 | tf_op jit(solution)/shard_map/ppermute | solution.py:18
  34.6 1.4 collective-permute-done.2.refs_4_
  36.1 3.4 %copy-done.14 = bf16[2048,2048]{1,0:T(8,128)(2,1)S(1)} copy-done((bf16[2048,2048]{1,0:T(8,128)(2,1)S(1)}, bf16[2048,2048]{1,0:T(8,128)(2,1)}, u32[]{:S(2)}) %copy-start.14) | copy-done | bytes 8388632
  39.4 1.0 copy-done.15
  40.4 4.8 %shard_map.138 = (bf16[384,2048]{1,0:T(8,128)(2,1)S(1)}, bf16[384,2048]{1,0:T(8,128)(2,1)S(1)}) custom-call(s32[1]{0:T(128)} %bitcast.t_ref.refs_0_, bf16[2048,2048]{1,0:T(8,128)(2,1)S(1)} %copy-done.14, bf16[96,2048]{1,0:T(8,128)(2,1)S(1)} %copy-done.15, bf16[96,2048]{1,0:T(8,128)(2,1)S(1)} %collective-permute-done.refs_3_, ...), custom_call_target="tpu_custom_call" | custom-call | flops 3221225472 | bytes 13107200 | tf_op jit(solution)/shard_map/pallas_call | solution.py:128
  45.2 1.1 copy-done.7
  46.4 1.1 copy-done.8
  47.7 2.2 %copy-done.1 = bf16[1024,2048]{1,0:T(8,128)(2,1)S(1)} copy-done((bf16[1024,2048]{1,0:T(8,128)(2,1)S(1)}, bf16[1024,2048]{1,0:T(8,128)(2,1)}, u32[]{:S(2)}) %copy-start.1) | copy-done | bytes 4194328
  49.9 2.2 %copy-done.2 = bf16[2048,1024]{1,0:T(8,128)(2,1)S(1)} copy-done((bf16[2048,1024]{1,0:T(8,128)(2,1)S(1)}, bf16[2048,1024]{1,0:T(8,128)(2,1)}, u32[]{:S(2)}) %copy-start.2) | copy-done | bytes 4194328
  52.0 6.3 %shard_map.139 = (bf16[4,2048,128]{2,1,0:T(8,128)(2,1)S(1)}, f32[1,2048]{1,0:T(1,128)S(1)}) custom-call(s32[1]{0:T(128)} %bitcast.1.core_ref, s32[1]{0:T(128)} %bitcast.2.z_ref, s32[4]{0:T(128)S(1)} %copy-done.11, s32[4]{0:T(128)S(1)} %copy-done.13, s32[4]{0:T(128)S(1)} %copy-done.12, bf16[1024,2048]{1,0:T(8,128)(2,1)S(1)} %copy-done.1, ...), custom_call_target="tpu_custom_call" | custom-call | flops 2147483648 | bytes 9437184 | tf_op jit(solution)/shard_map/pallas_call | solution.py:264
  58.4 1.3 copy-done.4
  59.8 0.7 collective-permute-start.9
  60.5 3.5 %collective-permute-start.8 = (bf16[2048,128]{1,0:T(8,128)(2,1)S(1)}, bf16[2048,128]{1,0:T(8,128)(2,1)S(1)}, u32[]{:S(2)}, u32[]{:S(2)}) collective-permute-start(bf16[2048,128]{1,0:T(8,128)(2,1)S(1)} %get-tuple-element.73), channel_id=1, source_target_pairs={{0,4},{1,5},{2,6},{3,7},{16,20},{17,21},{18,22},{19,23}} | collective-permute-start | bytes 1572872 | tf_op jit(solution)/shard_map/ppermute | solution.py:78
  64.5 30.1 %collective-permute-done.10 = bf16[768,128]{1,0:T(8,128)(2,1)S(1)} collective-permute-done((bf16[768,128]{1,0:T(8,128)(2,1)S(1)}, bf16[768,128]{1,0:T(8,128)(2,1)S(1)}, u32[]{:S(2)}, u32[]{:S(2)}) %collective-permute-start.10) | collective-permute-done | bytes 196640 | tf_op jit(solution)/shard_map/ppermute | solution.py:18
  94.6 1.7 collective-permute-start.13
  96.4 0.7 collective-permute-start.12
  97.1 1.6 collective-permute-start.11
  98.6 2.0 collective-permute-done.13
  100.6 3.5 %collective-permute-done.12 = bf16[768,128]{1,0:T(8,128)(2,1)S(1)} collective-permute-done((bf16[768,128]{1,0:T(8,128)(2,1)S(1)}, bf16[768,128]{1,0:T(8,128)(2,1)S(1)}, u32[]{:S(2)}, u32[]{:S(2)}) %collective-permute-start.12) | collective-permute-done | bytes 196640 | tf_op jit(solution)/shard_map/ppermute | solution.py:18
  104.1 1.0 broadcast_select_fusion.13
  105.1 1.0 pad_maximum_fusion.2
  106.1 2.6 %copy.23 = bf16[384,2048]{0,1:T(8,128)(2,1)} copy(bf16[384,2048]{1,0:T(8,128)(2,1)} %copy-done.8) | data formatting | bytes 3145728 | tf_op jit(solution)/shard_map/pallas_call | solution.py:128
  109.2 2.7 %fusion.6 = (bf16[2048,128]{1,0:T(8,128)(2,1)}, bf16[2048,128]{1,0:T(8,128)(2,1)}) fusion(bf16[2048,128]{1,0:T(8,128)(2,1)S(1)} %copy-done.17, bf16[4,2048,128]{2,1,0:T(8,128)(2,1)} %copy-done.4, s32[]{:T(128)S(6)} %min.22, bf16[2048,128]{1,0:T(8,128)(2,1)} %copy-done.18, s32[]{:T(128)S(6)} %min.21), kind=kLoop, calls=%fused_computation.16 | loop fusion | flops 2097152 | bytes 3145736 | tf_op jit(solution)/shard_map/convert_element_type | solution.py:75
  111.9 1.5 collective-permute-start.16
  113.4 5.4 %collective-permute-start.15 = (bf16[2048,128]{1,0:T(8,128)(2,1)}, bf16[2048,128]{1,0:T(8,128)(2,1)}, u32[]{:S(2)}, u32[]{:S(2)}) collective-permute-start(bf16[2048,128]{1,0:T(8,128)(2,1)} %get-tuple-element.71), channel_id=1, source_target_pairs={{0,4},{4,8},{1,5},{5,9},{2,6},{6,10},{3,7},{7,11},{16,20},{20,24},... | collective-permute-start | bytes 1572872 | tf_op jit(solution)/shard_map/ppermute | solution.py:78
  118.8 1.6 broadcast_select_fusion.1
  120.4 1.4 fusion.9.grad_ref
  121.8 3.5 %fusion.grad_ref = f32[768,1024]{1,0:T(8,128)} fusion(bf16[2048,1024]{1,0:T(8,128)(2,1)S(1)} %copy-done.3, s32[]{:T(128)S(6)} %select_n.188, bf16[768,512]{1,0:T(8,128)(2,1)S(1)} %get-tuple-element.75, bf16[768,512]{1,0:T(8,128)(2,1)S(1)} %get-tuple-element.74), kind=kOutput, calls=%fused_computation.2 | convolution fusion | flops 1613758464 | bytes 6815748 | tf_op jit(solution)/shard_map/dot_general | solution.py:474
  125.3 1.1 add_convert_fusion.rows_ref
  126.4 3.2 %collective-permute-done.15 = bf16[2048,128]{1,0:T(8,128)(2,1)} collective-permute-done((bf16[2048,128]{1,0:T(8,128)(2,1)}, bf16[2048,128]{1,0:T(8,128)(2,1)}, u32[]{:S(2)}, u32[]{:S(2)}) %collective-permute-start.15) | collective-permute-done | bytes 524320 | tf_op jit(solution)/shard_map/ppermute | solution.py:78
  130.1 1.1 collective-permute-done.17
  131.2 0.8 pad_maximum_fusion.4
  132.6 0.9 constant_dynamic-slice_fusion.1
  133.6 0.9 constant_dynamic-slice_fusion
  134.8 1.2 collective-permute-start.20
  136.0 1.1 collective-permute-start.19
  137.1 1.2 collective-permute-start.18
  138.3 0.8 pad_maximum_fusion.3.cot_ref
  139.6 1.1 collective-permute-done.18
  140.7 2.5 %collective-permute-start.23 = (f32[3328]{0:T(1024)S(1)}, f32[3328]{0:T(1024)S(1)}, u32[]{:S(2)}, u32[]{:S(2)}) collective-permute-start(f32[3328]{0:T(1024)S(1)} %pad_maximum_fusion.9), channel_id=1, source_target_pairs={{0,4},{4,0},{8,12},{12,8},{1,5},{5,1},{9,13},{13,9},{2,6},{6,2},{1... | collective-permute-start | bytes 39944 | tf_op jit(solution)/shard_map/ppermute | solution.py:18
  143.2 1.9 collective-permute-start.22
  145.1 1.4 collective-permute-start.21
  146.5 2.1 %maximum_bitcast_fusion.act_ref = bf16[2048,768]{1,0:T(8,128)(2,1)S(1)} fusion(bf16[384,2048]{0,1:T(8,128)(2,1)} %collective-permute-done.4, bf16[384,2048]{0,1:T(8,128)(2,1)} %copy.23), kind=kLoop, calls=%fused_computation.1 | loop fusion | flops 6291456 | bytes 6291456 | tf_op jit(solution)/shard_map/transpose | solution.py:522
  148.7 0.8 collective-permute-done.22
  149.5 1.6 collective-permute-done.21
  151.4 2.5 %fusion.4 = (bf16[2048,128]{1,0:T(8,128)(2,1)}, bf16[2048,128]{1,0:T(8,128)(2,1)}) fusion(bf16[2048,128]{1,0:T(8,128)(2,1)} %collective-permute-done.15, bf16[4,2048,128]{2,1,0:T(8,128)(2,1)S(1)} %copy-done.5, s32[]{:T(128)S(6)} %min.23, bf16[2048,128]{1,0:T(8,128)(2,1)} %collective-permute-done.16, s32[]{:T(128)S(6)} %min.24), kind=kLoop, calls=%fused_computation.12 | loop fusion | flops 2097152 | bytes 3145736 | tf_op jit(solution)/shard_map/convert_element_type | solution.py:75
  153.9 3.9 %collective-permute-start.26 = (bf16[2048,128]{1,0:T(8,128)(2,1)}, bf16[2048,128]{1,0:T(8,128)(2,1)}, u32[]{:S(2)}, u32[]{:S(2)}) collective-permute-start(bf16[2048,128]{1,0:T(8,128)(2,1)} %get-tuple-element.68), channel_id=1, source_target_pairs={{0,4},{4,8},{8,12},{1,5},{5,9},{9,13},{2,6},{6,10},{10,14},{3,7},{... | collective-permute-start | bytes 1572872 | tf_op jit(solution)/shard_map/ppermute | solution.py:78
  157.8 1.5 collective-permute-start.27
  159.3 0.6 copy.24
  160.6 16.4 %all-gather.2.cloned.1.call-done.rows_ref = bf16[768,1024]{1,0:T(8,128)(2,1)} async-done(((bf16[192,1024]{1,0:T(8,128)(2,1)}), bf16[768,1024]{1,0:T(8,128)(2,1)}) %all-gather.2.cloned.1.call-update) | async-done | bytes 1572880 | tf_op jit(solution)/shard_map/all_gather | solution.py:494
  177.0 5.7 %shard_map.141 = (bf16[768,1024]{1,0:T(8,128)(2,1)}, f32[1024,128]{1,0:T(8,128)}, bf16[1024,128]{1,0:T(8,128)(2,1)}, f32[2,1024]{1,0:T(2,128)}) custom-call(s32[1]{0:T(128)} %bitcast.1.core_ref, f32[768,1024]{1,0:T(8,128)} %fusion.grad_ref, f32[1,1024]{1,0:T(1,128)} %bitcast.53, bf16[768,256]{1,0:T(8,128)(2,1)} %pad_maximum_fusion.3.cot_ref, ...), custom_call_target="tpu_custom_call" | custom-call | flops 402653184 | bytes 6291456 | tf_op jit(solution)/shard_map/pallas_call | solution.py:364
  183.1 1.4 copy-done.6
  184.5 6.9 %shard_map.142 = f32[16384,128]{1,0:T(8,128)} custom-call(bf16[2048,768]{1,0:T(8,128)(2,1)S(1)} %maximum_bitcast_fusion.act_ref, bf16[768,1024]{1,0:T(8,128)(2,1)S(1)} %copy-done.6), custom_call_target="tpu_custom_call" | custom-call | flops 3221225472 | bytes 13107200 | tf_op jit(solution)/shard_map/pallas_call | solution.py:394
  191.5 0.6 pad_maximum_fusion.11
  192.8 2.7 %fusion.2 = f32[2048,128]{1,0:T(8,128)} fusion(f32[1024,128]{1,0:T(8,128)S(1)} %get-tuple-element.77, f32[1024,128]{1,0:T(8,128)S(1)} %get-tuple-element.76, bf16[2048,128]{1,0:T(8,128)(2,1)} %collective-permute-done.27, bf16[2048,128]{1,0:T(8,128)(2,1)} %collective-permute-done.26, f32[2048]{0:T(1024)S(1)} %copy-done.9, bf16[4,2048,128]{2,1,0:T(8,128)(2,1)} %copy-done.4, ...), kind=kLoop, calls=%fused_computation.8 | loop fusion | flops 2097152 | bytes 3678212 | tf_op jit(solution)/shard_map/mul | solution.py:527
  (94 shorter events, 5.2 us)
Async XLA Ops:
  7.2 118.2 %reduce-scatter.2.cloned.1.call-start = ((), (), s32[]{:S(2)}) async-start(), calls=%async_computation.1 | async-start | bytes 1966080 | tf_op jit(solution)/shard_map/reduce_scatter | solution.py:463
  12.6 13.5 %collective-permute-start = (bf16[96,2048]{1,0:T(8,128)(2,1)}, bf16[96,2048]{1,0:T(8,128)(2,1)S(1)}, u32[]{:S(2)}, u32[]{:S(2)}) collective-permute-start(bf16[96,2048]{1,0:T(8,128)(2,1)} %get-tuple-element.29.refs_2_), channel_id=1, source_target_pairs={{0,1},{1,0},{2,3},{3,2},{4,5},{5,4},{6,7},{7,6},{8,9},{9,8},{10,11... | collective-permute-start | bytes 1179656 | tf_op jit(solution)/shard_map/ppermute | solution.py:18
  15.5 19.1 %collective-permute-start.3 = (bf16[96,2048]{1,0:T(8,128)(2,1)}, bf16[96,2048]{1,0:T(8,128)(2,1)S(1)}, u32[]{:S(2)}, u32[]{:S(2)}) collective-permute-start(bf16[96,2048]{1,0:T(8,128)(2,1)} %get-tuple-element.29.refs_2_), channel_id=1, source_target_pairs={{0,3},{1,2},{2,1},{3,0},{4,7},{5,6},{6,5},{7,4},{8,11},{9,10},{10,... | collective-permute-start | bytes 1179656 | tf_op jit(solution)/shard_map/ppermute | solution.py:18
  17.0 19.1 %collective-permute-start.2 = (bf16[96,2048]{1,0:T(8,128)(2,1)}, bf16[96,2048]{1,0:T(8,128)(2,1)S(1)}, u32[]{:S(2)}, u32[]{:S(2)}) collective-permute-start(bf16[96,2048]{1,0:T(8,128)(2,1)} %get-tuple-element.29.refs_2_), channel_id=1, source_target_pairs={{0,2},{1,3},{2,0},{3,1},{4,6},{5,7},{6,4},{7,5},{8,10},{9,11},{10,... | collective-permute-start | bytes 1179656 | tf_op jit(solution)/shard_map/ppermute | solution.py:18
  17.0 6.3 %collective-permute-start.1 = (bf16[768,128]{1,0:T(8,128)(2,1)}, bf16[768,128]{1,0:T(8,128)(2,1)S(1)}, u32[]{:S(2)}, u32[]{:S(2)}) collective-permute-start(bf16[768,128]{1,0:T(8,128)(2,1)} %get-tuple-element.31), channel_id=1, source_target_pairs={{0,4},{4,0},{8,12},{12,8},{1,5},{5,1},{9,13},{13,9},{2,6},{6,2},{1... | collective-permute-start | bytes 589832 | tf_op jit(solution)/shard_map/ppermute | solution.py:18
  19.1 28.5 %collective-permute-start.7 = (f32[1,1024]{1,0:T(1,128)}, f32[1,1024]{1,0:T(1,128)S(1)}, u32[]{:S(2)}, u32[]{:S(2)}) collective-permute-start(f32[1,1024]{1,0:T(1,128)} %get-tuple-element.35.refs_0_), channel_id=1, source_target_pairs={{0,3},{1,2},{2,1},{3,0},{4,7},{5,6},{6,5},{7,4},{8,11},{9,10},{10,... | collective-permute-start | bytes 12296 | tf_op jit(solution)/shard_map/ppermute | solution.py:18
  23.3 24.3 %collective-permute-start.6 = (f32[1,1024]{1,0:T(1,128)}, f32[1,1024]{1,0:T(1,128)S(1)}, u32[]{:S(2)}, u32[]{:S(2)}) collective-permute-start(f32[1,1024]{1,0:T(1,128)} %get-tuple-element.35.refs_0_), channel_id=1, source_target_pairs={{0,2},{1,3},{2,0},{3,1},{4,6},{5,7},{6,4},{7,5},{8,10},{9,11},{10,... | collective-permute-start | bytes 12296 | tf_op jit(solution)/shard_map/ppermute | solution.py:18
  26.0 21.6 %copy-start.10 = (f32[1,1024]{1,0:T(1,128)S(1)}, f32[1,1024]{1,0:T(1,128)}, u32[]{:S(2)}) copy-start(f32[1,1024]{1,0:T(1,128)} %get-tuple-element.35.refs_0_) | copy-start | bytes 12292
  26.0 21.6 %copy-start.11 = (s32[4]{0:T(128)S(1)}, s32[4]{0:T(128)}, u32[]{:S(2)}) copy-start(s32[4]{0:T(128)} %tiles_ref.3) | copy-start | bytes 52
  26.0 21.6 %copy-start.12 = (s32[4]{0:T(128)S(1)}, s32[4]{0:T(128)}, u32[]{:S(2)}) copy-start(s32[4]{0:T(128)} %owners_ref.3) | copy-start | bytes 52
  26.0 21.6 %copy-start.13 = (s32[4]{0:T(128)S(1)}, s32[4]{0:T(128)}, u32[]{:S(2)}) copy-start(s32[4]{0:T(128)} %texts_ref.1) | copy-start | bytes 52
  26.1 21.5 %collective-permute-start.5 = (f32[1,1024]{1,0:T(1,128)}, f32[1,1024]{1,0:T(1,128)S(1)}, u32[]{:S(2)}, u32[]{:S(2)}) collective-permute-start(f32[1,1024]{1,0:T(1,128)} %get-tuple-element.35.refs_0_), channel_id=1, source_target_pairs={{0,1},{1,0},{2,3},{3,2},{4,5},{5,4},{6,7},{7,6},{8,9},{9,8},{10,11... | collective-permute-start | bytes 12296 | tf_op jit(solution)/shard_map/ppermute | solution.py:18
  36.1 3.4 %copy-start.14 = (bf16[2048,2048]{1,0:T(8,128)(2,1)S(1)}, bf16[2048,2048]{1,0:T(8,128)(2,1)}, u32[]{:S(2)}) copy-start(bf16[2048,2048]{1,0:T(8,128)(2,1)} %refs_1_.1) | copy-start | bytes 25165828
  39.4 1.0 copy-start.15
  40.4 7.2 %copy-start = (bf16[1024,1024]{1,0:T(8,128)(2,1)S(1)}, bf16[1024,1024]{1,0:T(8,128)(2,1)}, u32[]{:S(2)}) copy-start(bf16[1024,1024]{1,0:T(8,128)(2,1)} %cot_ref.3) | copy-start | bytes 6291460
  45.2 1.1 copy-start.7
  46.4 1.1 copy-start.8
  47.5 129.4 %all-gather.2.cloned.1.call-start = ((), (), s32[]{:S(2)}) async-start(), calls=%async_computation.2 | async-start | bytes 1966080 | tf_op jit(solution)/shard_map/all_gather | solution.py:494
  47.7 2.2 %copy-start.1 = (bf16[1024,2048]{1,0:T(8,128)(2,1)S(1)}, bf16[1024,2048]{1,0:T(8,128)(2,1)}, u32[]{:S(2)}) copy-start(bf16[1024,2048]{1,0:T(8,128)(2,1)} %text_ref.3) | copy-start | bytes 12582916
  49.9 2.2 %copy-start.2 = (bf16[2048,1024]{1,0:T(8,128)(2,1)S(1)}, bf16[2048,1024]{1,0:T(8,128)(2,1)}, u32[]{:S(2)}) copy-start(bf16[2048,1024]{1,0:T(8,128)(2,1)} %weight_ref.1) | copy-start | bytes 12582916
  58.4 1.4 copy-start.4
  59.8 34.8 %collective-permute-start.9 = (bf16[2048,128]{1,0:T(8,128)(2,1)S(1)}, bf16[2048,128]{1,0:T(8,128)(2,1)S(1)}, u32[]{:S(2)}, u32[]{:S(2)}) collective-permute-start(bf16[2048,128]{1,0:T(8,128)(2,1)S(1)} %get-tuple-element.72), channel_id=1, source_target_pairs={{12,8},{13,9},{14,10},{15,11},{28,24},{29,25},{30,26},{31,27}} | collective-permute-start | bytes 1572872 | tf_op jit(solution)/shard_map/ppermute | solution.py:78
  60.5 34.1 %collective-permute-start.8 = (bf16[2048,128]{1,0:T(8,128)(2,1)S(1)}, bf16[2048,128]{1,0:T(8,128)(2,1)S(1)}, u32[]{:S(2)}, u32[]{:S(2)}) collective-permute-start(bf16[2048,128]{1,0:T(8,128)(2,1)S(1)} %get-tuple-element.73), channel_id=1, source_target_pairs={{0,4},{1,5},{2,6},{3,7},{16,20},{17,21},{18,22},{19,23}} | collective-permute-start | bytes 1572872 | tf_op jit(solution)/shard_map/ppermute | solution.py:78
  64.0 30.5 %collective-permute-start.10 = (bf16[768,128]{1,0:T(8,128)(2,1)S(1)}, bf16[768,128]{1,0:T(8,128)(2,1)S(1)}, u32[]{:S(2)}, u32[]{:S(2)}) collective-permute-start(bf16[768,128]{1,0:T(8,128)(2,1)S(1)} %add.91), channel_id=1, source_target_pairs={{0,8},{4,12},{8,0},{12,4},{1,9},{5,13},{9,1},{13,5},{2,10},{6,14},... | collective-permute-start | bytes 589832 | tf_op jit(solution)/shard_map/ppermute | solution.py:18
  94.6 9.5 %copy-start.16 = (bf16[2048,128]{1,0:T(8,128)(2,1)}, bf16[2048,128]{1,0:T(8,128)(2,1)S(1)}, u32[]{:S(2)}) copy-start(bf16[2048,128]{1,0:T(8,128)(2,1)S(1)} %collective-permute-done.9) | copy-start | bytes 1572868
  94.6 1.7 copy-start.18
  94.6 6.0 %collective-permute-start.13 = (bf16[768,128]{1,0:T(8,128)(2,1)S(1)}, bf16[768,128]{1,0:T(8,128)(2,1)S(1)}, u32[]{:S(2)}, u32[]{:S(2)}) collective-permute-start(bf16[768,128]{1,0:T(8,128)(2,1)S(1)} %add.94), channel_id=1, source_target_pairs={{0,1},{1,0},{2,3},{3,2},{4,5},{5,4},{6,7},{7,6},{8,9},{9,8},{10,11... | collective-permute-start | bytes 589832 | tf_op jit(solution)/shard_map/ppermute | solution.py:18
  96.4 7.8 %collective-permute-start.12 = (bf16[768,128]{1,0:T(8,128)(2,1)S(1)}, bf16[768,128]{1,0:T(8,128)(2,1)S(1)}, u32[]{:S(2)}, u32[]{:S(2)}) collective-permute-start(bf16[768,128]{1,0:T(8,128)(2,1)S(1)} %add.94), channel_id=1, source_target_pairs={{0,2},{1,3},{2,0},{3,1},{4,6},{5,7},{6,4},{7,5},{8,10},{9,11},{10,... | collective-permute-start | bytes 589832 | tf_op jit(solution)/shard_map/ppermute | solution.py:18
  97.1 7.1 %collective-permute-start.11 = (bf16[768,128]{1,0:T(8,128)(2,1)S(1)}, bf16[768,128]{1,0:T(8,128)(2,1)}, u32[]{:S(2)}, u32[]{:S(2)}) collective-permute-start(bf16[768,128]{1,0:T(8,128)(2,1)S(1)} %add.94), channel_id=1, source_target_pairs={{0,3},{1,2},{2,1},{3,0},{4,7},{5,6},{6,5},{7,4},{8,11},{9,10},{10,... | collective-permute-start | bytes 589832 | tf_op jit(solution)/shard_map/ppermute | solution.py:18
  105.1 4.1 %copy-start.17 = (bf16[2048,128]{1,0:T(8,128)(2,1)S(1)}, bf16[2048,128]{1,0:T(8,128)(2,1)}, u32[]{:S(2)}) copy-start(bf16[2048,128]{1,0:T(8,128)(2,1)} %copy-done.16) | copy-start | bytes 1572868
  106.1 12.7 %collective-permute-start.14 = (bf16[768,512]{1,0:T(8,128)(2,1)}, bf16[768,512]{1,0:T(8,128)(2,1)}, u32[]{:S(2)}, u32[]{:S(2)}) collective-permute-start(bf16[768,512]{1,0:T(8,128)(2,1)} %pad_maximum_fusion.2), channel_id=1, source_target_pairs={{0,16},{16,0},{1,17},{17,1},{2,18},{18,2},{3,19},{19,3},{4,20},{20... | collective-permute-start | bytes 2359304 | tf_op jit(solution)/shard_map/ppermute | solution.py:18
  108.7 37.8 %collective-permute-start.4 = (bf16[384,2048]{0,1:T(8,128)(2,1)}, bf16[384,2048]{0,1:T(8,128)(2,1)}, u32[]{:S(2)}, u32[]{:S(2)}) collective-permute-start(bf16[384,2048]{0,1:T(8,128)(2,1)} %copy.23), channel_id=1, source_target_pairs={{0,16},{16,0},{1,17},{17,1},{2,18},{18,2},{3,19},{19,3},{4,20},{20... | collective-permute-start | bytes 4718600 | tf_op jit(solution)/shard_map/ppermute | solution.py:18
  109.2 11.2 %copy-start.3 = (bf16[2048,1024]{1,0:T(8,128)(2,1)S(1)}, bf16[2048,1024]{1,0:T(8,128)(2,1)}, u32[]{:S(2)}) copy-start(bf16[2048,1024]{1,0:T(8,128)(2,1)} %weight_ref.1) | copy-start | bytes 12582916
  111.9 14.5 %collective-permute-start.16 = (bf16[2048,128]{1,0:T(8,128)(2,1)}, bf16[2048,128]{1,0:T(8,128)(2,1)}, u32[]{:S(2)}, u32[]{:S(2)}) collective-permute-start(bf16[2048,128]{1,0:T(8,128)(2,1)} %get-tuple-element.70), channel_id=1, source_target_pairs={{12,8},{8,4},{13,9},{9,5},{14,10},{10,6},{15,11},{11,7},{28,24},{2... | collective-permute-start | bytes 1572872 | tf_op jit(solution)/shard_map/ppermute | solution.py:78
  113.4 16.2 %collective-permute-start.15 = (bf16[2048,128]{1,0:T(8,128)(2,1)}, bf16[2048,128]{1,0:T(8,128)(2,1)}, u32[]{:S(2)}, u32[]{:S(2)}) collective-permute-start(bf16[2048,128]{1,0:T(8,128)(2,1)} %get-tuple-element.71), channel_id=1, source_target_pairs={{0,4},{4,8},{1,5},{5,9},{2,6},{6,10},{3,7},{7,11},{16,20},{20,24},... | collective-permute-start | bytes 1572872 | tf_op jit(solution)/shard_map/ppermute | solution.py:78
  121.8 3.5 %copy-start.20 = (f32[2048]{0:T(1024)S(1)}, f32[2048]{0:T(1024)}, u32[]{:S(2)}) copy-start(f32[2048]{0:T(1024)} %param.12) | copy-start | bytes 24580
  129.7 2.4 %copy-start.9 = (f32[2048]{0:T(1024)S(1)}, f32[2048]{0:T(1024)}, u32[]{:S(2)}) copy-start(f32[2048]{0:T(1024)} %param.14) | copy-start | bytes 24580
  129.7 1.5 collective-permute-start.17
  134.8 4.5 %collective-permute-start.20 = (f32[2,128]{1,0:T(2,128)S(1)}, f32[2,128]{1,0:T(2,128)S(1)}, u32[]{:S(2)}, u32[]{:S(2)}) collective-permute-start(f32[2,128]{1,0:T(2,128)S(1)} %shard_map.140), channel_id=1, source_target_pairs={{0,3},{1,2},{2,1},{3,0},{4,7},{5,6},{6,5},{7,4},{8,11},{9,10},{10,... | collective-permute-start | bytes 3080 | tf_op jit(solution)/shard_map/ppermute | solution.py:18
  136.0 3.6 %collective-permute-start.19 = (f32[2,128]{1,0:T(2,128)S(1)}, f32[2,128]{1,0:T(2,128)S(1)}, u32[]{:S(2)}, u32[]{:S(2)}) collective-permute-start(f32[2,128]{1,0:T(2,128)S(1)} %shard_map.140), channel_id=1, source_target_pairs={{0,2},{1,3},{2,0},{3,1},{4,6},{5,7},{6,4},{7,5},{8,10},{9,11},{10,... | collective-permute-start | bytes 3080 | tf_op jit(solution)/shard_map/ppermute | solution.py:18
  137.1 3.6 %collective-permute-start.18 = (f32[2,128]{1,0:T(2,128)S(1)}, f32[2,128]{1,0:T(2,128)S(1)}, u32[]{:S(2)}, u32[]{:S(2)}) collective-permute-start(f32[2,128]{1,0:T(2,128)S(1)} %shard_map.140), channel_id=1, source_target_pairs={{0,1},{1,0},{2,3},{3,2},{4,5},{5,4},{6,7},{7,6},{8,9},{9,8},{10,11... | collective-permute-start | bytes 3080 | tf_op jit(solution)/shard_map/ppermute | solution.py:18
  140.7 10.7 %copy-start.5 = (bf16[4,2048,128]{2,1,0:T(8,128)(2,1)S(1)}, bf16[4,2048,128]{2,1,0:T(8,128)(2,1)}, u32[]{:S(2)}) copy-start(bf16[4,2048,128]{2,1,0:T(8,128)(2,1)} %copy-done.4) | copy-start | bytes 6291460
  140.7 8.0 %collective-permute-start.23 = (f32[3328]{0:T(1024)S(1)}, f32[3328]{0:T(1024)S(1)}, u32[]{:S(2)}, u32[]{:S(2)}) collective-permute-start(f32[3328]{0:T(1024)S(1)} %pad_maximum_fusion.9), channel_id=1, source_target_pairs={{0,4},{4,0},{8,12},{12,8},{1,5},{5,1},{9,13},{13,9},{2,6},{6,2},{1... | collective-permute-start | bytes 39944 | tf_op jit(solution)/shard_map/ppermute | solution.py:18
  143.2 6.2 %collective-permute-start.22 = (f32[3328]{0:T(1024)S(1)}, f32[3328]{0:T(1024)S(1)}, u32[]{:S(2)}, u32[]{:S(2)}) collective-permute-start(f32[3328]{0:T(1024)S(1)} %pad_maximum_fusion.9), channel_id=1, source_target_pairs={{0,8},{4,12},{8,0},{12,4},{1,9},{5,13},{9,1},{13,5},{2,10},{6,14},... | collective-permute-start | bytes 39944 | tf_op jit(solution)/shard_map/ppermute | solution.py:18
  145.1 6.0 %collective-permute-start.21 = (f32[3328]{0:T(1024)S(1)}, f32[3328]{0:T(1024)S(1)}, u32[]{:S(2)}, u32[]{:S(2)}) collective-permute-start(f32[3328]{0:T(1024)S(1)} %pad_maximum_fusion.9), channel_id=1, source_target_pairs={{0,12},{4,8},{8,4},{12,0},{1,13},{5,9},{9,5},{13,1},{2,14},{6,10},... | collective-permute-start | bytes 39944 | tf_op jit(solution)/shard_map/ppermute | solution.py:18
  151.3 8.0 %collective-permute-start.24 = (f32[4096]{0:T(1024)S(1)}, f32[4096]{0:T(1024)S(1)}, u32[]{:S(2)}, u32[]{:S(2)}) collective-permute-start(f32[4096]{0:T(1024)S(1)} %pad_maximum_fusion.10), channel_id=1, source_target_pairs={{0,16},{16,0},{1,17},{17,1},{2,18},{18,2},{3,19},{19,3},{4,20},{20... | collective-permute-start | bytes 49160 | tf_op jit(solution)/shard_map/ppermute | solution.py:18
  153.9 38.9 %collective-permute-start.26 = (bf16[2048,128]{1,0:T(8,128)(2,1)}, bf16[2048,128]{1,0:T(8,128)(2,1)}, u32[]{:S(2)}, u32[]{:S(2)}) collective-permute-start(bf16[2048,128]{1,0:T(8,128)(2,1)} %get-tuple-element.68), channel_id=1, source_target_pairs={{0,4},{4,8},{8,12},{1,5},{5,9},{9,13},{2,6},{6,10},{10,14},{3,7},{... | collective-permute-start | bytes 1572872 | tf_op jit(solution)/shard_map/ppermute | solution.py:78
  157.8 35.0 %collective-permute-start.27 = (bf16[2048,128]{1,0:T(8,128)(2,1)}, bf16[2048,128]{1,0:T(8,128)(2,1)}, u32[]{:S(2)}, u32[]{:S(2)}) collective-permute-start(bf16[2048,128]{1,0:T(8,128)(2,1)} %get-tuple-element.69), channel_id=1, source_target_pairs={{12,8},{8,4},{4,0},{13,9},{9,5},{5,1},{14,10},{10,6},{6,2},{15,11}... | collective-permute-start | bytes 1572872 | tf_op jit(solution)/shard_map/ppermute | solution.py:78
  182.6 8.8 %collective-permute-start.25 = (f32[2,1024]{1,0:T(2,128)}, f32[2,1024]{1,0:T(2,128)S(1)}, u32[]{:S(2)}, u32[]{:S(2)}) collective-permute-start(f32[2,1024]{1,0:T(2,128)} %get-tuple-element.48), channel_id=1, source_target_pairs={{0,16},{16,0},{1,17},{17,1},{2,18},{18,2},{3,19},{19,3},{4,20},{20... | collective-permute-start | bytes 24584 | tf_op jit(solution)/shard_map/ppermute | solution.py:18
  182.6 10.1 %collective-permute-start.28 = (bf16[1024,128]{1,0:T(8,128)(2,1)}, bf16[1024,128]{1,0:T(8,128)(2,1)S(1)}, u32[]{:S(2)}, u32[]{:S(2)}) collective-permute-start(bf16[1024,128]{1,0:T(8,128)(2,1)} %get-tuple-element.51), channel_id=1, source_target_pairs={{0,16},{16,0},{1,17},{17,1},{2,18},{18,2},{3,19},{19,3},{4,20},{20... | collective-permute-start | bytes 786440 | tf_op jit(solution)/shard_map/ppermute | solution.py:18
  183.1 1.4 copy-start.6
  184.5 6.9 %copy-start.21 = (f32[2,1024]{1,0:T(2,128)S(1)}, f32[2,1024]{1,0:T(2,128)}, u32[]{:S(2)}) copy-start(f32[2,1024]{1,0:T(2,128)} %get-tuple-element.48) | copy-start | bytes 24580
  184.5 8.1 %copy-start.19 = (f32[1024,128]{1,0:T(8,128)S(1)}, f32[1024,128]{1,0:T(8,128)}, u32[]{:S(2)}) copy-start(f32[1024,128]{1,0:T(8,128)} %get-tuple-element.52) | copy-start | bytes 1572868
Sparse Core Ops, SparseCore 0:
  47.7 51.0 reduce-scatter.1
  132.1 44.7 all-gather.1
